TPU v7x, 32 devices: a whole 2x2x4 slice. The times are simulated.
32 devices in a mesh: row: 4 (over x, core), col: 8 (over z, y).
Axes of the slice: x: 2, y: 2, z: 4, core: 2. Of those that a mesh axis runs over, the one named last changes fastest.
Arguments:
- queries: float32 [32, 16384], P(None, ('row', 'col'))
- block_spots: int32 [4, 8, 256], P('row', 'col'), may hold values from 0 to 511, as said below
- live_blocks: int32 [4, 8], P('row', 'col'), may hold values from 1 to 256, as said below
- neighbor_cols: int32 [4, 8, 256, 16, 128], P('row', 'col'), may hold values from 0 to 127
- neighbor_sims: bfloat16 [4, 8, 256, 16, 128], P('row', 'col'), may hold values from 0.099609375 to 1
Outputs:
- solution: float32 [32, 16384], P(None, ('row', 'col'))
- residual: float32 [32, 16384], P(None, ('row', 'col'))
Inputs may be any that keep to these rules, and one draw needn't show every extreme that they name: `block_spots`: within each index of the first two dimensions the 256 spots are distinct. `live_blocks`: some index of the array holds exactly 256.
All inputs are finite; a program needn't handle non-finite values.
Results may differ from a plain program's by a relative error of at most 0.01.
Values may be sent and summed in bfloat16 or wider, within the bound.
No kernel may reach another device: no remote copies, remote signals or barrier semaphores. Data moves between devices by JAX's collectives and lax.ppermute only.
A program may use at most 128 MiB of HBM per device.

v0:
```python
import functools

import jax
import jax.numpy as jnp
from jax import lax
from jax.experimental import pallas as pl
from jax.experimental.pallas import tpu as pltpu
from jax.sharding import PartitionSpec as P

graph_weight = 0.95
GROUP = 16
BATCH = 32
VMEM_LIMIT = 60 * 1024 * 1024


def dot_plain(left, right, **kwargs):
    return lax.dot_general(
        left, right, (((1,), (0,)), ((), ())), preferred_element_type=jnp.float32, **kwargs
    )


def dot_across(left, right, **kwargs):
    return lax.dot_general(
        left, right, (((1,), (1,)), ((), ())), preferred_element_type=jnp.float32, **kwargs
    )


exact_plain = functools.partial(dot_plain, precision=lax.Precision.HIGHEST)
exact_across = functools.partial(dot_across, precision=lax.Precision.HIGHEST)


LIVE, ROW, COL, PLACES = 0, 1, 2, 4


def group_count(facts_ref, group):
    return (facts_ref[LIVE] + group - 1) // group


def group_copy(source, target, sems, index, group):
    window = pl.ds(index * group, group)
    return pltpu.make_async_copy(source.at[window], target.at[window], sems.at[index])


def build_kernel(row_count, facts_ref, index_hbm, value_hbm, block_hbm, *refs):
    row_outs = refs[:row_count]
    (
        col_out_ref,
        index_ref,
        value_ref,
        block_ref,
        row_ref,
        col_ref,
        index_sems,
        value_sems,
        block_sems,
    ) = refs[row_count:]
    slots = index_ref.shape[0]
    per_seg = row_outs[0].shape[0]
    groups = group_count(facts_ref, BATCH) * (BATCH // GROUP)

    def start_copies(index, _):
        group_copy(index_hbm, index_ref, index_sems, index, GROUP).start()
        group_copy(value_hbm, value_ref, value_sems, index, GROUP).start()
        return 0

    lax.fori_loop(0, groups, start_copies, 0)
    row_ref[...] = jnp.zeros_like(row_ref)
    col_ref[...] = jnp.zeros_like(col_ref)
    rows_16 = lax.broadcasted_iota(jnp.int32, (16, 128), 0).astype(jnp.float32)
    ones = jnp.ones((8, 128), jnp.bfloat16)
    zero = jnp.zeros((16, 128), jnp.bfloat16)

    def build_group(index, _):
        group_copy(index_hbm, index_ref, index_sems, index, GROUP).wait()
        group_copy(value_hbm, value_ref, value_sems, index, GROUP).wait()
        targets = [(rows_16 + 16.0 * part).astype(jnp.bfloat16) for part in range(8)]
        row_sums = []
        col_sums = []
        for inside in range(GROUP):
            slot = index * GROUP + inside
            active = (slot < facts_ref[LIVE]).astype(jnp.float32)
            index_f32 = index_ref[slot].astype(jnp.float32)
            value_f32 = value_ref[slot].astype(jnp.float32) * active
            sums = [zero] * 8
            for entry in range(16):
                index_row = jnp.broadcast_to(index_f32[entry : entry + 1], (16, 128)).astype(
                    jnp.bfloat16
                )
                value_row = jnp.broadcast_to(value_f32[entry : entry + 1], (16, 128)).astype(
                    jnp.bfloat16
                )
                for part in range(8):
                    sums[part] = sums[part] + jnp.where(
                        index_row == targets[part], value_row, zero
                    )
            block = jnp.concatenate(sums, axis=0)
            block_ref[slot] = block
            row_sums.append(dot_plain(ones, block))
            col_sums.append(dot_across(ones, block))
        group_copy(block_ref, block_hbm, block_sems, index, GROUP).start()
        for inside in range(GROUP):
            slot = index * GROUP + inside
            row_ref[facts_ref[PLACES + slot]] += row_sums[inside]
            col_ref[facts_ref[PLACES + slots + slot]] += col_sums[inside]
        return 0

    lax.fori_loop(0, groups, build_group, 0)
    for ahead, out in enumerate(row_outs):
        first = lax.rem(facts_ref[ROW] + ahead, row_count) * per_seg
        for part in range(per_seg):
            out[part : part + 1] = row_ref[first + part][:1]
    for col_block in range(col_out_ref.shape[0]):
        col_out_ref[col_block : col_block + 1] = col_ref[col_block][:1]

    def finish_copies(index, _):
        group_copy(block_ref, block_hbm, block_sems, index, GROUP).wait()
        return 0

    lax.fori_loop(0, groups, finish_copies, 0)


SCALARS = pl.BlockSpec(memory_space=pltpu.SMEM)
ANYWHERE = pl.BlockSpec(memory_space=pl.ANY)
IN_VMEM = pl.BlockSpec(memory_space=pltpu.VMEM)


def build_blocks(facts, index_table, value_table, row_count, col_count, per_seg):
    slots = index_table.shape[0]
    groups = slots // GROUP
    sum_shapes = [(per_seg, 128)] * row_count + [(col_count * per_seg, 128)]
    return pl.pallas_call(
        functools.partial(build_kernel, row_count),
        in_specs=[SCALARS, ANYWHERE, ANYWHERE],
        out_specs=[ANYWHERE] + [IN_VMEM] * len(sum_shapes),
        out_shape=[jax.ShapeDtypeStruct((slots, 128, 128), jnp.bfloat16)]
        + [jax.ShapeDtypeStruct(shape, jnp.float32) for shape in sum_shapes],
        scratch_shapes=[
            pltpu.VMEM(index_table.shape, index_table.dtype),
            pltpu.VMEM(value_table.shape, value_table.dtype),
            pltpu.VMEM((slots, 128, 128), jnp.bfloat16),
            pltpu.VMEM((row_count * per_seg, 8, 128), jnp.float32),
            pltpu.VMEM((col_count * per_seg, 8, 128), jnp.float32),
            pltpu.SemaphoreType.DMA((groups,)),
            pltpu.SemaphoreType.DMA((groups,)),
            pltpu.SemaphoreType.DMA((groups,)),
        ],
        compiler_params=pltpu.CompilerParams(vmem_limit_bytes=VMEM_LIMIT),
        name="build_blocks",
    )(facts, index_table, value_table)


def each_group(facts_ref, block_hbm, block_ref, sems, prepare, run_group):
    groups = group_count(facts_ref, BATCH)

    def start_copy(index, _):
        group_copy(block_hbm, block_ref, sems, index, BATCH).start()
        return 0

    lax.fori_loop(0, groups, start_copy, 0)
    prepare()

    def one_group(index, _):
        group_copy(block_hbm, block_ref, sems, index, BATCH).wait()
        run_group(index * BATCH)
        return 0

    lax.fori_loop(0, groups, one_group, 0)


def add_products(dot, facts_ref, first_slot, block_ref, dir_ref, sources, total_refs, targets):
    sums = []
    for inside in range(BATCH):
        slot = first_slot + inside
        sums.append(dot(dir_ref[facts_ref[sources + slot]], block_ref[slot]))
    for inside in range(BATCH):
        total_ref = total_refs[inside % len(total_refs)]
        total_ref[facts_ref[targets + first_slot + inside]] += sums[inside]


def fill_directions(pieces, dir_ref, mine, per_seg):
    for behind, piece in enumerate(pieces):
        first = lax.rem(mine + (len(pieces) - behind), len(pieces)) * per_seg
        for part in range(per_seg):
            dir_ref[first + part] = piece[part]


def backward_kernel(facts_ref, block_hbm, *refs):
    *row_pieces, col_out_ref, block_ref, row_dir_ref, even_ref, odd_ref, sems = refs
    per_seg = row_pieces[0].shape[0]
    slots = block_ref.shape[0]

    def prepare():
        even_ref[...] = jnp.zeros_like(even_ref)
        odd_ref[...] = jnp.zeros_like(odd_ref)
        fill_directions(row_pieces, row_dir_ref, facts_ref[ROW], per_seg)

    def run_group(first_slot):
        add_products(
            dot_across,
            facts_ref,
            first_slot,
            block_ref,
            row_dir_ref,
            PLACES,
            [even_ref, odd_ref],
            PLACES + slots,
        )

    each_group(facts_ref, block_hbm, block_ref, sems, prepare, run_group)
    col_out_ref[...] = (even_ref[...] + odd_ref[...]).astype(col_out_ref.dtype)


def forward_kernel(row_count, with_gram, facts_ref, block_hbm, col_dir_ref, *refs):
    refs = list(refs)

    def take(count):
        taken = refs[:count]
        del refs[:count]
        return taken

    row_pieces = take(row_count if with_gram else 0)
    gram_in = take(int(with_gram))
    row_outs = take(row_count)
    gram_out = take(int(with_gram))
    block_ref, even_ref, odd_ref, sems = refs
    per_seg, size, _ = row_outs[0].shape
    slots = block_ref.shape[0]

    def prepare():
        even_ref[...] = jnp.zeros_like(even_ref)
        odd_ref[...] = jnp.zeros_like(odd_ref)

    def run_group(first_slot):
        add_products(
            dot_plain,
            facts_ref,
            first_slot,
            block_ref,
            col_dir_ref,
            PLACES + slots,
            [even_ref, odd_ref],
            PLACES,
        )

    each_group(facts_ref, block_hbm, block_ref, sems, prepare, run_group)
    gram = jnp.zeros((2 * size, 128), jnp.float32)
    for ahead, out in enumerate(row_outs):
        first = lax.rem(facts_ref[ROW] + ahead, row_count) * per_seg
        for part in range(per_seg):
            values = even_ref[first + part] + odd_ref[first + part]
            high = values.astype(out.dtype)
            out[part] = high
            if with_gram:
                low = (values - high.astype(jnp.float32)).astype(out.dtype)
                piece = row_pieces[(row_count - ahead) % row_count]
                gram += dot_across(jnp.concatenate([high, low], axis=0), tall(piece[part]))
    if with_gram:
        gram = gram[:size] + gram[size:]
        gram_out[0][...] = gram_in[0][...] + pltpu.roll(gram, 3 * size, 1)


def over_blocks(kernel, name, facts, blocks, inputs, outputs, scratch):
    slots = blocks.shape[0]
    return pl.pallas_call(
        kernel,
        in_specs=[SCALARS, ANYWHERE] + [IN_VMEM] * len(inputs),
        out_specs=[IN_VMEM] * len(outputs),
        out_shape=outputs,
        scratch_shapes=[pltpu.VMEM(blocks.shape, blocks.dtype)]
        + scratch
        + [pltpu.SemaphoreType.DMA((slots // BATCH,))],
        compiler_params=pltpu.CompilerParams(vmem_limit_bytes=VMEM_LIMIT),
        cost_estimate=pl.CostEstimate(
            flops=2 * slots * 32 * 128 * 128, bytes_accessed=2 * blocks.size, transcendentals=0
        ),
        name=name,
    )(facts, blocks, *inputs)


def backward_product(facts, blocks, row_pieces, col_count):
    per_seg, rows, lanes = row_pieces[0].shape
    col_shape = (col_count * per_seg, rows, lanes)
    (total,) = over_blocks(
        backward_kernel,
        "backward_product",
        facts,
        blocks,
        row_pieces,
        [jax.ShapeDtypeStruct(col_shape, jnp.bfloat16)],
        [
            pltpu.VMEM((len(row_pieces) * per_seg, rows, lanes), jnp.bfloat16),
            pltpu.VMEM(col_shape, jnp.float32),
            pltpu.VMEM(col_shape, jnp.float32),
        ],
    )
    return total


def forward_product(facts, blocks, col_dirs, row_pieces, gram=None):
    piece = row_pieces[0]
    inputs = [col_dirs]
    outputs = [jax.ShapeDtypeStruct(piece.shape, jnp.bfloat16)] * len(row_pieces)
    if gram is not None:
        inputs += [*row_pieces, gram]
        outputs += [jax.ShapeDtypeStruct(gram.shape, jnp.float32)]
    row_shape = (len(row_pieces) * piece.shape[0],) + piece.shape[1:]
    return over_blocks(
        functools.partial(forward_kernel, len(row_pieces), gram is not None),
        "forward_product",
        facts,
        blocks,
        inputs,
        outputs,
        [pltpu.VMEM(row_shape, jnp.float32), pltpu.VMEM(row_shape, jnp.float32)],
    )


def total_of(values):
    total = values[0].astype(jnp.float32)
    for value in values[1:]:
        total = total + value.astype(jnp.float32)
    return total


def leading(ref):
    return [ref.at[index] for index in range(ref.shape[0])]


def start_kernel(*refs):
    *row_refs, col_ref, query_ref, scaling_ref, scaled_ref, copies_ref = refs
    degree = 1.0 + 0.5 * total_of([ref[...] for ref in [*row_refs, *leading(col_ref)]])
    scaling = 1.0 / jnp.sqrt(degree)
    scaling_ref[...] = scaling
    for part in range(scaling.shape[0]):
        scaled = (
            scaling[part : part + 1] * query_ref[:, part * 128 : part * 128 + 128]
        ).astype(jnp.bfloat16)
        scaled_ref[part] = scaled
        for copy in range(copies_ref.shape[0]):
            copies_ref[copy, part] = scaled


def scaled_sum(row_refs, col_ref, scaling_ref, part):
    scaling = scaling_ref[part : part + 1]
    total = total_of([ref[part] for ref in [*row_refs, *leading(col_ref)]])
    return scaling * (0.5 * total)


def middle_kernel(*refs):
    *row_refs, col_ref, scaling_ref, query_ref, first_ref, scaled_ref, copies_ref, gram_ref = refs
    size = query_ref.shape[0]
    pair_gram = jnp.zeros((2 * size, 128), jnp.float32)
    for part in range(scaling_ref.shape[0]):
        first = scaled_sum(row_refs, col_ref, scaling_ref, part)
        first_ref[part] = first
        scaled = (scaling_ref[part : part + 1] * first).astype(jnp.bfloat16)
        scaled_ref[part] = scaled
        for copy in range(copies_ref.shape[0]):
            copies_ref[copy, part] = scaled
        pair = jnp.concatenate(
            [query_ref[:, part * 128 : part * 128 + 128], first], axis=0
        )
        pair_gram += exact_across(pair, tall(pair))
    gram_ref[...] = beside(
        pair_gram[:size], pltpu.roll(window(pair_gram[size:], 1), size, 1)
    )


def tall(flat):
    rest = flat.shape[1] - flat.shape[0]
    return jnp.concatenate([flat, jnp.zeros((rest, flat.shape[1]), flat.dtype)], axis=0)


def flipped(flat):
    return tall(flat).T[: flat.shape[0]]


def times(left, right):
    return exact_plain(left, tall(right))


def beside(left, right):
    return left + pltpu.roll(right, left.shape[0], 1)


def stacked(upper, lower):
    rest = jnp.zeros((upper.shape[1] - 2 * upper.shape[0], upper.shape[1]), upper.dtype)
    return jnp.concatenate([upper, lower, rest], axis=0)


def sandwich(rows, middle):
    return exact_across(exact_plain(rows, middle), tall(rows))


def symmetric(flat):
    return 0.5 * (flat + flipped(flat))


def window(flat, place):
    size = flat.shape[0]
    if place:
        flat = pltpu.roll(flat, flat.shape[1] - place * size, 1)
    lanes = lax.broadcasted_iota(jnp.int32, flat.shape, 1)
    return jnp.where(lanes < size, flat, 0.0)


def solve_many(pairs):
    size = pairs[0][0].shape[0]
    systems = [matrix + pltpu.roll(side, size, 1) for matrix, side in pairs]
    sublanes = lax.broadcasted_iota(jnp.int32, systems[0].shape, 0)
    for pivot in range(0, size, 2):
        updated = []
        for system in systems:
            upper, lower = system[pivot : pivot + 1, :], system[pivot + 1 : pivot + 2, :]
            left, right = system[:, pivot : pivot + 1], system[:, pivot + 1 : pivot + 2]
            inverse = 1.0 / left[pivot : pivot + 1, :]
            upper = upper * inverse
            ratio = left[pivot + 1 : pivot + 2, :]
            across = right[pivot : pivot + 1, :] * inverse
            inverse = 1.0 / (right[pivot + 1 : pivot + 2, :] - ratio * across)
            new_lower = (lower - ratio * upper) * inverse
            new_upper = upper - across * new_lower
            rest = system - left * new_upper - right * new_lower
            rest = jnp.where(sublanes == pivot, new_upper, rest)
            updated.append(jnp.where(sublanes == pivot + 1, new_lower, rest))
        systems = updated
    return [window(system, 1) for system in systems]


def close_kernel(*refs):
    *row_refs, col_ref, gram_ref, scaling_ref, query_ref, first_ref = refs[:-2]
    solution_ref, residual_ref = refs[-2:]
    size = query_ref.shape[0]
    weight = graph_weight
    total = total_of([ref[...] for ref in leading(gram_ref)])
    g00 = symmetric(window(total, 0))
    g01 = window(total, 1)
    g11 = symmetric(window(total, 2))
    g12 = symmetric(window(total, 3))
    eye = (
        lax.broadcasted_iota(jnp.int32, total.shape, 0)
        == lax.broadcasted_iota(jnp.int32, total.shape, 1)
    ).astype(jnp.float32)
    curve = symmetric(g00 - weight * g01)
    steps, inverse = solve_many([(curve, g00), (g00, eye)])
    steps_t = flipped(steps)
    plain_gram = stacked(beside(g00, g01), beside(flipped(g01), g11))
    through_gram = stacked(beside(g01, g11), beside(g11, g12))
    after_first = beside(eye - steps_t, weight * steps_t)
    new_gram = symmetric(sandwich(after_first, plain_gram))
    mixing = times(inverse, new_gram)
    direction = after_first + flipped(mixing)
    curve = symmetric(sandwich(direction, plain_gram - weight * through_gram))
    (steps,) = solve_many([(curve, new_gram)])
    steps_t2 = flipped(steps)
    applied = direction - weight * pltpu.roll(direction, size, 1)
    solution_rows = exact_plain(beside(eye, steps_t2), stacked(steps_t, direction))
    residual_rows = exact_plain(beside(eye, -steps_t2), stacked(after_first, applied))
    rows = jnp.concatenate([solution_rows, residual_rows], axis=0)
    for part in range(first_ref.shape[0]):
        lanes = slice(part * 128, part * 128 + 128)
        basis = jnp.concatenate(
            [
                query_ref[:, lanes],
                first_ref[part],
                scaled_sum(row_refs, col_ref, scaling_ref, part),
                jnp.zeros_like(eye),
            ],
            axis=0,
        )
        values = exact_plain(rows, basis)
        solution_ref[:, lanes] = values[:size]
        residual_ref[:, lanes] = values[size:]


def pass_around(pieces, axis):
    count = len(pieces)
    return [pieces[0]] + [
        lax.ppermute(pieces[ahead], axis, [(at, (at + ahead) % count) for at in range(count)])
        for ahead in range(1, count)
    ]


def exchange(pieces, axis):
    return lax.all_to_all(pieces, axis, 0, 0, tiled=True)


def simple_call(kernel, shapes, name, *operands):
    return pl.pallas_call(
        kernel,
        out_shape=shapes,
        compiler_params=pltpu.CompilerParams(vmem_limit_bytes=VMEM_LIMIT),
        name=name,
    )(*operands)


def sum_kernel(*refs):
    *piece_refs, copies_ref = refs
    total = total_of([ref[...] for ref in piece_refs])
    for copy in range(copies_ref.shape[0]):
        copies_ref[copy] = total


def body(queries, block_spots, live_blocks, neighbor_cols, neighbor_sims):
    row_count = lax.axis_size("row")
    col_count = lax.axis_size("col")
    query_rows, seg_len = queries.shape
    per_seg = seg_len // 128
    spots = block_spots[0, 0]
    col_blocks = col_count * per_seg
    heads = [live_blocks[0, 0], lax.axis_index("row"), lax.axis_index("col"), 0]
    facts = jnp.concatenate(
        [jnp.stack(heads).astype(jnp.int32), spots // col_blocks, spots % col_blocks]
    )
    piece = (per_seg, query_rows, 128)
    wide = jax.ShapeDtypeStruct(piece, jnp.float32)
    narrow = jax.ShapeDtypeStruct(piece, jnp.bfloat16)
    copies = jax.ShapeDtypeStruct((col_count,) + piece, jnp.bfloat16)
    gram_shape = jax.ShapeDtypeStruct((query_rows, 128), jnp.float32)
    gram_copies = jax.ShapeDtypeStruct((col_count, query_rows, 128), jnp.float32)

    blocks, *row_sums, col_sums = build_blocks(
        facts, neighbor_cols[0, 0], neighbor_sims[0, 0], row_count, col_count, per_seg
    )
    col_part = exchange(col_sums.reshape(col_count, per_seg, 128), "col")
    row_parts = pass_around(row_sums, "row")
    scaling, scaled, scaled_copies = simple_call(
        start_kernel,
        [jax.ShapeDtypeStruct((per_seg, 128), jnp.float32), narrow, copies],
        "start",
        *row_parts,
        col_part,
        queries,
    )

    def product(vectors, vector_copies, gram=None):
        col_dirs = exchange(vector_copies, "col").reshape((col_count * per_seg,) + piece[1:])
        row_pieces = pass_around([vectors] * row_count, "row")
        total = backward_product(facts, blocks, row_pieces, col_count)
        col_part = exchange(total.reshape((col_count,) + piece), "col")
        totals = forward_product(facts, blocks, col_dirs, row_pieces, gram)
        row_parts = pass_around(totals[:row_count], "row")
        return row_parts, col_part, totals[row_count:]

    row_parts, col_part, _ = product(scaled, scaled_copies)
    first, scaled, scaled_copies, gram = simple_call(
        middle_kernel,
        [wide, narrow, copies, gram_shape],
        "middle",
        *row_parts,
        col_part,
        scaling,
        queries,
    )
    row_parts, col_part, (gram,) = product(scaled, scaled_copies, gram)
    (grams,) = simple_call(
        sum_kernel, [gram_copies], "gram_sum", *pass_around([gram] * row_count, "row")
    )
    flat = jax.ShapeDtypeStruct(queries.shape, jnp.float32)
    return tuple(
        simple_call(
            close_kernel,
            [flat, flat],
            "close",
            *row_parts,
            col_part,
            exchange(grams, "col"),
            scaling,
            queries,
            first,
        )
    )


def solution(mesh):
    placed = (
        P(None, ("row", "col")),
        P("row", "col", None),
        P("row", "col"),
        P("row", "col", None, None, None),
        P("row", "col", None, None, None),
    )
    return jax.shard_map(
        body,
        mesh=mesh,
        in_specs=placed,
        out_specs=(P(None, ("row", "col")), P(None, ("row", "col"))),
        check_vma=False,
    )
```

profile of v0, /device:TPU:0, one launch (start us, length us, event | category | flops | bytes accessed | tf_op | source)
XLA Modules:
  0.0 141.0 jit_solution(2753814966537357528)
XLA Ops:
  2.6 10.4 %build_blocks.1 = (bf16[256,128,128]{2,1,0:T(8,128)(2,1)}, f32[4,128]{1,0:T(4,128)}, f32[4,128]{1,0:T(4,128)}, f32[4,128]{1,0:T(4,128)}, f32[4,128]{1,0:T(4,128)}, /*index=5*/f32[32,128]{1,0:T(8,128)}) custom-call(s32[516]{0:T(1024)} %concatenate.3.facts_ref, s32[256,16,128]{2,1,0:T(8,128)} %bitcast.12, bf16[256,16,128]{2,1,0:T(8,128)(2,1)} %bitcast.17), custom_call_target="tpu_custom_call" | custom-call | tf_op jit(solution)/shard_map/build_blocks/pallas_call | solution.py:131
  13.0 18.1 %all-to-all-start = ((f32[8,4,128]{2,1,0:T(4,128)}), f32[8,4,128]{2,1,0:T(4,128)S(1)}, u32[]{:S(2)}, u32[]{:S(2)}) async-start(f32[8,4,128]{2,1,0:T(4,128)} %bitcast.18), calls=%async_computation | async-start | bytes 32768 | tf_op jit(solution)/shard_map/all_to_all | solution.py:485
  31.2 1.7 %collective-permute-start.2 = (f32[4,128]{1,0:T(4,128)}, f32[4,128]{1,0:T(4,128)S(1)}, u32[]{:S(2)}, u32[]{:S(2)}) collective-permute-start(f32[4,128]{1,0:T(4,128)} %get-tuple-element.28), channel_id=1, source_target_pairs={{0,24},{8,0},{16,8},{24,16},{1,25},{9,1},{17,9},{25,17},{2,26},{10... | collective-permute-start | bytes 6152 | tf_op jit(solution)/shard_map/ppermute | solution.py:479
  32.9 1.4 %collective-permute-done.refs_1_ = f32[4,128]{1,0:T(4,128)S(1)} collective-permute-done((f32[4,128]{1,0:T(4,128)}, f32[4,128]{1,0:T(4,128)S(1)}, u32[]{:S(2)}, u32[]{:S(2)}) %collective-permute-start) | collective-permute-done | bytes 2080 | tf_op jit(solution)/shard_map/ppermute | solution.py:479
  35.0 2.7 %all-to-all-done.refs_4_ = f32[8,4,128]{2,1,0:T(4,128)S(1)} async-done(((f32[8,4,128]{2,1,0:T(4,128)}), f32[8,4,128]{2,1,0:T(4,128)S(1)}, u32[]{:S(2)}, u32[]{:S(2)}) %all-to-all-start) | async-done | bytes 16416 | tf_op jit(solution)/shard_map/all_to_all | solution.py:485
  38.3 1.6 %start.1 = (f32[4,128]{1,0:T(4,128)}, bf16[4,32,128]{2,1,0:T(8,128)(2,1)}, bf16[8,4,32,128]{3,2,1,0:T(8,128)(2,1)}) custom-call(f32[4,128]{1,0:T(4,128)} %get-tuple-element.25.refs_0_, f32[4,128]{1,0:T(4,128)} %copy-done.21, f32[4,128]{1,0:T(4,128)} %copy-done.22, f32[4,128]{1,0:T(4,128)} %copy-done.23, f32[8,4,128]{2,1,0:T(4,128)} %copy-done.8, ...), custom_call_target="tpu_custom_call" | custom-call | tf_op jit(solution)/shard_map/start/pallas_call | solution.py:489
  39.9 3.4 %all-to-all-start.1 = ((bf16[8,4,32,128]{3,2,1,0:T(8,128)(2,1)}), bf16[8,4,32,128]{3,2,1,0:T(8,128)(2,1)S(1)}, u32[]{:S(2)}, u32[]{:S(2)}) async-start(bf16[8,4,32,128]{3,2,1,0:T(8,128)(2,1)} %get-tuple-element.30), calls=%async_computation.1 | async-start | bytes 524288 | tf_op jit(solution)/shard_map/all_to_all | solution.py:485
  44.1 1.7 %collective-permute-start.7 = (bf16[4,32,128]{2,1,0:T(8,128)(2,1)}, bf16[4,32,128]{2,1,0:T(8,128)(2,1)S(1)}, u32[]{:S(2)}, u32[]{:S(2)}) collective-permute-start(bf16[4,32,128]{2,1,0:T(8,128)(2,1)} %get-tuple-element.35.refs_0_), channel_id=1, source_target_pairs={{0,16},{8,24},{16,0},{24,8},{1,17},{9,25},{17,1},{25,9},{2,18},{10... | collective-permute-start | bytes 98312 | tf_op jit(solution)/shard_map/ppermute | solution.py:479
  46.0 2.2 %collective-permute-done.7.refs_2_ = bf16[4,32,128]{2,1,0:T(8,128)(2,1)S(1)} collective-permute-done((bf16[4,32,128]{2,1,0:T(8,128)(2,1)}, bf16[4,32,128]{2,1,0:T(8,128)(2,1)S(1)}, u32[]{:S(2)}, u32[]{:S(2)}) %collective-permute-start.7) | collective-permute-done | bytes 32800 | tf_op jit(solution)/shard_map/ppermute | solution.py:479
  48.2 1.1 collective-permute-done.6.refs_1_
  50.0 4.9 %backward_product.2 = bf16[32,32,128]{2,1,0:T(8,128)(2,1)} custom-call(s32[516]{0:T(1024)} %concatenate.3.facts_ref, bf16[256,128,128]{2,1,0:T(8,128)(2,1)} %get-tuple-element.24.block_hbm, bf16[4,32,128]{2,1,0:T(8,128)(2,1)} %get-tuple-element.35.refs_0_, bf16[4,32,128]{2,1,0:T(8,128)(2,1)} %copy-done.11, bf16[4,32,128]{2,1,0:T(8,128)(2,1)} %copy-done.10, ...), custom_call_target="tpu_custom_call" | custom-call | flops 268435456 | bytes 8388608 | tf_op jit(solution)/shard_map/backward_product/pallas_call | solution.py:264
  54.9 8.2 %all-to-all-start.2 = ((bf16[8,4,32,128]{3,2,1,0:T(8,128)(2,1)}), bf16[8,4,32,128]{3,2,1,0:T(8,128)(2,1)S(1)}, u32[]{:S(2)}, u32[]{:S(2)}) async-start(bf16[8,4,32,128]{3,2,1,0:T(8,128)(2,1)} %bitcast.16), calls=%async_computation.2 | async-start | bytes 524288 | tf_op jit(solution)/shard_map/all_to_all | solution.py:485
  63.0 4.1 %forward_product.2 = (bf16[4,32,128]{2,1,0:T(8,128)(2,1)}, bf16[4,32,128]{2,1,0:T(8,128)(2,1)}, bf16[4,32,128]{2,1,0:T(8,128)(2,1)}, bf16[4,32,128]{2,1,0:T(8,128)(2,1)}) custom-call(s32[516]{0:T(1024)} %concatenate.3.facts_ref, bf16[256,128,128]{2,1,0:T(8,128)(2,1)} %get-tuple-element.24.block_hbm, bf16[32,32,128]{2,1,0:T(8,128)(2,1)} %bitcast.14), custom_call_target="tpu_custom_call" | custom-call | flops 268435456 | bytes 8388608 | tf_op jit(solution)/shard_map/forward_product/pallas_call | solution.py:264
  67.3 1.7 %collective-permute-start.5 = (bf16[4,32,128]{2,1,0:T(8,128)(2,1)}, bf16[4,32,128]{2,1,0:T(8,128)(2,1)S(1)}, u32[]{:S(2)}, u32[]{:S(2)}) collective-permute-start(bf16[4,32,128]{2,1,0:T(8,128)(2,1)} %get-tuple-element.34), channel_id=1, source_target_pairs={{0,24},{8,0},{16,8},{24,16},{1,25},{9,1},{17,9},{25,17},{2,26},{10... | collective-permute-start | bytes 98312 | tf_op jit(solution)/shard_map/ppermute | solution.py:479
  69.0 2.3 %all-to-all-done.2.refs_4_ = bf16[8,4,32,128]{3,2,1,0:T(8,128)(2,1)S(1)} async-done(((bf16[8,4,32,128]{3,2,1,0:T(8,128)(2,1)}), bf16[8,4,32,128]{3,2,1,0:T(8,128)(2,1)S(1)}, u32[]{:S(2)}, u32[]{:S(2)}) %all-to-all-start.2) | async-done | bytes 262176 | tf_op jit(solution)/shard_map/all_to_all | solution.py:485
  72.1 2.2 %middle.1 = (f32[4,32,128]{2,1,0:T(8,128)}, bf16[4,32,128]{2,1,0:T(8,128)(2,1)}, bf16[8,4,32,128]{3,2,1,0:T(8,128)(2,1)}, f32[32,128]{1,0:T(8,128)}) custom-call(bf16[4,32,128]{2,1,0:T(8,128)(2,1)} %get-tuple-element.31.refs_0_, bf16[4,32,128]{2,1,0:T(8,128)(2,1)} %copy-done.12, bf16[4,32,128]{2,1,0:T(8,128)(2,1)} %copy-done.13, ...), custom_call_target="tpu_custom_call" | custom-call | tf_op jit(solution)/shard_map/middle/pallas_call | solution.py:489
  74.3 7.1 %all-to-all-start.3 = ((bf16[8,4,32,128]{3,2,1,0:T(8,128)(2,1)}), bf16[8,4,32,128]{3,2,1,0:T(8,128)(2,1)S(1)}, u32[]{:S(2)}, u32[]{:S(2)}) async-start(bf16[8,4,32,128]{3,2,1,0:T(8,128)(2,1)} %get-tuple-element.37), calls=%async_computation.3 | async-start | bytes 524288 | tf_op jit(solution)/shard_map/all_to_all | solution.py:485
  82.2 1.7 %collective-permute-start.10 = (bf16[4,32,128]{2,1,0:T(8,128)(2,1)}, bf16[4,32,128]{2,1,0:T(8,128)(2,1)S(1)}, u32[]{:S(2)}, u32[]{:S(2)}) collective-permute-start(bf16[4,32,128]{2,1,0:T(8,128)(2,1)} %get-tuple-element.38.refs_0_), channel_id=1, source_target_pairs={{0,16},{8,24},{16,0},{24,8},{1,17},{9,25},{17,1},{25,9},{2,18},{10... | collective-permute-start | bytes 98312 | tf_op jit(solution)/shard_map/ppermute | solution.py:479
  84.2 2.2 %collective-permute-done.10.refs_2_ = bf16[4,32,128]{2,1,0:T(8,128)(2,1)S(1)} collective-permute-done((bf16[4,32,128]{2,1,0:T(8,128)(2,1)}, bf16[4,32,128]{2,1,0:T(8,128)(2,1)S(1)}, u32[]{:S(2)}, u32[]{:S(2)}) %collective-permute-start.10) | collective-permute-done | bytes 32800 | tf_op jit(solution)/shard_map/ppermute | solution.py:479
  86.3 1.1 collective-permute-done.9.refs_1_
  88.0 4.9 %backward_product.3 = bf16[32,32,128]{2,1,0:T(8,128)(2,1)} custom-call(s32[516]{0:T(1024)} %concatenate.3.facts_ref, bf16[256,128,128]{2,1,0:T(8,128)(2,1)} %get-tuple-element.24.block_hbm, bf16[4,32,128]{2,1,0:T(8,128)(2,1)} %get-tuple-element.38.refs_0_, bf16[4,32,128]{2,1,0:T(8,128)(2,1)} %copy-done.7, bf16[4,32,128]{2,1,0:T(8,128)(2,1)} %copy-done.6, ...), custom_call_target="tpu_custom_call" | custom-call | flops 268435456 | bytes 8388608 | tf_op jit(solution)/shard_map/backward_product/pallas_call | solution.py:264
  93.0 8.2 %all-to-all-start.4 = ((bf16[8,4,32,128]{3,2,1,0:T(8,128)(2,1)}), bf16[8,4,32,128]{3,2,1,0:T(8,128)(2,1)S(1)}, u32[]{:S(2)}, u32[]{:S(2)}) async-start(bf16[8,4,32,128]{3,2,1,0:T(8,128)(2,1)} %bitcast.13), calls=%async_computation.4 | async-start | bytes 524288 | tf_op jit(solution)/shard_map/all_to_all | solution.py:485
  101.1 4.4 %forward_product.3 = (bf16[4,32,128]{2,1,0:T(8,128)(2,1)}, bf16[4,32,128]{2,1,0:T(8,128)(2,1)}, bf16[4,32,128]{2,1,0:T(8,128)(2,1)}, bf16[4,32,128]{2,1,0:T(8,128)(2,1)}, f32[32,128]{1,0:T(8,128)}) custom-call(s32[516]{0:T(1024)} %concatenate.3.facts_ref, bf16[256,128,128]{2,1,0:T(8,128)(2,1)} %get-tuple-element.24.block_hbm, bf16[32,32,128]{2,1,0:T(8,128)(2,1)} %bitcast.15, ...), custom_call_target="tpu_custom_call" | custom-call | flops 268435456 | bytes 8388608 | tf_op jit(solution)/shard_map/forward_product/pallas_call | solution.py:264
  106.1 1.1 collective-permute-done.17.refs_3_
  107.3 2.4 %collective-permute-done.16.refs_2_ = f32[32,128]{1,0:T(8,128)S(1)} collective-permute-done((f32[32,128]{1,0:T(8,128)}, f32[32,128]{1,0:T(8,128)S(1)}, u32[]{:S(2)}, u32[]{:S(2)}) %collective-permute-start.16) | collective-permute-done | bytes 16416 | tf_op jit(solution)/shard_map/ppermute | solution.py:479
  110.8 1.4 %gram_sum.1 = f32[8,32,128]{2,1,0:T(8,128)} custom-call(f32[32,128]{1,0:T(8,128)} %get-tuple-element.44.refs_0_, f32[32,128]{1,0:T(8,128)} %copy-done.20, f32[32,128]{1,0:T(8,128)} %copy-done.19, f32[32,128]{1,0:T(8,128)} %copy-done.18), custom_call_target="tpu_custom_call" | custom-call | tf_op jit(solution)/shard_map/gram_sum/pallas_call | solution.py:489
  112.3 7.1 %all-to-all-start.5 = ((f32[8,32,128]{2,1,0:T(8,128)}), f32[8,32,128]{2,1,0:T(8,128)S(1)}, u32[]{:S(2)}, u32[]{:S(2)}) async-start(f32[8,32,128]{2,1,0:T(8,128)} %gram_sum.1), calls=%async_computation.5 | async-start | bytes 262144 | tf_op jit(solution)/shard_map/all_to_all | solution.py:485
  120.3 1.4 collective-permute-start.14
  121.7 1.2 collective-permute-done.12.refs_1_
  122.9 0.9 collective-permute-done.13.refs_2_
  123.8 2.9 %all-to-all-done.5.refs_5_ = f32[8,32,128]{2,1,0:T(8,128)S(1)} async-done(((f32[8,32,128]{2,1,0:T(8,128)}), f32[8,32,128]{2,1,0:T(8,128)S(1)}, u32[]{:S(2)}, u32[]{:S(2)}) %all-to-all-start.5) | async-done | bytes 131104 | tf_op jit(solution)/shard_map/all_to_all | solution.py:485
  127.3 13.7 %close.1 = (f32[32,512]{1,0:T(8,128)}, f32[32,512]{1,0:T(8,128)}) custom-call(bf16[4,32,128]{2,1,0:T(8,128)(2,1)} %get-tuple-element.40.refs_0_, bf16[4,32,128]{2,1,0:T(8,128)(2,1)} %copy-done.15, bf16[4,32,128]{2,1,0:T(8,128)(2,1)} %copy-done.16, bf16[4,32,128]{2,1,0:T(8,128)(2,1)} %copy-done.17, bf16[8,4,32,128]{3,2,1,0:T(8,128)(2,1)} %copy-done.3, ...), custom_call_target="tpu_custom_call" | custom-call | tf_op jit(solution)/shard_map/close/pallas_call | solution.py:489
  (75 shorter events, 10.2 us)
Async XLA Ops:
  13.0 24.7 %all-to-all-start = ((f32[8,4,128]{2,1,0:T(4,128)}), f32[8,4,128]{2,1,0:T(4,128)S(1)}, u32[]{:S(2)}, u32[]{:S(2)}) async-start(f32[8,4,128]{2,1,0:T(4,128)} %bitcast.18), calls=%async_computation | async-start | bytes 32768 | tf_op jit(solution)/shard_map/all_to_all | solution.py:485
  31.1 3.2 %collective-permute-start = (f32[4,128]{1,0:T(4,128)}, f32[4,128]{1,0:T(4,128)S(1)}, u32[]{:S(2)}, u32[]{:S(2)}) collective-permute-start(f32[4,128]{1,0:T(4,128)} %get-tuple-element.26), channel_id=1, source_target_pairs={{0,8},{8,16},{16,24},{24,0},{1,9},{9,17},{17,25},{25,1},{2,10},{10... | collective-permute-start | bytes 6152 | tf_op jit(solution)/shard_map/ppermute | solution.py:479
  31.1 3.9 %collective-permute-start.1 = (f32[4,128]{1,0:T(4,128)}, f32[4,128]{1,0:T(4,128)S(1)}, u32[]{:S(2)}, u32[]{:S(2)}) collective-permute-start(f32[4,128]{1,0:T(4,128)} %get-tuple-element.27), channel_id=1, source_target_pairs={{0,16},{8,24},{16,0},{24,8},{1,17},{9,25},{17,1},{25,9},{2,18},{10... | collective-permute-start | bytes 6152 | tf_op jit(solution)/shard_map/ppermute | solution.py:479
  31.2 3.8 %collective-permute-start.2 = (f32[4,128]{1,0:T(4,128)}, f32[4,128]{1,0:T(4,128)S(1)}, u32[]{:S(2)}, u32[]{:S(2)}) collective-permute-start(f32[4,128]{1,0:T(4,128)} %get-tuple-element.28), channel_id=1, source_target_pairs={{0,24},{8,0},{16,8},{24,16},{1,25},{9,1},{17,9},{25,17},{2,26},{10... | collective-permute-start | bytes 6152 | tf_op jit(solution)/shard_map/ppermute | solution.py:479
  34.3 3.4 %copy-start.21 = (f32[4,128]{1,0:T(4,128)}, f32[4,128]{1,0:T(4,128)S(1)}, u32[]{:S(2)}) copy-start(f32[4,128]{1,0:T(4,128)S(1)} %collective-permute-done.refs_1_) | copy-start | bytes 6148
  39.9 14.9 %all-to-all-start.1 = ((bf16[8,4,32,128]{3,2,1,0:T(8,128)(2,1)}), bf16[8,4,32,128]{3,2,1,0:T(8,128)(2,1)S(1)}, u32[]{:S(2)}, u32[]{:S(2)}) async-start(bf16[8,4,32,128]{3,2,1,0:T(8,128)(2,1)} %get-tuple-element.30), calls=%async_computation.1 | async-start | bytes 524288 | tf_op jit(solution)/shard_map/all_to_all | solution.py:485
  43.4 2.7 %collective-permute-start.8 = (bf16[4,32,128]{2,1,0:T(8,128)(2,1)}, bf16[4,32,128]{2,1,0:T(8,128)(2,1)S(1)}, u32[]{:S(2)}, u32[]{:S(2)}) collective-permute-start(bf16[4,32,128]{2,1,0:T(8,128)(2,1)} %get-tuple-element.35.refs_0_), channel_id=1, source_target_pairs={{0,24},{8,0},{16,8},{24,16},{1,25},{9,1},{17,9},{25,17},{2,26},{10... | collective-permute-start | bytes 98312 | tf_op jit(solution)/shard_map/ppermute | solution.py:479
  44.1 4.2 %collective-permute-start.7 = (bf16[4,32,128]{2,1,0:T(8,128)(2,1)}, bf16[4,32,128]{2,1,0:T(8,128)(2,1)S(1)}, u32[]{:S(2)}, u32[]{:S(2)}) collective-permute-start(bf16[4,32,128]{2,1,0:T(8,128)(2,1)} %get-tuple-element.35.refs_0_), channel_id=1, source_target_pairs={{0,16},{8,24},{16,0},{24,8},{1,17},{9,25},{17,1},{25,9},{2,18},{10... | collective-permute-start | bytes 98312 | tf_op jit(solution)/shard_map/ppermute | solution.py:479
  45.8 3.6 %collective-permute-start.6 = (bf16[4,32,128]{2,1,0:T(8,128)(2,1)}, bf16[4,32,128]{2,1,0:T(8,128)(2,1)S(1)}, u32[]{:S(2)}, u32[]{:S(2)}) collective-permute-start(bf16[4,32,128]{2,1,0:T(8,128)(2,1)} %get-tuple-element.35.refs_0_), channel_id=1, source_target_pairs={{0,8},{8,16},{16,24},{24,0},{1,9},{9,17},{17,25},{25,1},{2,10},{10... | collective-permute-start | bytes 98312 | tf_op jit(solution)/shard_map/ppermute | solution.py:479
  46.0 3.3 %copy-start.9 = (bf16[4,32,128]{2,1,0:T(8,128)(2,1)}, bf16[4,32,128]{2,1,0:T(8,128)(2,1)S(1)}, u32[]{:S(2)}) copy-start(bf16[4,32,128]{2,1,0:T(8,128)(2,1)S(1)} %collective-permute-done.8.refs_3_) | copy-start | bytes 98308
  54.9 8.2 %copy-start = (bf16[8,4,32,128]{3,2,1,0:T(8,128)(2,1)}, bf16[8,4,32,128]{3,2,1,0:T(8,128)(2,1)S(1)}, u32[]{:S(2)}) copy-start(bf16[8,4,32,128]{3,2,1,0:T(8,128)(2,1)S(1)} %all-to-all-done.1) | copy-start | bytes 786436
  54.9 16.4 %all-to-all-start.2 = ((bf16[8,4,32,128]{3,2,1,0:T(8,128)(2,1)}), bf16[8,4,32,128]{3,2,1,0:T(8,128)(2,1)S(1)}, u32[]{:S(2)}, u32[]{:S(2)}) async-start(bf16[8,4,32,128]{3,2,1,0:T(8,128)(2,1)} %bitcast.16), calls=%async_computation.2 | async-start | bytes 524288 | tf_op jit(solution)/shard_map/all_to_all | solution.py:485
  67.2 4.1 %collective-permute-start.3 = (bf16[4,32,128]{2,1,0:T(8,128)(2,1)}, bf16[4,32,128]{2,1,0:T(8,128)(2,1)S(1)}, u32[]{:S(2)}, u32[]{:S(2)}) collective-permute-start(bf16[4,32,128]{2,1,0:T(8,128)(2,1)} %get-tuple-element.32), channel_id=1, source_target_pairs={{0,8},{8,16},{16,24},{24,0},{1,9},{9,17},{17,25},{25,1},{2,10},{10... | collective-permute-start | bytes 98312 | tf_op jit(solution)/shard_map/ppermute | solution.py:479
  67.2 4.2 %collective-permute-start.4 = (bf16[4,32,128]{2,1,0:T(8,128)(2,1)}, bf16[4,32,128]{2,1,0:T(8,128)(2,1)S(1)}, u32[]{:S(2)}, u32[]{:S(2)}) collective-permute-start(bf16[4,32,128]{2,1,0:T(8,128)(2,1)} %get-tuple-element.33), channel_id=1, source_target_pairs={{0,16},{8,24},{16,0},{24,8},{1,17},{9,25},{17,1},{25,9},{2,18},{10... | collective-permute-start | bytes 98312 | tf_op jit(solution)/shard_map/ppermute | solution.py:479
  67.3 4.2 %collective-permute-start.5 = (bf16[4,32,128]{2,1,0:T(8,128)(2,1)}, bf16[4,32,128]{2,1,0:T(8,128)(2,1)S(1)}, u32[]{:S(2)}, u32[]{:S(2)}) collective-permute-start(bf16[4,32,128]{2,1,0:T(8,128)(2,1)} %get-tuple-element.34), channel_id=1, source_target_pairs={{0,24},{8,0},{16,8},{24,16},{1,25},{9,1},{17,9},{25,17},{2,26},{10... | collective-permute-start | bytes 98312 | tf_op jit(solution)/shard_map/ppermute | solution.py:479
  74.3 18.7 %all-to-all-start.3 = ((bf16[8,4,32,128]{3,2,1,0:T(8,128)(2,1)}), bf16[8,4,32,128]{3,2,1,0:T(8,128)(2,1)S(1)}, u32[]{:S(2)}, u32[]{:S(2)}) async-start(bf16[8,4,32,128]{3,2,1,0:T(8,128)(2,1)} %get-tuple-element.37), calls=%async_computation.3 | async-start | bytes 524288 | tf_op jit(solution)/shard_map/all_to_all | solution.py:485
  81.4 2.8 %collective-permute-start.11 = (bf16[4,32,128]{2,1,0:T(8,128)(2,1)}, bf16[4,32,128]{2,1,0:T(8,128)(2,1)S(1)}, u32[]{:S(2)}, u32[]{:S(2)}) collective-permute-start(bf16[4,32,128]{2,1,0:T(8,128)(2,1)} %get-tuple-element.38.refs_0_), channel_id=1, source_target_pairs={{0,24},{8,0},{16,8},{24,16},{1,25},{9,1},{17,9},{25,17},{2,26},{10... | collective-permute-start | bytes 98312 | tf_op jit(solution)/shard_map/ppermute | solution.py:479
  82.2 4.2 %collective-permute-start.10 = (bf16[4,32,128]{2,1,0:T(8,128)(2,1)}, bf16[4,32,128]{2,1,0:T(8,128)(2,1)S(1)}, u32[]{:S(2)}, u32[]{:S(2)}) collective-permute-start(bf16[4,32,128]{2,1,0:T(8,128)(2,1)} %get-tuple-element.38.refs_0_), channel_id=1, source_target_pairs={{0,16},{8,24},{16,0},{24,8},{1,17},{9,25},{17,1},{25,9},{2,18},{10... | collective-permute-start | bytes 98312 | tf_op jit(solution)/shard_map/ppermute | solution.py:479
  83.9 3.6 %collective-permute-start.9 = (bf16[4,32,128]{2,1,0:T(8,128)(2,1)}, bf16[4,32,128]{2,1,0:T(8,128)(2,1)S(1)}, u32[]{:S(2)}, u32[]{:S(2)}) collective-permute-start(bf16[4,32,128]{2,1,0:T(8,128)(2,1)} %get-tuple-element.38.refs_0_), channel_id=1, source_target_pairs={{0,8},{8,16},{16,24},{24,0},{1,9},{9,17},{17,25},{25,1},{2,10},{10... | collective-permute-start | bytes 98312 | tf_op jit(solution)/shard_map/ppermute | solution.py:479
  84.2 3.3 %copy-start.5 = (bf16[4,32,128]{2,1,0:T(8,128)(2,1)}, bf16[4,32,128]{2,1,0:T(8,128)(2,1)S(1)}, u32[]{:S(2)}) copy-start(bf16[4,32,128]{2,1,0:T(8,128)(2,1)S(1)} %collective-permute-done.11.refs_3_) | copy-start | bytes 98308
  93.0 8.2 %copy-start.1 = (bf16[8,4,32,128]{3,2,1,0:T(8,128)(2,1)}, bf16[8,4,32,128]{3,2,1,0:T(8,128)(2,1)S(1)}, u32[]{:S(2)}) copy-start(bf16[8,4,32,128]{3,2,1,0:T(8,128)(2,1)S(1)} %all-to-all-done.3) | copy-start | bytes 786436
  93.0 19.3 %all-to-all-start.4 = ((bf16[8,4,32,128]{3,2,1,0:T(8,128)(2,1)}), bf16[8,4,32,128]{3,2,1,0:T(8,128)(2,1)S(1)}, u32[]{:S(2)}, u32[]{:S(2)}) async-start(bf16[8,4,32,128]{3,2,1,0:T(8,128)(2,1)} %bitcast.13), calls=%async_computation.4 | async-start | bytes 524288 | tf_op jit(solution)/shard_map/all_to_all | solution.py:485
  105.6 1.7 %collective-permute-start.17 = (f32[32,128]{1,0:T(8,128)}, f32[32,128]{1,0:T(8,128)S(1)}, u32[]{:S(2)}, u32[]{:S(2)}) collective-permute-start(f32[32,128]{1,0:T(8,128)} %get-tuple-element.44.refs_0_), channel_id=1, source_target_pairs={{0,24},{8,0},{16,8},{24,16},{1,25},{9,1},{17,9},{25,17},{2,26},{10... | collective-permute-start | bytes 49160 | tf_op jit(solution)/shard_map/ppermute | solution.py:479
  105.6 4.0 %collective-permute-start.16 = (f32[32,128]{1,0:T(8,128)}, f32[32,128]{1,0:T(8,128)S(1)}, u32[]{:S(2)}, u32[]{:S(2)}) collective-permute-start(f32[32,128]{1,0:T(8,128)} %get-tuple-element.44.refs_0_), channel_id=1, source_target_pairs={{0,16},{8,24},{16,0},{24,8},{1,17},{9,25},{17,1},{25,9},{2,18},{10... | collective-permute-start | bytes 49160 | tf_op jit(solution)/shard_map/ppermute | solution.py:479
  105.7 3.9 %collective-permute-start.15 = (f32[32,128]{1,0:T(8,128)}, f32[32,128]{1,0:T(8,128)S(1)}, u32[]{:S(2)}, u32[]{:S(2)}) collective-permute-start(f32[32,128]{1,0:T(8,128)} %get-tuple-element.44.refs_0_), channel_id=1, source_target_pairs={{0,8},{8,16},{16,24},{24,0},{1,9},{9,17},{17,25},{25,1},{2,10},{10... | collective-permute-start | bytes 49160 | tf_op jit(solution)/shard_map/ppermute | solution.py:479
  112.3 14.4 %copy-start.3 = (bf16[8,4,32,128]{3,2,1,0:T(8,128)(2,1)}, bf16[8,4,32,128]{3,2,1,0:T(8,128)(2,1)S(1)}, u32[]{:S(2)}) copy-start(bf16[8,4,32,128]{3,2,1,0:T(8,128)(2,1)S(1)} %all-to-all-done.4.refs_4_) | copy-start | bytes 786436
  112.3 14.4 %all-to-all-start.5 = ((f32[8,32,128]{2,1,0:T(8,128)}), f32[8,32,128]{2,1,0:T(8,128)S(1)}, u32[]{:S(2)}, u32[]{:S(2)}) async-start(f32[8,32,128]{2,1,0:T(8,128)} %gram_sum.1), calls=%async_computation.5 | async-start | bytes 262144 | tf_op jit(solution)/shard_map/all_to_all | solution.py:485
  119.3 3.6 %collective-permute-start.12 = (bf16[4,32,128]{2,1,0:T(8,128)(2,1)}, bf16[4,32,128]{2,1,0:T(8,128)(2,1)S(1)}, u32[]{:S(2)}, u32[]{:S(2)}) collective-permute-start(bf16[4,32,128]{2,1,0:T(8,128)(2,1)} %get-tuple-element.41), channel_id=1, source_target_pairs={{0,8},{8,16},{16,24},{24,0},{1,9},{9,17},{17,25},{25,1},{2,10},{10... | collective-permute-start | bytes 98312 | tf_op jit(solution)/shard_map/ppermute | solution.py:479
  119.4 4.5 %collective-permute-start.13 = (bf16[4,32,128]{2,1,0:T(8,128)(2,1)}, bf16[4,32,128]{2,1,0:T(8,128)(2,1)S(1)}, u32[]{:S(2)}, u32[]{:S(2)}) collective-permute-start(bf16[4,32,128]{2,1,0:T(8,128)(2,1)} %get-tuple-element.42), channel_id=1, source_target_pairs={{0,16},{8,24},{16,0},{24,8},{1,17},{9,25},{17,1},{25,9},{2,18},{10... | collective-permute-start | bytes 98312 | tf_op jit(solution)/shard_map/ppermute | solution.py:479
  120.3 3.6 %collective-permute-start.14 = (bf16[4,32,128]{2,1,0:T(8,128)(2,1)}, bf16[4,32,128]{2,1,0:T(8,128)(2,1)S(1)}, u32[]{:S(2)}, u32[]{:S(2)}) collective-permute-start(bf16[4,32,128]{2,1,0:T(8,128)(2,1)} %get-tuple-element.43), channel_id=1, source_target_pairs={{0,24},{8,0},{16,8},{24,16},{1,25},{9,1},{17,9},{25,17},{2,26},{10... | collective-permute-start | bytes 98312 | tf_op jit(solution)/shard_map/ppermute | solution.py:479
  122.9 3.8 %copy-start.15 = (bf16[4,32,128]{2,1,0:T(8,128)(2,1)}, bf16[4,32,128]{2,1,0:T(8,128)(2,1)S(1)}, u32[]{:S(2)}) copy-start(bf16[4,32,128]{2,1,0:T(8,128)(2,1)S(1)} %collective-permute-done.12.refs_1_) | copy-start | bytes 98308
  123.8 2.9 %copy-start.17 = (bf16[4,32,128]{2,1,0:T(8,128)(2,1)}, bf16[4,32,128]{2,1,0:T(8,128)(2,1)S(1)}, u32[]{:S(2)}) copy-start(bf16[4,32,128]{2,1,0:T(8,128)(2,1)S(1)} %collective-permute-done.14.refs_3_) | copy-start | bytes 98308
  (16 other events, 19.2 us)
where the time goes:
time: 139 us; the launch traced here: 141 us
  starting transfers between devices  63.4 us (46%)
  Pallas kernels  47.7 us (34%)
  waiting for transfers between devices  22.9 us (16%)
  local copies, waits for them, and re-layouts  4.96 us (4%)
  between operations  1.48 us (1%)
    all_to_all x6, starting transfers between devices, exchange(): return lax.all_to_all(pieces, axis, 0, 0, tiled=True)  52 us
    pallas_call x4, Pallas kernels, simple_call(): pl.pallas_call(kernel, out_shape=shapes, compiler_params=pltpu.CompilerPa...  19 us
    pallas_call x4, Pallas kernels, over_blocks(): pl.pallas_call(kernel, in_specs=[SCALARS, ANYWHERE] + [IN_VMEM] * len(inp...  18.3 us
    ppermute x18, waiting for transfers between devices, pass_around(): lax.ppermute(pieces[ahead], axis, [(at, (at + ahead) % count) for at in r...  15.1 us
    ppermute x18, starting transfers between devices, pass_around(): lax.ppermute(pieces[ahead], axis, [(at, (at + ahead) % count) for at in r...  11.4 us
    pallas_call x1, Pallas kernels, build_blocks(): pl.pallas_call(functools.partial(build_kernel, row_count), in_specs=[SCAL...  10.4 us
    all_to_all x6, waiting for transfers between devices, exchange(): return lax.all_to_all(pieces, axis, 0, 0, tiled=True)  7.83 us
    unnamed x48, local copies, waits for them, and re-layouts  4.3 us
  transfers between devices with their start and end apart: 24, of which 16 were waited for; matrix products, arithmetic and copies ran while one was open for 0% of the time, Pallas kernels for 14%

commit v1 on v0

--- a/solution.py
+++ b/solution.py
@@ -9,7 +9,8 @@
 
 graph_weight = 0.95
 GROUP = 16
-BATCH = 32
+BATCH = 64
+GRAM_TERMS = 3
 VMEM_LIMIT = 60 * 1024 * 1024
 
 
@@ -29,11 +30,15 @@
 exact_across = functools.partial(dot_across, precision=lax.Precision.HIGHEST)
 
 
-LIVE, ROW, COL, PLACES = 0, 1, 2, 4
-
-
-def group_count(facts_ref, group):
-    return (facts_ref[LIVE] + group - 1) // group
+def place_of(spots_ref, slot, col_blocks):
+    spot = spots_ref[0, 0, slot]
+    if col_blocks & (col_blocks - 1):
+        return lax.div(spot, col_blocks), lax.rem(spot, col_blocks)
+    return spot >> (col_blocks.bit_length() - 1), spot & (col_blocks - 1)
+
+
+def group_count(live_ref, group):
+    return (live_ref[0, 0] + group - 1) // group
 
 
 def group_copy(source, target, sems, index, group):
@@ -41,7 +46,7 @@
     return pltpu.make_async_copy(source.at[window], target.at[window], sems.at[index])
 
 
-def build_kernel(row_count, facts_ref, index_hbm, value_hbm, block_hbm, *refs):
+def build_kernel(row_count, spots_ref, live_ref, index_hbm, value_hbm, block_hbm, *refs):
     row_outs = refs[:row_count]
     (
         col_out_ref,
@@ -54,9 +59,9 @@
         value_sems,
         block_sems,
     ) = refs[row_count:]
-    slots = index_ref.shape[0]
     per_seg = row_outs[0].shape[0]
-    groups = group_count(facts_ref, BATCH) * (BATCH // GROUP)
+    col_blocks = col_out_ref.shape[0]
+    groups = group_count(live_ref, BATCH) * (BATCH // GROUP)
 
     def start_copies(index, _):
         group_copy(index_hbm, index_ref, index_sems, index, GROUP).start()
@@ -66,25 +71,25 @@
     lax.fori_loop(0, groups, start_copies, 0)
     row_ref[...] = jnp.zeros_like(row_ref)
     col_ref[...] = jnp.zeros_like(col_ref)
-    rows_16 = lax.broadcasted_iota(jnp.int32, (16, 128), 0).astype(jnp.float32)
+    rows_16 = lax.broadcasted_iota(jnp.int32, (16, 128), 0)
     ones = jnp.ones((8, 128), jnp.bfloat16)
     zero = jnp.zeros((16, 128), jnp.bfloat16)
 
     def build_group(index, _):
         group_copy(index_hbm, index_ref, index_sems, index, GROUP).wait()
         group_copy(value_hbm, value_ref, value_sems, index, GROUP).wait()
-        targets = [(rows_16 + 16.0 * part).astype(jnp.bfloat16) for part in range(8)]
+        targets = [(rows_16 + 16 * part).astype(jnp.int16) for part in range(8)]
         row_sums = []
         col_sums = []
         for inside in range(GROUP):
             slot = index * GROUP + inside
-            active = (slot < facts_ref[LIVE]).astype(jnp.float32)
-            index_f32 = index_ref[slot].astype(jnp.float32)
+            active = (slot < live_ref[0, 0]).astype(jnp.float32)
+            index_i32 = index_ref[slot]
             value_f32 = value_ref[slot].astype(jnp.float32) * active
             sums = [zero] * 8
             for entry in range(16):
-                index_row = jnp.broadcast_to(index_f32[entry : entry + 1], (16, 128)).astype(
-                    jnp.bfloat16
+                index_row = jnp.broadcast_to(index_i32[entry : entry + 1], (16, 128)).astype(
+                    jnp.int16
                 )
                 value_row = jnp.broadcast_to(value_f32[entry : entry + 1], (16, 128)).astype(
                     jnp.bfloat16
@@ -100,16 +105,17 @@
         group_copy(block_ref, block_hbm, block_sems, index, GROUP).start()
         for inside in range(GROUP):
             slot = index * GROUP + inside
-            row_ref[facts_ref[PLACES + slot]] += row_sums[inside]
-            col_ref[facts_ref[PLACES + slots + slot]] += col_sums[inside]
+            row_block, col_block = place_of(spots_ref, slot, col_blocks)
+            row_ref[row_block] += row_sums[inside]
+            col_ref[col_block] += col_sums[inside]
         return 0
 
     lax.fori_loop(0, groups, build_group, 0)
     for ahead, out in enumerate(row_outs):
-        first = lax.rem(facts_ref[ROW] + ahead, row_count) * per_seg
+        first = lax.rem(lax.axis_index("row") + ahead, row_count) * per_seg
         for part in range(per_seg):
             out[part : part + 1] = row_ref[first + part][:1]
-    for col_block in range(col_out_ref.shape[0]):
+    for col_block in range(col_blocks):
         col_out_ref[col_block : col_block + 1] = col_ref[col_block][:1]
 
     def finish_copies(index, _):
@@ -124,13 +130,13 @@
 IN_VMEM = pl.BlockSpec(memory_space=pltpu.VMEM)
 
 
-def build_blocks(facts, index_table, value_table, row_count, col_count, per_seg):
+def build_blocks(spots, live, index_table, value_table, row_count, col_count, per_seg):
     slots = index_table.shape[0]
     groups = slots // GROUP
     sum_shapes = [(per_seg, 128)] * row_count + [(col_count * per_seg, 128)]
     return pl.pallas_call(
         functools.partial(build_kernel, row_count),
-        in_specs=[SCALARS, ANYWHERE, ANYWHERE],
+        in_specs=[SCALARS, SCALARS, ANYWHERE, ANYWHERE],
         out_specs=[ANYWHERE] + [IN_VMEM] * len(sum_shapes),
         out_shape=[jax.ShapeDtypeStruct((slots, 128, 128), jnp.bfloat16)]
         + [jax.ShapeDtypeStruct(shape, jnp.float32) for shape in sum_shapes],
@@ -146,11 +152,11 @@
         ],
         compiler_params=pltpu.CompilerParams(vmem_limit_bytes=VMEM_LIMIT),
         name="build_blocks",
-    )(facts, index_table, value_table)
-
-
-def each_group(facts_ref, block_hbm, block_ref, sems, prepare, run_group):
-    groups = group_count(facts_ref, BATCH)
+    )(spots, live, index_table, value_table)
+
+
+def each_group(live_ref, block_hbm, block_ref, sems, prepare, run_group):
+    groups = group_count(live_ref, BATCH)
 
     def start_copy(index, _):
         group_copy(block_hbm, block_ref, sems, index, BATCH).start()
@@ -167,14 +173,14 @@
     lax.fori_loop(0, groups, one_group, 0)
 
 
-def add_products(dot, facts_ref, first_slot, block_ref, dir_ref, sources, total_refs, targets):
+def add_products(dot, places, first_slot, block_ref, dir_ref, total_refs):
     sums = []
     for inside in range(BATCH):
         slot = first_slot + inside
-        sums.append(dot(dir_ref[facts_ref[sources + slot]], block_ref[slot]))
+        sums.append(dot(dir_ref[places(slot)[0]], block_ref[slot]))
     for inside in range(BATCH):
         total_ref = total_refs[inside % len(total_refs)]
-        total_ref[facts_ref[targets + first_slot + inside]] += sums[inside]
+        total_ref[places(first_slot + inside)[1]] += sums[inside]
 
 
 def fill_directions(pieces, dir_ref, mine, per_seg):
@@ -184,33 +190,31 @@
             dir_ref[first + part] = piece[part]
 
 
-def backward_kernel(facts_ref, block_hbm, *refs):
+def backward_kernel(spots_ref, live_ref, block_hbm, *refs):
     *row_pieces, col_out_ref, block_ref, row_dir_ref, even_ref, odd_ref, sems = refs
     per_seg = row_pieces[0].shape[0]
-    slots = block_ref.shape[0]
+    col_blocks = even_ref.shape[0]
 
     def prepare():
         even_ref[...] = jnp.zeros_like(even_ref)
         odd_ref[...] = jnp.zeros_like(odd_ref)
-        fill_directions(row_pieces, row_dir_ref, facts_ref[ROW], per_seg)
+        fill_directions(row_pieces, row_dir_ref, lax.axis_index("row"), per_seg)
 
     def run_group(first_slot):
         add_products(
             dot_across,
-            facts_ref,
+            lambda slot: place_of(spots_ref, slot, col_blocks),
             first_slot,
             block_ref,
             row_dir_ref,
-            PLACES,
             [even_ref, odd_ref],
-            PLACES + slots,
         )
 
-    each_group(facts_ref, block_hbm, block_ref, sems, prepare, run_group)
+    each_group(live_ref, block_hbm, block_ref, sems, prepare, run_group)
     col_out_ref[...] = (even_ref[...] + odd_ref[...]).astype(col_out_ref.dtype)
 
 
-def forward_kernel(row_count, with_gram, facts_ref, block_hbm, col_dir_ref, *refs):
+def forward_kernel(row_count, with_gram, spots_ref, live_ref, block_hbm, col_dir_ref, *refs):
     refs = list(refs)
 
     def take(count):
@@ -221,10 +225,10 @@
     row_pieces = take(row_count if with_gram else 0)
     gram_in = take(int(with_gram))
     row_outs = take(row_count)
-    gram_out = take(int(with_gram))
     block_ref, even_ref, odd_ref, sems = refs
-    per_seg, size, _ = row_outs[0].shape
-    slots = block_ref.shape[0]
+    _, size, _ = row_outs[0].shape
+    per_seg = even_ref.shape[0] // row_count
+    col_blocks = col_dir_ref.shape[0]
 
     def prepare():
         even_ref[...] = jnp.zeros_like(even_ref)
@@ -233,19 +237,17 @@
     def run_group(first_slot):
         add_products(
             dot_plain,
-            facts_ref,
+            lambda slot: place_of(spots_ref, slot, col_blocks)[::-1],
             first_slot,
             block_ref,
             col_dir_ref,
-            PLACES + slots,
             [even_ref, odd_ref],
-            PLACES,
         )
 
-    each_group(facts_ref, block_hbm, block_ref, sems, prepare, run_group)
+    each_group(live_ref, block_hbm, block_ref, sems, prepare, run_group)
     gram = jnp.zeros((2 * size, 128), jnp.float32)
     for ahead, out in enumerate(row_outs):
-        first = lax.rem(facts_ref[ROW] + ahead, row_count) * per_seg
+        first = lax.rem(lax.axis_index("row") + ahead, row_count) * per_seg
         for part in range(per_seg):
             values = even_ref[first + part] + odd_ref[first + part]
             high = values.astype(out.dtype)
@@ -255,15 +257,19 @@
                 piece = row_pieces[(row_count - ahead) % row_count]
                 gram += dot_across(jnp.concatenate([high, low], axis=0), tall(piece[part]))
     if with_gram:
-        gram = gram[:size] + gram[size:]
-        gram_out[0][...] = gram_in[0][...] + pltpu.roll(gram, 3 * size, 1)
-
-
-def over_blocks(kernel, name, facts, blocks, inputs, outputs, scratch):
+        gram = gram_in[0][...] + pltpu.roll(gram[:size] + gram[size:], 3 * size, 1)
+        for term in range(GRAM_TERMS):
+            rounded = gram.astype(jnp.bfloat16)
+            gram = gram - rounded.astype(jnp.float32)
+            for out in row_outs:
+                out[per_seg + term] = rounded
+
+
+def over_blocks(kernel, name, places, blocks, inputs, outputs, scratch):
     slots = blocks.shape[0]
     return pl.pallas_call(
         kernel,
-        in_specs=[SCALARS, ANYWHERE] + [IN_VMEM] * len(inputs),
+        in_specs=[SCALARS, SCALARS, ANYWHERE] + [IN_VMEM] * len(inputs),
         out_specs=[IN_VMEM] * len(outputs),
         out_shape=outputs,
         scratch_shapes=[pltpu.VMEM(blocks.shape, blocks.dtype)]
@@ -274,16 +280,16 @@
             flops=2 * slots * 32 * 128 * 128, bytes_accessed=2 * blocks.size, transcendentals=0
         ),
         name=name,
-    )(facts, blocks, *inputs)
-
-
-def backward_product(facts, blocks, row_pieces, col_count):
+    )(*places, blocks, *inputs)
+
+
+def backward_product(places, blocks, row_pieces, col_count):
     per_seg, rows, lanes = row_pieces[0].shape
     col_shape = (col_count * per_seg, rows, lanes)
     (total,) = over_blocks(
         backward_kernel,
         "backward_product",
-        facts,
+        places,
         blocks,
         row_pieces,
         [jax.ShapeDtypeStruct(col_shape, jnp.bfloat16)],
@@ -296,18 +302,19 @@
     return total
 
 
-def forward_product(facts, blocks, col_dirs, row_pieces, gram=None):
+def forward_product(places, blocks, col_dirs, row_pieces, gram=None):
     piece = row_pieces[0]
     inputs = [col_dirs]
-    outputs = [jax.ShapeDtypeStruct(piece.shape, jnp.bfloat16)] * len(row_pieces)
+    sent = piece.shape[0]
     if gram is not None:
         inputs += [*row_pieces, gram]
-        outputs += [jax.ShapeDtypeStruct(gram.shape, jnp.float32)]
+        sent += GRAM_TERMS
+    outputs = [jax.ShapeDtypeStruct((sent,) + piece.shape[1:], jnp.bfloat16)] * len(row_pieces)
     row_shape = (len(row_pieces) * piece.shape[0],) + piece.shape[1:]
     return over_blocks(
         functools.partial(forward_kernel, len(row_pieces), gram is not None),
         "forward_product",
-        facts,
+        places,
         blocks,
         inputs,
         outputs,
@@ -408,21 +415,12 @@
     size = pairs[0][0].shape[0]
     systems = [matrix + pltpu.roll(side, size, 1) for matrix, side in pairs]
     sublanes = lax.broadcasted_iota(jnp.int32, systems[0].shape, 0)
-    for pivot in range(0, size, 2):
+    for pivot in range(size):
         updated = []
         for system in systems:
-            upper, lower = system[pivot : pivot + 1, :], system[pivot + 1 : pivot + 2, :]
-            left, right = system[:, pivot : pivot + 1], system[:, pivot + 1 : pivot + 2]
-            inverse = 1.0 / left[pivot : pivot + 1, :]
-            upper = upper * inverse
-            ratio = left[pivot + 1 : pivot + 2, :]
-            across = right[pivot : pivot + 1, :] * inverse
-            inverse = 1.0 / (right[pivot + 1 : pivot + 2, :] - ratio * across)
-            new_lower = (lower - ratio * upper) * inverse
-            new_upper = upper - across * new_lower
-            rest = system - left * new_upper - right * new_lower
-            rest = jnp.where(sublanes == pivot, new_upper, rest)
-            updated.append(jnp.where(sublanes == pivot + 1, new_lower, rest))
+            column = system[:, pivot : pivot + 1]
+            row = system[pivot : pivot + 1, :] / column[pivot : pivot + 1, :]
+            updated.append(jnp.where(sublanes == pivot, row, system - column * row))
         systems = updated
     return [window(system, 1) for system in systems]
 
@@ -496,7 +494,10 @@
 
 def sum_kernel(*refs):
     *piece_refs, copies_ref = refs
-    total = total_of([ref[...] for ref in piece_refs])
+    first = piece_refs[0].shape[0] - GRAM_TERMS
+    total = total_of(
+        [ref[first + term] for term in range(GRAM_TERMS) for ref in piece_refs]
+    )
     for copy in range(copies_ref.shape[0]):
         copies_ref[copy] = total
 
@@ -506,12 +507,7 @@
     col_count = lax.axis_size("col")
     query_rows, seg_len = queries.shape
     per_seg = seg_len // 128
-    spots = block_spots[0, 0]
-    col_blocks = col_count * per_seg
-    heads = [live_blocks[0, 0], lax.axis_index("row"), lax.axis_index("col"), 0]
-    facts = jnp.concatenate(
-        [jnp.stack(heads).astype(jnp.int32), spots // col_blocks, spots % col_blocks]
-    )
+    places = (block_spots, live_blocks)
     piece = (per_seg, query_rows, 128)
     wide = jax.ShapeDtypeStruct(piece, jnp.float32)
     narrow = jax.ShapeDtypeStruct(piece, jnp.bfloat16)
@@ -520,7 +516,7 @@
     gram_copies = jax.ShapeDtypeStruct((col_count, query_rows, 128), jnp.float32)
 
     blocks, *row_sums, col_sums = build_blocks(
-        facts, neighbor_cols[0, 0], neighbor_sims[0, 0], row_count, col_count, per_seg
+        *places, neighbor_cols[0, 0], neighbor_sims[0, 0], row_count, col_count, per_seg
     )
     col_part = exchange(col_sums.reshape(col_count, per_seg, 128), "col")
     row_parts = pass_around(row_sums, "row")
@@ -536,13 +532,12 @@
     def product(vectors, vector_copies, gram=None):
         col_dirs = exchange(vector_copies, "col").reshape((col_count * per_seg,) + piece[1:])
         row_pieces = pass_around([vectors] * row_count, "row")
-        total = backward_product(facts, blocks, row_pieces, col_count)
+        total = backward_product(places, blocks, row_pieces, col_count)
         col_part = exchange(total.reshape((col_count,) + piece), "col")
-        totals = forward_product(facts, blocks, col_dirs, row_pieces, gram)
-        row_parts = pass_around(totals[:row_count], "row")
-        return row_parts, col_part, totals[row_count:]
-
-    row_parts, col_part, _ = product(scaled, scaled_copies)
+        totals = forward_product(places, blocks, col_dirs, row_pieces, gram)
+        return pass_around(totals, "row"), col_part
+
+    row_parts, col_part = product(scaled, scaled_copies)
     first, scaled, scaled_copies, gram = simple_call(
         middle_kernel,
         [wide, narrow, copies, gram_shape],
@@ -552,10 +547,8 @@
         scaling,
         queries,
     )
-    row_parts, col_part, (gram,) = product(scaled, scaled_copies, gram)
-    (grams,) = simple_call(
-        sum_kernel, [gram_copies], "gram_sum", *pass_around([gram] * row_count, "row")
-    )
+    row_parts, col_part = product(scaled, scaled_copies, gram)
+    (grams,) = simple_call(sum_kernel, [gram_copies], "gram_sum", *row_parts)
     flat = jax.ShapeDtypeStruct(queries.shape, jnp.float32)
     return tuple(
         simple_call(

time: 139 us -> 131 us (0.942)
  blocking collectives: 0 us -> 15.6 us
  waiting for transfers between devices: 22.9 us -> 14 us
  Pallas kernels: 47.7 us -> 40 us
  starting transfers between devices: 63.4 us -> 59.2 us
  local copies, waits for them, and re-layouts: 4.96 us -> 3.19 us
    all_to_all x0 -> x1, blocking collectives: none -> 15.6 us  [exchange(): return lax.all_to_all(pieces, axis, 0, 0, tiled=True)]
    all_to_all x6 -> x5, starting transfers between devices: 52 us -> 39.1 us  [exchange(): return lax.all_to_all(pieces, axis, 0, 0, tiled=True)]
    ppermute x18 -> x15, starting transfers between devices: 11.4 us -> 20.1 us  [pass_around(): lax.ppermute(pieces[ahead], axis, [(at, (at + ahead) % count) for at in r...]
    all_to_all x6 -> x5, waiting for transfers between devices: 7.83 us -> 2.06 us  [exchange(): return lax.all_to_all(pieces, axis, 0, 0, tiled=True)]
    pallas_call x4, Pallas kernels: 19 us -> 15 us  [simple_call(): pl.pallas_call(kernel, out_shape=shapes, compiler_params=pltpu.CompilerPa...]
    ppermute x18 -> x15, waiting for transfers between devices: 15.1 us -> 11.9 us  [pass_around(): lax.ppermute(pieces[ahead], axis, [(at, (at + ahead) % count) for at in r...]
    pallas_call x1, Pallas kernels: 10.4 us -> 7.87 us  [build_blocks(): pl.pallas_call(functools.partial(build_kernel, row_count), in_specs=[SCAL...]
    unnamed x48 -> x40, local copies, waits for them, and re-layouts: 4.3 us -> 3.19 us
  transfers between devices with their start and end apart: 24 -> 20, of which waited for: 16 -> 13; matrix products, arithmetic and copies ran while one was open for 0% -> 0% of each run, Pallas kernels for 14% -> 14%
where the time goes in v1:
time: 131 us; the launch traced here: 133 us
  starting transfers between devices  59.2 us (45%)
  Pallas kernels  40 us (31%)
  blocking collectives  15.6 us (12%)
  waiting for transfers between devices  14 us (11%)
  local copies, waits for them, and re-layouts  3.19 us (2%)
  between operations  1.44 us (1%)
    all_to_all x5, starting transfers between devices, exchange(): return lax.all_to_all(pieces, axis, 0, 0, tiled=True)  39.1 us
    ppermute x15, starting transfers between devices, pass_around(): lax.ppermute(pieces[ahead], axis, [(at, (at + ahead) % count) for at in r...  20.1 us
    pallas_call x4, Pallas kernels, over_blocks(): pl.pallas_call(kernel, in_specs=[SCALARS, SCALARS, ANYWHERE] + [IN_VMEM]...  17.1 us
    all_to_all x1, blocking collectives, exchange(): return lax.all_to_all(pieces, axis, 0, 0, tiled=True)  15.6 us
    pallas_call x4, Pallas kernels, simple_call(): pl.pallas_call(kernel, out_shape=shapes, compiler_params=pltpu.CompilerPa...  15 us
    ppermute x15, waiting for transfers between devices, pass_around(): lax.ppermute(pieces[ahead], axis, [(at, (at + ahead) % count) for at in r...  11.9 us
    pallas_call x1, Pallas kernels, build_blocks(): pl.pallas_call(functools.partial(build_kernel, row_count), in_specs=[SCAL...  7.87 us
    unnamed x40, local copies, waits for them, and re-layouts  3.19 us
  transfers between devices with their start and end apart: 20, of which 13 were waited for; matrix products, arithmetic and copies ran while one was open for 0% of the time, Pallas kernels for 14%

profile of v1, /device:TPU:0, one launch (start us, length us, event | category | flops | bytes accessed | tf_op | source)
XLA Modules:
  0.0 133.4 jit_solution(12991672894392835073)
XLA Ops:
  1.3 7.9 %build_blocks.1 = (bf16[256,128,128]{2,1,0:T(8,128)(2,1)}, f32[4,128]{1,0:T(4,128)}, f32[4,128]{1,0:T(4,128)}, f32[4,128]{1,0:T(4,128)}, f32[4,128]{1,0:T(4,128)}, /*index=5*/f32[32,128]{1,0:T(8,128)}) custom-call(s32[1,1,256]{2,1,0:T(1,128)} %spots_ref.9, s32[1,1]{1,0:T(1,128)S(6)} %copy.7.live_ref, s32[256,16,128]{2,1,0:T(8,128)} %bitcast.7, ...), custom_call_target="tpu_custom_call" | custom-call | tf_op jit(solution)/shard_map/build_blocks/pallas_call | solution.py:137
  9.2 11.8 %all-to-all-start = ((f32[8,4,128]{2,1,0:T(4,128)}), f32[8,4,128]{2,1,0:T(4,128)S(1)}, u32[]{:S(2)}, u32[]{:S(2)}) async-start(f32[8,4,128]{2,1,0:T(4,128)} %bitcast.13), calls=%async_computation | async-start | bytes 32768 | tf_op jit(solution)/shard_map/all_to_all | solution.py:483
  21.0 10.2 %collective-permute-start.1 = (f32[4,128]{1,0:T(4,128)}, f32[4,128]{1,0:T(4,128)S(1)}, u32[]{:S(2)}, u32[]{:S(2)}) collective-permute-start(f32[4,128]{1,0:T(4,128)} %get-tuple-element.26), channel_id=1, source_target_pairs={{0,16},{8,24},{16,0},{24,8},{1,17},{9,25},{17,1},{25,9},{2,18},{10... | collective-permute-start | bytes 6152 | tf_op jit(solution)/shard_map/ppermute | solution.py:477
  31.2 1.1 collective-permute-done.refs_1_
  32.3 0.7 collective-permute-done.1.refs_2_
  33.6 1.7 %start.1 = (f32[4,128]{1,0:T(4,128)}, bf16[4,32,128]{2,1,0:T(8,128)(2,1)}, bf16[8,4,32,128]{3,2,1,0:T(8,128)(2,1)}) custom-call(f32[4,128]{1,0:T(4,128)} %get-tuple-element.24.refs_0_, f32[4,128]{1,0:T(4,128)} %copy-done.17, f32[4,128]{1,0:T(4,128)} %copy-done.18, f32[4,128]{1,0:T(4,128)} %copy-done.19, f32[8,4,128]{2,1,0:T(4,128)} %copy-done.10, ...), custom_call_target="tpu_custom_call" | custom-call | tf_op jit(solution)/shard_map/start/pallas_call | solution.py:487
  35.2 5.7 %all-to-all-start.1 = ((bf16[8,4,32,128]{3,2,1,0:T(8,128)(2,1)}), bf16[8,4,32,128]{3,2,1,0:T(8,128)(2,1)S(1)}, u32[]{:S(2)}, u32[]{:S(2)}) async-start(bf16[8,4,32,128]{3,2,1,0:T(8,128)(2,1)} %get-tuple-element.29), calls=%async_computation.1 | async-start | bytes 524288 | tf_op jit(solution)/shard_map/all_to_all | solution.py:483
  41.0 1.5 %collective-permute-start.8 = (bf16[4,32,128]{2,1,0:T(8,128)(2,1)}, bf16[4,32,128]{2,1,0:T(8,128)(2,1)S(1)}, u32[]{:S(2)}, u32[]{:S(2)}) collective-permute-start(bf16[4,32,128]{2,1,0:T(8,128)(2,1)} %get-tuple-element.34.refs_0_), channel_id=1, source_target_pairs={{0,24},{8,0},{16,8},{24,16},{1,25},{9,1},{17,9},{25,17},{2,26},{10... | collective-permute-start | bytes 98312 | tf_op jit(solution)/shard_map/ppermute | solution.py:477
  42.4 1.1 collective-permute-start.7
  43.5 0.9 collective-permute-done.8.refs_3_
  44.4 2.1 %collective-permute-done.7.refs_2_ = bf16[4,32,128]{2,1,0:T(8,128)(2,1)S(1)} collective-permute-done((bf16[4,32,128]{2,1,0:T(8,128)(2,1)}, bf16[4,32,128]{2,1,0:T(8,128)(2,1)S(1)}, u32[]{:S(2)}, u32[]{:S(2)}) %collective-permute-start.7) | collective-permute-done | bytes 32800 | tf_op jit(solution)/shard_map/ppermute | solution.py:477
  47.6 4.4 %backward_product.2 = bf16[32,32,128]{2,1,0:T(8,128)(2,1)} custom-call(s32[1,1,256]{2,1,0:T(1,128)} %spots_ref.9, s32[1,1]{1,0:T(1,128)S(6)} %copy.7.live_ref, bf16[256,128,128]{2,1,0:T(8,128)(2,1)} %get-tuple-element.23.block_hbm, bf16[4,32,128]{2,1,0:T(8,128)(2,1)} %get-tuple-element.34.refs_0_, bf16[4,32,128]{2,1,0:T(8,128)(2,1)} %copy-done.13, ...), custom_call_target="tpu_custom_call" | custom-call | flops 268435456 | bytes 8388608 | tf_op jit(solution)/shard_map/backward_product/pallas_call | solution.py:270
  52.1 6.9 %all-to-all-start.2 = ((bf16[8,4,32,128]{3,2,1,0:T(8,128)(2,1)}), bf16[8,4,32,128]{3,2,1,0:T(8,128)(2,1)S(1)}, u32[]{:S(2)}, u32[]{:S(2)}) async-start(bf16[8,4,32,128]{3,2,1,0:T(8,128)(2,1)} %bitcast.11), calls=%async_computation.2 | async-start | bytes 524288 | tf_op jit(solution)/shard_map/all_to_all | solution.py:483
  59.0 3.9 %forward_product.2 = (bf16[4,32,128]{2,1,0:T(8,128)(2,1)}, bf16[4,32,128]{2,1,0:T(8,128)(2,1)}, bf16[4,32,128]{2,1,0:T(8,128)(2,1)}, bf16[4,32,128]{2,1,0:T(8,128)(2,1)}) custom-call(s32[1,1,256]{2,1,0:T(1,128)} %spots_ref.9, s32[1,1]{1,0:T(1,128)S(6)} %copy.7.live_ref, bf16[256,128,128]{2,1,0:T(8,128)(2,1)} %get-tuple-element.23.block_hbm, ...), custom_call_target="tpu_custom_call" | custom-call | flops 268435456 | bytes 8388608 | tf_op jit(solution)/shard_map/forward_product/pallas_call | solution.py:270
  63.0 2.2 %collective-permute-start.4 = (bf16[4,32,128]{2,1,0:T(8,128)(2,1)}, bf16[4,32,128]{2,1,0:T(8,128)(2,1)S(1)}, u32[]{:S(2)}, u32[]{:S(2)}) collective-permute-start(bf16[4,32,128]{2,1,0:T(8,128)(2,1)} %get-tuple-element.32), channel_id=1, source_target_pairs={{0,16},{8,24},{16,0},{24,8},{1,17},{9,25},{17,1},{25,9},{2,18},{10... | collective-permute-start | bytes 98312 | tf_op jit(solution)/shard_map/ppermute | solution.py:477
  65.2 2.0 %all-to-all-done.2.refs_4_ = bf16[8,4,32,128]{3,2,1,0:T(8,128)(2,1)S(1)} async-done(((bf16[8,4,32,128]{3,2,1,0:T(8,128)(2,1)}), bf16[8,4,32,128]{3,2,1,0:T(8,128)(2,1)S(1)}, u32[]{:S(2)}, u32[]{:S(2)}) %all-to-all-start.2) | async-done | bytes 262176 | tf_op jit(solution)/shard_map/all_to_all | solution.py:483
  68.0 2.2 %middle.1 = (f32[4,32,128]{2,1,0:T(8,128)}, bf16[4,32,128]{2,1,0:T(8,128)(2,1)}, bf16[8,4,32,128]{3,2,1,0:T(8,128)(2,1)}, f32[32,128]{1,0:T(8,128)}) custom-call(bf16[4,32,128]{2,1,0:T(8,128)(2,1)} %get-tuple-element.30.refs_0_, bf16[4,32,128]{2,1,0:T(8,128)(2,1)} %copy-done.14, bf16[4,32,128]{2,1,0:T(8,128)(2,1)} %copy-done.15, ...), custom_call_target="tpu_custom_call" | custom-call | tf_op jit(solution)/shard_map/middle/pallas_call | solution.py:487
  70.2 7.7 %all-to-all-start.3 = ((bf16[8,4,32,128]{3,2,1,0:T(8,128)(2,1)}), bf16[8,4,32,128]{3,2,1,0:T(8,128)(2,1)S(1)}, u32[]{:S(2)}, u32[]{:S(2)}) async-start(bf16[8,4,32,128]{3,2,1,0:T(8,128)(2,1)} %get-tuple-element.36), calls=%async_computation.3 | async-start | bytes 524288 | tf_op jit(solution)/shard_map/all_to_all | solution.py:483
  78.0 1.4 %collective-permute-start.11 = (bf16[4,32,128]{2,1,0:T(8,128)(2,1)}, bf16[4,32,128]{2,1,0:T(8,128)(2,1)S(1)}, u32[]{:S(2)}, u32[]{:S(2)}) collective-permute-start(bf16[4,32,128]{2,1,0:T(8,128)(2,1)} %get-tuple-element.37.refs_0_), channel_id=1, source_target_pairs={{0,24},{8,0},{16,8},{24,16},{1,25},{9,1},{17,9},{25,17},{2,26},{10... | collective-permute-start | bytes 98312 | tf_op jit(solution)/shard_map/ppermute | solution.py:477
  79.4 1.1 collective-permute-start.10
  80.4 1.0 collective-permute-done.11.refs_3_
  81.4 2.1 %collective-permute-done.10.refs_2_ = bf16[4,32,128]{2,1,0:T(8,128)(2,1)S(1)} collective-permute-done((bf16[4,32,128]{2,1,0:T(8,128)(2,1)}, bf16[4,32,128]{2,1,0:T(8,128)(2,1)S(1)}, u32[]{:S(2)}, u32[]{:S(2)}) %collective-permute-start.10) | collective-permute-done | bytes 32800 | tf_op jit(solution)/shard_map/ppermute | solution.py:477
  84.7 4.4 %backward_product.3 = bf16[32,32,128]{2,1,0:T(8,128)(2,1)} custom-call(s32[1,1,256]{2,1,0:T(1,128)} %spots_ref.9, s32[1,1]{1,0:T(1,128)S(6)} %copy.7.live_ref, bf16[256,128,128]{2,1,0:T(8,128)(2,1)} %get-tuple-element.23.block_hbm, bf16[4,32,128]{2,1,0:T(8,128)(2,1)} %get-tuple-element.37.refs_0_, bf16[4,32,128]{2,1,0:T(8,128)(2,1)} %copy-done.9, ...), custom_call_target="tpu_custom_call" | custom-call | flops 268435456 | bytes 8388608 | tf_op jit(solution)/shard_map/backward_product/pallas_call | solution.py:270
  89.1 6.9 %all-to-all-start.4 = ((bf16[8,4,32,128]{3,2,1,0:T(8,128)(2,1)}), bf16[8,4,32,128]{3,2,1,0:T(8,128)(2,1)S(1)}, u32[]{:S(2)}, u32[]{:S(2)}) async-start(bf16[8,4,32,128]{3,2,1,0:T(8,128)(2,1)} %bitcast.8), calls=%async_computation.4 | async-start | bytes 524288 | tf_op jit(solution)/shard_map/all_to_all | solution.py:483
  96.1 4.3 %forward_product.3 = (bf16[7,32,128]{2,1,0:T(8,128)(2,1)}, bf16[7,32,128]{2,1,0:T(8,128)(2,1)}, bf16[7,32,128]{2,1,0:T(8,128)(2,1)}, bf16[7,32,128]{2,1,0:T(8,128)(2,1)}) custom-call(s32[1,1,256]{2,1,0:T(1,128)} %spots_ref.9, s32[1,1]{1,0:T(1,128)S(6)} %copy.7.live_ref, bf16[256,128,128]{2,1,0:T(8,128)(2,1)} %get-tuple-element.23.block_hbm, ...), custom_call_target="tpu_custom_call" | custom-call | flops 268435456 | bytes 8388608 | tf_op jit(solution)/shard_map/forward_product/pallas_call | solution.py:270
  100.5 2.6 %collective-permute-start.13 = (bf16[7,32,128]{2,1,0:T(8,128)(2,1)}, bf16[7,32,128]{2,1,0:T(8,128)(2,1)S(1)}, u32[]{:S(2)}, u32[]{:S(2)}) collective-permute-start(bf16[7,32,128]{2,1,0:T(8,128)(2,1)} %get-tuple-element.41), channel_id=1, source_target_pairs={{0,16},{8,24},{16,0},{24,8},{1,17},{9,25},{17,1},{25,9},{2,18},{10... | collective-permute-start | bytes 172040 | tf_op jit(solution)/shard_map/ppermute | solution.py:477
  103.1 1.7 %collective-permute-done.12.refs_1_ = bf16[7,32,128]{2,1,0:T(8,128)(2,1)S(1)} collective-permute-done((bf16[7,32,128]{2,1,0:T(8,128)(2,1)}, bf16[7,32,128]{2,1,0:T(8,128)(2,1)S(1)}, u32[]{:S(2)}, u32[]{:S(2)}) %collective-permute-start.12) | collective-permute-done | bytes 57376 | tf_op jit(solution)/shard_map/ppermute | solution.py:477
  104.8 1.2 collective-permute-done.13.refs_2_
  106.0 0.6 copy-done.5
  106.6 1.6 %gram_sum.1 = f32[8,32,128]{2,1,0:T(8,128)} custom-call(bf16[7,32,128]{2,1,0:T(8,128)(2,1)} %get-tuple-element.39.refs_0_, bf16[7,32,128]{2,1,0:T(8,128)(2,1)} %copy-done.4, bf16[7,32,128]{2,1,0:T(8,128)(2,1)} %copy-done.5, bf16[7,32,128]{2,1,0:T(8,128)(2,1)} %copy-done.6), custom_call_target="tpu_custom_call" | custom-call | tf_op jit(solution)/shard_map/gram_sum/pallas_call | solution.py:487
  108.2 15.6 %all_to_all.30.refs_5_ = f32[8,32,128]{2,1,0:T(8,128)} all-to-all(f32[8,32,128]{2,1,0:T(8,128)} %gram_sum.1), channel_id=1, replica_groups=mesh['row'=4,'col'=8] {'col'}, dimensions={0} | all-to-all | bytes 262144 | tf_op jit(solution)/shard_map/all_to_all | solution.py:483
  123.8 9.6 %close.1 = (f32[32,512]{1,0:T(8,128)}, f32[32,512]{1,0:T(8,128)}) custom-call(bf16[7,32,128]{2,1,0:T(8,128)(2,1)} %get-tuple-element.39.refs_0_, bf16[7,32,128]{2,1,0:T(8,128)(2,1)} %copy-done.4, bf16[7,32,128]{2,1,0:T(8,128)(2,1)} %copy-done.5, bf16[7,32,128]{2,1,0:T(8,128)(2,1)} %copy-done.6, bf16[8,4,32,128]{3,2,1,0:T(8,128)(2,1)} %copy-done, ...), custom_call_target="tpu_custom_call" | custom-call | tf_op jit(solution)/shard_map/close/pallas_call | solution.py:487
  (58 shorter events, 3.9 us)
Async XLA Ops:
  9.2 23.8 %all-to-all-start = ((f32[8,4,128]{2,1,0:T(4,128)}), f32[8,4,128]{2,1,0:T(4,128)S(1)}, u32[]{:S(2)}, u32[]{:S(2)}) async-start(f32[8,4,128]{2,1,0:T(4,128)} %bitcast.13), calls=%async_computation | async-start | bytes 32768 | tf_op jit(solution)/shard_map/all_to_all | solution.py:483
  21.0 11.3 %collective-permute-start = (f32[4,128]{1,0:T(4,128)}, f32[4,128]{1,0:T(4,128)S(1)}, u32[]{:S(2)}, u32[]{:S(2)}) collective-permute-start(f32[4,128]{1,0:T(4,128)} %get-tuple-element.25), channel_id=1, source_target_pairs={{0,8},{8,16},{16,24},{24,0},{1,9},{9,17},{17,25},{25,1},{2,10},{10... | collective-permute-start | bytes 6152 | tf_op jit(solution)/shard_map/ppermute | solution.py:477
  21.0 12.0 %collective-permute-start.1 = (f32[4,128]{1,0:T(4,128)}, f32[4,128]{1,0:T(4,128)S(1)}, u32[]{:S(2)}, u32[]{:S(2)}) collective-permute-start(f32[4,128]{1,0:T(4,128)} %get-tuple-element.26), channel_id=1, source_target_pairs={{0,16},{8,24},{16,0},{24,8},{1,17},{9,25},{17,1},{25,9},{2,18},{10... | collective-permute-start | bytes 6152 | tf_op jit(solution)/shard_map/ppermute | solution.py:477
  31.2 1.8 %collective-permute-start.2 = (f32[4,128]{1,0:T(4,128)}, f32[4,128]{1,0:T(4,128)S(1)}, u32[]{:S(2)}, u32[]{:S(2)}) collective-permute-start(f32[4,128]{1,0:T(4,128)} %get-tuple-element.27), channel_id=1, source_target_pairs={{0,24},{8,0},{16,8},{24,16},{1,25},{9,1},{17,9},{25,17},{2,26},{10... | collective-permute-start | bytes 6152 | tf_op jit(solution)/shard_map/ppermute | solution.py:477
  32.3 0.7 copy-start.17
  35.2 16.8 %all-to-all-start.1 = ((bf16[8,4,32,128]{3,2,1,0:T(8,128)(2,1)}), bf16[8,4,32,128]{3,2,1,0:T(8,128)(2,1)S(1)}, u32[]{:S(2)}, u32[]{:S(2)}) async-start(bf16[8,4,32,128]{3,2,1,0:T(8,128)(2,1)} %get-tuple-element.29), calls=%async_computation.1 | async-start | bytes 524288 | tf_op jit(solution)/shard_map/all_to_all | solution.py:483
  41.0 3.4 %collective-permute-start.8 = (bf16[4,32,128]{2,1,0:T(8,128)(2,1)}, bf16[4,32,128]{2,1,0:T(8,128)(2,1)S(1)}, u32[]{:S(2)}, u32[]{:S(2)}) collective-permute-start(bf16[4,32,128]{2,1,0:T(8,128)(2,1)} %get-tuple-element.34.refs_0_), channel_id=1, source_target_pairs={{0,24},{8,0},{16,8},{24,16},{1,25},{9,1},{17,9},{25,17},{2,26},{10... | collective-permute-start | bytes 98312 | tf_op jit(solution)/shard_map/ppermute | solution.py:477
  42.4 4.1 %collective-permute-start.7 = (bf16[4,32,128]{2,1,0:T(8,128)(2,1)}, bf16[4,32,128]{2,1,0:T(8,128)(2,1)S(1)}, u32[]{:S(2)}, u32[]{:S(2)}) collective-permute-start(bf16[4,32,128]{2,1,0:T(8,128)(2,1)} %get-tuple-element.34.refs_0_), channel_id=1, source_target_pairs={{0,16},{8,24},{16,0},{24,8},{1,17},{9,25},{17,1},{25,9},{2,18},{10... | collective-permute-start | bytes 98312 | tf_op jit(solution)/shard_map/ppermute | solution.py:477
  43.5 3.6 %collective-permute-start.6 = (bf16[4,32,128]{2,1,0:T(8,128)(2,1)}, bf16[4,32,128]{2,1,0:T(8,128)(2,1)S(1)}, u32[]{:S(2)}, u32[]{:S(2)}) collective-permute-start(bf16[4,32,128]{2,1,0:T(8,128)(2,1)} %get-tuple-element.34.refs_0_), channel_id=1, source_target_pairs={{0,8},{8,16},{16,24},{24,0},{1,9},{9,17},{17,25},{25,1},{2,10},{10... | collective-permute-start | bytes 98312 | tf_op jit(solution)/shard_map/ppermute | solution.py:477
  44.4 2.6 %copy-start.11 = (bf16[4,32,128]{2,1,0:T(8,128)(2,1)}, bf16[4,32,128]{2,1,0:T(8,128)(2,1)S(1)}, u32[]{:S(2)}) copy-start(bf16[4,32,128]{2,1,0:T(8,128)(2,1)S(1)} %collective-permute-done.8.refs_3_) | copy-start | bytes 98308
  52.1 7.0 %copy-start.1 = (bf16[8,4,32,128]{3,2,1,0:T(8,128)(2,1)}, bf16[8,4,32,128]{3,2,1,0:T(8,128)(2,1)S(1)}, u32[]{:S(2)}) copy-start(bf16[8,4,32,128]{3,2,1,0:T(8,128)(2,1)S(1)} %all-to-all-done.1) | copy-start | bytes 786436
  52.1 15.2 %all-to-all-start.2 = ((bf16[8,4,32,128]{3,2,1,0:T(8,128)(2,1)}), bf16[8,4,32,128]{3,2,1,0:T(8,128)(2,1)S(1)}, u32[]{:S(2)}, u32[]{:S(2)}) async-start(bf16[8,4,32,128]{3,2,1,0:T(8,128)(2,1)} %bitcast.11), calls=%async_computation.2 | async-start | bytes 524288 | tf_op jit(solution)/shard_map/all_to_all | solution.py:483
  63.0 4.3 %collective-permute-start.3 = (bf16[4,32,128]{2,1,0:T(8,128)(2,1)}, bf16[4,32,128]{2,1,0:T(8,128)(2,1)S(1)}, u32[]{:S(2)}, u32[]{:S(2)}) collective-permute-start(bf16[4,32,128]{2,1,0:T(8,128)(2,1)} %get-tuple-element.31), channel_id=1, source_target_pairs={{0,8},{8,16},{16,24},{24,0},{1,9},{9,17},{17,25},{25,1},{2,10},{10... | collective-permute-start | bytes 98312 | tf_op jit(solution)/shard_map/ppermute | solution.py:477
  63.0 4.3 %collective-permute-start.4 = (bf16[4,32,128]{2,1,0:T(8,128)(2,1)}, bf16[4,32,128]{2,1,0:T(8,128)(2,1)S(1)}, u32[]{:S(2)}, u32[]{:S(2)}) collective-permute-start(bf16[4,32,128]{2,1,0:T(8,128)(2,1)} %get-tuple-element.32), channel_id=1, source_target_pairs={{0,16},{8,24},{16,0},{24,8},{1,17},{9,25},{17,1},{25,9},{2,18},{10... | collective-permute-start | bytes 98312 | tf_op jit(solution)/shard_map/ppermute | solution.py:477
  65.2 2.2 %collective-permute-start.5 = (bf16[4,32,128]{2,1,0:T(8,128)(2,1)}, bf16[4,32,128]{2,1,0:T(8,128)(2,1)S(1)}, u32[]{:S(2)}, u32[]{:S(2)}) collective-permute-start(bf16[4,32,128]{2,1,0:T(8,128)(2,1)} %get-tuple-element.33), channel_id=1, source_target_pairs={{0,24},{8,0},{16,8},{24,16},{1,25},{9,1},{17,9},{25,17},{2,26},{10... | collective-permute-start | bytes 98312 | tf_op jit(solution)/shard_map/ppermute | solution.py:477
  67.3 0.7 copy-start.3
  67.3 0.7 copy-start.14
  67.3 0.7 copy-start.15
  70.2 18.9 %all-to-all-start.3 = ((bf16[8,4,32,128]{3,2,1,0:T(8,128)(2,1)}), bf16[8,4,32,128]{3,2,1,0:T(8,128)(2,1)S(1)}, u32[]{:S(2)}, u32[]{:S(2)}) async-start(bf16[8,4,32,128]{3,2,1,0:T(8,128)(2,1)} %get-tuple-element.36), calls=%async_computation.3 | async-start | bytes 524288 | tf_op jit(solution)/shard_map/all_to_all | solution.py:483
  78.0 3.4 %collective-permute-start.11 = (bf16[4,32,128]{2,1,0:T(8,128)(2,1)}, bf16[4,32,128]{2,1,0:T(8,128)(2,1)S(1)}, u32[]{:S(2)}, u32[]{:S(2)}) collective-permute-start(bf16[4,32,128]{2,1,0:T(8,128)(2,1)} %get-tuple-element.37.refs_0_), channel_id=1, source_target_pairs={{0,24},{8,0},{16,8},{24,16},{1,25},{9,1},{17,9},{25,17},{2,26},{10... | collective-permute-start | bytes 98312 | tf_op jit(solution)/shard_map/ppermute | solution.py:477
  79.4 4.1 %collective-permute-start.10 = (bf16[4,32,128]{2,1,0:T(8,128)(2,1)}, bf16[4,32,128]{2,1,0:T(8,128)(2,1)S(1)}, u32[]{:S(2)}, u32[]{:S(2)}) collective-permute-start(bf16[4,32,128]{2,1,0:T(8,128)(2,1)} %get-tuple-element.37.refs_0_), channel_id=1, source_target_pairs={{0,16},{8,24},{16,0},{24,8},{1,17},{9,25},{17,1},{25,9},{2,18},{10... | collective-permute-start | bytes 98312 | tf_op jit(solution)/shard_map/ppermute | solution.py:477
  80.4 3.6 %collective-permute-start.9 = (bf16[4,32,128]{2,1,0:T(8,128)(2,1)}, bf16[4,32,128]{2,1,0:T(8,128)(2,1)S(1)}, u32[]{:S(2)}, u32[]{:S(2)}) collective-permute-start(bf16[4,32,128]{2,1,0:T(8,128)(2,1)} %get-tuple-element.37.refs_0_), channel_id=1, source_target_pairs={{0,8},{8,16},{16,24},{24,0},{1,9},{9,17},{17,25},{25,1},{2,10},{10... | collective-permute-start | bytes 98312 | tf_op jit(solution)/shard_map/ppermute | solution.py:477
  81.4 2.6 %copy-start.7 = (bf16[4,32,128]{2,1,0:T(8,128)(2,1)}, bf16[4,32,128]{2,1,0:T(8,128)(2,1)S(1)}, u32[]{:S(2)}) copy-start(bf16[4,32,128]{2,1,0:T(8,128)(2,1)S(1)} %collective-permute-done.11.refs_3_) | copy-start | bytes 98308
  89.1 7.0 %copy-start.2 = (bf16[8,4,32,128]{3,2,1,0:T(8,128)(2,1)}, bf16[8,4,32,128]{3,2,1,0:T(8,128)(2,1)S(1)}, u32[]{:S(2)}) copy-start(bf16[8,4,32,128]{3,2,1,0:T(8,128)(2,1)S(1)} %all-to-all-done.3) | copy-start | bytes 786436
  89.1 19.1 %all-to-all-start.4 = ((bf16[8,4,32,128]{3,2,1,0:T(8,128)(2,1)}), bf16[8,4,32,128]{3,2,1,0:T(8,128)(2,1)S(1)}, u32[]{:S(2)}, u32[]{:S(2)}) async-start(bf16[8,4,32,128]{3,2,1,0:T(8,128)(2,1)} %bitcast.8), calls=%async_computation.4 | async-start | bytes 524288 | tf_op jit(solution)/shard_map/all_to_all | solution.py:483
  100.4 4.3 %collective-permute-start.12 = (bf16[7,32,128]{2,1,0:T(8,128)(2,1)}, bf16[7,32,128]{2,1,0:T(8,128)(2,1)S(1)}, u32[]{:S(2)}, u32[]{:S(2)}) collective-permute-start(bf16[7,32,128]{2,1,0:T(8,128)(2,1)} %get-tuple-element.40), channel_id=1, source_target_pairs={{0,8},{8,16},{16,24},{24,0},{1,9},{9,17},{17,25},{25,1},{2,10},{10... | collective-permute-start | bytes 172040 | tf_op jit(solution)/shard_map/ppermute | solution.py:477
  100.5 5.5 %collective-permute-start.13 = (bf16[7,32,128]{2,1,0:T(8,128)(2,1)}, bf16[7,32,128]{2,1,0:T(8,128)(2,1)S(1)}, u32[]{:S(2)}, u32[]{:S(2)}) collective-permute-start(bf16[7,32,128]{2,1,0:T(8,128)(2,1)} %get-tuple-element.41), channel_id=1, source_target_pairs={{0,16},{8,24},{16,0},{24,8},{1,17},{9,25},{17,1},{25,9},{2,18},{10... | collective-permute-start | bytes 172040 | tf_op jit(solution)/shard_map/ppermute | solution.py:477
  103.1 2.9 %collective-permute-start.14 = (bf16[7,32,128]{2,1,0:T(8,128)(2,1)}, bf16[7,32,128]{2,1,0:T(8,128)(2,1)S(1)}, u32[]{:S(2)}, u32[]{:S(2)}) collective-permute-start(bf16[7,32,128]{2,1,0:T(8,128)(2,1)} %get-tuple-element.42), channel_id=1, source_target_pairs={{0,24},{8,0},{16,8},{24,16},{1,25},{9,1},{17,9},{25,17},{2,26},{10... | collective-permute-start | bytes 172040 | tf_op jit(solution)/shard_map/ppermute | solution.py:477
  104.7 1.2 copy-start.4
  106.0 0.6 copy-start.5
  106.0 0.6 copy-start.6
  108.2 15.6 %copy-start = (bf16[8,4,32,128]{3,2,1,0:T(8,128)(2,1)}, bf16[8,4,32,128]{3,2,1,0:T(8,128)(2,1)S(1)}, u32[]{:S(2)}) copy-start(bf16[8,4,32,128]{3,2,1,0:T(8,128)(2,1)S(1)} %all-to-all-done.4.refs_4_) | copy-start | bytes 786436
  (8 other events, 4.8 us)

commit v2 on v1

--- a/solution.py
+++ b/solution.py
@@ -11,7 +11,7 @@
 GROUP = 16
 BATCH = 64
 GRAM_TERMS = 3
-VMEM_LIMIT = 60 * 1024 * 1024
+VMEM_LIMIT = 24 * 1024 * 1024
 
 
 def dot_plain(left, right, **kwargs):
@@ -46,18 +46,17 @@
     return pltpu.make_async_copy(source.at[window], target.at[window], sems.at[index])
 
 
-def build_kernel(row_count, spots_ref, live_ref, index_hbm, value_hbm, block_hbm, *refs):
+def build_kernel(row_count, spots_ref, live_ref, index_hbm, value_hbm, block_ref, *refs):
     row_outs = refs[:row_count]
     (
         col_out_ref,
         index_ref,
         value_ref,
-        block_ref,
+        wide_ref,
         row_ref,
         col_ref,
         index_sems,
         value_sems,
-        block_sems,
     ) = refs[row_count:]
     per_seg = row_outs[0].shape[0]
     col_blocks = col_out_ref.shape[0]
@@ -80,32 +79,32 @@
         group_copy(value_hbm, value_ref, value_sems, index, GROUP).wait()
         targets = [(rows_16 + 16 * part).astype(jnp.int16) for part in range(8)]
         row_sums = []
+        for inside in range(GROUP):
+            slot = index * GROUP + inside
+            active = (slot < live_ref[0, 0]).astype(jnp.float32)
+            value_f32 = value_ref[slot].astype(jnp.float32) * active
+            wide_ref[inside] = value_f32
+            row_sums.append(value_f32[:8] + value_f32[8:])
         col_sums = []
         for inside in range(GROUP):
             slot = index * GROUP + inside
-            active = (slot < live_ref[0, 0]).astype(jnp.float32)
-            index_i32 = index_ref[slot]
-            value_f32 = value_ref[slot].astype(jnp.float32) * active
             sums = [zero] * 8
             for entry in range(16):
-                index_row = jnp.broadcast_to(index_i32[entry : entry + 1], (16, 128)).astype(
-                    jnp.int16
-                )
-                value_row = jnp.broadcast_to(value_f32[entry : entry + 1], (16, 128)).astype(
-                    jnp.bfloat16
-                )
+                index_row = jnp.broadcast_to(
+                    index_ref[slot, entry : entry + 1, :], (16, 128)
+                ).astype(jnp.int16)
+                value_row = jnp.broadcast_to(
+                    wide_ref[inside, entry : entry + 1, :], (16, 128)
+                ).astype(jnp.bfloat16)
                 for part in range(8):
                     sums[part] = sums[part] + jnp.where(
                         index_row == targets[part], value_row, zero
                     )
             block = jnp.concatenate(sums, axis=0)
             block_ref[slot] = block
-            row_sums.append(dot_plain(ones, block))
             col_sums.append(dot_across(ones, block))
-        group_copy(block_ref, block_hbm, block_sems, index, GROUP).start()
         for inside in range(GROUP):
-            slot = index * GROUP + inside
-            row_block, col_block = place_of(spots_ref, slot, col_blocks)
+            row_block, col_block = place_of(spots_ref, index * GROUP + inside, col_blocks)
             row_ref[row_block] += row_sums[inside]
             col_ref[col_block] += col_sums[inside]
         return 0
@@ -114,19 +113,13 @@
     for ahead, out in enumerate(row_outs):
         first = lax.rem(lax.axis_index("row") + ahead, row_count) * per_seg
         for part in range(per_seg):
-            out[part : part + 1] = row_ref[first + part][:1]
+            out[part : part + 1] = jnp.sum(row_ref[first + part], axis=0, keepdims=True)
     for col_block in range(col_blocks):
         col_out_ref[col_block : col_block + 1] = col_ref[col_block][:1]
 
-    def finish_copies(index, _):
-        group_copy(block_ref, block_hbm, block_sems, index, GROUP).wait()
-        return 0
-
-    lax.fori_loop(0, groups, finish_copies, 0)
-
 
 SCALARS = pl.BlockSpec(memory_space=pltpu.SMEM)
-ANYWHERE = pl.BlockSpec(memory_space=pl.ANY)
+IN_HBM = pl.BlockSpec(memory_space=pltpu.HBM)
 IN_VMEM = pl.BlockSpec(memory_space=pltpu.VMEM)
 
 
@@ -136,17 +129,16 @@
     sum_shapes = [(per_seg, 128)] * row_count + [(col_count * per_seg, 128)]
     return pl.pallas_call(
         functools.partial(build_kernel, row_count),
-        in_specs=[SCALARS, SCALARS, ANYWHERE, ANYWHERE],
-        out_specs=[ANYWHERE] + [IN_VMEM] * len(sum_shapes),
+        in_specs=[SCALARS, SCALARS, IN_HBM, IN_HBM],
+        out_specs=[IN_VMEM] * (1 + len(sum_shapes)),
         out_shape=[jax.ShapeDtypeStruct((slots, 128, 128), jnp.bfloat16)]
         + [jax.ShapeDtypeStruct(shape, jnp.float32) for shape in sum_shapes],
         scratch_shapes=[
             pltpu.VMEM(index_table.shape, index_table.dtype),
             pltpu.VMEM(value_table.shape, value_table.dtype),
-            pltpu.VMEM((slots, 128, 128), jnp.bfloat16),
+            pltpu.VMEM((GROUP, 16, 128), jnp.float32),
             pltpu.VMEM((row_count * per_seg, 8, 128), jnp.float32),
             pltpu.VMEM((col_count * per_seg, 8, 128), jnp.float32),
-            pltpu.SemaphoreType.DMA((groups,)),
             pltpu.SemaphoreType.DMA((groups,)),
             pltpu.SemaphoreType.DMA((groups,)),
         ],
@@ -155,22 +147,12 @@
     )(spots, live, index_table, value_table)
 
 
-def each_group(live_ref, block_hbm, block_ref, sems, prepare, run_group):
-    groups = group_count(live_ref, BATCH)
-
-    def start_copy(index, _):
-        group_copy(block_hbm, block_ref, sems, index, BATCH).start()
-        return 0
-
-    lax.fori_loop(0, groups, start_copy, 0)
-    prepare()
-
+def each_group(live_ref, run_group):
     def one_group(index, _):
-        group_copy(block_hbm, block_ref, sems, index, BATCH).wait()
         run_group(index * BATCH)
         return 0
 
-    lax.fori_loop(0, groups, one_group, 0)
+    lax.fori_loop(0, group_count(live_ref, BATCH), one_group, 0)
 
 
 def add_products(dot, places, first_slot, block_ref, dir_ref, total_refs):
@@ -190,15 +172,21 @@
             dir_ref[first + part] = piece[part]
 
 
-def backward_kernel(spots_ref, live_ref, block_hbm, *refs):
-    *row_pieces, col_out_ref, block_ref, row_dir_ref, even_ref, odd_ref, sems = refs
-    per_seg = row_pieces[0].shape[0]
+def add_gram(total, values, high, directions):
+    low = (values - high.astype(jnp.float32)).astype(high.dtype)
+    return total + dot_across(jnp.concatenate([high, low], axis=0), tall(directions))
+
+
+def backward_kernel(row_count, spots_ref, live_ref, block_ref, *refs):
+    row_pieces = refs[:row_count]
+    gram_refs = refs[row_count:-4]
+    col_out_ref, row_dir_ref, even_ref, odd_ref = refs[-4:]
+    per_seg, size, _ = row_pieces[0].shape
     col_blocks = even_ref.shape[0]
-
-    def prepare():
-        even_ref[...] = jnp.zeros_like(even_ref)
-        odd_ref[...] = jnp.zeros_like(odd_ref)
-        fill_directions(row_pieces, row_dir_ref, lax.axis_index("row"), per_seg)
+    col_count, sent = col_out_ref.shape[:2]
+    even_ref[...] = jnp.zeros_like(even_ref)
+    odd_ref[...] = jnp.zeros_like(odd_ref)
+    fill_directions(row_pieces, row_dir_ref, lax.axis_index("row"), per_seg)
 
     def run_group(first_slot):
         add_products(
@@ -210,29 +198,34 @@
             [even_ref, odd_ref],
         )
 
-    each_group(live_ref, block_hbm, block_ref, sems, prepare, run_group)
-    col_out_ref[...] = (even_ref[...] + odd_ref[...]).astype(col_out_ref.dtype)
-
-
-def forward_kernel(row_count, with_gram, spots_ref, live_ref, block_hbm, col_dir_ref, *refs):
-    refs = list(refs)
-
-    def take(count):
-        taken = refs[:count]
-        del refs[:count]
-        return taken
-
-    row_pieces = take(row_count if with_gram else 0)
-    gram_in = take(int(with_gram))
-    row_outs = take(row_count)
-    block_ref, even_ref, odd_ref, sems = refs
-    _, size, _ = row_outs[0].shape
-    per_seg = even_ref.shape[0] // row_count
+    each_group(live_ref, run_group)
+
+    def send_segment(segment, gram):
+        for part in range(per_seg):
+            col_block = segment * per_seg + part
+            values = even_ref[col_block] + odd_ref[col_block]
+            high = values.astype(col_out_ref.dtype)
+            col_out_ref[segment, part] = high
+            if gram_refs:
+                gram = add_gram(gram, values, high, gram_refs[0][col_block])
+        return gram
+
+    gram = lax.fori_loop(0, col_count, send_segment, jnp.zeros((2 * size, 128), jnp.float32))
+    if gram_refs:
+        gram = gram_refs[1][...] + pltpu.roll(gram[:size] + gram[size:], 3 * size, 1)
+        for term in range(GRAM_TERMS):
+            rounded = gram.astype(col_out_ref.dtype)
+            gram = gram - rounded.astype(jnp.float32)
+            for segment in range(col_count):
+                col_out_ref[segment, per_seg + term] = rounded
+
+
+def forward_kernel(spots_ref, live_ref, block_ref, col_dir_ref, *refs):
+    *row_outs, even_ref, odd_ref = refs
+    per_seg = row_outs[0].shape[0]
     col_blocks = col_dir_ref.shape[0]
-
-    def prepare():
-        even_ref[...] = jnp.zeros_like(even_ref)
-        odd_ref[...] = jnp.zeros_like(odd_ref)
+    even_ref[...] = jnp.zeros_like(even_ref)
+    odd_ref[...] = jnp.zeros_like(odd_ref)
 
     def run_group(first_slot):
         add_products(
@@ -244,37 +237,22 @@
             [even_ref, odd_ref],
         )
 
-    each_group(live_ref, block_hbm, block_ref, sems, prepare, run_group)
-    gram = jnp.zeros((2 * size, 128), jnp.float32)
+    each_group(live_ref, run_group)
     for ahead, out in enumerate(row_outs):
-        first = lax.rem(lax.axis_index("row") + ahead, row_count) * per_seg
+        first = lax.rem(lax.axis_index("row") + ahead, len(row_outs)) * per_seg
         for part in range(per_seg):
             values = even_ref[first + part] + odd_ref[first + part]
-            high = values.astype(out.dtype)
-            out[part] = high
-            if with_gram:
-                low = (values - high.astype(jnp.float32)).astype(out.dtype)
-                piece = row_pieces[(row_count - ahead) % row_count]
-                gram += dot_across(jnp.concatenate([high, low], axis=0), tall(piece[part]))
-    if with_gram:
-        gram = gram_in[0][...] + pltpu.roll(gram[:size] + gram[size:], 3 * size, 1)
-        for term in range(GRAM_TERMS):
-            rounded = gram.astype(jnp.bfloat16)
-            gram = gram - rounded.astype(jnp.float32)
-            for out in row_outs:
-                out[per_seg + term] = rounded
+            out[part] = values.astype(out.dtype)
 
 
 def over_blocks(kernel, name, places, blocks, inputs, outputs, scratch):
     slots = blocks.shape[0]
     return pl.pallas_call(
         kernel,
-        in_specs=[SCALARS, SCALARS, ANYWHERE] + [IN_VMEM] * len(inputs),
+        in_specs=[SCALARS, SCALARS] + [IN_VMEM] * (1 + len(inputs)),
         out_specs=[IN_VMEM] * len(outputs),
         out_shape=outputs,
-        scratch_shapes=[pltpu.VMEM(blocks.shape, blocks.dtype)]
-        + scratch
-        + [pltpu.SemaphoreType.DMA((slots // BATCH,))],
+        scratch_shapes=scratch,
         compiler_params=pltpu.CompilerParams(vmem_limit_bytes=VMEM_LIMIT),
         cost_estimate=pl.CostEstimate(
             flops=2 * slots * 32 * 128 * 128, bytes_accessed=2 * blocks.size, transcendentals=0
@@ -283,16 +261,17 @@
     )(*places, blocks, *inputs)
 
 
-def backward_product(places, blocks, row_pieces, col_count):
+def backward_product(places, blocks, row_pieces, col_count, grams=()):
     per_seg, rows, lanes = row_pieces[0].shape
+    sent = per_seg + (GRAM_TERMS if grams else 0)
     col_shape = (col_count * per_seg, rows, lanes)
     (total,) = over_blocks(
-        backward_kernel,
+        functools.partial(backward_kernel, len(row_pieces)),
         "backward_product",
         places,
         blocks,
-        row_pieces,
-        [jax.ShapeDtypeStruct(col_shape, jnp.bfloat16)],
+        [*row_pieces, *grams],
+        [jax.ShapeDtypeStruct((col_count, sent, rows, lanes), jnp.bfloat16)],
         [
             pltpu.VMEM((len(row_pieces) * per_seg, rows, lanes), jnp.bfloat16),
             pltpu.VMEM(col_shape, jnp.float32),
@@ -302,22 +281,15 @@
     return total
 
 
-def forward_product(places, blocks, col_dirs, row_pieces, gram=None):
-    piece = row_pieces[0]
-    inputs = [col_dirs]
-    sent = piece.shape[0]
-    if gram is not None:
-        inputs += [*row_pieces, gram]
-        sent += GRAM_TERMS
-    outputs = [jax.ShapeDtypeStruct((sent,) + piece.shape[1:], jnp.bfloat16)] * len(row_pieces)
-    row_shape = (len(row_pieces) * piece.shape[0],) + piece.shape[1:]
+def forward_product(places, blocks, col_dirs, row_count, piece):
+    row_shape = (row_count * piece[0],) + piece[1:]
     return over_blocks(
-        functools.partial(forward_kernel, len(row_pieces), gram is not None),
+        forward_kernel,
         "forward_product",
         places,
         blocks,
-        inputs,
-        outputs,
+        [col_dirs],
+        [jax.ShapeDtypeStruct(piece, jnp.bfloat16)] * row_count,
         [pltpu.VMEM(row_shape, jnp.float32), pltpu.VMEM(row_shape, jnp.float32)],
     )
 
@@ -426,11 +398,13 @@
 
 
 def close_kernel(*refs):
-    *row_refs, col_ref, gram_ref, scaling_ref, query_ref, first_ref = refs[:-2]
-    solution_ref, residual_ref = refs[-2:]
+    row_count = (len(refs) - 6) // 2
+    row_refs = refs[:row_count]
+    gram_refs = refs[row_count : 2 * row_count]
+    col_ref, scaling_ref, query_ref, first_ref, solution_ref, residual_ref = refs[-6:]
     size = query_ref.shape[0]
     weight = graph_weight
-    total = total_of([ref[...] for ref in leading(gram_ref)])
+    total = total_of([ref[...] for ref in gram_refs])
     g00 = symmetric(window(total, 0))
     g01 = window(total, 1)
     g11 = symmetric(window(total, 2))
@@ -492,14 +466,15 @@
     )(*operands)
 
 
-def sum_kernel(*refs):
-    *piece_refs, copies_ref = refs
-    first = piece_refs[0].shape[0] - GRAM_TERMS
-    total = total_of(
-        [ref[first + term] for term in range(GRAM_TERMS) for ref in piece_refs]
-    )
-    for copy in range(copies_ref.shape[0]):
-        copies_ref[copy] = total
+def sum_kernel(col_ref, total_ref):
+    col_count, sent = col_ref.shape[:2]
+    total_ref[...] = total_of(
+        [
+            col_ref[segment, sent - GRAM_TERMS + term]
+            for term in range(GRAM_TERMS)
+            for segment in range(col_count)
+        ]
+    )
 
 
 def body(queries, block_spots, live_blocks, neighbor_cols, neighbor_sims):
@@ -513,7 +488,6 @@
     narrow = jax.ShapeDtypeStruct(piece, jnp.bfloat16)
     copies = jax.ShapeDtypeStruct((col_count,) + piece, jnp.bfloat16)
     gram_shape = jax.ShapeDtypeStruct((query_rows, 128), jnp.float32)
-    gram_copies = jax.ShapeDtypeStruct((col_count, query_rows, 128), jnp.float32)
 
     blocks, *row_sums, col_sums = build_blocks(
         *places, neighbor_cols[0, 0], neighbor_sims[0, 0], row_count, col_count, per_seg
@@ -529,12 +503,14 @@
         queries,
     )
 
-    def product(vectors, vector_copies, gram=None):
+    def product(vectors, vector_copies, *grams):
         col_dirs = exchange(vector_copies, "col").reshape((col_count * per_seg,) + piece[1:])
         row_pieces = pass_around([vectors] * row_count, "row")
-        total = backward_product(places, blocks, row_pieces, col_count)
-        col_part = exchange(total.reshape((col_count,) + piece), "col")
-        totals = forward_product(places, blocks, col_dirs, row_pieces, gram)
+        if grams:
+            grams = (col_dirs, *grams)
+        total = backward_product(places, blocks, row_pieces, col_count, grams)
+        col_part = exchange(total, "col")
+        totals = forward_product(places, blocks, col_dirs, row_count, piece)
         return pass_around(totals, "row"), col_part
 
     row_parts, col_part = product(scaled, scaled_copies)
@@ -548,7 +524,7 @@
         queries,
     )
     row_parts, col_part = product(scaled, scaled_copies, gram)
-    (grams,) = simple_call(sum_kernel, [gram_copies], "gram_sum", *row_parts)
+    (gram,) = simple_call(sum_kernel, [gram_shape], "gram_sum", col_part)
     flat = jax.ShapeDtypeStruct(queries.shape, jnp.float32)
     return tuple(
         simple_call(
@@ -556,8 +532,8 @@
             [flat, flat],
             "close",
             *row_parts,
+            *pass_around([gram] * row_count, "row"),
             col_part,
-            exchange(grams, "col"),
             scaling,
             queries,
             first,

time: 131 us -> 133 us (1.015); the launches traced: 133 us -> 132 us
  local copies, waits for them, and re-layouts: 3.19 us -> 21.8 us
  blocking collectives: 15.6 us -> 0 us
  waiting for transfers between devices: 14 us -> 26.4 us
  starting transfers between devices: 59.2 us -> 47.3 us
  Pallas kernels: 40 us -> 35.2 us
    unnamed x40 -> x24, local copies, waits for them, and re-layouts: 3.19 us -> 21.8 us
    all_to_all x1 -> x0, blocking collectives: 15.6 us -> none  [exchange(): return lax.all_to_all(pieces, axis, 0, 0, tiled=True)]
    all_to_all x5, waiting for transfers between devices: 2.06 us -> 13.3 us  [exchange(): return lax.all_to_all(pieces, axis, 0, 0, tiled=True)]
    ppermute x15 -> x18, starting transfers between devices: 20.1 us -> 10.7 us  [pass_around(): lax.ppermute(pieces[ahead], axis, [(at, (at + ahead) % count) for at in r...]
    pallas_call x4, Pallas kernels: 15 us -> 10 us  [simple_call(): pl.pallas_call(kernel, out_shape=shapes, compiler_params=pltpu.CompilerPa...]
    pallas_call x1, Pallas kernels: 7.87 us -> 12.3 us  [build_blocks(): pl.pallas_call(functools.partial(build_kernel, row_count), in_specs=[SCAL...]
    pallas_call x4, Pallas kernels: 17.1 us -> 12.9 us  [over_blocks(): pl.pallas_call(kernel, in_specs=[SCALARS, SCALARS] + [IN_VMEM] * (1 + len...]
    all_to_all x5, starting transfers between devices: 39.1 us -> 36.6 us  [exchange(): return lax.all_to_all(pieces, axis, 0, 0, tiled=True)]
  transfers between devices with their start and end apart: 20 -> 23, of which waited for: 13 -> 14; matrix products, arithmetic and copies ran while one was open for 0% -> 0% of each run, Pallas kernels for 14% -> 6%
where the time goes in v2:
time: 133 us; the launch traced here: 132 us
  starting transfers between devices  47.3 us (36%)
  Pallas kernels  35.2 us (26%)
  waiting for transfers between devices  26.4 us (20%)
  local copies, waits for them, and re-layouts  21.8 us (16%)
  between operations  1.44 us (1%)
    all_to_all x5, starting transfers between devices, exchange(): return lax.all_to_all(pieces, axis, 0, 0, tiled=True)  36.6 us
    unnamed x24, local copies, waits for them, and re-layouts  21.8 us
    all_to_all x5, waiting for transfers between devices, exchange(): return lax.all_to_all(pieces, axis, 0, 0, tiled=True)  13.3 us
    ppermute x18, waiting for transfers between devices, pass_around(): lax.ppermute(pieces[ahead], axis, [(at, (at + ahead) % count) for at in r...  13.1 us
    pallas_call x4, Pallas kernels, over_blocks(): pl.pallas_call(kernel, in_specs=[SCALARS, SCALARS] + [IN_VMEM] * (1 + len...  12.9 us
    pallas_call x1, Pallas kernels, build_blocks(): pl.pallas_call(functools.partial(build_kernel, row_count), in_specs=[SCAL...  12.3 us
    ppermute x18, starting transfers between devices, pass_around(): lax.ppermute(pieces[ahead], axis, [(at, (at + ahead) % count) for at in r...  10.7 us
    pallas_call x4, Pallas kernels, simple_call(): pl.pallas_call(kernel, out_shape=shapes, compiler_params=pltpu.CompilerPa...  10 us
  transfers between devices with their start and end apart: 23, of which 14 were waited for; matrix products, arithmetic and copies ran while one was open for 0% of the time, Pallas kernels for 6%

profile of v2, /device:TPU:0, one launch (start us, length us, event | category | flops | bytes accessed | tf_op | source)
XLA Modules:
  0.0 132.1 jit_solution(8607017284422683912)
XLA Ops:
  1.3 1.6 %copy-done.5 = s32[1,1,256,16,128]{4,3,2,1,0:T(8,128)S(1)} copy-done((s32[1,1,256,16,128]{4,3,2,1,0:T(8,128)S(1)}, s32[1,1,256,16,128]{4,3,2,1,0:T(8,128)}, u32[]{:S(2)}) %copy-start.5) | copy-done | bytes 2097176
  2.9 1.2 copy-done.6
  4.8 12.3 %build_blocks.1 = (bf16[256,128,128]{2,1,0:T(8,128)(2,1)S(1)}, f32[4,128]{1,0:T(4,128)S(1)}, f32[4,128]{1,0:T(4,128)S(1)}, f32[4,128]{1,0:T(4,128)S(1)}, f32[4,128]{1,0:T(4,128)S(1)}, /*index=5*/f32[32,128]{1,0:T(8,128)}) custom-call(s32[1,1,256]{2,1,0:T(1,128)S(1)} %copy-done.9, s32[1,1]{1,0:T(1,128)S(6)} %copy.7.live_ref, s32[256,16,128]{2,1,0:T(8,128)S(1)} %bitcast.7, ...), custom_call_target="tpu_custom_call" | custom-call | tf_op jit(solution)/shard_map/build_blocks/pallas_call | solution.py:130
  17.1 3.3 %copy-done = bf16[256,128,128]{2,1,0:T(8,128)(2,1)} copy-done((bf16[256,128,128]{2,1,0:T(8,128)(2,1)}, bf16[256,128,128]{2,1,0:T(8,128)(2,1)S(1)}, u32[]{:S(2)}) %copy-start) | copy-done | bytes 8388632
  20.4 16.1 %all-to-all-start = ((f32[8,4,128]{2,1,0:T(4,128)}), f32[8,4,128]{2,1,0:T(4,128)S(1)}, u32[]{:S(2)}, u32[]{:S(2)}) async-start(f32[8,4,128]{2,1,0:T(4,128)} %bitcast.2), calls=%async_computation | async-start | bytes 32768 | tf_op jit(solution)/shard_map/all_to_all | solution.py:457
  36.5 1.7 %collective-permute-start.2 = (f32[4,128]{1,0:T(4,128)S(1)}, f32[4,128]{1,0:T(4,128)S(1)}, u32[]{:S(2)}, u32[]{:S(2)}) collective-permute-start(f32[4,128]{1,0:T(4,128)S(1)} %get-tuple-element.27), channel_id=1, source_target_pairs={{0,24},{8,0},{16,8},{24,16},{1,25},{9,1},{17,9},{25,17},{2,26},{10... | collective-permute-start | bytes 6152 | tf_op jit(solution)/shard_map/ppermute | solution.py:451
  38.2 1.2 collective-permute-done.refs_1_
  40.1 2.9 %all-to-all-done.refs_4_ = f32[8,4,128]{2,1,0:T(4,128)S(1)} async-done(((f32[8,4,128]{2,1,0:T(4,128)}), f32[8,4,128]{2,1,0:T(4,128)S(1)}, u32[]{:S(2)}, u32[]{:S(2)}) %all-to-all-start) | async-done | bytes 16416 | tf_op jit(solution)/shard_map/all_to_all | solution.py:457
  44.6 3.4 %all-to-all-start.1 = ((bf16[8,4,32,128]{3,2,1,0:T(8,128)(2,1)}), bf16[8,4,32,128]{3,2,1,0:T(8,128)(2,1)S(1)}, u32[]{:S(2)}, u32[]{:S(2)}) async-start(bf16[8,4,32,128]{3,2,1,0:T(8,128)(2,1)} %get-tuple-element.29), calls=%async_computation.1 | async-start | bytes 524288 | tf_op jit(solution)/shard_map/all_to_all | solution.py:457
  48.6 1.7 %collective-permute-start.7 = (bf16[4,32,128]{2,1,0:T(8,128)(2,1)S(1)}, bf16[4,32,128]{2,1,0:T(8,128)(2,1)S(1)}, u32[]{:S(2)}, u32[]{:S(2)}) collective-permute-start(bf16[4,32,128]{2,1,0:T(8,128)(2,1)S(1)} %get-tuple-element.34.refs_0_), channel_id=1, source_target_pairs={{0,16},{8,24},{16,0},{24,8},{1,17},{9,25},{17,1},{25,9},{2,18},{10... | collective-permute-start | bytes 98312 | tf_op jit(solution)/shard_map/ppermute | solution.py:451
  50.3 2.2 %collective-permute-done.7.refs_2_ = bf16[4,32,128]{2,1,0:T(8,128)(2,1)S(1)} collective-permute-done((bf16[4,32,128]{2,1,0:T(8,128)(2,1)S(1)}, bf16[4,32,128]{2,1,0:T(8,128)(2,1)S(1)}, u32[]{:S(2)}, u32[]{:S(2)}) %collective-permute-start.7) | collective-permute-done | bytes 32800 | tf_op jit(solution)/shard_map/ppermute | solution.py:451
  52.5 1.1 collective-permute-done.6.refs_1_
  53.6 3.4 %copy-done.1 = bf16[256,128,128]{2,1,0:T(8,128)(2,1)S(1)} copy-done((bf16[256,128,128]{2,1,0:T(8,128)(2,1)S(1)}, bf16[256,128,128]{2,1,0:T(8,128)(2,1)}, u32[]{:S(2)}) %copy-start.1) | copy-done | bytes 8388632
  57.7 3.9 %backward_product.2 = bf16[8,4,32,128]{3,2,1,0:T(8,128)(2,1)} custom-call(s32[1,1,256]{2,1,0:T(1,128)S(1)} %copy-done.10, s32[1,1]{1,0:T(1,128)S(6)} %copy.7.live_ref, bf16[256,128,128]{2,1,0:T(8,128)(2,1)S(1)} %copy-done.1, bf16[4,32,128]{2,1,0:T(8,128)(2,1)S(1)} %get-tuple-element.34.refs_0_, bf16[4,32,128]{2,1,0:T(8,128)(2,1)S(1)} %collective-permute-done.6.refs_1_, ...), custom_call_target="tpu_custom_call" | custom-call | flops 268435456 | bytes 8388608 | tf_op jit(solution)/shard_map/backward_product/pallas_call | solution.py:250
  61.5 6.3 %all-to-all-start.2 = ((bf16[8,4,32,128]{3,2,1,0:T(8,128)(2,1)}), bf16[8,4,32,128]{3,2,1,0:T(8,128)(2,1)S(1)}, u32[]{:S(2)}, u32[]{:S(2)}) async-start(bf16[8,4,32,128]{3,2,1,0:T(8,128)(2,1)} %backward_product.2), calls=%async_computation.2 | async-start | bytes 524288 | tf_op jit(solution)/shard_map/all_to_all | solution.py:457
  67.9 3.4 %copy-done.2 = bf16[256,128,128]{2,1,0:T(8,128)(2,1)S(1)} copy-done((bf16[256,128,128]{2,1,0:T(8,128)(2,1)S(1)}, bf16[256,128,128]{2,1,0:T(8,128)(2,1)}, u32[]{:S(2)}) %copy-start.2) | copy-done | bytes 8388632
  71.3 2.0 %forward_product.2 = (bf16[4,32,128]{2,1,0:T(8,128)(2,1)S(1)}, bf16[4,32,128]{2,1,0:T(8,128)(2,1)S(1)}, bf16[4,32,128]{2,1,0:T(8,128)(2,1)S(1)}, bf16[4,32,128]{2,1,0:T(8,128)(2,1)S(1)}) custom-call(s32[1,1,256]{2,1,0:T(1,128)S(1)} %copy-done.11, s32[1,1]{1,0:T(1,128)S(6)} %copy.7.live_ref, bf16[256,128,128]{2,1,0:T(8,128)(2,1)S(1)} %copy-done.2, ...), custom_call_target="tpu_custom_call" | custom-call | flops 268435456 | bytes 8388608 | tf_op jit(solution)/shard_map/forward_product/pallas_call | solution.py:250
  73.4 1.7 %collective-permute-start.5 = (bf16[4,32,128]{2,1,0:T(8,128)(2,1)S(1)}, bf16[4,32,128]{2,1,0:T(8,128)(2,1)S(1)}, u32[]{:S(2)}, u32[]{:S(2)}) collective-permute-start(bf16[4,32,128]{2,1,0:T(8,128)(2,1)S(1)} %get-tuple-element.33), channel_id=1, source_target_pairs={{0,24},{8,0},{16,8},{24,16},{1,25},{9,1},{17,9},{25,17},{2,26},{10... | collective-permute-start | bytes 98312 | tf_op jit(solution)/shard_map/ppermute | solution.py:451
  78.1 6.0 %all-to-all-start.3 = ((bf16[8,4,32,128]{3,2,1,0:T(8,128)(2,1)}), bf16[8,4,32,128]{3,2,1,0:T(8,128)(2,1)S(1)}, u32[]{:S(2)}, u32[]{:S(2)}) async-start(bf16[8,4,32,128]{3,2,1,0:T(8,128)(2,1)} %get-tuple-element.36), calls=%async_computation.3 | async-start | bytes 524288 | tf_op jit(solution)/shard_map/all_to_all | solution.py:457
  84.9 1.7 %collective-permute-start.13 = (bf16[4,32,128]{2,1,0:T(8,128)(2,1)S(1)}, bf16[4,32,128]{2,1,0:T(8,128)(2,1)S(1)}, u32[]{:S(2)}, u32[]{:S(2)}) collective-permute-start(bf16[4,32,128]{2,1,0:T(8,128)(2,1)S(1)} %get-tuple-element.41.refs_0_), channel_id=1, source_target_pairs={{0,16},{8,24},{16,0},{24,8},{1,17},{9,25},{17,1},{25,9},{2,18},{10... | collective-permute-start | bytes 98312 | tf_op jit(solution)/shard_map/ppermute | solution.py:451
  86.6 2.2 %collective-permute-done.13.refs_2_ = bf16[4,32,128]{2,1,0:T(8,128)(2,1)S(1)} collective-permute-done((bf16[4,32,128]{2,1,0:T(8,128)(2,1)S(1)}, bf16[4,32,128]{2,1,0:T(8,128)(2,1)S(1)}, u32[]{:S(2)}, u32[]{:S(2)}) %collective-permute-start.13) | collective-permute-done | bytes 32800 | tf_op jit(solution)/shard_map/ppermute | solution.py:451
  88.9 1.1 collective-permute-done.12.refs_1_
  90.0 4.3 %all-to-all-done.3 = bf16[8,4,32,128]{3,2,1,0:T(8,128)(2,1)S(1)} async-done(((bf16[8,4,32,128]{3,2,1,0:T(8,128)(2,1)}), bf16[8,4,32,128]{3,2,1,0:T(8,128)(2,1)S(1)}, u32[]{:S(2)}, u32[]{:S(2)}) %all-to-all-start.3) | async-done | bytes 262176 | tf_op jit(solution)/shard_map/all_to_all | solution.py:457
  94.3 3.4 %copy-done.3 = bf16[256,128,128]{2,1,0:T(8,128)(2,1)S(1)} copy-done((bf16[256,128,128]{2,1,0:T(8,128)(2,1)S(1)}, bf16[256,128,128]{2,1,0:T(8,128)(2,1)}, u32[]{:S(2)}) %copy-start.3) | copy-done | bytes 8388632
  97.7 5.1 %backward_product.3 = bf16[8,7,32,128]{3,2,1,0:T(8,128)(2,1)} custom-call(s32[1,1,256]{2,1,0:T(1,128)S(1)} %copy-done.11, s32[1,1]{1,0:T(1,128)S(6)} %copy.7.live_ref, bf16[256,128,128]{2,1,0:T(8,128)(2,1)S(1)} %copy-done.3, bf16[4,32,128]{2,1,0:T(8,128)(2,1)S(1)} %get-tuple-element.41.refs_0_, bf16[4,32,128]{2,1,0:T(8,128)(2,1)S(1)} %collective-permute-done.12.refs_1_, ...), custom_call_target="tpu_custom_call" | custom-call | flops 268435456 | bytes 8388608 | tf_op jit(solution)/shard_map/backward_product/pallas_call | solution.py:250
  102.8 4.8 %all-to-all-start.4 = ((bf16[8,7,32,128]{3,2,1,0:T(8,128)(2,1)}), bf16[8,7,32,128]{3,2,1,0:T(8,128)(2,1)S(1)}, u32[]{:S(2)}, u32[]{:S(2)}) async-start(bf16[8,7,32,128]{3,2,1,0:T(8,128)(2,1)} %backward_product.3), calls=%async_computation.4 | async-start | bytes 917504 | tf_op jit(solution)/shard_map/all_to_all | solution.py:457
  107.6 3.4 %copy-done.4 = bf16[256,128,128]{2,1,0:T(8,128)(2,1)S(1)} copy-done((bf16[256,128,128]{2,1,0:T(8,128)(2,1)S(1)}, bf16[256,128,128]{2,1,0:T(8,128)(2,1)}, u32[]{:S(2)}) %copy-start.4) | copy-done | bytes 8388632
  111.0 2.0 %forward_product.3 = (bf16[4,32,128]{2,1,0:T(8,128)(2,1)S(1)}, bf16[4,32,128]{2,1,0:T(8,128)(2,1)S(1)}, bf16[4,32,128]{2,1,0:T(8,128)(2,1)S(1)}, bf16[4,32,128]{2,1,0:T(8,128)(2,1)S(1)}) custom-call(s32[1,1,256]{2,1,0:T(1,128)S(1)} %copy-done.11, s32[1,1]{1,0:T(1,128)S(6)} %copy.7.live_ref, bf16[256,128,128]{2,1,0:T(8,128)(2,1)S(1)} %copy-done.4, ...), custom_call_target="tpu_custom_call" | custom-call | flops 268435456 | bytes 8388608 | tf_op jit(solution)/shard_map/forward_product/pallas_call | solution.py:250
  113.1 1.7 %collective-permute-start.11 = (bf16[4,32,128]{2,1,0:T(8,128)(2,1)S(1)}, bf16[4,32,128]{2,1,0:T(8,128)(2,1)S(1)}, u32[]{:S(2)}, u32[]{:S(2)}) collective-permute-start(bf16[4,32,128]{2,1,0:T(8,128)(2,1)S(1)} %get-tuple-element.40), channel_id=1, source_target_pairs={{0,24},{8,0},{16,8},{24,16},{1,25},{9,1},{17,9},{25,17},{2,26},{10... | collective-permute-start | bytes 98312 | tf_op jit(solution)/shard_map/ppermute | solution.py:451
  114.8 5.0 %all-to-all-done.4.col_ref.refs_8_ = bf16[8,7,32,128]{3,2,1,0:T(8,128)(2,1)S(1)} async-done(((bf16[8,7,32,128]{3,2,1,0:T(8,128)(2,1)}), bf16[8,7,32,128]{3,2,1,0:T(8,128)(2,1)S(1)}, u32[]{:S(2)}, u32[]{:S(2)}) %all-to-all-start.4) | async-done | bytes 458784 | tf_op jit(solution)/shard_map/all_to_all | solution.py:457
  121.4 2.4 %collective-permute-done.16.refs_6_ = f32[32,128]{1,0:T(8,128)S(1)} collective-permute-done((f32[32,128]{1,0:T(8,128)S(1)}, f32[32,128]{1,0:T(8,128)S(1)}, u32[]{:S(2)}, u32[]{:S(2)}) %collective-permute-start.16) | collective-permute-done | bytes 16416 | tf_op jit(solution)/shard_map/ppermute | solution.py:451
  123.7 8.4 %close.1 = (f32[32,512]{1,0:T(8,128)}, f32[32,512]{1,0:T(8,128)}) custom-call(bf16[4,32,128]{2,1,0:T(8,128)(2,1)S(1)} %get-tuple-element.37.refs_0_, bf16[4,32,128]{2,1,0:T(8,128)(2,1)S(1)} %collective-permute-done.9.refs_1_, bf16[4,32,128]{2,1,0:T(8,128)(2,1)S(1)} %collective-permute-done.10.refs_2_, ...), custom_call_target="tpu_custom_call" | custom-call | tf_op jit(solution)/shard_map/close/pallas_call | solution.py:461
  (47 shorter events, 9.9 us)
Async XLA Ops:
  0.6 67.2 %copy-start.11 = (s32[1,1,256]{2,1,0:T(1,128)S(1)}, s32[1,1,256]{2,1,0:T(1,128)}, u32[]{:S(2)}) copy-start(s32[1,1,256]{2,1,0:T(1,128)} %spots_ref.9) | copy-start | bytes 3076
  1.3 1.6 %copy-start.5 = (s32[1,1,256,16,128]{4,3,2,1,0:T(8,128)S(1)}, s32[1,1,256,16,128]{4,3,2,1,0:T(8,128)}, u32[]{:S(2)}) copy-start(s32[1,1,256,16,128]{4,3,2,1,0:T(8,128)} %param.8) | copy-start | bytes 6291460
  2.9 1.2 copy-start.6
  17.1 3.3 %copy-start = (bf16[256,128,128]{2,1,0:T(8,128)(2,1)}, bf16[256,128,128]{2,1,0:T(8,128)(2,1)S(1)}, u32[]{:S(2)}) copy-start(bf16[256,128,128]{2,1,0:T(8,128)(2,1)S(1)} %get-tuple-element.23.block_ref) | copy-start | bytes 25165828
  20.4 22.6 %all-to-all-start = ((f32[8,4,128]{2,1,0:T(4,128)}), f32[8,4,128]{2,1,0:T(4,128)S(1)}, u32[]{:S(2)}, u32[]{:S(2)}) async-start(f32[8,4,128]{2,1,0:T(4,128)} %bitcast.2), calls=%async_computation | async-start | bytes 32768 | tf_op jit(solution)/shard_map/all_to_all | solution.py:457
  36.4 3.0 %collective-permute-start = (f32[4,128]{1,0:T(4,128)S(1)}, f32[4,128]{1,0:T(4,128)S(1)}, u32[]{:S(2)}, u32[]{:S(2)}) collective-permute-start(f32[4,128]{1,0:T(4,128)S(1)} %get-tuple-element.25), channel_id=1, source_target_pairs={{0,8},{8,16},{16,24},{24,0},{1,9},{9,17},{17,25},{25,1},{2,10},{10... | collective-permute-start | bytes 6152 | tf_op jit(solution)/shard_map/ppermute | solution.py:451
  36.4 3.7 %collective-permute-start.1 = (f32[4,128]{1,0:T(4,128)S(1)}, f32[4,128]{1,0:T(4,128)S(1)}, u32[]{:S(2)}, u32[]{:S(2)}) collective-permute-start(f32[4,128]{1,0:T(4,128)S(1)} %get-tuple-element.26), channel_id=1, source_target_pairs={{0,16},{8,24},{16,0},{24,8},{1,17},{9,25},{17,1},{25,9},{2,18},{10... | collective-permute-start | bytes 6152 | tf_op jit(solution)/shard_map/ppermute | solution.py:451
  36.5 3.6 %collective-permute-start.2 = (f32[4,128]{1,0:T(4,128)S(1)}, f32[4,128]{1,0:T(4,128)S(1)}, u32[]{:S(2)}, u32[]{:S(2)}) collective-permute-start(f32[4,128]{1,0:T(4,128)S(1)} %get-tuple-element.27), channel_id=1, source_target_pairs={{0,24},{8,0},{16,8},{24,16},{1,25},{9,1},{17,9},{25,17},{2,26},{10... | collective-permute-start | bytes 6152 | tf_op jit(solution)/shard_map/ppermute | solution.py:451
  44.6 16.9 %all-to-all-start.1 = ((bf16[8,4,32,128]{3,2,1,0:T(8,128)(2,1)}), bf16[8,4,32,128]{3,2,1,0:T(8,128)(2,1)S(1)}, u32[]{:S(2)}, u32[]{:S(2)}) async-start(bf16[8,4,32,128]{3,2,1,0:T(8,128)(2,1)} %get-tuple-element.29), calls=%async_computation.1 | async-start | bytes 524288 | tf_op jit(solution)/shard_map/all_to_all | solution.py:457
  48.0 2.2 %collective-permute-start.8 = (bf16[4,32,128]{2,1,0:T(8,128)(2,1)S(1)}, bf16[4,32,128]{2,1,0:T(8,128)(2,1)S(1)}, u32[]{:S(2)}, u32[]{:S(2)}) collective-permute-start(bf16[4,32,128]{2,1,0:T(8,128)(2,1)S(1)} %get-tuple-element.34.refs_0_), channel_id=1, source_target_pairs={{0,24},{8,0},{16,8},{24,16},{1,25},{9,1},{17,9},{25,17},{2,26},{10... | collective-permute-start | bytes 98312 | tf_op jit(solution)/shard_map/ppermute | solution.py:451
  48.6 4.0 %collective-permute-start.7 = (bf16[4,32,128]{2,1,0:T(8,128)(2,1)S(1)}, bf16[4,32,128]{2,1,0:T(8,128)(2,1)S(1)}, u32[]{:S(2)}, u32[]{:S(2)}) collective-permute-start(bf16[4,32,128]{2,1,0:T(8,128)(2,1)S(1)} %get-tuple-element.34.refs_0_), channel_id=1, source_target_pairs={{0,16},{8,24},{16,0},{24,8},{1,17},{9,25},{17,1},{25,9},{2,18},{10... | collective-permute-start | bytes 98312 | tf_op jit(solution)/shard_map/ppermute | solution.py:451
  50.3 3.3 %collective-permute-start.6 = (bf16[4,32,128]{2,1,0:T(8,128)(2,1)S(1)}, bf16[4,32,128]{2,1,0:T(8,128)(2,1)S(1)}, u32[]{:S(2)}, u32[]{:S(2)}) collective-permute-start(bf16[4,32,128]{2,1,0:T(8,128)(2,1)S(1)} %get-tuple-element.34.refs_0_), channel_id=1, source_target_pairs={{0,8},{8,16},{16,24},{24,0},{1,9},{9,17},{17,25},{25,1},{2,10},{10... | collective-permute-start | bytes 98312 | tf_op jit(solution)/shard_map/ppermute | solution.py:451
  53.6 3.4 %copy-start.1 = (bf16[256,128,128]{2,1,0:T(8,128)(2,1)S(1)}, bf16[256,128,128]{2,1,0:T(8,128)(2,1)}, u32[]{:S(2)}) copy-start(bf16[256,128,128]{2,1,0:T(8,128)(2,1)} %copy-done) | copy-start | bytes 25165828
  57.7 19.7 %copy-start.8 = (f32[32,512]{1,0:T(8,128)S(1)}, f32[32,512]{1,0:T(8,128)}, u32[]{:S(2)}) copy-start(f32[32,512]{1,0:T(8,128)} %refs_10_.1) | copy-start | bytes 196612
  61.5 14.6 %all-to-all-start.2 = ((bf16[8,4,32,128]{3,2,1,0:T(8,128)(2,1)}), bf16[8,4,32,128]{3,2,1,0:T(8,128)(2,1)S(1)}, u32[]{:S(2)}, u32[]{:S(2)}) async-start(bf16[8,4,32,128]{3,2,1,0:T(8,128)(2,1)} %backward_product.2), calls=%async_computation.2 | async-start | bytes 524288 | tf_op jit(solution)/shard_map/all_to_all | solution.py:457
  67.9 3.4 %copy-start.2 = (bf16[256,128,128]{2,1,0:T(8,128)(2,1)S(1)}, bf16[256,128,128]{2,1,0:T(8,128)(2,1)}, u32[]{:S(2)}) copy-start(bf16[256,128,128]{2,1,0:T(8,128)(2,1)} %copy-done) | copy-start | bytes 25165828
  73.2 3.4 %collective-permute-start.3 = (bf16[4,32,128]{2,1,0:T(8,128)(2,1)S(1)}, bf16[4,32,128]{2,1,0:T(8,128)(2,1)S(1)}, u32[]{:S(2)}, u32[]{:S(2)}) collective-permute-start(bf16[4,32,128]{2,1,0:T(8,128)(2,1)S(1)} %get-tuple-element.31), channel_id=1, source_target_pairs={{0,8},{8,16},{16,24},{24,0},{1,9},{9,17},{17,25},{25,1},{2,10},{10... | collective-permute-start | bytes 98312 | tf_op jit(solution)/shard_map/ppermute | solution.py:451
  73.3 4.0 %collective-permute-start.4 = (bf16[4,32,128]{2,1,0:T(8,128)(2,1)S(1)}, bf16[4,32,128]{2,1,0:T(8,128)(2,1)S(1)}, u32[]{:S(2)}, u32[]{:S(2)}) collective-permute-start(bf16[4,32,128]{2,1,0:T(8,128)(2,1)S(1)} %get-tuple-element.32), channel_id=1, source_target_pairs={{0,16},{8,24},{16,0},{24,8},{1,17},{9,25},{17,1},{25,9},{2,18},{10... | collective-permute-start | bytes 98312 | tf_op jit(solution)/shard_map/ppermute | solution.py:451
  73.4 4.0 %collective-permute-start.5 = (bf16[4,32,128]{2,1,0:T(8,128)(2,1)S(1)}, bf16[4,32,128]{2,1,0:T(8,128)(2,1)S(1)}, u32[]{:S(2)}, u32[]{:S(2)}) collective-permute-start(bf16[4,32,128]{2,1,0:T(8,128)(2,1)S(1)} %get-tuple-element.33), channel_id=1, source_target_pairs={{0,24},{8,0},{16,8},{24,16},{1,25},{9,1},{17,9},{25,17},{2,26},{10... | collective-permute-start | bytes 98312 | tf_op jit(solution)/shard_map/ppermute | solution.py:451
  78.1 16.2 %all-to-all-start.3 = ((bf16[8,4,32,128]{3,2,1,0:T(8,128)(2,1)}), bf16[8,4,32,128]{3,2,1,0:T(8,128)(2,1)S(1)}, u32[]{:S(2)}, u32[]{:S(2)}) async-start(bf16[8,4,32,128]{3,2,1,0:T(8,128)(2,1)} %get-tuple-element.36), calls=%async_computation.3 | async-start | bytes 524288 | tf_op jit(solution)/shard_map/all_to_all | solution.py:457
  84.1 2.5 %collective-permute-start.14 = (bf16[4,32,128]{2,1,0:T(8,128)(2,1)S(1)}, bf16[4,32,128]{2,1,0:T(8,128)(2,1)S(1)}, u32[]{:S(2)}, u32[]{:S(2)}) collective-permute-start(bf16[4,32,128]{2,1,0:T(8,128)(2,1)S(1)} %get-tuple-element.41.refs_0_), channel_id=1, source_target_pairs={{0,24},{8,0},{16,8},{24,16},{1,25},{9,1},{17,9},{25,17},{2,26},{10... | collective-permute-start | bytes 98312 | tf_op jit(solution)/shard_map/ppermute | solution.py:451
  84.9 3.9 %collective-permute-start.13 = (bf16[4,32,128]{2,1,0:T(8,128)(2,1)S(1)}, bf16[4,32,128]{2,1,0:T(8,128)(2,1)S(1)}, u32[]{:S(2)}, u32[]{:S(2)}) collective-permute-start(bf16[4,32,128]{2,1,0:T(8,128)(2,1)S(1)} %get-tuple-element.41.refs_0_), channel_id=1, source_target_pairs={{0,16},{8,24},{16,0},{24,8},{1,17},{9,25},{17,1},{25,9},{2,18},{10... | collective-permute-start | bytes 98312 | tf_op jit(solution)/shard_map/ppermute | solution.py:451
  86.6 3.3 %collective-permute-start.12 = (bf16[4,32,128]{2,1,0:T(8,128)(2,1)S(1)}, bf16[4,32,128]{2,1,0:T(8,128)(2,1)S(1)}, u32[]{:S(2)}, u32[]{:S(2)}) collective-permute-start(bf16[4,32,128]{2,1,0:T(8,128)(2,1)S(1)} %get-tuple-element.41.refs_0_), channel_id=1, source_target_pairs={{0,8},{8,16},{16,24},{24,0},{1,9},{9,17},{17,25},{25,1},{2,10},{10... | collective-permute-start | bytes 98312 | tf_op jit(solution)/shard_map/ppermute | solution.py:451
  94.3 3.4 %copy-start.3 = (bf16[256,128,128]{2,1,0:T(8,128)(2,1)S(1)}, bf16[256,128,128]{2,1,0:T(8,128)(2,1)}, u32[]{:S(2)}) copy-start(bf16[256,128,128]{2,1,0:T(8,128)(2,1)} %copy-done) | copy-start | bytes 25165828
  102.8 17.0 %all-to-all-start.4 = ((bf16[8,7,32,128]{3,2,1,0:T(8,128)(2,1)}), bf16[8,7,32,128]{3,2,1,0:T(8,128)(2,1)S(1)}, u32[]{:S(2)}, u32[]{:S(2)}) async-start(bf16[8,7,32,128]{3,2,1,0:T(8,128)(2,1)} %backward_product.3), calls=%async_computation.4 | async-start | bytes 917504 | tf_op jit(solution)/shard_map/all_to_all | solution.py:457
  107.6 3.4 %copy-start.4 = (bf16[256,128,128]{2,1,0:T(8,128)(2,1)S(1)}, bf16[256,128,128]{2,1,0:T(8,128)(2,1)}, u32[]{:S(2)}) copy-start(bf16[256,128,128]{2,1,0:T(8,128)(2,1)} %copy-done) | copy-start | bytes 25165828
  113.0 7.3 %collective-permute-start.9 = (bf16[4,32,128]{2,1,0:T(8,128)(2,1)S(1)}, bf16[4,32,128]{2,1,0:T(8,128)(2,1)S(1)}, u32[]{:S(2)}, u32[]{:S(2)}) collective-permute-start(bf16[4,32,128]{2,1,0:T(8,128)(2,1)S(1)} %get-tuple-element.38), channel_id=1, source_target_pairs={{0,8},{8,16},{16,24},{24,0},{1,9},{9,17},{17,25},{25,1},{2,10},{10... | collective-permute-start | bytes 98312 | tf_op jit(solution)/shard_map/ppermute | solution.py:451
  113.0 7.4 %collective-permute-start.10 = (bf16[4,32,128]{2,1,0:T(8,128)(2,1)S(1)}, bf16[4,32,128]{2,1,0:T(8,128)(2,1)S(1)}, u32[]{:S(2)}, u32[]{:S(2)}) collective-permute-start(bf16[4,32,128]{2,1,0:T(8,128)(2,1)S(1)} %get-tuple-element.39), channel_id=1, source_target_pairs={{0,16},{8,24},{16,0},{24,8},{1,17},{9,25},{17,1},{25,9},{2,18},{10... | collective-permute-start | bytes 98312 | tf_op jit(solution)/shard_map/ppermute | solution.py:451
  113.1 7.3 %collective-permute-start.11 = (bf16[4,32,128]{2,1,0:T(8,128)(2,1)S(1)}, bf16[4,32,128]{2,1,0:T(8,128)(2,1)S(1)}, u32[]{:S(2)}, u32[]{:S(2)}) collective-permute-start(bf16[4,32,128]{2,1,0:T(8,128)(2,1)S(1)} %get-tuple-element.40), channel_id=1, source_target_pairs={{0,24},{8,0},{16,8},{24,16},{1,25},{9,1},{17,9},{25,17},{2,26},{10... | collective-permute-start | bytes 98312 | tf_op jit(solution)/shard_map/ppermute | solution.py:451
  119.9 1.5 %collective-permute-start.17 = (f32[32,128]{1,0:T(8,128)S(1)}, f32[32,128]{1,0:T(8,128)S(1)}, u32[]{:S(2)}, u32[]{:S(2)}) collective-permute-start(f32[32,128]{1,0:T(8,128)S(1)} %gram_sum.1.refs_4_), channel_id=1, source_target_pairs={{0,24},{8,0},{16,8},{24,16},{1,25},{9,1},{17,9},{25,17},{2,26},{10... | collective-permute-start | bytes 49160 | tf_op jit(solution)/shard_map/ppermute | solution.py:451
  119.9 3.8 %collective-permute-start.16 = (f32[32,128]{1,0:T(8,128)S(1)}, f32[32,128]{1,0:T(8,128)S(1)}, u32[]{:S(2)}, u32[]{:S(2)}) collective-permute-start(f32[32,128]{1,0:T(8,128)S(1)} %gram_sum.1.refs_4_), channel_id=1, source_target_pairs={{0,16},{8,24},{16,0},{24,8},{1,17},{9,25},{17,1},{25,9},{2,18},{10... | collective-permute-start | bytes 49160 | tf_op jit(solution)/shard_map/ppermute | solution.py:451
  120.2 3.5 %collective-permute-start.15 = (f32[32,128]{1,0:T(8,128)S(1)}, f32[32,128]{1,0:T(8,128)S(1)}, u32[]{:S(2)}, u32[]{:S(2)}) collective-permute-start(f32[32,128]{1,0:T(8,128)S(1)} %gram_sum.1.refs_4_), channel_id=1, source_target_pairs={{0,8},{8,16},{16,24},{24,0},{1,9},{9,17},{17,25},{25,1},{2,10},{10... | collective-permute-start | bytes 49160 | tf_op jit(solution)/shard_map/ppermute | solution.py:451
  (3 other events, 2.2 us)

commit v3 on v2

--- a/solution.py
+++ b/solution.py
@@ -9,9 +9,11 @@
 
 graph_weight = 0.95
 GROUP = 16
-BATCH = 64
+BATCH = 32
+AHEAD = 3
 GRAM_TERMS = 3
-VMEM_LIMIT = 24 * 1024 * 1024
+LARGE_GRANT = 60 * 1024 * 1024
+SMALL_GRANT = 24 * 1024 * 1024
 
 
 def dot_plain(left, right, **kwargs):
@@ -46,17 +48,18 @@
     return pltpu.make_async_copy(source.at[window], target.at[window], sems.at[index])
 
 
-def build_kernel(row_count, spots_ref, live_ref, index_hbm, value_hbm, block_ref, *refs):
+def build_kernel(row_count, spots_ref, live_ref, index_hbm, value_hbm, block_hbm, *refs):
     row_outs = refs[:row_count]
     (
         col_out_ref,
         index_ref,
         value_ref,
-        wide_ref,
+        block_ref,
         row_ref,
         col_ref,
         index_sems,
         value_sems,
+        block_sems,
     ) = refs[row_count:]
     per_seg = row_outs[0].shape[0]
     col_blocks = col_out_ref.shape[0]
@@ -71,42 +74,36 @@
     row_ref[...] = jnp.zeros_like(row_ref)
     col_ref[...] = jnp.zeros_like(col_ref)
     rows_16 = lax.broadcasted_iota(jnp.int32, (16, 128), 0)
-    ones = jnp.ones((8, 128), jnp.bfloat16)
+    ones = jnp.ones((128, 128), jnp.bfloat16)
     zero = jnp.zeros((16, 128), jnp.bfloat16)
 
     def build_group(index, _):
         group_copy(index_hbm, index_ref, index_sems, index, GROUP).wait()
         group_copy(value_hbm, value_ref, value_sems, index, GROUP).wait()
         targets = [(rows_16 + 16 * part).astype(jnp.int16) for part in range(8)]
-        row_sums = []
         for inside in range(GROUP):
             slot = index * GROUP + inside
+            row_block, col_block = place_of(spots_ref, slot, col_blocks)
             active = (slot < live_ref[0, 0]).astype(jnp.float32)
+            index_i32 = index_ref[slot]
             value_f32 = value_ref[slot].astype(jnp.float32) * active
-            wide_ref[inside] = value_f32
-            row_sums.append(value_f32[:8] + value_f32[8:])
-        col_sums = []
-        for inside in range(GROUP):
-            slot = index * GROUP + inside
             sums = [zero] * 8
             for entry in range(16):
-                index_row = jnp.broadcast_to(
-                    index_ref[slot, entry : entry + 1, :], (16, 128)
-                ).astype(jnp.int16)
-                value_row = jnp.broadcast_to(
-                    wide_ref[inside, entry : entry + 1, :], (16, 128)
-                ).astype(jnp.bfloat16)
+                index_row = jnp.broadcast_to(index_i32[entry : entry + 1], (16, 128)).astype(
+                    jnp.int16
+                )
+                value_row = jnp.broadcast_to(value_f32[entry : entry + 1], (16, 128)).astype(
+                    jnp.bfloat16
+                )
                 for part in range(8):
                     sums[part] = sums[part] + jnp.where(
                         index_row == targets[part], value_row, zero
                     )
             block = jnp.concatenate(sums, axis=0)
             block_ref[slot] = block
-            col_sums.append(dot_across(ones, block))
-        for inside in range(GROUP):
-            row_block, col_block = place_of(spots_ref, index * GROUP + inside, col_blocks)
-            row_ref[row_block] += row_sums[inside]
-            col_ref[col_block] += col_sums[inside]
+            row_ref[row_block] += value_f32[:8] + value_f32[8:]
+            col_ref[col_block] += dot_plain(block, ones)
+        group_copy(block_ref, block_hbm, block_sems, index, GROUP).start()
         return 0
 
     lax.fori_loop(0, groups, build_group, 0)
@@ -114,12 +111,23 @@
         first = lax.rem(lax.axis_index("row") + ahead, row_count) * per_seg
         for part in range(per_seg):
             out[part : part + 1] = jnp.sum(row_ref[first + part], axis=0, keepdims=True)
+    diagonal = lax.broadcasted_iota(jnp.int32, (128, 128), 0) == lax.broadcasted_iota(
+        jnp.int32, (128, 128), 1
+    )
     for col_block in range(col_blocks):
-        col_out_ref[col_block : col_block + 1] = col_ref[col_block][:1]
+        col_out_ref[col_block : col_block + 1] = jnp.sum(
+            jnp.where(diagonal, col_ref[col_block], 0.0), axis=0, keepdims=True
+        )
+
+    def finish_copies(index, _):
+        group_copy(block_ref, block_hbm, block_sems, index, GROUP).wait()
+        return 0
+
+    lax.fori_loop(0, groups, finish_copies, 0)
 
 
 SCALARS = pl.BlockSpec(memory_space=pltpu.SMEM)
-IN_HBM = pl.BlockSpec(memory_space=pltpu.HBM)
+ANYWHERE = pl.BlockSpec(memory_space=pl.ANY)
 IN_VMEM = pl.BlockSpec(memory_space=pltpu.VMEM)
 
 
@@ -129,30 +137,44 @@
     sum_shapes = [(per_seg, 128)] * row_count + [(col_count * per_seg, 128)]
     return pl.pallas_call(
         functools.partial(build_kernel, row_count),
-        in_specs=[SCALARS, SCALARS, IN_HBM, IN_HBM],
-        out_specs=[IN_VMEM] * (1 + len(sum_shapes)),
+        in_specs=[SCALARS, SCALARS, ANYWHERE, ANYWHERE],
+        out_specs=[ANYWHERE] + [IN_VMEM] * len(sum_shapes),
         out_shape=[jax.ShapeDtypeStruct((slots, 128, 128), jnp.bfloat16)]
         + [jax.ShapeDtypeStruct(shape, jnp.float32) for shape in sum_shapes],
         scratch_shapes=[
             pltpu.VMEM(index_table.shape, index_table.dtype),
             pltpu.VMEM(value_table.shape, value_table.dtype),
-            pltpu.VMEM((GROUP, 16, 128), jnp.float32),
+            pltpu.VMEM((slots, 128, 128), jnp.bfloat16),
             pltpu.VMEM((row_count * per_seg, 8, 128), jnp.float32),
-            pltpu.VMEM((col_count * per_seg, 8, 128), jnp.float32),
+            pltpu.VMEM((col_count * per_seg, 128, 128), jnp.float32),
+            pltpu.SemaphoreType.DMA((groups,)),
             pltpu.SemaphoreType.DMA((groups,)),
             pltpu.SemaphoreType.DMA((groups,)),
         ],
-        compiler_params=pltpu.CompilerParams(vmem_limit_bytes=VMEM_LIMIT),
+        compiler_params=pltpu.CompilerParams(vmem_limit_bytes=LARGE_GRANT),
         name="build_blocks",
     )(spots, live, index_table, value_table)
 
 
-def each_group(live_ref, run_group):
+def each_group(live_ref, block_hbm, block_ref, sems, prepare, run_group):
+    groups = group_count(live_ref, BATCH)
+
+    def start_copy(index):
+        @pl.when(index < groups)
+        def _():
+            group_copy(block_hbm, block_ref, sems, index, BATCH).start()
+
+    for index in range(min(AHEAD, block_ref.shape[0] // BATCH)):
+        start_copy(index)
+    prepare()
+
     def one_group(index, _):
+        group_copy(block_hbm, block_ref, sems, index, BATCH).wait()
+        start_copy(index + AHEAD)
         run_group(index * BATCH)
         return 0
 
-    lax.fori_loop(0, group_count(live_ref, BATCH), one_group, 0)
+    lax.fori_loop(0, groups, one_group, 0)
 
 
 def add_products(dot, places, first_slot, block_ref, dir_ref, total_refs):
@@ -177,16 +199,18 @@
     return total + dot_across(jnp.concatenate([high, low], axis=0), tall(directions))
 
 
-def backward_kernel(row_count, spots_ref, live_ref, block_ref, *refs):
+def backward_kernel(row_count, spots_ref, live_ref, block_hbm, *refs):
     row_pieces = refs[:row_count]
-    gram_refs = refs[row_count:-4]
-    col_out_ref, row_dir_ref, even_ref, odd_ref = refs[-4:]
+    gram_refs = refs[row_count:-6]
+    col_out_ref, block_ref, sems, row_dir_ref, even_ref, odd_ref = refs[-6:]
     per_seg, size, _ = row_pieces[0].shape
     col_blocks = even_ref.shape[0]
     col_count, sent = col_out_ref.shape[:2]
-    even_ref[...] = jnp.zeros_like(even_ref)
-    odd_ref[...] = jnp.zeros_like(odd_ref)
-    fill_directions(row_pieces, row_dir_ref, lax.axis_index("row"), per_seg)
+
+    def prepare():
+        even_ref[...] = jnp.zeros_like(even_ref)
+        odd_ref[...] = jnp.zeros_like(odd_ref)
+        fill_directions(row_pieces, row_dir_ref, lax.axis_index("row"), per_seg)
 
     def run_group(first_slot):
         add_products(
@@ -198,7 +222,7 @@
             [even_ref, odd_ref],
         )
 
-    each_group(live_ref, run_group)
+    each_group(live_ref, block_hbm, block_ref, sems, prepare, run_group)
 
     def send_segment(segment, gram):
         for part in range(per_seg):
@@ -220,12 +244,14 @@
                 col_out_ref[segment, per_seg + term] = rounded
 
 
-def forward_kernel(spots_ref, live_ref, block_ref, col_dir_ref, *refs):
-    *row_outs, even_ref, odd_ref = refs
+def forward_kernel(spots_ref, live_ref, block_hbm, col_dir_ref, *refs):
+    *row_outs, block_ref, sems, even_ref, odd_ref = refs
     per_seg = row_outs[0].shape[0]
     col_blocks = col_dir_ref.shape[0]
-    even_ref[...] = jnp.zeros_like(even_ref)
-    odd_ref[...] = jnp.zeros_like(odd_ref)
+
+    def prepare():
+        even_ref[...] = jnp.zeros_like(even_ref)
+        odd_ref[...] = jnp.zeros_like(odd_ref)
 
     def run_group(first_slot):
         add_products(
@@ -237,7 +263,7 @@
             [even_ref, odd_ref],
         )
 
-    each_group(live_ref, run_group)
+    each_group(live_ref, block_hbm, block_ref, sems, prepare, run_group)
     for ahead, out in enumerate(row_outs):
         first = lax.rem(lax.axis_index("row") + ahead, len(row_outs)) * per_seg
         for part in range(per_seg):
@@ -249,11 +275,15 @@
     slots = blocks.shape[0]
     return pl.pallas_call(
         kernel,
-        in_specs=[SCALARS, SCALARS] + [IN_VMEM] * (1 + len(inputs)),
+        in_specs=[SCALARS, SCALARS, ANYWHERE] + [IN_VMEM] * len(inputs),
         out_specs=[IN_VMEM] * len(outputs),
         out_shape=outputs,
-        scratch_shapes=scratch,
-        compiler_params=pltpu.CompilerParams(vmem_limit_bytes=VMEM_LIMIT),
+        scratch_shapes=[
+            pltpu.VMEM(blocks.shape, blocks.dtype),
+            pltpu.SemaphoreType.DMA((slots // BATCH,)),
+        ]
+        + scratch,
+        compiler_params=pltpu.CompilerParams(vmem_limit_bytes=LARGE_GRANT),
         cost_estimate=pl.CostEstimate(
             flops=2 * slots * 32 * 128 * 128, bytes_accessed=2 * blocks.size, transcendentals=0
         ),
@@ -461,7 +491,7 @@
     return pl.pallas_call(
         kernel,
         out_shape=shapes,
-        compiler_params=pltpu.CompilerParams(vmem_limit_bytes=VMEM_LIMIT),
+        compiler_params=pltpu.CompilerParams(vmem_limit_bytes=SMALL_GRANT),
         name=name,
     )(*operands)
 

time: 133 us -> 122 us (0.917); the launches traced: 132 us -> 120 us
  local copies, waits for them, and re-layouts: 21.8 us -> 4.96 us
  Pallas kernels: 35.2 us -> 39.7 us
  waiting for transfers between devices: 26.4 us -> 24.6 us
  starting transfers between devices: 47.3 us -> 48.9 us
    unnamed x24 -> x32, local copies, waits for them, and re-layouts: 21.8 us -> 4.96 us
    ppermute x18, starting transfers between devices: 10.7 us -> 19.8 us  [pass_around(): lax.ppermute(pieces[ahead], axis, [(at, (at + ahead) % count) for at in r...]
    all_to_all x5, starting transfers between devices: 36.6 us -> 29.1 us  [exchange(): return lax.all_to_all(pieces, axis, 0, 0, tiled=True)]
    pallas_call x4, Pallas kernels: 12.9 us -> 19.6 us  [over_blocks(): pl.pallas_call(kernel, in_specs=[SCALARS, SCALARS, ANYWHERE] + [IN_VMEM]...]
    pallas_call x1, Pallas kernels: 12.3 us -> 10.1 us  [build_blocks(): pl.pallas_call(functools.partial(build_kernel, row_count), in_specs=[SCAL...]
  transfers between devices with their start and end apart: 23 -> 23, of which waited for: 14 -> 12; matrix products, arithmetic and copies ran while one was open for 0% -> 0% of each run, Pallas kernels for 6% -> 11%
where the time goes in v3:
time: 122 us; the launch traced here: 120 us
  starting transfers between devices  48.9 us (40%)
  Pallas kernels  39.7 us (33%)
  waiting for transfers between devices  24.6 us (20%)
  local copies, waits for them, and re-layouts  4.96 us (4%)
  between operations  1.43 us (1%)
    all_to_all x5, starting transfers between devices, exchange(): return lax.all_to_all(pieces, axis, 0, 0, tiled=True)  29.1 us
    ppermute x18, starting transfers between devices, pass_around(): lax.ppermute(pieces[ahead], axis, [(at, (at + ahead) % count) for at in r...  19.8 us
    pallas_call x4, Pallas kernels, over_blocks(): pl.pallas_call(kernel, in_specs=[SCALARS, SCALARS, ANYWHERE] + [IN_VMEM]...  19.6 us
    ppermute x18, waiting for transfers between devices, pass_around(): lax.ppermute(pieces[ahead], axis, [(at, (at + ahead) % count) for at in r...  12.4 us
    all_to_all x5, waiting for transfers between devices, exchange(): return lax.all_to_all(pieces, axis, 0, 0, tiled=True)  12.2 us
    pallas_call x1, Pallas kernels, build_blocks(): pl.pallas_call(functools.partial(build_kernel, row_count), in_specs=[SCAL...  10.1 us
    pallas_call x4, Pallas kernels, simple_call(): pl.pallas_call(kernel, out_shape=shapes, compiler_params=pltpu.CompilerPa...  10 us
    unnamed x32, local copies, waits for them, and re-layouts  4.96 us
  transfers between devices with their start and end apart: 23, of which 12 were waited for; matrix products, arithmetic and copies ran while one was open for 0% of the time, Pallas kernels for 11%

profile of v3, /device:TPU:0, one launch (start us, length us, event | category | flops | bytes accessed | tf_op | source)
XLA Modules:
  0.0 119.6 jit_solution(6301003009626904658)
XLA Ops:
  1.3 10.1 %build_blocks.1 = (bf16[256,128,128]{2,1,0:T(8,128)(2,1)}, f32[4,128]{1,0:T(4,128)}, f32[4,128]{1,0:T(4,128)}, f32[4,128]{1,0:T(4,128)}, f32[4,128]{1,0:T(4,128)}, /*index=5*/f32[32,128]{1,0:T(8,128)}) custom-call(s32[1,1,256]{2,1,0:T(1,128)} %spots_ref.9, s32[1,1]{1,0:T(1,128)S(6)} %copy.7.live_ref, s32[256,16,128]{2,1,0:T(8,128)} %bitcast.7, ...), custom_call_target="tpu_custom_call" | custom-call | tf_op jit(solution)/shard_map/build_blocks/pallas_call | solution.py:138
  11.3 8.6 %all-to-all-start = ((f32[8,4,128]{2,1,0:T(4,128)}), f32[8,4,128]{2,1,0:T(4,128)S(1)}, u32[]{:S(2)}, u32[]{:S(2)}) async-start(f32[8,4,128]{2,1,0:T(4,128)} %bitcast.10), calls=%async_computation | async-start | bytes 32768 | tf_op jit(solution)/shard_map/all_to_all | solution.py:487
  19.9 6.5 %collective-permute-start = (f32[4,128]{1,0:T(4,128)}, f32[4,128]{1,0:T(4,128)S(1)}, u32[]{:S(2)}, u32[]{:S(2)}) collective-permute-start(f32[4,128]{1,0:T(4,128)} %get-tuple-element.25), channel_id=1, source_target_pairs={{0,8},{8,16},{16,24},{24,0},{1,9},{9,17},{17,25},{25,1},{2,10},{10... | collective-permute-start | bytes 6152 | tf_op jit(solution)/shard_map/ppermute | solution.py:481
  26.4 1.4 %collective-permute-start.2 = (f32[4,128]{1,0:T(4,128)}, f32[4,128]{1,0:T(4,128)S(1)}, u32[]{:S(2)}, u32[]{:S(2)}) collective-permute-start(f32[4,128]{1,0:T(4,128)} %get-tuple-element.27), channel_id=1, source_target_pairs={{0,24},{8,0},{16,8},{24,16},{1,25},{9,1},{17,9},{25,17},{2,26},{10... | collective-permute-start | bytes 6152 | tf_op jit(solution)/shard_map/ppermute | solution.py:481
  27.9 2.4 %collective-permute-done.1.refs_2_ = f32[4,128]{1,0:T(4,128)S(1)} collective-permute-done((f32[4,128]{1,0:T(4,128)}, f32[4,128]{1,0:T(4,128)S(1)}, u32[]{:S(2)}, u32[]{:S(2)}) %collective-permute-start.1) | collective-permute-done | bytes 2080 | tf_op jit(solution)/shard_map/ppermute | solution.py:481
  30.2 0.8 copy-done
  31.8 0.8 start.1
  32.5 5.7 %all-to-all-start.1 = ((bf16[8,4,32,128]{3,2,1,0:T(8,128)(2,1)}), bf16[8,4,32,128]{3,2,1,0:T(8,128)(2,1)S(1)}, u32[]{:S(2)}, u32[]{:S(2)}) async-start(bf16[8,4,32,128]{3,2,1,0:T(8,128)(2,1)} %get-tuple-element.29), calls=%async_computation.1 | async-start | bytes 524288 | tf_op jit(solution)/shard_map/all_to_all | solution.py:487
  38.7 1.0 collective-permute-start.7
  40.3 2.3 %collective-permute-done.7.refs_2_ = bf16[4,32,128]{2,1,0:T(8,128)(2,1)S(1)} collective-permute-done((bf16[4,32,128]{2,1,0:T(8,128)(2,1)S(1)}, bf16[4,32,128]{2,1,0:T(8,128)(2,1)S(1)}, u32[]{:S(2)}, u32[]{:S(2)}) %collective-permute-start.7) | collective-permute-done | bytes 32800 | tf_op jit(solution)/shard_map/ppermute | solution.py:481
  43.7 5.0 %backward_product.2 = bf16[8,4,32,128]{3,2,1,0:T(8,128)(2,1)} custom-call(s32[1,1,256]{2,1,0:T(1,128)} %spots_ref.9, s32[1,1]{1,0:T(1,128)S(6)} %copy.7.live_ref, bf16[256,128,128]{2,1,0:T(8,128)(2,1)} %get-tuple-element.23.block_hbm, bf16[4,32,128]{2,1,0:T(8,128)(2,1)} %copy-done.3, bf16[4,32,128]{2,1,0:T(8,128)(2,1)} %copy-done.15, ...), custom_call_target="tpu_custom_call" | custom-call | flops 268435456 | bytes 8388608 | tf_op jit(solution)/shard_map/backward_product/pallas_call | solution.py:276
  48.6 5.5 %all-to-all-start.2 = ((bf16[8,4,32,128]{3,2,1,0:T(8,128)(2,1)}), bf16[8,4,32,128]{3,2,1,0:T(8,128)(2,1)S(1)}, u32[]{:S(2)}, u32[]{:S(2)}) async-start(bf16[8,4,32,128]{3,2,1,0:T(8,128)(2,1)} %backward_product.2), calls=%async_computation.2 | async-start | bytes 524288 | tf_op jit(solution)/shard_map/all_to_all | solution.py:487
  54.1 4.1 %forward_product.2 = (bf16[4,32,128]{2,1,0:T(8,128)(2,1)}, bf16[4,32,128]{2,1,0:T(8,128)(2,1)}, bf16[4,32,128]{2,1,0:T(8,128)(2,1)}, bf16[4,32,128]{2,1,0:T(8,128)(2,1)}) custom-call(s32[1,1,256]{2,1,0:T(1,128)} %spots_ref.9, s32[1,1]{1,0:T(1,128)S(6)} %copy.7.live_ref, bf16[256,128,128]{2,1,0:T(8,128)(2,1)} %get-tuple-element.23.block_hbm, ...), custom_call_target="tpu_custom_call" | custom-call | flops 268435456 | bytes 8388608 | tf_op jit(solution)/shard_map/forward_product/pallas_call | solution.py:276
  58.3 1.4 %collective-permute-start.4 = (bf16[4,32,128]{2,1,0:T(8,128)(2,1)}, bf16[4,32,128]{2,1,0:T(8,128)(2,1)S(1)}, u32[]{:S(2)}, u32[]{:S(2)}) collective-permute-start(bf16[4,32,128]{2,1,0:T(8,128)(2,1)} %get-tuple-element.32), channel_id=1, source_target_pairs={{0,16},{8,24},{16,0},{24,8},{1,17},{9,25},{17,1},{25,9},{2,18},{10... | collective-permute-start | bytes 98312 | tf_op jit(solution)/shard_map/ppermute | solution.py:481
  59.7 1.4 %collective-permute-start.5 = (bf16[4,32,128]{2,1,0:T(8,128)(2,1)}, bf16[4,32,128]{2,1,0:T(8,128)(2,1)S(1)}, u32[]{:S(2)}, u32[]{:S(2)}) collective-permute-start(bf16[4,32,128]{2,1,0:T(8,128)(2,1)} %get-tuple-element.33), channel_id=1, source_target_pairs={{0,24},{8,0},{16,8},{24,16},{1,25},{9,1},{17,9},{25,17},{2,26},{10... | collective-permute-start | bytes 98312 | tf_op jit(solution)/shard_map/ppermute | solution.py:481
  61.1 2.1 %all-to-all-done.2.refs_4_ = bf16[8,4,32,128]{3,2,1,0:T(8,128)(2,1)S(1)} async-done(((bf16[8,4,32,128]{3,2,1,0:T(8,128)(2,1)}), bf16[8,4,32,128]{3,2,1,0:T(8,128)(2,1)S(1)}, u32[]{:S(2)}, u32[]{:S(2)}) %all-to-all-start.2) | async-done | bytes 262176 | tf_op jit(solution)/shard_map/all_to_all | solution.py:487
  63.9 0.8 middle.1
  65.4 5.8 %all-to-all-start.3 = ((bf16[8,4,32,128]{3,2,1,0:T(8,128)(2,1)}), bf16[8,4,32,128]{3,2,1,0:T(8,128)(2,1)S(1)}, u32[]{:S(2)}, u32[]{:S(2)}) async-start(bf16[8,4,32,128]{3,2,1,0:T(8,128)(2,1)} %get-tuple-element.36), calls=%async_computation.3 | async-start | bytes 524288 | tf_op jit(solution)/shard_map/all_to_all | solution.py:487
  71.2 1.4 %collective-permute-start.14 = (bf16[4,32,128]{2,1,0:T(8,128)(2,1)S(1)}, bf16[4,32,128]{2,1,0:T(8,128)(2,1)S(1)}, u32[]{:S(2)}, u32[]{:S(2)}) collective-permute-start(bf16[4,32,128]{2,1,0:T(8,128)(2,1)S(1)} %get-tuple-element.41.refs_0_), channel_id=1, source_target_pairs={{0,24},{8,0},{16,8},{24,16},{1,25},{9,1},{17,9},{25,17},{2,26},{10... | collective-permute-start | bytes 98312 | tf_op jit(solution)/shard_map/ppermute | solution.py:481
  73.0 1.2 collective-permute-done.14.refs_3_
  74.1 2.5 %collective-permute-done.13.refs_2_ = bf16[4,32,128]{2,1,0:T(8,128)(2,1)S(1)} collective-permute-done((bf16[4,32,128]{2,1,0:T(8,128)(2,1)S(1)}, bf16[4,32,128]{2,1,0:T(8,128)(2,1)S(1)}, u32[]{:S(2)}, u32[]{:S(2)}) %collective-permute-start.13) | collective-permute-done | bytes 32800 | tf_op jit(solution)/shard_map/ppermute | solution.py:481
  76.7 4.0 %all-to-all-done.3 = bf16[8,4,32,128]{3,2,1,0:T(8,128)(2,1)S(1)} async-done(((bf16[8,4,32,128]{3,2,1,0:T(8,128)(2,1)}), bf16[8,4,32,128]{3,2,1,0:T(8,128)(2,1)S(1)}, u32[]{:S(2)}, u32[]{:S(2)}) %all-to-all-start.3) | async-done | bytes 262176 | tf_op jit(solution)/shard_map/all_to_all | solution.py:487
  81.4 6.4 %backward_product.3 = bf16[8,7,32,128]{3,2,1,0:T(8,128)(2,1)} custom-call(s32[1,1,256]{2,1,0:T(1,128)} %spots_ref.9, s32[1,1]{1,0:T(1,128)S(6)} %copy.7.live_ref, bf16[256,128,128]{2,1,0:T(8,128)(2,1)} %get-tuple-element.23.block_hbm, bf16[4,32,128]{2,1,0:T(8,128)(2,1)} %copy-done.2, bf16[4,32,128]{2,1,0:T(8,128)(2,1)} %copy-done.13, ...), custom_call_target="tpu_custom_call" | custom-call | flops 268435456 | bytes 8388608 | tf_op jit(solution)/shard_map/backward_product/pallas_call | solution.py:276
  87.9 3.5 %all-to-all-start.4 = ((bf16[8,7,32,128]{3,2,1,0:T(8,128)(2,1)}), bf16[8,7,32,128]{3,2,1,0:T(8,128)(2,1)S(1)}, u32[]{:S(2)}, u32[]{:S(2)}) async-start(bf16[8,7,32,128]{3,2,1,0:T(8,128)(2,1)} %backward_product.3), calls=%async_computation.4 | async-start | bytes 917504 | tf_op jit(solution)/shard_map/all_to_all | solution.py:487
  91.3 4.1 %forward_product.3 = (bf16[4,32,128]{2,1,0:T(8,128)(2,1)}, bf16[4,32,128]{2,1,0:T(8,128)(2,1)}, bf16[4,32,128]{2,1,0:T(8,128)(2,1)}, bf16[4,32,128]{2,1,0:T(8,128)(2,1)}) custom-call(s32[1,1,256]{2,1,0:T(1,128)} %spots_ref.9, s32[1,1]{1,0:T(1,128)S(6)} %copy.7.live_ref, bf16[256,128,128]{2,1,0:T(8,128)(2,1)} %get-tuple-element.23.block_hbm, ...), custom_call_target="tpu_custom_call" | custom-call | flops 268435456 | bytes 8388608 | tf_op jit(solution)/shard_map/forward_product/pallas_call | solution.py:276
  95.5 2.2 %collective-permute-start.10 = (bf16[4,32,128]{2,1,0:T(8,128)(2,1)}, bf16[4,32,128]{2,1,0:T(8,128)(2,1)S(1)}, u32[]{:S(2)}, u32[]{:S(2)}) collective-permute-start(bf16[4,32,128]{2,1,0:T(8,128)(2,1)} %get-tuple-element.39), channel_id=1, source_target_pairs={{0,16},{8,24},{16,0},{24,8},{1,17},{9,25},{17,1},{25,9},{2,18},{10... | collective-permute-start | bytes 98312 | tf_op jit(solution)/shard_map/ppermute | solution.py:481
  97.7 1.0 collective-permute-start.11
  98.7 6.1 %all-to-all-done.4.col_ref.refs_8_ = bf16[8,7,32,128]{3,2,1,0:T(8,128)(2,1)S(1)} async-done(((bf16[8,7,32,128]{3,2,1,0:T(8,128)(2,1)}), bf16[8,7,32,128]{3,2,1,0:T(8,128)(2,1)S(1)}, u32[]{:S(2)}, u32[]{:S(2)}) %all-to-all-start.4) | async-done | bytes 458784 | tf_op jit(solution)/shard_map/all_to_all | solution.py:487
  104.8 1.7 %collective-permute-start.17 = (f32[32,128]{1,0:T(8,128)S(1)}, f32[32,128]{1,0:T(8,128)S(1)}, u32[]{:S(2)}, u32[]{:S(2)}) collective-permute-start(f32[32,128]{1,0:T(8,128)S(1)} %gram_sum.1.refs_4_), channel_id=1, source_target_pairs={{0,24},{8,0},{16,8},{24,16},{1,25},{9,1},{17,9},{25,17},{2,26},{10... | collective-permute-start | bytes 49160 | tf_op jit(solution)/shard_map/ppermute | solution.py:481
  106.5 0.8 collective-permute-start.16
  107.9 2.3 %collective-permute-done.16.refs_6_ = f32[32,128]{1,0:T(8,128)S(1)} collective-permute-done((f32[32,128]{1,0:T(8,128)S(1)}, f32[32,128]{1,0:T(8,128)S(1)}, u32[]{:S(2)}, u32[]{:S(2)}) %collective-permute-start.16) | collective-permute-done | bytes 16416 | tf_op jit(solution)/shard_map/ppermute | solution.py:481
  111.2 8.4 %close.1 = (f32[32,512]{1,0:T(8,128)}, f32[32,512]{1,0:T(8,128)}) custom-call(bf16[4,32,128]{2,1,0:T(8,128)(2,1)S(1)} %copy-done.5, bf16[4,32,128]{2,1,0:T(8,128)(2,1)S(1)} %collective-permute-done.9.refs_1_, bf16[4,32,128]{2,1,0:T(8,128)(2,1)S(1)} %collective-permute-done.10.refs_2_, bf16[4,32,128]{2,1,0:T(8,128)(2,1)S(1)} %collective-permute-done.11.refs_3_, ...), custom_call_target="tpu_custom_call" | custom-call | tf_op jit(solution)/shard_map/close/pallas_call | solution.py:491
  (55 shorter events, 7.1 us)
Async XLA Ops:
  11.3 18.9 %all-to-all-start = ((f32[8,4,128]{2,1,0:T(4,128)}), f32[8,4,128]{2,1,0:T(4,128)S(1)}, u32[]{:S(2)}, u32[]{:S(2)}) async-start(f32[8,4,128]{2,1,0:T(4,128)} %bitcast.10), calls=%async_computation | async-start | bytes 32768 | tf_op jit(solution)/shard_map/all_to_all | solution.py:487
  19.9 7.9 %collective-permute-start = (f32[4,128]{1,0:T(4,128)}, f32[4,128]{1,0:T(4,128)S(1)}, u32[]{:S(2)}, u32[]{:S(2)}) collective-permute-start(f32[4,128]{1,0:T(4,128)} %get-tuple-element.25), channel_id=1, source_target_pairs={{0,8},{8,16},{16,24},{24,0},{1,9},{9,17},{17,25},{25,1},{2,10},{10... | collective-permute-start | bytes 6152 | tf_op jit(solution)/shard_map/ppermute | solution.py:481
  26.4 3.8 %collective-permute-start.1 = (f32[4,128]{1,0:T(4,128)}, f32[4,128]{1,0:T(4,128)S(1)}, u32[]{:S(2)}, u32[]{:S(2)}) collective-permute-start(f32[4,128]{1,0:T(4,128)} %get-tuple-element.26), channel_id=1, source_target_pairs={{0,16},{8,24},{16,0},{24,8},{1,17},{9,25},{17,1},{25,9},{2,18},{10... | collective-permute-start | bytes 6152 | tf_op jit(solution)/shard_map/ppermute | solution.py:481
  26.4 3.8 %collective-permute-start.2 = (f32[4,128]{1,0:T(4,128)}, f32[4,128]{1,0:T(4,128)S(1)}, u32[]{:S(2)}, u32[]{:S(2)}) collective-permute-start(f32[4,128]{1,0:T(4,128)} %get-tuple-element.27), channel_id=1, source_target_pairs={{0,24},{8,0},{16,8},{24,16},{1,25},{9,1},{17,9},{25,17},{2,26},{10... | collective-permute-start | bytes 6152 | tf_op jit(solution)/shard_map/ppermute | solution.py:481
  30.2 0.8 copy-start
  32.5 10.5 %copy-start.3 = (bf16[4,32,128]{2,1,0:T(8,128)(2,1)}, bf16[4,32,128]{2,1,0:T(8,128)(2,1)S(1)}, u32[]{:S(2)}) copy-start(bf16[4,32,128]{2,1,0:T(8,128)(2,1)S(1)} %get-tuple-element.34.refs_0_) | copy-start | bytes 98308
  32.5 16.1 %all-to-all-start.1 = ((bf16[8,4,32,128]{3,2,1,0:T(8,128)(2,1)}), bf16[8,4,32,128]{3,2,1,0:T(8,128)(2,1)S(1)}, u32[]{:S(2)}, u32[]{:S(2)}) async-start(bf16[8,4,32,128]{3,2,1,0:T(8,128)(2,1)} %get-tuple-element.29), calls=%async_computation.1 | async-start | bytes 524288 | tf_op jit(solution)/shard_map/all_to_all | solution.py:487
  38.2 2.1 %collective-permute-start.8 = (bf16[4,32,128]{2,1,0:T(8,128)(2,1)S(1)}, bf16[4,32,128]{2,1,0:T(8,128)(2,1)S(1)}, u32[]{:S(2)}, u32[]{:S(2)}) collective-permute-start(bf16[4,32,128]{2,1,0:T(8,128)(2,1)S(1)} %get-tuple-element.34.refs_0_), channel_id=1, source_target_pairs={{0,24},{8,0},{16,8},{24,16},{1,25},{9,1},{17,9},{25,17},{2,26},{10... | collective-permute-start | bytes 98312 | tf_op jit(solution)/shard_map/ppermute | solution.py:481
  38.7 3.9 %collective-permute-start.7 = (bf16[4,32,128]{2,1,0:T(8,128)(2,1)S(1)}, bf16[4,32,128]{2,1,0:T(8,128)(2,1)S(1)}, u32[]{:S(2)}, u32[]{:S(2)}) collective-permute-start(bf16[4,32,128]{2,1,0:T(8,128)(2,1)S(1)} %get-tuple-element.34.refs_0_), channel_id=1, source_target_pairs={{0,16},{8,24},{16,0},{24,8},{1,17},{9,25},{17,1},{25,9},{2,18},{10... | collective-permute-start | bytes 98312 | tf_op jit(solution)/shard_map/ppermute | solution.py:481
  39.7 3.3 %collective-permute-start.6 = (bf16[4,32,128]{2,1,0:T(8,128)(2,1)S(1)}, bf16[4,32,128]{2,1,0:T(8,128)(2,1)S(1)}, u32[]{:S(2)}, u32[]{:S(2)}) collective-permute-start(bf16[4,32,128]{2,1,0:T(8,128)(2,1)S(1)} %get-tuple-element.34.refs_0_), channel_id=1, source_target_pairs={{0,8},{8,16},{16,24},{24,0},{1,9},{9,17},{17,25},{25,1},{2,10},{10... | collective-permute-start | bytes 98312 | tf_op jit(solution)/shard_map/ppermute | solution.py:481
  40.3 2.7 %copy-start.12 = (bf16[4,32,128]{2,1,0:T(8,128)(2,1)}, bf16[4,32,128]{2,1,0:T(8,128)(2,1)S(1)}, u32[]{:S(2)}) copy-start(bf16[4,32,128]{2,1,0:T(8,128)(2,1)S(1)} %collective-permute-done.8.refs_3_) | copy-start | bytes 98308
  43.7 19.5 %copy-start.1 = (f32[32,512]{1,0:T(8,128)S(1)}, f32[32,512]{1,0:T(8,128)}, u32[]{:S(2)}) copy-start(f32[32,512]{1,0:T(8,128)} %refs_10_.1) | copy-start | bytes 196612
  48.6 5.5 %copy-start.9 = (bf16[8,4,32,128]{3,2,1,0:T(8,128)(2,1)}, bf16[8,4,32,128]{3,2,1,0:T(8,128)(2,1)S(1)}, u32[]{:S(2)}) copy-start(bf16[8,4,32,128]{3,2,1,0:T(8,128)(2,1)S(1)} %all-to-all-done.1) | copy-start | bytes 786436
  48.6 14.5 %all-to-all-start.2 = ((bf16[8,4,32,128]{3,2,1,0:T(8,128)(2,1)}), bf16[8,4,32,128]{3,2,1,0:T(8,128)(2,1)S(1)}, u32[]{:S(2)}, u32[]{:S(2)}) async-start(bf16[8,4,32,128]{3,2,1,0:T(8,128)(2,1)} %backward_product.2), calls=%async_computation.2 | async-start | bytes 524288 | tf_op jit(solution)/shard_map/all_to_all | solution.py:487
  58.3 4.9 %collective-permute-start.3 = (bf16[4,32,128]{2,1,0:T(8,128)(2,1)}, bf16[4,32,128]{2,1,0:T(8,128)(2,1)S(1)}, u32[]{:S(2)}, u32[]{:S(2)}) collective-permute-start(bf16[4,32,128]{2,1,0:T(8,128)(2,1)} %get-tuple-element.31), channel_id=1, source_target_pairs={{0,8},{8,16},{16,24},{24,0},{1,9},{9,17},{17,25},{25,1},{2,10},{10... | collective-permute-start | bytes 98312 | tf_op jit(solution)/shard_map/ppermute | solution.py:481
  58.3 4.8 %collective-permute-start.4 = (bf16[4,32,128]{2,1,0:T(8,128)(2,1)}, bf16[4,32,128]{2,1,0:T(8,128)(2,1)S(1)}, u32[]{:S(2)}, u32[]{:S(2)}) collective-permute-start(bf16[4,32,128]{2,1,0:T(8,128)(2,1)} %get-tuple-element.32), channel_id=1, source_target_pairs={{0,16},{8,24},{16,0},{24,8},{1,17},{9,25},{17,1},{25,9},{2,18},{10... | collective-permute-start | bytes 98312 | tf_op jit(solution)/shard_map/ppermute | solution.py:481
  59.7 3.5 %collective-permute-start.5 = (bf16[4,32,128]{2,1,0:T(8,128)(2,1)}, bf16[4,32,128]{2,1,0:T(8,128)(2,1)S(1)}, u32[]{:S(2)}, u32[]{:S(2)}) collective-permute-start(bf16[4,32,128]{2,1,0:T(8,128)(2,1)} %get-tuple-element.33), channel_id=1, source_target_pairs={{0,24},{8,0},{16,8},{24,16},{1,25},{9,1},{17,9},{25,17},{2,26},{10... | collective-permute-start | bytes 98312 | tf_op jit(solution)/shard_map/ppermute | solution.py:481
  65.3 15.3 %copy-start.2 = (bf16[4,32,128]{2,1,0:T(8,128)(2,1)}, bf16[4,32,128]{2,1,0:T(8,128)(2,1)S(1)}, u32[]{:S(2)}) copy-start(bf16[4,32,128]{2,1,0:T(8,128)(2,1)S(1)} %get-tuple-element.41.refs_0_) | copy-start | bytes 98308
  65.4 15.3 %all-to-all-start.3 = ((bf16[8,4,32,128]{3,2,1,0:T(8,128)(2,1)}), bf16[8,4,32,128]{3,2,1,0:T(8,128)(2,1)S(1)}, u32[]{:S(2)}, u32[]{:S(2)}) async-start(bf16[8,4,32,128]{3,2,1,0:T(8,128)(2,1)} %get-tuple-element.36), calls=%async_computation.3 | async-start | bytes 524288 | tf_op jit(solution)/shard_map/all_to_all | solution.py:487
  71.2 3.0 %collective-permute-start.14 = (bf16[4,32,128]{2,1,0:T(8,128)(2,1)S(1)}, bf16[4,32,128]{2,1,0:T(8,128)(2,1)S(1)}, u32[]{:S(2)}, u32[]{:S(2)}) collective-permute-start(bf16[4,32,128]{2,1,0:T(8,128)(2,1)S(1)} %get-tuple-element.41.refs_0_), channel_id=1, source_target_pairs={{0,24},{8,0},{16,8},{24,16},{1,25},{9,1},{17,9},{25,17},{2,26},{10... | collective-permute-start | bytes 98312 | tf_op jit(solution)/shard_map/ppermute | solution.py:481
  72.5 4.1 %collective-permute-start.13 = (bf16[4,32,128]{2,1,0:T(8,128)(2,1)S(1)}, bf16[4,32,128]{2,1,0:T(8,128)(2,1)S(1)}, u32[]{:S(2)}, u32[]{:S(2)}) collective-permute-start(bf16[4,32,128]{2,1,0:T(8,128)(2,1)S(1)} %get-tuple-element.41.refs_0_), channel_id=1, source_target_pairs={{0,16},{8,24},{16,0},{24,8},{1,17},{9,25},{17,1},{25,9},{2,18},{10... | collective-permute-start | bytes 98312 | tf_op jit(solution)/shard_map/ppermute | solution.py:481
  73.0 3.7 %collective-permute-start.12 = (bf16[4,32,128]{2,1,0:T(8,128)(2,1)S(1)}, bf16[4,32,128]{2,1,0:T(8,128)(2,1)S(1)}, u32[]{:S(2)}, u32[]{:S(2)}) collective-permute-start(bf16[4,32,128]{2,1,0:T(8,128)(2,1)S(1)} %get-tuple-element.41.refs_0_), channel_id=1, source_target_pairs={{0,8},{8,16},{16,24},{24,0},{1,9},{9,17},{17,25},{25,1},{2,10},{10... | collective-permute-start | bytes 98312 | tf_op jit(solution)/shard_map/ppermute | solution.py:481
  74.1 6.6 %copy-start.10 = (bf16[4,32,128]{2,1,0:T(8,128)(2,1)}, bf16[4,32,128]{2,1,0:T(8,128)(2,1)S(1)}, u32[]{:S(2)}) copy-start(bf16[4,32,128]{2,1,0:T(8,128)(2,1)S(1)} %collective-permute-done.14.refs_3_) | copy-start | bytes 98308
  76.6 4.0 %copy-start.11 = (bf16[4,32,128]{2,1,0:T(8,128)(2,1)}, bf16[4,32,128]{2,1,0:T(8,128)(2,1)S(1)}, u32[]{:S(2)}) copy-start(bf16[4,32,128]{2,1,0:T(8,128)(2,1)S(1)} %collective-permute-done.13.refs_2_) | copy-start | bytes 98308
  76.6 4.1 %copy-start.13 = (bf16[4,32,128]{2,1,0:T(8,128)(2,1)}, bf16[4,32,128]{2,1,0:T(8,128)(2,1)S(1)}, u32[]{:S(2)}) copy-start(bf16[4,32,128]{2,1,0:T(8,128)(2,1)S(1)} %collective-permute-done.12.refs_1_) | copy-start | bytes 98308
  87.9 16.9 %all-to-all-start.4 = ((bf16[8,7,32,128]{3,2,1,0:T(8,128)(2,1)}), bf16[8,7,32,128]{3,2,1,0:T(8,128)(2,1)S(1)}, u32[]{:S(2)}, u32[]{:S(2)}) async-start(bf16[8,7,32,128]{3,2,1,0:T(8,128)(2,1)} %backward_product.3), calls=%async_computation.4 | async-start | bytes 917504 | tf_op jit(solution)/shard_map/all_to_all | solution.py:487
  95.5 11.8 %collective-permute-start.9 = (bf16[4,32,128]{2,1,0:T(8,128)(2,1)}, bf16[4,32,128]{2,1,0:T(8,128)(2,1)S(1)}, u32[]{:S(2)}, u32[]{:S(2)}) collective-permute-start(bf16[4,32,128]{2,1,0:T(8,128)(2,1)} %get-tuple-element.38), channel_id=1, source_target_pairs={{0,8},{8,16},{16,24},{24,0},{1,9},{9,17},{17,25},{25,1},{2,10},{10... | collective-permute-start | bytes 98312 | tf_op jit(solution)/shard_map/ppermute | solution.py:481
  95.5 11.9 %collective-permute-start.10 = (bf16[4,32,128]{2,1,0:T(8,128)(2,1)}, bf16[4,32,128]{2,1,0:T(8,128)(2,1)S(1)}, u32[]{:S(2)}, u32[]{:S(2)}) collective-permute-start(bf16[4,32,128]{2,1,0:T(8,128)(2,1)} %get-tuple-element.39), channel_id=1, source_target_pairs={{0,16},{8,24},{16,0},{24,8},{1,17},{9,25},{17,1},{25,9},{2,18},{10... | collective-permute-start | bytes 98312 | tf_op jit(solution)/shard_map/ppermute | solution.py:481
  97.7 9.7 %collective-permute-start.11 = (bf16[4,32,128]{2,1,0:T(8,128)(2,1)}, bf16[4,32,128]{2,1,0:T(8,128)(2,1)S(1)}, u32[]{:S(2)}, u32[]{:S(2)}) collective-permute-start(bf16[4,32,128]{2,1,0:T(8,128)(2,1)} %get-tuple-element.40), channel_id=1, source_target_pairs={{0,24},{8,0},{16,8},{24,16},{1,25},{9,1},{17,9},{25,17},{2,26},{10... | collective-permute-start | bytes 98312 | tf_op jit(solution)/shard_map/ppermute | solution.py:481
  104.8 3.1 %collective-permute-start.17 = (f32[32,128]{1,0:T(8,128)S(1)}, f32[32,128]{1,0:T(8,128)S(1)}, u32[]{:S(2)}, u32[]{:S(2)}) collective-permute-start(f32[32,128]{1,0:T(8,128)S(1)} %gram_sum.1.refs_4_), channel_id=1, source_target_pairs={{0,24},{8,0},{16,8},{24,16},{1,25},{9,1},{17,9},{25,17},{2,26},{10... | collective-permute-start | bytes 49160 | tf_op jit(solution)/shard_map/ppermute | solution.py:481
  106.5 3.7 %collective-permute-start.16 = (f32[32,128]{1,0:T(8,128)S(1)}, f32[32,128]{1,0:T(8,128)S(1)}, u32[]{:S(2)}, u32[]{:S(2)}) collective-permute-start(f32[32,128]{1,0:T(8,128)S(1)} %gram_sum.1.refs_4_), channel_id=1, source_target_pairs={{0,16},{8,24},{16,0},{24,8},{1,17},{9,25},{17,1},{25,9},{2,18},{10... | collective-permute-start | bytes 49160 | tf_op jit(solution)/shard_map/ppermute | solution.py:481
  107.2 3.2 %collective-permute-start.15 = (f32[32,128]{1,0:T(8,128)S(1)}, f32[32,128]{1,0:T(8,128)S(1)}, u32[]{:S(2)}, u32[]{:S(2)}) collective-permute-start(f32[32,128]{1,0:T(8,128)S(1)} %gram_sum.1.refs_4_), channel_id=1, source_target_pairs={{0,8},{8,16},{16,24},{24,0},{1,9},{9,17},{17,25},{25,1},{2,10},{10... | collective-permute-start | bytes 49160 | tf_op jit(solution)/shard_map/ppermute | solution.py:481
  (7 other events, 4.7 us)

commit v4 on v3

--- a/solution.py
+++ b/solution.py
@@ -10,9 +10,9 @@
 graph_weight = 0.95
 GROUP = 16
 BATCH = 32
-AHEAD = 3
 GRAM_TERMS = 3
-LARGE_GRANT = 60 * 1024 * 1024
+BUILD_GRANT = 60 * 1024 * 1024
+PRODUCT_GRANT = 57 * 1024 * 1024
 SMALL_GRANT = 24 * 1024 * 1024
 
 
@@ -76,29 +76,33 @@
     rows_16 = lax.broadcasted_iota(jnp.int32, (16, 128), 0)
     ones = jnp.ones((128, 128), jnp.bfloat16)
     zero = jnp.zeros((16, 128), jnp.bfloat16)
+    one = jnp.ones((16, 128), jnp.bfloat16)
 
     def build_group(index, _):
         group_copy(index_hbm, index_ref, index_sems, index, GROUP).wait()
         group_copy(value_hbm, value_ref, value_sems, index, GROUP).wait()
-        targets = [(rows_16 + 16 * part).astype(jnp.int16) for part in range(8)]
+        targets = [(rows_16 + 16 * half).astype(jnp.int16) for half in range(2)]
         for inside in range(GROUP):
             slot = index * GROUP + inside
             row_block, col_block = place_of(spots_ref, slot, col_blocks)
             active = (slot < live_ref[0, 0]).astype(jnp.float32)
             index_i32 = index_ref[slot]
             value_f32 = value_ref[slot].astype(jnp.float32) * active
+            quarter = index_i32 >> 5
+            within = index_i32 & 31
+            quarter_values = [jnp.where(quarter == part, value_f32, 0.0) for part in range(4)]
             sums = [zero] * 8
             for entry in range(16):
-                index_row = jnp.broadcast_to(index_i32[entry : entry + 1], (16, 128)).astype(
-                    jnp.int16
-                )
-                value_row = jnp.broadcast_to(value_f32[entry : entry + 1], (16, 128)).astype(
-                    jnp.bfloat16
-                )
-                for part in range(8):
-                    sums[part] = sums[part] + jnp.where(
-                        index_row == targets[part], value_row, zero
+                row = slice(entry, entry + 1)
+                within_row = jnp.broadcast_to(within[row], (16, 128)).astype(jnp.int16)
+                hits = [jnp.where(within_row == target, one, zero) for target in targets]
+                for part in range(4):
+                    value_row = jnp.broadcast_to(quarter_values[part][row], (16, 128)).astype(
+                        jnp.bfloat16
                     )
+                    for half in range(2):
+                        place = 2 * part + half
+                        sums[place] = sums[place] + hits[half] * value_row
             block = jnp.concatenate(sums, axis=0)
             block_ref[slot] = block
             row_ref[row_block] += value_f32[:8] + value_f32[8:]
@@ -151,7 +155,7 @@
             pltpu.SemaphoreType.DMA((groups,)),
             pltpu.SemaphoreType.DMA((groups,)),
         ],
-        compiler_params=pltpu.CompilerParams(vmem_limit_bytes=LARGE_GRANT),
+        compiler_params=pltpu.CompilerParams(vmem_limit_bytes=BUILD_GRANT),
         name="build_blocks",
     )(spots, live, index_table, value_table)
 
@@ -159,18 +163,15 @@
 def each_group(live_ref, block_hbm, block_ref, sems, prepare, run_group):
     groups = group_count(live_ref, BATCH)
 
-    def start_copy(index):
-        @pl.when(index < groups)
-        def _():
-            group_copy(block_hbm, block_ref, sems, index, BATCH).start()
-
-    for index in range(min(AHEAD, block_ref.shape[0] // BATCH)):
-        start_copy(index)
+    def start_copy(index, _):
+        group_copy(block_hbm, block_ref, sems, index, BATCH).start()
+        return 0
+
+    lax.fori_loop(0, groups, start_copy, 0)
     prepare()
 
     def one_group(index, _):
         group_copy(block_hbm, block_ref, sems, index, BATCH).wait()
-        start_copy(index + AHEAD)
         run_group(index * BATCH)
         return 0
 
@@ -194,18 +195,11 @@
             dir_ref[first + part] = piece[part]
 
 
-def add_gram(total, values, high, directions):
-    low = (values - high.astype(jnp.float32)).astype(high.dtype)
-    return total + dot_across(jnp.concatenate([high, low], axis=0), tall(directions))
-
-
 def backward_kernel(row_count, spots_ref, live_ref, block_hbm, *refs):
     row_pieces = refs[:row_count]
-    gram_refs = refs[row_count:-6]
-    col_out_ref, block_ref, sems, row_dir_ref, even_ref, odd_ref = refs[-6:]
-    per_seg, size, _ = row_pieces[0].shape
+    col_out_ref, block_ref, sems, row_dir_ref, even_ref, odd_ref = refs[row_count:]
+    per_seg = row_pieces[0].shape[0]
     col_blocks = even_ref.shape[0]
-    col_count, sent = col_out_ref.shape[:2]
 
     def prepare():
         even_ref[...] = jnp.zeros_like(even_ref)
@@ -223,25 +217,32 @@
         )
 
     each_group(live_ref, block_hbm, block_ref, sems, prepare, run_group)
-
-    def send_segment(segment, gram):
+    for segment in range(col_out_ref.shape[0]):
         for part in range(per_seg):
             col_block = segment * per_seg + part
             values = even_ref[col_block] + odd_ref[col_block]
-            high = values.astype(col_out_ref.dtype)
-            col_out_ref[segment, part] = high
-            if gram_refs:
-                gram = add_gram(gram, values, high, gram_refs[0][col_block])
+            col_out_ref[segment, part] = values.astype(col_out_ref.dtype)
+
+
+def attach_kernel(col_dir_ref, gram_ref, total_ref, message_ref):
+    col_count, sent, size, _ = message_ref.shape
+    per_seg = sent - GRAM_TERMS
+    def add_segment(segment, gram):
+        for part in range(per_seg):
+            values = total_ref[segment, part]
+            message_ref[segment, part] = values
+            gram += dot_across(values, tall(col_dir_ref[segment * per_seg + part]))
         return gram
 
-    gram = lax.fori_loop(0, col_count, send_segment, jnp.zeros((2 * size, 128), jnp.float32))
-    if gram_refs:
-        gram = gram_refs[1][...] + pltpu.roll(gram[:size] + gram[size:], 3 * size, 1)
-        for term in range(GRAM_TERMS):
-            rounded = gram.astype(col_out_ref.dtype)
-            gram = gram - rounded.astype(jnp.float32)
-            for segment in range(col_count):
-                col_out_ref[segment, per_seg + term] = rounded
+    gram = lax.fori_loop(
+        0, col_count, add_segment, jnp.zeros((size, 128), jnp.float32), unroll=4
+    )
+    gram = gram_ref[...] + pltpu.roll(gram, 3 * size, 1)
+    for term in range(GRAM_TERMS):
+        rounded = gram.astype(message_ref.dtype)
+        gram = gram - rounded.astype(jnp.float32)
+        for segment in range(col_count):
+            message_ref[segment, per_seg + term] = rounded
 
 
 def forward_kernel(spots_ref, live_ref, block_hbm, col_dir_ref, *refs):
@@ -283,7 +284,7 @@
             pltpu.SemaphoreType.DMA((slots // BATCH,)),
         ]
         + scratch,
-        compiler_params=pltpu.CompilerParams(vmem_limit_bytes=LARGE_GRANT),
+        compiler_params=pltpu.CompilerParams(vmem_limit_bytes=PRODUCT_GRANT),
         cost_estimate=pl.CostEstimate(
             flops=2 * slots * 32 * 128 * 128, bytes_accessed=2 * blocks.size, transcendentals=0
         ),
@@ -291,17 +292,16 @@
     )(*places, blocks, *inputs)
 
 
-def backward_product(places, blocks, row_pieces, col_count, grams=()):
+def backward_product(places, blocks, row_pieces, col_count):
     per_seg, rows, lanes = row_pieces[0].shape
-    sent = per_seg + (GRAM_TERMS if grams else 0)
     col_shape = (col_count * per_seg, rows, lanes)
     (total,) = over_blocks(
         functools.partial(backward_kernel, len(row_pieces)),
         "backward_product",
         places,
         blocks,
-        [*row_pieces, *grams],
-        [jax.ShapeDtypeStruct((col_count, sent, rows, lanes), jnp.bfloat16)],
+        row_pieces,
+        [jax.ShapeDtypeStruct((col_count, per_seg, rows, lanes), jnp.bfloat16)],
         [
             pltpu.VMEM((len(row_pieces) * per_seg, rows, lanes), jnp.bfloat16),
             pltpu.VMEM(col_shape, jnp.float32),
@@ -536,9 +536,12 @@
     def product(vectors, vector_copies, *grams):
         col_dirs = exchange(vector_copies, "col").reshape((col_count * per_seg,) + piece[1:])
         row_pieces = pass_around([vectors] * row_count, "row")
+        total = backward_product(places, blocks, row_pieces, col_count)
         if grams:
-            grams = (col_dirs, *grams)
-        total = backward_product(places, blocks, row_pieces, col_count, grams)
+            message = jax.ShapeDtypeStruct(
+                (col_count, per_seg + GRAM_TERMS) + piece[1:], jnp.bfloat16
+            )
+            (total,) = simple_call(attach_kernel, [message], "attach", col_dirs, *grams, total)
         col_part = exchange(total, "col")
         totals = forward_product(places, blocks, col_dirs, row_count, piece)
         return pass_around(totals, "row"), col_part

time: 122 us -> 125 us (1.025); the launches traced: 120 us -> 127 us
  starting transfers between devices: 48.9 us -> 65.6 us
  waiting for transfers between devices: 24.6 us -> 18.6 us
  Pallas kernels: 39.7 us -> 35.7 us
    all_to_all x5, starting transfers between devices: 29.1 us -> 39.6 us  [exchange(): return lax.all_to_all(pieces, axis, 0, 0, tiled=True)]
    all_to_all x5, waiting for transfers between devices: 12.2 us -> 5.59 us  [exchange(): return lax.all_to_all(pieces, axis, 0, 0, tiled=True)]
    ppermute x18, starting transfers between devices: 19.8 us -> 26 us  [pass_around(): lax.ppermute(pieces[ahead], axis, [(at, (at + ahead) % count) for at in r...]
    pallas_call x4, Pallas kernels: 19.6 us -> 15.9 us  [over_blocks(): pl.pallas_call(kernel, in_specs=[SCALARS, SCALARS, ANYWHERE] + [IN_VMEM]...]
    pallas_call x1, Pallas kernels: 10.1 us -> 8.57 us  [build_blocks(): pl.pallas_call(functools.partial(build_kernel, row_count), in_specs=[SCAL...]
    pallas_call x4 -> x5, Pallas kernels: 10 us -> 11.3 us  [simple_call(): pl.pallas_call(kernel, out_shape=shapes, compiler_params=pltpu.CompilerPa...]
  transfers between devices with their start and end apart: 23 -> 23, of which waited for: 12 -> 15; matrix products, arithmetic and copies ran while one was open for 0% -> 0% of each run, Pallas kernels for 11% -> 13%
where the time goes in v4:
time: 125 us; the launch traced here: 127 us
  starting transfers between devices  65.6 us (52%)
  Pallas kernels  35.7 us (29%)
  waiting for transfers between devices  18.6 us (15%)
  local copies, waits for them, and re-layouts  5.44 us (4%)
  between operations  1.42 us (1%)
    all_to_all x5, starting transfers between devices, exchange(): return lax.all_to_all(pieces, axis, 0, 0, tiled=True)  39.6 us
    ppermute x18, starting transfers between devices, pass_around(): lax.ppermute(pieces[ahead], axis, [(at, (at + ahead) % count) for at in r...  26 us
    pallas_call x4, Pallas kernels, over_blocks(): pl.pallas_call(kernel, in_specs=[SCALARS, SCALARS, ANYWHERE] + [IN_VMEM]...  15.9 us
    ppermute x18, waiting for transfers between devices, pass_around(): lax.ppermute(pieces[ahead], axis, [(at, (at + ahead) % count) for at in r...  13 us
    pallas_call x5, Pallas kernels, simple_call(): pl.pallas_call(kernel, out_shape=shapes, compiler_params=pltpu.CompilerPa...  11.3 us
    pallas_call x1, Pallas kernels, build_blocks(): pl.pallas_call(functools.partial(build_kernel, row_count), in_specs=[SCAL...  8.57 us
    all_to_all x5, waiting for transfers between devices, exchange(): return lax.all_to_all(pieces, axis, 0, 0, tiled=True)  5.59 us
    unnamed x32, local copies, waits for them, and re-layouts  5.44 us
  transfers between devices with their start and end apart: 23, of which 15 were waited for; matrix products, arithmetic and copies ran while one was open for 0% of the time, Pallas kernels for 13%

profile of v4, /device:TPU:0, one launch (start us, length us, event | category | flops | bytes accessed | tf_op | source)
XLA Modules:
  0.0 126.7 jit_solution(12050734295006287219)
XLA Ops:
  1.3 8.6 %build_blocks.1 = (bf16[256,128,128]{2,1,0:T(8,128)(2,1)}, f32[4,128]{1,0:T(4,128)}, f32[4,128]{1,0:T(4,128)}, f32[4,128]{1,0:T(4,128)}, f32[4,128]{1,0:T(4,128)}, /*index=5*/f32[32,128]{1,0:T(8,128)}) custom-call(s32[1,1,256]{2,1,0:T(1,128)} %spots_ref.9, s32[1,1]{1,0:T(1,128)S(6)} %copy.7.live_ref, s32[256,16,128]{2,1,0:T(8,128)} %bitcast.7, ...), custom_call_target="tpu_custom_call" | custom-call | tf_op jit(solution)/shard_map/build_blocks/pallas_call | solution.py:142
  9.9 12.5 %all-to-all-start = ((f32[8,4,128]{2,1,0:T(4,128)}), f32[8,4,128]{2,1,0:T(4,128)S(1)}, u32[]{:S(2)}, u32[]{:S(2)}) async-start(f32[8,4,128]{2,1,0:T(4,128)} %bitcast.10), calls=%async_computation | async-start | bytes 32768 | tf_op jit(solution)/shard_map/all_to_all | solution.py:487
  22.3 11.4 %collective-permute-start.1 = (f32[4,128]{1,0:T(4,128)}, f32[4,128]{1,0:T(4,128)S(1)}, u32[]{:S(2)}, u32[]{:S(2)}) collective-permute-start(f32[4,128]{1,0:T(4,128)} %get-tuple-element.26), channel_id=1, source_target_pairs={{0,16},{8,24},{16,0},{24,8},{1,17},{9,25},{17,1},{25,9},{2,18},{10... | collective-permute-start | bytes 6152 | tf_op jit(solution)/shard_map/ppermute | solution.py:481
  33.8 1.1 collective-permute-done.refs_1_
  35.6 0.8 copy-done.2
  37.1 0.8 start.1
  37.8 5.7 %all-to-all-start.1 = ((bf16[8,4,32,128]{3,2,1,0:T(8,128)(2,1)}), bf16[8,4,32,128]{3,2,1,0:T(8,128)(2,1)S(1)}, u32[]{:S(2)}, u32[]{:S(2)}) async-start(bf16[8,4,32,128]{3,2,1,0:T(8,128)(2,1)} %get-tuple-element.29), calls=%async_computation.1 | async-start | bytes 524288 | tf_op jit(solution)/shard_map/all_to_all | solution.py:487
  43.6 1.5 %collective-permute-start.8 = (bf16[4,32,128]{2,1,0:T(8,128)(2,1)S(1)}, bf16[4,32,128]{2,1,0:T(8,128)(2,1)S(1)}, u32[]{:S(2)}, u32[]{:S(2)}) collective-permute-start(bf16[4,32,128]{2,1,0:T(8,128)(2,1)S(1)} %get-tuple-element.34.refs_0_), channel_id=1, source_target_pairs={{0,24},{8,0},{16,8},{24,16},{1,25},{9,1},{17,9},{25,17},{2,26},{10... | collective-permute-start | bytes 98312 | tf_op jit(solution)/shard_map/ppermute | solution.py:481
  45.0 1.1 collective-permute-start.7
  46.7 2.2 %collective-permute-done.7.refs_2_ = bf16[4,32,128]{2,1,0:T(8,128)(2,1)S(1)} collective-permute-done((bf16[4,32,128]{2,1,0:T(8,128)(2,1)S(1)}, bf16[4,32,128]{2,1,0:T(8,128)(2,1)S(1)}, u32[]{:S(2)}, u32[]{:S(2)}) %collective-permute-start.7) | collective-permute-done | bytes 32800 | tf_op jit(solution)/shard_map/ppermute | solution.py:481
  50.0 4.3 %backward_product.2 = bf16[8,4,32,128]{3,2,1,0:T(8,128)(2,1)} custom-call(s32[1,1,256]{2,1,0:T(1,128)} %spots_ref.9, s32[1,1]{1,0:T(1,128)S(6)} %copy.7.live_ref, bf16[256,128,128]{2,1,0:T(8,128)(2,1)} %get-tuple-element.23.block_hbm, bf16[4,32,128]{2,1,0:T(8,128)(2,1)} %copy-done.4, bf16[4,32,128]{2,1,0:T(8,128)(2,1)} %copy-done.14, ...), custom_call_target="tpu_custom_call" | custom-call | flops 268435456 | bytes 8388608 | tf_op jit(solution)/shard_map/backward_product/pallas_call | solution.py:277
  54.3 7.1 %all-to-all-start.2 = ((bf16[8,4,32,128]{3,2,1,0:T(8,128)(2,1)}), bf16[8,4,32,128]{3,2,1,0:T(8,128)(2,1)S(1)}, u32[]{:S(2)}, u32[]{:S(2)}) async-start(bf16[8,4,32,128]{3,2,1,0:T(8,128)(2,1)} %backward_product.2), calls=%async_computation.2 | async-start | bytes 524288 | tf_op jit(solution)/shard_map/all_to_all | solution.py:487
  61.4 3.7 %forward_product.2 = (bf16[4,32,128]{2,1,0:T(8,128)(2,1)}, bf16[4,32,128]{2,1,0:T(8,128)(2,1)}, bf16[4,32,128]{2,1,0:T(8,128)(2,1)}, bf16[4,32,128]{2,1,0:T(8,128)(2,1)}) custom-call(s32[1,1,256]{2,1,0:T(1,128)} %spots_ref.9, s32[1,1]{1,0:T(1,128)S(6)} %copy.7.live_ref, bf16[256,128,128]{2,1,0:T(8,128)(2,1)} %get-tuple-element.23.block_hbm, ...), custom_call_target="tpu_custom_call" | custom-call | flops 268435456 | bytes 8388608 | tf_op jit(solution)/shard_map/forward_product/pallas_call | solution.py:277
  65.2 3.2 %collective-permute-start.4 = (bf16[4,32,128]{2,1,0:T(8,128)(2,1)}, bf16[4,32,128]{2,1,0:T(8,128)(2,1)S(1)}, u32[]{:S(2)}, u32[]{:S(2)}) collective-permute-start(bf16[4,32,128]{2,1,0:T(8,128)(2,1)} %get-tuple-element.32), channel_id=1, source_target_pairs={{0,16},{8,24},{16,0},{24,8},{1,17},{9,25},{17,1},{25,9},{2,18},{10... | collective-permute-start | bytes 98312 | tf_op jit(solution)/shard_map/ppermute | solution.py:481
  68.4 1.2 all-to-all-done.2.refs_4_
  71.3 0.8 middle.1
  72.2 7.3 %all-to-all-start.3 = ((bf16[8,4,32,128]{3,2,1,0:T(8,128)(2,1)}), bf16[8,4,32,128]{3,2,1,0:T(8,128)(2,1)S(1)}, u32[]{:S(2)}, u32[]{:S(2)}) async-start(bf16[8,4,32,128]{3,2,1,0:T(8,128)(2,1)} %get-tuple-element.36), calls=%async_computation.3 | async-start | bytes 524288 | tf_op jit(solution)/shard_map/all_to_all | solution.py:487
  79.5 1.4 %collective-permute-start.14 = (bf16[4,32,128]{2,1,0:T(8,128)(2,1)S(1)}, bf16[4,32,128]{2,1,0:T(8,128)(2,1)S(1)}, u32[]{:S(2)}, u32[]{:S(2)}) collective-permute-start(bf16[4,32,128]{2,1,0:T(8,128)(2,1)S(1)} %get-tuple-element.42.refs_0_), channel_id=1, source_target_pairs={{0,24},{8,0},{16,8},{24,16},{1,25},{9,1},{17,9},{25,17},{2,26},{10... | collective-permute-start | bytes 98312 | tf_op jit(solution)/shard_map/ppermute | solution.py:481
  80.9 1.1 collective-permute-start.13
  82.6 2.2 %collective-permute-done.13.refs_2_ = bf16[4,32,128]{2,1,0:T(8,128)(2,1)S(1)} collective-permute-done((bf16[4,32,128]{2,1,0:T(8,128)(2,1)S(1)}, bf16[4,32,128]{2,1,0:T(8,128)(2,1)S(1)}, u32[]{:S(2)}, u32[]{:S(2)}) %collective-permute-start.13) | collective-permute-done | bytes 32800 | tf_op jit(solution)/shard_map/ppermute | solution.py:481
  86.0 4.2 %backward_product.3.total_ref = bf16[8,4,32,128]{3,2,1,0:T(8,128)(2,1)} custom-call(s32[1,1,256]{2,1,0:T(1,128)} %spots_ref.9, s32[1,1]{1,0:T(1,128)S(6)} %copy.7.live_ref, bf16[256,128,128]{2,1,0:T(8,128)(2,1)} %get-tuple-element.23.block_hbm, bf16[4,32,128]{2,1,0:T(8,128)(2,1)} %copy-done.5, bf16[4,32,128]{2,1,0:T(8,128)(2,1)} %copy-done.15, ...), custom_call_target="tpu_custom_call" | custom-call | flops 268435456 | bytes 8388608 | tf_op jit(solution)/shard_map/backward_product/pallas_call | solution.py:277
  90.3 1.0 copy-done.1
  91.3 1.2 attach.1
  92.5 7.0 %all-to-all-start.4 = ((bf16[8,7,32,128]{3,2,1,0:T(8,128)(2,1)}), bf16[8,7,32,128]{3,2,1,0:T(8,128)(2,1)S(1)}, u32[]{:S(2)}, u32[]{:S(2)}) async-start(bf16[8,7,32,128]{3,2,1,0:T(8,128)(2,1)} %attach.1), calls=%async_computation.4 | async-start | bytes 917504 | tf_op jit(solution)/shard_map/all_to_all | solution.py:487
  99.6 3.7 %forward_product.3 = (bf16[4,32,128]{2,1,0:T(8,128)(2,1)}, bf16[4,32,128]{2,1,0:T(8,128)(2,1)}, bf16[4,32,128]{2,1,0:T(8,128)(2,1)}, bf16[4,32,128]{2,1,0:T(8,128)(2,1)}) custom-call(s32[1,1,256]{2,1,0:T(1,128)} %spots_ref.9, s32[1,1]{1,0:T(1,128)S(6)} %copy.7.live_ref, bf16[256,128,128]{2,1,0:T(8,128)(2,1)} %get-tuple-element.23.block_hbm, ...), custom_call_target="tpu_custom_call" | custom-call | flops 268435456 | bytes 8388608 | tf_op jit(solution)/shard_map/forward_product/pallas_call | solution.py:277
  103.4 3.6 %collective-permute-start.10 = (bf16[4,32,128]{2,1,0:T(8,128)(2,1)}, bf16[4,32,128]{2,1,0:T(8,128)(2,1)S(1)}, u32[]{:S(2)}, u32[]{:S(2)}) collective-permute-start(bf16[4,32,128]{2,1,0:T(8,128)(2,1)} %get-tuple-element.39), channel_id=1, source_target_pairs={{0,16},{8,24},{16,0},{24,8},{1,17},{9,25},{17,1},{25,9},{2,18},{10... | collective-permute-start | bytes 98312 | tf_op jit(solution)/shard_map/ppermute | solution.py:481
  107.0 4.3 %all-to-all-done.4.col_ref.refs_8_ = bf16[8,7,32,128]{3,2,1,0:T(8,128)(2,1)S(1)} async-done(((bf16[8,7,32,128]{3,2,1,0:T(8,128)(2,1)}), bf16[8,7,32,128]{3,2,1,0:T(8,128)(2,1)S(1)}, u32[]{:S(2)}, u32[]{:S(2)}) %all-to-all-start.4) | async-done | bytes 458784 | tf_op jit(solution)/shard_map/all_to_all | solution.py:487
  111.4 2.4 %collective-permute-start.17 = (f32[32,128]{1,0:T(8,128)S(1)}, f32[32,128]{1,0:T(8,128)S(1)}, u32[]{:S(2)}, u32[]{:S(2)}) collective-permute-start(f32[32,128]{1,0:T(8,128)S(1)} %gram_sum.1.refs_4_), channel_id=1, source_target_pairs={{0,24},{8,0},{16,8},{24,16},{1,25},{9,1},{17,9},{25,17},{2,26},{10... | collective-permute-start | bytes 49160 | tf_op jit(solution)/shard_map/ppermute | solution.py:481
  114.0 1.2 collective-permute-done.17.refs_7_
  115.3 2.3 %collective-permute-done.16.refs_6_ = f32[32,128]{1,0:T(8,128)S(1)} collective-permute-done((f32[32,128]{1,0:T(8,128)S(1)}, f32[32,128]{1,0:T(8,128)S(1)}, u32[]{:S(2)}, u32[]{:S(2)}) %collective-permute-start.16) | collective-permute-done | bytes 16416 | tf_op jit(solution)/shard_map/ppermute | solution.py:481
  117.6 0.8 copy-done.7
  118.3 8.4 %close.1 = (f32[32,512]{1,0:T(8,128)}, f32[32,512]{1,0:T(8,128)}) custom-call(bf16[4,32,128]{2,1,0:T(8,128)(2,1)S(1)} %copy-done.7, bf16[4,32,128]{2,1,0:T(8,128)(2,1)S(1)} %collective-permute-done.9.refs_1_, bf16[4,32,128]{2,1,0:T(8,128)(2,1)S(1)} %collective-permute-done.10.refs_2_, bf16[4,32,128]{2,1,0:T(8,128)(2,1)S(1)} %collective-permute-done.11.refs_3_, ...), custom_call_target="tpu_custom_call" | custom-call | tf_op jit(solution)/shard_map/close/pallas_call | solution.py:491
  (56 shorter events, 7.1 us)
Async XLA Ops:
  9.9 25.7 %all-to-all-start = ((f32[8,4,128]{2,1,0:T(4,128)}), f32[8,4,128]{2,1,0:T(4,128)S(1)}, u32[]{:S(2)}, u32[]{:S(2)}) async-start(f32[8,4,128]{2,1,0:T(4,128)} %bitcast.10), calls=%async_computation | async-start | bytes 32768 | tf_op jit(solution)/shard_map/all_to_all | solution.py:487
  22.3 12.5 %collective-permute-start = (f32[4,128]{1,0:T(4,128)}, f32[4,128]{1,0:T(4,128)S(1)}, u32[]{:S(2)}, u32[]{:S(2)}) collective-permute-start(f32[4,128]{1,0:T(4,128)} %get-tuple-element.25), channel_id=1, source_target_pairs={{0,8},{8,16},{16,24},{24,0},{1,9},{9,17},{17,25},{25,1},{2,10},{10... | collective-permute-start | bytes 6152 | tf_op jit(solution)/shard_map/ppermute | solution.py:481
  22.3 13.2 %collective-permute-start.1 = (f32[4,128]{1,0:T(4,128)}, f32[4,128]{1,0:T(4,128)S(1)}, u32[]{:S(2)}, u32[]{:S(2)}) collective-permute-start(f32[4,128]{1,0:T(4,128)} %get-tuple-element.26), channel_id=1, source_target_pairs={{0,16},{8,24},{16,0},{24,8},{1,17},{9,25},{17,1},{25,9},{2,18},{10... | collective-permute-start | bytes 6152 | tf_op jit(solution)/shard_map/ppermute | solution.py:481
  33.8 1.8 %collective-permute-start.2 = (f32[4,128]{1,0:T(4,128)}, f32[4,128]{1,0:T(4,128)S(1)}, u32[]{:S(2)}, u32[]{:S(2)}) collective-permute-start(f32[4,128]{1,0:T(4,128)} %get-tuple-element.27), channel_id=1, source_target_pairs={{0,24},{8,0},{16,8},{24,16},{1,25},{9,1},{17,9},{25,17},{2,26},{10... | collective-permute-start | bytes 6152 | tf_op jit(solution)/shard_map/ppermute | solution.py:481
  35.5 0.8 copy-start.2
  37.8 11.6 %copy-start.4 = (bf16[4,32,128]{2,1,0:T(8,128)(2,1)}, bf16[4,32,128]{2,1,0:T(8,128)(2,1)S(1)}, u32[]{:S(2)}) copy-start(bf16[4,32,128]{2,1,0:T(8,128)(2,1)S(1)} %get-tuple-element.34.refs_0_) | copy-start | bytes 98308
  37.8 16.5 %all-to-all-start.1 = ((bf16[8,4,32,128]{3,2,1,0:T(8,128)(2,1)}), bf16[8,4,32,128]{3,2,1,0:T(8,128)(2,1)S(1)}, u32[]{:S(2)}, u32[]{:S(2)}) async-start(bf16[8,4,32,128]{3,2,1,0:T(8,128)(2,1)} %get-tuple-element.29), calls=%async_computation.1 | async-start | bytes 524288 | tf_op jit(solution)/shard_map/all_to_all | solution.py:487
  43.6 3.1 %collective-permute-start.8 = (bf16[4,32,128]{2,1,0:T(8,128)(2,1)S(1)}, bf16[4,32,128]{2,1,0:T(8,128)(2,1)S(1)}, u32[]{:S(2)}, u32[]{:S(2)}) collective-permute-start(bf16[4,32,128]{2,1,0:T(8,128)(2,1)S(1)} %get-tuple-element.34.refs_0_), channel_id=1, source_target_pairs={{0,24},{8,0},{16,8},{24,16},{1,25},{9,1},{17,9},{25,17},{2,26},{10... | collective-permute-start | bytes 98312 | tf_op jit(solution)/shard_map/ppermute | solution.py:481
  45.0 3.9 %collective-permute-start.7 = (bf16[4,32,128]{2,1,0:T(8,128)(2,1)S(1)}, bf16[4,32,128]{2,1,0:T(8,128)(2,1)S(1)}, u32[]{:S(2)}, u32[]{:S(2)}) collective-permute-start(bf16[4,32,128]{2,1,0:T(8,128)(2,1)S(1)} %get-tuple-element.34.refs_0_), channel_id=1, source_target_pairs={{0,16},{8,24},{16,0},{24,8},{1,17},{9,25},{17,1},{25,9},{2,18},{10... | collective-permute-start | bytes 98312 | tf_op jit(solution)/shard_map/ppermute | solution.py:481
  46.1 3.3 %collective-permute-start.6 = (bf16[4,32,128]{2,1,0:T(8,128)(2,1)S(1)}, bf16[4,32,128]{2,1,0:T(8,128)(2,1)S(1)}, u32[]{:S(2)}, u32[]{:S(2)}) collective-permute-start(bf16[4,32,128]{2,1,0:T(8,128)(2,1)S(1)} %get-tuple-element.34.refs_0_), channel_id=1, source_target_pairs={{0,8},{8,16},{16,24},{24,0},{1,9},{9,17},{17,25},{25,1},{2,10},{10... | collective-permute-start | bytes 98312 | tf_op jit(solution)/shard_map/ppermute | solution.py:481
  46.7 2.7 %copy-start.10 = (bf16[4,32,128]{2,1,0:T(8,128)(2,1)}, bf16[4,32,128]{2,1,0:T(8,128)(2,1)S(1)}, u32[]{:S(2)}) copy-start(bf16[4,32,128]{2,1,0:T(8,128)(2,1)S(1)} %collective-permute-done.8.refs_3_) | copy-start | bytes 98308
  50.0 20.6 %copy-start.3 = (f32[32,512]{1,0:T(8,128)S(1)}, f32[32,512]{1,0:T(8,128)}, u32[]{:S(2)}) copy-start(f32[32,512]{1,0:T(8,128)} %refs_10_.1) | copy-start | bytes 196612
  54.3 7.1 %copy-start.9 = (bf16[8,4,32,128]{3,2,1,0:T(8,128)(2,1)}, bf16[8,4,32,128]{3,2,1,0:T(8,128)(2,1)S(1)}, u32[]{:S(2)}) copy-start(bf16[8,4,32,128]{3,2,1,0:T(8,128)(2,1)S(1)} %all-to-all-done.1) | copy-start | bytes 786436
  54.3 15.3 %all-to-all-start.2 = ((bf16[8,4,32,128]{3,2,1,0:T(8,128)(2,1)}), bf16[8,4,32,128]{3,2,1,0:T(8,128)(2,1)S(1)}, u32[]{:S(2)}, u32[]{:S(2)}) async-start(bf16[8,4,32,128]{3,2,1,0:T(8,128)(2,1)} %backward_product.2), calls=%async_computation.2 | async-start | bytes 524288 | tf_op jit(solution)/shard_map/all_to_all | solution.py:487
  65.1 4.7 %collective-permute-start.3 = (bf16[4,32,128]{2,1,0:T(8,128)(2,1)}, bf16[4,32,128]{2,1,0:T(8,128)(2,1)S(1)}, u32[]{:S(2)}, u32[]{:S(2)}) collective-permute-start(bf16[4,32,128]{2,1,0:T(8,128)(2,1)} %get-tuple-element.31), channel_id=1, source_target_pairs={{0,8},{8,16},{16,24},{24,0},{1,9},{9,17},{17,25},{25,1},{2,10},{10... | collective-permute-start | bytes 98312 | tf_op jit(solution)/shard_map/ppermute | solution.py:481
  65.2 5.3 %collective-permute-start.4 = (bf16[4,32,128]{2,1,0:T(8,128)(2,1)}, bf16[4,32,128]{2,1,0:T(8,128)(2,1)S(1)}, u32[]{:S(2)}, u32[]{:S(2)}) collective-permute-start(bf16[4,32,128]{2,1,0:T(8,128)(2,1)} %get-tuple-element.32), channel_id=1, source_target_pairs={{0,16},{8,24},{16,0},{24,8},{1,17},{9,25},{17,1},{25,9},{2,18},{10... | collective-permute-start | bytes 98312 | tf_op jit(solution)/shard_map/ppermute | solution.py:481
  68.4 2.2 %collective-permute-start.5 = (bf16[4,32,128]{2,1,0:T(8,128)(2,1)}, bf16[4,32,128]{2,1,0:T(8,128)(2,1)S(1)}, u32[]{:S(2)}, u32[]{:S(2)}) collective-permute-start(bf16[4,32,128]{2,1,0:T(8,128)(2,1)} %get-tuple-element.33), channel_id=1, source_target_pairs={{0,24},{8,0},{16,8},{24,16},{1,25},{9,1},{17,9},{25,17},{2,26},{10... | collective-permute-start | bytes 98312 | tf_op jit(solution)/shard_map/ppermute | solution.py:481
  72.2 13.1 %copy-start.5 = (bf16[4,32,128]{2,1,0:T(8,128)(2,1)}, bf16[4,32,128]{2,1,0:T(8,128)(2,1)S(1)}, u32[]{:S(2)}) copy-start(bf16[4,32,128]{2,1,0:T(8,128)(2,1)S(1)} %get-tuple-element.42.refs_0_) | copy-start | bytes 98308
  72.2 18.1 %all-to-all-start.3 = ((bf16[8,4,32,128]{3,2,1,0:T(8,128)(2,1)}), bf16[8,4,32,128]{3,2,1,0:T(8,128)(2,1)S(1)}, u32[]{:S(2)}, u32[]{:S(2)}) async-start(bf16[8,4,32,128]{3,2,1,0:T(8,128)(2,1)} %get-tuple-element.36), calls=%async_computation.3 | async-start | bytes 524288 | tf_op jit(solution)/shard_map/all_to_all | solution.py:487
  79.5 3.1 %collective-permute-start.14 = (bf16[4,32,128]{2,1,0:T(8,128)(2,1)S(1)}, bf16[4,32,128]{2,1,0:T(8,128)(2,1)S(1)}, u32[]{:S(2)}, u32[]{:S(2)}) collective-permute-start(bf16[4,32,128]{2,1,0:T(8,128)(2,1)S(1)} %get-tuple-element.42.refs_0_), channel_id=1, source_target_pairs={{0,24},{8,0},{16,8},{24,16},{1,25},{9,1},{17,9},{25,17},{2,26},{10... | collective-permute-start | bytes 98312 | tf_op jit(solution)/shard_map/ppermute | solution.py:481
  80.9 3.9 %collective-permute-start.13 = (bf16[4,32,128]{2,1,0:T(8,128)(2,1)S(1)}, bf16[4,32,128]{2,1,0:T(8,128)(2,1)S(1)}, u32[]{:S(2)}, u32[]{:S(2)}) collective-permute-start(bf16[4,32,128]{2,1,0:T(8,128)(2,1)S(1)} %get-tuple-element.42.refs_0_), channel_id=1, source_target_pairs={{0,16},{8,24},{16,0},{24,8},{1,17},{9,25},{17,1},{25,9},{2,18},{10... | collective-permute-start | bytes 98312 | tf_op jit(solution)/shard_map/ppermute | solution.py:481
  81.9 3.3 %collective-permute-start.12 = (bf16[4,32,128]{2,1,0:T(8,128)(2,1)S(1)}, bf16[4,32,128]{2,1,0:T(8,128)(2,1)S(1)}, u32[]{:S(2)}, u32[]{:S(2)}) collective-permute-start(bf16[4,32,128]{2,1,0:T(8,128)(2,1)S(1)} %get-tuple-element.42.refs_0_), channel_id=1, source_target_pairs={{0,8},{8,16},{16,24},{24,0},{1,9},{9,17},{17,25},{25,1},{2,10},{10... | collective-permute-start | bytes 98312 | tf_op jit(solution)/shard_map/ppermute | solution.py:481
  82.6 2.7 %copy-start.11 = (bf16[4,32,128]{2,1,0:T(8,128)(2,1)}, bf16[4,32,128]{2,1,0:T(8,128)(2,1)S(1)}, u32[]{:S(2)}) copy-start(bf16[4,32,128]{2,1,0:T(8,128)(2,1)S(1)} %collective-permute-done.14.refs_3_) | copy-start | bytes 98308
  90.2 9.3 %copy-start = (bf16[8,4,32,128]{3,2,1,0:T(8,128)(2,1)}, bf16[8,4,32,128]{3,2,1,0:T(8,128)(2,1)S(1)}, u32[]{:S(2)}) copy-start(bf16[8,4,32,128]{3,2,1,0:T(8,128)(2,1)S(1)} %all-to-all-done.3) | copy-start | bytes 786436
  90.3 1.0 copy-start.1
  92.5 18.8 %all-to-all-start.4 = ((bf16[8,7,32,128]{3,2,1,0:T(8,128)(2,1)}), bf16[8,7,32,128]{3,2,1,0:T(8,128)(2,1)S(1)}, u32[]{:S(2)}, u32[]{:S(2)}) async-start(bf16[8,7,32,128]{3,2,1,0:T(8,128)(2,1)} %attach.1), calls=%async_computation.4 | async-start | bytes 917504 | tf_op jit(solution)/shard_map/all_to_all | solution.py:487
  103.3 10.5 %collective-permute-start.9 = (bf16[4,32,128]{2,1,0:T(8,128)(2,1)}, bf16[4,32,128]{2,1,0:T(8,128)(2,1)S(1)}, u32[]{:S(2)}, u32[]{:S(2)}) collective-permute-start(bf16[4,32,128]{2,1,0:T(8,128)(2,1)} %get-tuple-element.38), channel_id=1, source_target_pairs={{0,8},{8,16},{16,24},{24,0},{1,9},{9,17},{17,25},{25,1},{2,10},{10... | collective-permute-start | bytes 98312 | tf_op jit(solution)/shard_map/ppermute | solution.py:481
  103.4 10.7 %collective-permute-start.10 = (bf16[4,32,128]{2,1,0:T(8,128)(2,1)}, bf16[4,32,128]{2,1,0:T(8,128)(2,1)S(1)}, u32[]{:S(2)}, u32[]{:S(2)}) collective-permute-start(bf16[4,32,128]{2,1,0:T(8,128)(2,1)} %get-tuple-element.39), channel_id=1, source_target_pairs={{0,16},{8,24},{16,0},{24,8},{1,17},{9,25},{17,1},{25,9},{2,18},{10... | collective-permute-start | bytes 98312 | tf_op jit(solution)/shard_map/ppermute | solution.py:481
  107.0 7.0 %collective-permute-start.11 = (bf16[4,32,128]{2,1,0:T(8,128)(2,1)}, bf16[4,32,128]{2,1,0:T(8,128)(2,1)S(1)}, u32[]{:S(2)}, u32[]{:S(2)}) collective-permute-start(bf16[4,32,128]{2,1,0:T(8,128)(2,1)} %get-tuple-element.40), channel_id=1, source_target_pairs={{0,24},{8,0},{16,8},{24,16},{1,25},{9,1},{17,9},{25,17},{2,26},{10... | collective-permute-start | bytes 98312 | tf_op jit(solution)/shard_map/ppermute | solution.py:481
  111.4 3.9 %collective-permute-start.17 = (f32[32,128]{1,0:T(8,128)S(1)}, f32[32,128]{1,0:T(8,128)S(1)}, u32[]{:S(2)}, u32[]{:S(2)}) collective-permute-start(f32[32,128]{1,0:T(8,128)S(1)} %gram_sum.1.refs_4_), channel_id=1, source_target_pairs={{0,24},{8,0},{16,8},{24,16},{1,25},{9,1},{17,9},{25,17},{2,26},{10... | collective-permute-start | bytes 49160 | tf_op jit(solution)/shard_map/ppermute | solution.py:481
  113.8 3.7 %collective-permute-start.16 = (f32[32,128]{1,0:T(8,128)S(1)}, f32[32,128]{1,0:T(8,128)S(1)}, u32[]{:S(2)}, u32[]{:S(2)}) collective-permute-start(f32[32,128]{1,0:T(8,128)S(1)} %gram_sum.1.refs_4_), channel_id=1, source_target_pairs={{0,16},{8,24},{16,0},{24,8},{1,17},{9,25},{17,1},{25,9},{2,18},{10... | collective-permute-start | bytes 49160 | tf_op jit(solution)/shard_map/ppermute | solution.py:481
  113.8 3.7 %collective-permute-start.15 = (f32[32,128]{1,0:T(8,128)S(1)}, f32[32,128]{1,0:T(8,128)S(1)}, u32[]{:S(2)}, u32[]{:S(2)}) collective-permute-start(f32[32,128]{1,0:T(8,128)S(1)} %gram_sum.1.refs_4_), channel_id=1, source_target_pairs={{0,8},{8,16},{16,24},{24,0},{1,9},{9,17},{17,25},{25,1},{2,10},{10... | collective-permute-start | bytes 49160 | tf_op jit(solution)/shard_map/ppermute | solution.py:481
  (7 other events, 4.7 us)

commit v5 on v4

--- a/solution.py
+++ b/solution.py
@@ -10,9 +10,11 @@
 graph_weight = 0.95
 GROUP = 16
 BATCH = 32
+SPARE = 4
 GRAM_TERMS = 3
+PANEL = 8
 BUILD_GRANT = 60 * 1024 * 1024
-PRODUCT_GRANT = 57 * 1024 * 1024
+PRODUCT_GRANT = 40 * 1024 * 1024
 SMALL_GRANT = 24 * 1024 * 1024
 
 
@@ -32,11 +34,14 @@
 exact_across = functools.partial(dot_across, precision=lax.Precision.HIGHEST)
 
 
+def divided(number, size):
+    if size & (size - 1):
+        return lax.div(number, size), lax.rem(number, size)
+    return number >> (size.bit_length() - 1), number & (size - 1)
+
+
 def place_of(spots_ref, slot, col_blocks):
-    spot = spots_ref[0, 0, slot]
-    if col_blocks & (col_blocks - 1):
-        return lax.div(spot, col_blocks), lax.rem(spot, col_blocks)
-    return spot >> (col_blocks.bit_length() - 1), spot & (col_blocks - 1)
+    return divided(spots_ref[0, 0, slot], col_blocks)
 
 
 def group_count(live_ref, group):
@@ -76,33 +81,29 @@
     rows_16 = lax.broadcasted_iota(jnp.int32, (16, 128), 0)
     ones = jnp.ones((128, 128), jnp.bfloat16)
     zero = jnp.zeros((16, 128), jnp.bfloat16)
-    one = jnp.ones((16, 128), jnp.bfloat16)
 
     def build_group(index, _):
         group_copy(index_hbm, index_ref, index_sems, index, GROUP).wait()
         group_copy(value_hbm, value_ref, value_sems, index, GROUP).wait()
-        targets = [(rows_16 + 16 * half).astype(jnp.int16) for half in range(2)]
+        targets = [(rows_16 + 16 * part).astype(jnp.int16) for part in range(8)]
         for inside in range(GROUP):
             slot = index * GROUP + inside
             row_block, col_block = place_of(spots_ref, slot, col_blocks)
             active = (slot < live_ref[0, 0]).astype(jnp.float32)
             index_i32 = index_ref[slot]
             value_f32 = value_ref[slot].astype(jnp.float32) * active
-            quarter = index_i32 >> 5
-            within = index_i32 & 31
-            quarter_values = [jnp.where(quarter == part, value_f32, 0.0) for part in range(4)]
             sums = [zero] * 8
             for entry in range(16):
-                row = slice(entry, entry + 1)
-                within_row = jnp.broadcast_to(within[row], (16, 128)).astype(jnp.int16)
-                hits = [jnp.where(within_row == target, one, zero) for target in targets]
-                for part in range(4):
-                    value_row = jnp.broadcast_to(quarter_values[part][row], (16, 128)).astype(
-                        jnp.bfloat16
+                index_row = jnp.broadcast_to(index_i32[entry : entry + 1], (16, 128)).astype(
+                    jnp.int16
+                )
+                value_row = jnp.broadcast_to(value_f32[entry : entry + 1], (16, 128)).astype(
+                    jnp.bfloat16
+                )
+                for part in range(8):
+                    sums[part] = sums[part] + jnp.where(
+                        index_row == targets[part], value_row, zero
                     )
-                    for half in range(2):
-                        place = 2 * part + half
-                        sums[place] = sums[place] + hits[half] * value_row
             block = jnp.concatenate(sums, axis=0)
             block_ref[slot] = block
             row_ref[row_block] += value_f32[:8] + value_f32[8:]
@@ -143,7 +144,7 @@
         functools.partial(build_kernel, row_count),
         in_specs=[SCALARS, SCALARS, ANYWHERE, ANYWHERE],
         out_specs=[ANYWHERE] + [IN_VMEM] * len(sum_shapes),
-        out_shape=[jax.ShapeDtypeStruct((slots, 128, 128), jnp.bfloat16)]
+        out_shape=[jax.ShapeDtypeStruct((SPARE * slots, 128, 128), jnp.bfloat16)]
         + [jax.ShapeDtypeStruct(shape, jnp.float32) for shape in sum_shapes],
         scratch_shapes=[
             pltpu.VMEM(index_table.shape, index_table.dtype),
@@ -178,11 +179,11 @@
     lax.fori_loop(0, groups, one_group, 0)
 
 
-def add_products(dot, places, first_slot, block_ref, dir_ref, total_refs):
+def add_products(dot, places, first_slot, block_ref, direction, total_refs):
     sums = []
     for inside in range(BATCH):
         slot = first_slot + inside
-        sums.append(dot(dir_ref[places(slot)[0]], block_ref[slot]))
+        sums.append(dot(direction(places(slot)[0]), block_ref[slot]))
     for inside in range(BATCH):
         total_ref = total_refs[inside % len(total_refs)]
         total_ref[places(first_slot + inside)[1]] += sums[inside]
@@ -212,7 +213,7 @@
             lambda slot: place_of(spots_ref, slot, col_blocks),
             first_slot,
             block_ref,
-            row_dir_ref,
+            lambda row_block: row_dir_ref[row_block],
             [even_ref, odd_ref],
         )
 
@@ -224,31 +225,45 @@
             col_out_ref[segment, part] = values.astype(col_out_ref.dtype)
 
 
-def attach_kernel(col_dir_ref, gram_ref, total_ref, message_ref):
-    col_count, sent, size, _ = message_ref.shape
-    per_seg = sent - GRAM_TERMS
+def in_terms(values):
+    terms = []
+    for _ in range(GRAM_TERMS):
+        terms.append(values.astype(jnp.bfloat16))
+        values = values - terms[-1].astype(jnp.float32)
+    return terms
+
+
+def attach_kernel(col_dir_ref, total_ref, message_ref, gram_ref):
+    col_count, per_seg, size, _ = total_ref.shape
+
     def add_segment(segment, gram):
         for part in range(per_seg):
             values = total_ref[segment, part]
             message_ref[segment, part] = values
-            gram += dot_across(values, tall(col_dir_ref[segment * per_seg + part]))
+            gram += dot_across(values, tall(col_dir_ref[segment, part]))
         return gram
 
     gram = lax.fori_loop(
         0, col_count, add_segment, jnp.zeros((size, 128), jnp.float32), unroll=4
     )
-    gram = gram_ref[...] + pltpu.roll(gram, 3 * size, 1)
-    for term in range(GRAM_TERMS):
-        rounded = gram.astype(message_ref.dtype)
-        gram = gram - rounded.astype(jnp.float32)
-        for segment in range(col_count):
-            message_ref[segment, per_seg + term] = rounded
+    together = jnp.zeros((size, 128), jnp.float32)
+    for term, values in enumerate(in_terms(gram)):
+        together = together + pltpu.roll(values.astype(jnp.float32), term * size, 1)
+    for segment in range(col_count):
+        message_ref[segment, per_seg] = together.astype(message_ref.dtype)
+    gram_ref[...] = total_of(
+        [
+            col_dir_ref[segment, per_seg + term]
+            for term in range(GRAM_TERMS)
+            for segment in range(col_count)
+        ]
+    )
 
 
 def forward_kernel(spots_ref, live_ref, block_hbm, col_dir_ref, *refs):
     *row_outs, block_ref, sems, even_ref, odd_ref = refs
     per_seg = row_outs[0].shape[0]
-    col_blocks = col_dir_ref.shape[0]
+    col_blocks = col_dir_ref.shape[0] * per_seg
 
     def prepare():
         even_ref[...] = jnp.zeros_like(even_ref)
@@ -260,7 +275,7 @@
             lambda slot: place_of(spots_ref, slot, col_blocks)[::-1],
             first_slot,
             block_ref,
-            col_dir_ref,
+            lambda col_block: col_dir_ref[divided(col_block, per_seg)],
             [even_ref, odd_ref],
         )
 
@@ -273,20 +288,20 @@
 
 
 def over_blocks(kernel, name, places, blocks, inputs, outputs, scratch):
-    slots = blocks.shape[0]
+    slots = blocks.shape[0] // SPARE
     return pl.pallas_call(
         kernel,
         in_specs=[SCALARS, SCALARS, ANYWHERE] + [IN_VMEM] * len(inputs),
         out_specs=[IN_VMEM] * len(outputs),
         out_shape=outputs,
         scratch_shapes=[
-            pltpu.VMEM(blocks.shape, blocks.dtype),
+            pltpu.VMEM((slots,) + blocks.shape[1:], blocks.dtype),
             pltpu.SemaphoreType.DMA((slots // BATCH,)),
         ]
         + scratch,
         compiler_params=pltpu.CompilerParams(vmem_limit_bytes=PRODUCT_GRANT),
         cost_estimate=pl.CostEstimate(
-            flops=2 * slots * 32 * 128 * 128, bytes_accessed=2 * blocks.size, transcendentals=0
+            flops=2 * slots * 32 * 128 * 128, bytes_accessed=2 * slots * 128 * 128, transcendentals=0
         ),
         name=name,
     )(*places, blocks, *inputs)
@@ -356,7 +371,7 @@
 
 
 def middle_kernel(*refs):
-    *row_refs, col_ref, scaling_ref, query_ref, first_ref, scaled_ref, copies_ref, gram_ref = refs
+    *row_refs, col_ref, scaling_ref, query_ref, first_ref, scaled_ref, copies_ref = refs
     size = query_ref.shape[0]
     pair_gram = jnp.zeros((2 * size, 128), jnp.float32)
     for part in range(scaling_ref.shape[0]):
@@ -370,9 +385,10 @@
             [query_ref[:, part * 128 : part * 128 + 128], first], axis=0
         )
         pair_gram += exact_across(pair, tall(pair))
-    gram_ref[...] = beside(
-        pair_gram[:size], pltpu.roll(window(pair_gram[size:], 1), size, 1)
-    )
+    grams = beside(pair_gram[:size], pltpu.roll(window(pair_gram[size:], 1), size, 1))
+    for term, values in enumerate(in_terms(grams)):
+        for copy in range(copies_ref.shape[0]):
+            copies_ref[copy, scaling_ref.shape[0] + term] = values
 
 
 def tall(flat):
@@ -417,13 +433,21 @@
     size = pairs[0][0].shape[0]
     systems = [matrix + pltpu.roll(side, size, 1) for matrix, side in pairs]
     sublanes = lax.broadcasted_iota(jnp.int32, systems[0].shape, 0)
-    for pivot in range(size):
-        updated = []
-        for system in systems:
-            column = system[:, pivot : pivot + 1]
-            row = system[pivot : pivot + 1, :] / column[pivot : pivot + 1, :]
-            updated.append(jnp.where(sublanes == pivot, row, system - column * row))
-        systems = updated
+
+    def eliminated(values, column, scale, pivot):
+        row = values[pivot : pivot + 1, :] * scale
+        return jnp.where(sublanes == pivot, row, values - column * row)
+
+    for first in range(0, size, PANEL):
+        panels = [
+            [jnp.broadcast_to(system[:, at : at + 1], system.shape) for at in range(first, first + PANEL)]
+            for system in systems
+        ]
+        for pivot in range(first, first + PANEL):
+            for which, (column, *later) in enumerate(panels):
+                scale = 1.0 / column[pivot : pivot + 1, :]
+                panels[which] = [eliminated(other, column, scale, pivot) for other in later]
+                systems[which] = eliminated(systems[which], column, scale, pivot)
     return [window(system, 1) for system in systems]
 
 
@@ -496,15 +520,11 @@
     )(*operands)
 
 
-def sum_kernel(col_ref, total_ref):
-    col_count, sent = col_ref.shape[:2]
-    total_ref[...] = total_of(
-        [
-            col_ref[segment, sent - GRAM_TERMS + term]
-            for term in range(GRAM_TERMS)
-            for segment in range(col_count)
-        ]
-    )
+def sum_kernel(col_ref, gram_ref, total_ref):
+    col_count, sent, size, _ = col_ref.shape
+    together = total_of([col_ref[segment, sent - 1] for segment in range(col_count)])
+    last = total_of([window(together, term) for term in range(GRAM_TERMS)])
+    total_ref[...] = gram_ref[...] + pltpu.roll(last, 3 * size, 1)
 
 
 def body(queries, block_spots, live_blocks, neighbor_cols, neighbor_sims):
@@ -533,31 +553,35 @@
         queries,
     )
 
-    def product(vectors, vector_copies, *grams):
-        col_dirs = exchange(vector_copies, "col").reshape((col_count * per_seg,) + piece[1:])
+    def product(vectors, vector_copies, with_grams):
+        col_dirs = exchange(vector_copies, "col")
         row_pieces = pass_around([vectors] * row_count, "row")
         total = backward_product(places, blocks, row_pieces, col_count)
-        if grams:
-            message = jax.ShapeDtypeStruct(
-                (col_count, per_seg + GRAM_TERMS) + piece[1:], jnp.bfloat16
+        gram = None
+        if with_grams:
+            message = jax.ShapeDtypeStruct((col_count, per_seg + 1) + piece[1:], jnp.bfloat16)
+            total, gram = simple_call(
+                attach_kernel, [message, gram_shape], "attach", col_dirs, total
             )
-            (total,) = simple_call(attach_kernel, [message], "attach", col_dirs, *grams, total)
         col_part = exchange(total, "col")
         totals = forward_product(places, blocks, col_dirs, row_count, piece)
-        return pass_around(totals, "row"), col_part
-
-    row_parts, col_part = product(scaled, scaled_copies)
-    first, scaled, scaled_copies, gram = simple_call(
+        return pass_around(totals, "row"), col_part, gram
+
+    row_parts, col_part, _ = product(scaled, scaled_copies, False)
+    more_copies = jax.ShapeDtypeStruct(
+        (col_count, per_seg + GRAM_TERMS) + piece[1:], jnp.bfloat16
+    )
+    first, scaled, scaled_copies = simple_call(
         middle_kernel,
-        [wide, narrow, copies, gram_shape],
+        [wide, narrow, more_copies],
         "middle",
         *row_parts,
         col_part,
         scaling,
         queries,
     )
-    row_parts, col_part = product(scaled, scaled_copies, gram)
-    (gram,) = simple_call(sum_kernel, [gram_shape], "gram_sum", col_part)
+    row_parts, col_part, gram = product(scaled, scaled_copies, True)
+    (gram,) = simple_call(sum_kernel, [gram_shape], "gram_sum", col_part, gram)
     flat = jax.ShapeDtypeStruct(queries.shape, jnp.float32)
     return tuple(
         simple_call(

time: 125 us -> 114 us (0.912)
  Pallas kernels: 35.7 us -> 28.5 us
  starting transfers between devices: 65.6 us -> 60.3 us
  waiting for transfers between devices: 18.6 us -> 23 us
  local copies, waits for them, and re-layouts: 5.44 us -> 2.21 us
    all_to_all x5, waiting for transfers between devices: 5.59 us -> 10.6 us  [exchange(): return lax.all_to_all(pieces, axis, 0, 0, tiled=True)]
    all_to_all x5, starting transfers between devices: 39.6 us -> 35.9 us  [exchange(): return lax.all_to_all(pieces, axis, 0, 0, tiled=True)]
    pallas_call x4, Pallas kernels: 15.9 us -> 12.5 us  [over_blocks(): pl.pallas_call(kernel, in_specs=[SCALARS, SCALARS, ANYWHERE] + [IN_VMEM]...]
    unnamed x32 -> x10, local copies, waits for them, and re-layouts: 5.44 us -> 2.21 us
    pallas_call x5, Pallas kernels: 11.3 us -> 8.12 us  [simple_call(): pl.pallas_call(kernel, out_shape=shapes, compiler_params=pltpu.CompilerPa...]
    ppermute x18, starting transfers between devices: 26 us -> 24.4 us  [pass_around(): lax.ppermute(pieces[ahead], axis, [(at, (at + ahead) % count) for at in r...]
  transfers between devices with their start and end apart: 23 -> 23, of which waited for: 15 -> 12; matrix products, arithmetic and copies ran while one was open for 0% -> 0% of each run, Pallas kernels for 13% -> 11%
where the time goes in v5:
time: 114 us; the launch traced here: 115 us
  starting transfers between devices  60.3 us (53%)
  Pallas kernels  28.5 us (25%)
  waiting for transfers between devices  23 us (20%)
  local copies, waits for them, and re-layouts  2.21 us (2%)
  between operations  1.4 us (1%)
    all_to_all x5, starting transfers between devices, exchange(): return lax.all_to_all(pieces, axis, 0, 0, tiled=True)  35.9 us
    ppermute x18, starting transfers between devices, pass_around(): lax.ppermute(pieces[ahead], axis, [(at, (at + ahead) % count) for at in r...  24.4 us
    pallas_call x4, Pallas kernels, over_blocks(): pl.pallas_call(kernel, in_specs=[SCALARS, SCALARS, ANYWHERE] + [IN_VMEM]...  12.5 us
    ppermute x18, waiting for transfers between devices, pass_around(): lax.ppermute(pieces[ahead], axis, [(at, (at + ahead) % count) for at in r...  12.4 us
    all_to_all x5, waiting for transfers between devices, exchange(): return lax.all_to_all(pieces, axis, 0, 0, tiled=True)  10.6 us
    pallas_call x5, Pallas kernels, simple_call(): pl.pallas_call(kernel, out_shape=shapes, compiler_params=pltpu.CompilerPa...  8.12 us
    pallas_call x1, Pallas kernels, build_blocks(): pl.pallas_call(functools.partial(build_kernel, row_count), in_specs=[SCAL...  7.84 us
  transfers between devices with their start and end apart: 23, of which 12 were waited for; matrix products, arithmetic and copies ran while one was open for 0% of the time, Pallas kernels for 11%

profile of v5, /device:TPU:0, one launch (start us, length us, event | category | flops | bytes accessed | tf_op | source)
XLA Modules:
  0.0 115.4 jit_solution(15888977889685986562)
XLA Ops:
  1.3 7.8 %build_blocks.1 = (bf16[1024,128,128]{2,1,0:T(8,128)(2,1)}, f32[4,128]{1,0:T(4,128)}, f32[4,128]{1,0:T(4,128)}, f32[4,128]{1,0:T(4,128)}, f32[4,128]{1,0:T(4,128)}, /*index=5*/f32[32,128]{1,0:T(8,128)}) custom-call(s32[1,1,256]{2,1,0:T(1,128)} %spots_ref.9, s32[1,1]{1,0:T(1,128)S(6)} %copy.7.live_ref, s32[256,16,128]{2,1,0:T(8,128)} %bitcast.3, ...), custom_call_target="tpu_custom_call" | custom-call | tf_op jit(solution)/shard_map/build_blocks/pallas_call | solution.py:143
  9.1 11.8 %all-to-all-start = ((f32[8,4,128]{2,1,0:T(4,128)}), f32[8,4,128]{2,1,0:T(4,128)S(1)}, u32[]{:S(2)}, u32[]{:S(2)}) async-start(f32[8,4,128]{2,1,0:T(4,128)} %bitcast.5), calls=%async_computation | async-start | bytes 32768 | tf_op jit(solution)/shard_map/all_to_all | solution.py:511
  20.9 9.5 %collective-permute-start.1 = (f32[4,128]{1,0:T(4,128)}, f32[4,128]{1,0:T(4,128)S(1)}, u32[]{:S(2)}, u32[]{:S(2)}) collective-permute-start(f32[4,128]{1,0:T(4,128)} %get-tuple-element.27), channel_id=1, source_target_pairs={{0,16},{8,24},{16,0},{24,8},{1,17},{9,25},{17,1},{25,9},{2,18},{10... | collective-permute-start | bytes 6152 | tf_op jit(solution)/shard_map/ppermute | solution.py:505
  30.4 1.4 %collective-permute-start.2 = (f32[4,128]{1,0:T(4,128)}, f32[4,128]{1,0:T(4,128)S(1)}, u32[]{:S(2)}, u32[]{:S(2)}) collective-permute-start(f32[4,128]{1,0:T(4,128)} %get-tuple-element.28), channel_id=1, source_target_pairs={{0,24},{8,0},{16,8},{24,16},{1,25},{9,1},{17,9},{25,17},{2,26},{10... | collective-permute-start | bytes 6152 | tf_op jit(solution)/shard_map/ppermute | solution.py:505
  32.2 1.1 collective-permute-done.2.refs_3_
  33.4 0.8 copy-done
  35.6 6.0 %all-to-all-start.1 = ((bf16[8,4,32,128]{3,2,1,0:T(8,128)(2,1)}), bf16[8,4,32,128]{3,2,1,0:T(8,128)(2,1)S(1)}, u32[]{:S(2)}, u32[]{:S(2)}) async-start(bf16[8,4,32,128]{3,2,1,0:T(8,128)(2,1)} %get-tuple-element.30), calls=%async_computation.1 | async-start | bytes 524288 | tf_op jit(solution)/shard_map/all_to_all | solution.py:511
  41.7 1.4 %collective-permute-start.8 = (bf16[4,32,128]{2,1,0:T(8,128)(2,1)S(1)}, bf16[4,32,128]{2,1,0:T(8,128)(2,1)S(1)}, u32[]{:S(2)}, u32[]{:S(2)}) collective-permute-start(bf16[4,32,128]{2,1,0:T(8,128)(2,1)S(1)} %get-tuple-element.35.refs_0_), channel_id=1, source_target_pairs={{0,24},{8,0},{16,8},{24,16},{1,25},{9,1},{17,9},{25,17},{2,26},{10... | collective-permute-start | bytes 98312 | tf_op jit(solution)/shard_map/ppermute | solution.py:505
  43.4 1.3 %collective-permute-done.8.refs_3_ = bf16[4,32,128]{2,1,0:T(8,128)(2,1)S(1)} collective-permute-done((bf16[4,32,128]{2,1,0:T(8,128)(2,1)S(1)}, bf16[4,32,128]{2,1,0:T(8,128)(2,1)S(1)}, u32[]{:S(2)}, u32[]{:S(2)}) %collective-permute-start.8) | collective-permute-done | bytes 32800 | tf_op jit(solution)/shard_map/ppermute | solution.py:505
  44.7 2.4 %collective-permute-done.7.refs_2_ = bf16[4,32,128]{2,1,0:T(8,128)(2,1)S(1)} collective-permute-done((bf16[4,32,128]{2,1,0:T(8,128)(2,1)S(1)}, bf16[4,32,128]{2,1,0:T(8,128)(2,1)S(1)}, u32[]{:S(2)}, u32[]{:S(2)}) %collective-permute-start.7) | collective-permute-done | bytes 32800 | tf_op jit(solution)/shard_map/ppermute | solution.py:505
  47.8 3.9 %backward_product.2 = bf16[8,4,32,128]{3,2,1,0:T(8,128)(2,1)} custom-call(s32[1,1,256]{2,1,0:T(1,128)S(1)} %copy-done.2, s32[1,1]{1,0:T(1,128)S(6)} %copy.7.live_ref, bf16[1024,128,128]{2,1,0:T(8,128)(2,1)} %get-tuple-element.24.block_hbm, bf16[4,32,128]{2,1,0:T(8,128)(2,1)S(1)} %get-tuple-element.35.refs_0_, ...), custom_call_target="tpu_custom_call" | custom-call | flops 268435456 | bytes 8388608 | tf_op jit(solution)/shard_map/backward_product/pallas_call | solution.py:292
  51.7 7.1 %all-to-all-start.2 = ((bf16[8,4,32,128]{3,2,1,0:T(8,128)(2,1)}), bf16[8,4,32,128]{3,2,1,0:T(8,128)(2,1)S(1)}, u32[]{:S(2)}, u32[]{:S(2)}) async-start(bf16[8,4,32,128]{3,2,1,0:T(8,128)(2,1)} %backward_product.2), calls=%async_computation.2 | async-start | bytes 524288 | tf_op jit(solution)/shard_map/all_to_all | solution.py:511
  58.8 2.7 %forward_product.2 = (bf16[4,32,128]{2,1,0:T(8,128)(2,1)S(1)}, bf16[4,32,128]{2,1,0:T(8,128)(2,1)S(1)}, bf16[4,32,128]{2,1,0:T(8,128)(2,1)S(1)}, bf16[4,32,128]{2,1,0:T(8,128)(2,1)S(1)}) custom-call(s32[1,1,256]{2,1,0:T(1,128)S(1)} %copy-done.3, s32[1,1]{1,0:T(1,128)S(6)} %copy.7.live_ref, bf16[1024,128,128]{2,1,0:T(8,128)(2,1)} %get-tuple-element.24.block_hbm, ...), custom_call_target="tpu_custom_call" | custom-call | flops 268435456 | bytes 8388608 | tf_op jit(solution)/shard_map/forward_product/pallas_call | solution.py:292
  61.5 3.2 %collective-permute-start.4 = (bf16[4,32,128]{2,1,0:T(8,128)(2,1)S(1)}, bf16[4,32,128]{2,1,0:T(8,128)(2,1)S(1)}, u32[]{:S(2)}, u32[]{:S(2)}) collective-permute-start(bf16[4,32,128]{2,1,0:T(8,128)(2,1)S(1)} %get-tuple-element.33), channel_id=1, source_target_pairs={{0,16},{8,24},{16,0},{24,8},{1,17},{9,25},{17,1},{25,9},{2,18},{10... | collective-permute-start | bytes 98312 | tf_op jit(solution)/shard_map/ppermute | solution.py:505
  64.7 1.4 %collective-permute-start.5 = (bf16[4,32,128]{2,1,0:T(8,128)(2,1)S(1)}, bf16[4,32,128]{2,1,0:T(8,128)(2,1)S(1)}, u32[]{:S(2)}, u32[]{:S(2)}) collective-permute-start(bf16[4,32,128]{2,1,0:T(8,128)(2,1)S(1)} %get-tuple-element.34), channel_id=1, source_target_pairs={{0,24},{8,0},{16,8},{24,16},{1,25},{9,1},{17,9},{25,17},{2,26},{10... | collective-permute-start | bytes 98312 | tf_op jit(solution)/shard_map/ppermute | solution.py:505
  66.1 1.1 all-to-all-done.2.refs_4_
  67.7 1.4 %middle.1 = (f32[4,32,128]{2,1,0:T(8,128)S(1)}, bf16[4,32,128]{2,1,0:T(8,128)(2,1)S(1)}, bf16[8,7,32,128]{3,2,1,0:T(8,128)(2,1)}) custom-call(bf16[4,32,128]{2,1,0:T(8,128)(2,1)S(1)} %get-tuple-element.31.refs_0_, bf16[4,32,128]{2,1,0:T(8,128)(2,1)S(1)} %collective-permute-done.3.refs_1_, bf16[4,32,128]{2,1,0:T(8,128)(2,1)S(1)} %collective-permute-done.4.refs_2_, ...), custom_call_target="tpu_custom_call" | custom-call | tf_op jit(solution)/shard_map/middle/pallas_call | solution.py:515
  69.0 7.5 %all-to-all-start.3 = ((bf16[8,7,32,128]{3,2,1,0:T(8,128)(2,1)}), bf16[8,7,32,128]{3,2,1,0:T(8,128)(2,1)S(1)}, u32[]{:S(2)}, u32[]{:S(2)}) async-start(bf16[8,7,32,128]{3,2,1,0:T(8,128)(2,1)} %get-tuple-element.37), calls=%async_computation.3 | async-start | bytes 917504 | tf_op jit(solution)/shard_map/all_to_all | solution.py:511
  76.5 1.5 %collective-permute-start.14 = (bf16[4,32,128]{2,1,0:T(8,128)(2,1)S(1)}, bf16[4,32,128]{2,1,0:T(8,128)(2,1)S(1)}, u32[]{:S(2)}, u32[]{:S(2)}) collective-permute-start(bf16[4,32,128]{2,1,0:T(8,128)(2,1)S(1)} %get-tuple-element.42.refs_0_), channel_id=1, source_target_pairs={{0,24},{8,0},{16,8},{24,16},{1,25},{9,1},{17,9},{25,17},{2,26},{10... | collective-permute-start | bytes 98312 | tf_op jit(solution)/shard_map/ppermute | solution.py:505
  78.3 1.3 %collective-permute-done.14.refs_3_ = bf16[4,32,128]{2,1,0:T(8,128)(2,1)S(1)} collective-permute-done((bf16[4,32,128]{2,1,0:T(8,128)(2,1)S(1)}, bf16[4,32,128]{2,1,0:T(8,128)(2,1)S(1)}, u32[]{:S(2)}, u32[]{:S(2)}) %collective-permute-start.14) | collective-permute-done | bytes 32800 | tf_op jit(solution)/shard_map/ppermute | solution.py:505
  79.6 2.4 %collective-permute-done.13.refs_2_ = bf16[4,32,128]{2,1,0:T(8,128)(2,1)S(1)} collective-permute-done((bf16[4,32,128]{2,1,0:T(8,128)(2,1)S(1)}, bf16[4,32,128]{2,1,0:T(8,128)(2,1)S(1)}, u32[]{:S(2)}, u32[]{:S(2)}) %collective-permute-start.13) | collective-permute-done | bytes 32800 | tf_op jit(solution)/shard_map/ppermute | solution.py:505
  82.0 3.2 %backward_product.3.total_ref = bf16[8,4,32,128]{3,2,1,0:T(8,128)(2,1)S(1)} custom-call(s32[1,1,256]{2,1,0:T(1,128)S(1)} %copy-done.3, s32[1,1]{1,0:T(1,128)S(6)} %copy.7.live_ref, bf16[1024,128,128]{2,1,0:T(8,128)(2,1)} %get-tuple-element.24.block_hbm, bf16[4,32,128]{2,1,0:T(8,128)(2,1)S(1)} %get-tuple-element.42.refs_0_, ...), custom_call_target="tpu_custom_call" | custom-call | flops 268435456 | bytes 8388608 | tf_op jit(solution)/shard_map/backward_product/pallas_call | solution.py:292
  85.2 5.0 %all-to-all-done.3.col_dir_ref = bf16[8,7,32,128]{3,2,1,0:T(8,128)(2,1)S(1)} async-done(((bf16[8,7,32,128]{3,2,1,0:T(8,128)(2,1)}), bf16[8,7,32,128]{3,2,1,0:T(8,128)(2,1)S(1)}, u32[]{:S(2)}, u32[]{:S(2)}) %all-to-all-start.3) | async-done | bytes 458784 | tf_op jit(solution)/shard_map/all_to_all | solution.py:511
  90.2 1.2 %attach.1 = (bf16[8,5,32,128]{3,2,1,0:T(8,128)(2,1)}, f32[32,128]{1,0:T(8,128)S(1)}) custom-call(bf16[8,7,32,128]{3,2,1,0:T(8,128)(2,1)S(1)} %all-to-all-done.3.col_dir_ref, bf16[8,4,32,128]{3,2,1,0:T(8,128)(2,1)S(1)} %backward_product.3.total_ref), custom_call_target="tpu_custom_call" | custom-call | tf_op jit(solution)/shard_map/attach/pallas_call | solution.py:515
  91.4 3.6 %all-to-all-start.4 = ((bf16[8,5,32,128]{3,2,1,0:T(8,128)(2,1)}), bf16[8,5,32,128]{3,2,1,0:T(8,128)(2,1)S(1)}, u32[]{:S(2)}, u32[]{:S(2)}) async-start(bf16[8,5,32,128]{3,2,1,0:T(8,128)(2,1)} %get-tuple-element.43), calls=%async_computation.4 | async-start | bytes 655360 | tf_op jit(solution)/shard_map/all_to_all | solution.py:511
  95.0 2.7 %forward_product.3 = (bf16[4,32,128]{2,1,0:T(8,128)(2,1)S(1)}, bf16[4,32,128]{2,1,0:T(8,128)(2,1)S(1)}, bf16[4,32,128]{2,1,0:T(8,128)(2,1)S(1)}, bf16[4,32,128]{2,1,0:T(8,128)(2,1)S(1)}) custom-call(s32[1,1,256]{2,1,0:T(1,128)S(1)} %copy-done.3, s32[1,1]{1,0:T(1,128)S(6)} %copy.7.live_ref, bf16[1024,128,128]{2,1,0:T(8,128)(2,1)} %get-tuple-element.24.block_hbm, ...), custom_call_target="tpu_custom_call" | custom-call | flops 268435456 | bytes 8388608 | tf_op jit(solution)/shard_map/forward_product/pallas_call | solution.py:292
  98.3 2.0 %collective-permute-start.10 = (bf16[4,32,128]{2,1,0:T(8,128)(2,1)S(1)}, bf16[4,32,128]{2,1,0:T(8,128)(2,1)S(1)}, u32[]{:S(2)}, u32[]{:S(2)}) collective-permute-start(bf16[4,32,128]{2,1,0:T(8,128)(2,1)S(1)} %get-tuple-element.40), channel_id=1, source_target_pairs={{0,16},{8,24},{16,0},{24,8},{1,17},{9,25},{17,1},{25,9},{2,18},{10... | collective-permute-start | bytes 98312 | tf_op jit(solution)/shard_map/ppermute | solution.py:505
  101.0 4.5 %all-to-all-done.4.col_ref.refs_8_ = bf16[8,5,32,128]{3,2,1,0:T(8,128)(2,1)S(1)} async-done(((bf16[8,5,32,128]{3,2,1,0:T(8,128)(2,1)}), bf16[8,5,32,128]{3,2,1,0:T(8,128)(2,1)S(1)}, u32[]{:S(2)}, u32[]{:S(2)}) %all-to-all-start.4) | async-done | bytes 327712 | tf_op jit(solution)/shard_map/all_to_all | solution.py:511
  105.7 1.9 %collective-permute-start.16 = (f32[32,128]{1,0:T(8,128)S(1)}, f32[32,128]{1,0:T(8,128)S(1)}, u32[]{:S(2)}, u32[]{:S(2)}) collective-permute-start(f32[32,128]{1,0:T(8,128)S(1)} %gram_sum.1.refs_4_), channel_id=1, source_target_pairs={{0,16},{8,24},{16,0},{24,8},{1,17},{9,25},{17,1},{25,9},{2,18},{10... | collective-permute-start | bytes 49160 | tf_op jit(solution)/shard_map/ppermute | solution.py:505
  107.8 1.7 %collective-permute-done.16.refs_6_ = f32[32,128]{1,0:T(8,128)S(1)} collective-permute-done((f32[32,128]{1,0:T(8,128)S(1)}, f32[32,128]{1,0:T(8,128)S(1)}, u32[]{:S(2)}, u32[]{:S(2)}) %collective-permute-start.16) | collective-permute-done | bytes 16416 | tf_op jit(solution)/shard_map/ppermute | solution.py:505
  109.5 1.3 %collective-permute-done.15.refs_5_ = f32[32,128]{1,0:T(8,128)S(1)} collective-permute-done((f32[32,128]{1,0:T(8,128)S(1)}, f32[32,128]{1,0:T(8,128)S(1)}, u32[]{:S(2)}, u32[]{:S(2)}) %collective-permute-start.15) | collective-permute-done | bytes 16416 | tf_op jit(solution)/shard_map/ppermute | solution.py:505
  110.8 4.7 %close.1 = (f32[32,512]{1,0:T(8,128)}, f32[32,512]{1,0:T(8,128)}) custom-call(bf16[4,32,128]{2,1,0:T(8,128)(2,1)S(1)} %get-tuple-element.38.refs_0_, bf16[4,32,128]{2,1,0:T(8,128)(2,1)S(1)} %collective-permute-done.9.refs_1_, bf16[4,32,128]{2,1,0:T(8,128)(2,1)S(1)} %collective-permute-done.10.refs_2_, ...), custom_call_target="tpu_custom_call" | custom-call | tf_op jit(solution)/shard_map/close/pallas_call | solution.py:515
  (34 shorter events, 5.4 us)
Async XLA Ops:
  0.6 58.1 %copy-start.3 = (s32[1,1,256]{2,1,0:T(1,128)S(1)}, s32[1,1,256]{2,1,0:T(1,128)}, u32[]{:S(2)}) copy-start(s32[1,1,256]{2,1,0:T(1,128)} %spots_ref.9) | copy-start | bytes 3076
  9.1 24.2 %all-to-all-start = ((f32[8,4,128]{2,1,0:T(4,128)}), f32[8,4,128]{2,1,0:T(4,128)S(1)}, u32[]{:S(2)}, u32[]{:S(2)}) async-start(f32[8,4,128]{2,1,0:T(4,128)} %bitcast.5), calls=%async_computation | async-start | bytes 32768 | tf_op jit(solution)/shard_map/all_to_all | solution.py:511
  20.9 10.9 %collective-permute-start = (f32[4,128]{1,0:T(4,128)}, f32[4,128]{1,0:T(4,128)S(1)}, u32[]{:S(2)}, u32[]{:S(2)}) collective-permute-start(f32[4,128]{1,0:T(4,128)} %get-tuple-element.26), channel_id=1, source_target_pairs={{0,8},{8,16},{16,24},{24,0},{1,9},{9,17},{17,25},{25,1},{2,10},{10... | collective-permute-start | bytes 6152 | tf_op jit(solution)/shard_map/ppermute | solution.py:505
  20.9 11.3 %collective-permute-start.1 = (f32[4,128]{1,0:T(4,128)}, f32[4,128]{1,0:T(4,128)S(1)}, u32[]{:S(2)}, u32[]{:S(2)}) collective-permute-start(f32[4,128]{1,0:T(4,128)} %get-tuple-element.27), channel_id=1, source_target_pairs={{0,16},{8,24},{16,0},{24,8},{1,17},{9,25},{17,1},{25,9},{2,18},{10... | collective-permute-start | bytes 6152 | tf_op jit(solution)/shard_map/ppermute | solution.py:505
  30.4 2.9 %collective-permute-start.2 = (f32[4,128]{1,0:T(4,128)}, f32[4,128]{1,0:T(4,128)S(1)}, u32[]{:S(2)}, u32[]{:S(2)}) collective-permute-start(f32[4,128]{1,0:T(4,128)} %get-tuple-element.28), channel_id=1, source_target_pairs={{0,24},{8,0},{16,8},{24,16},{1,25},{9,1},{17,9},{25,17},{2,26},{10... | collective-permute-start | bytes 6152 | tf_op jit(solution)/shard_map/ppermute | solution.py:505
  33.4 0.8 copy-start
  34.2 0.7 copy-start.4
  35.6 16.1 %all-to-all-start.1 = ((bf16[8,4,32,128]{3,2,1,0:T(8,128)(2,1)}), bf16[8,4,32,128]{3,2,1,0:T(8,128)(2,1)S(1)}, u32[]{:S(2)}, u32[]{:S(2)}) async-start(bf16[8,4,32,128]{3,2,1,0:T(8,128)(2,1)} %get-tuple-element.30), calls=%async_computation.1 | async-start | bytes 524288 | tf_op jit(solution)/shard_map/all_to_all | solution.py:511
  41.7 3.0 %collective-permute-start.8 = (bf16[4,32,128]{2,1,0:T(8,128)(2,1)S(1)}, bf16[4,32,128]{2,1,0:T(8,128)(2,1)S(1)}, u32[]{:S(2)}, u32[]{:S(2)}) collective-permute-start(bf16[4,32,128]{2,1,0:T(8,128)(2,1)S(1)} %get-tuple-element.35.refs_0_), channel_id=1, source_target_pairs={{0,24},{8,0},{16,8},{24,16},{1,25},{9,1},{17,9},{25,17},{2,26},{10... | collective-permute-start | bytes 98312 | tf_op jit(solution)/shard_map/ppermute | solution.py:505
  43.1 4.0 %collective-permute-start.7 = (bf16[4,32,128]{2,1,0:T(8,128)(2,1)S(1)}, bf16[4,32,128]{2,1,0:T(8,128)(2,1)S(1)}, u32[]{:S(2)}, u32[]{:S(2)}) collective-permute-start(bf16[4,32,128]{2,1,0:T(8,128)(2,1)S(1)} %get-tuple-element.35.refs_0_), channel_id=1, source_target_pairs={{0,16},{8,24},{16,0},{24,8},{1,17},{9,25},{17,1},{25,9},{2,18},{10... | collective-permute-start | bytes 98312 | tf_op jit(solution)/shard_map/ppermute | solution.py:505
  43.4 3.7 %collective-permute-start.6 = (bf16[4,32,128]{2,1,0:T(8,128)(2,1)S(1)}, bf16[4,32,128]{2,1,0:T(8,128)(2,1)S(1)}, u32[]{:S(2)}, u32[]{:S(2)}) collective-permute-start(bf16[4,32,128]{2,1,0:T(8,128)(2,1)S(1)} %get-tuple-element.35.refs_0_), channel_id=1, source_target_pairs={{0,8},{8,16},{16,24},{24,0},{1,9},{9,17},{17,25},{25,1},{2,10},{10... | collective-permute-start | bytes 98312 | tf_op jit(solution)/shard_map/ppermute | solution.py:505
  47.1 0.7 copy-start.2
  47.7 19.9 %copy-start.1 = (f32[32,512]{1,0:T(8,128)S(1)}, f32[32,512]{1,0:T(8,128)}, u32[]{:S(2)}) copy-start(f32[32,512]{1,0:T(8,128)} %refs_10_.1) | copy-start | bytes 196612
  51.7 15.5 %all-to-all-start.2 = ((bf16[8,4,32,128]{3,2,1,0:T(8,128)(2,1)}), bf16[8,4,32,128]{3,2,1,0:T(8,128)(2,1)S(1)}, u32[]{:S(2)}, u32[]{:S(2)}) async-start(bf16[8,4,32,128]{3,2,1,0:T(8,128)(2,1)} %backward_product.2), calls=%async_computation.2 | async-start | bytes 524288 | tf_op jit(solution)/shard_map/all_to_all | solution.py:511
  61.5 5.7 %collective-permute-start.3 = (bf16[4,32,128]{2,1,0:T(8,128)(2,1)S(1)}, bf16[4,32,128]{2,1,0:T(8,128)(2,1)S(1)}, u32[]{:S(2)}, u32[]{:S(2)}) collective-permute-start(bf16[4,32,128]{2,1,0:T(8,128)(2,1)S(1)} %get-tuple-element.32), channel_id=1, source_target_pairs={{0,8},{8,16},{16,24},{24,0},{1,9},{9,17},{17,25},{25,1},{2,10},{10... | collective-permute-start | bytes 98312 | tf_op jit(solution)/shard_map/ppermute | solution.py:505
  61.5 5.6 %collective-permute-start.4 = (bf16[4,32,128]{2,1,0:T(8,128)(2,1)S(1)}, bf16[4,32,128]{2,1,0:T(8,128)(2,1)S(1)}, u32[]{:S(2)}, u32[]{:S(2)}) collective-permute-start(bf16[4,32,128]{2,1,0:T(8,128)(2,1)S(1)} %get-tuple-element.33), channel_id=1, source_target_pairs={{0,16},{8,24},{16,0},{24,8},{1,17},{9,25},{17,1},{25,9},{2,18},{10... | collective-permute-start | bytes 98312 | tf_op jit(solution)/shard_map/ppermute | solution.py:505
  64.7 3.0 %collective-permute-start.5 = (bf16[4,32,128]{2,1,0:T(8,128)(2,1)S(1)}, bf16[4,32,128]{2,1,0:T(8,128)(2,1)S(1)}, u32[]{:S(2)}, u32[]{:S(2)}) collective-permute-start(bf16[4,32,128]{2,1,0:T(8,128)(2,1)S(1)} %get-tuple-element.34), channel_id=1, source_target_pairs={{0,24},{8,0},{16,8},{24,16},{1,25},{9,1},{17,9},{25,17},{2,26},{10... | collective-permute-start | bytes 98312 | tf_op jit(solution)/shard_map/ppermute | solution.py:505
  69.0 21.1 %all-to-all-start.3 = ((bf16[8,7,32,128]{3,2,1,0:T(8,128)(2,1)}), bf16[8,7,32,128]{3,2,1,0:T(8,128)(2,1)S(1)}, u32[]{:S(2)}, u32[]{:S(2)}) async-start(bf16[8,7,32,128]{3,2,1,0:T(8,128)(2,1)} %get-tuple-element.37), calls=%async_computation.3 | async-start | bytes 917504 | tf_op jit(solution)/shard_map/all_to_all | solution.py:511
  76.5 3.1 %collective-permute-start.14 = (bf16[4,32,128]{2,1,0:T(8,128)(2,1)S(1)}, bf16[4,32,128]{2,1,0:T(8,128)(2,1)S(1)}, u32[]{:S(2)}, u32[]{:S(2)}) collective-permute-start(bf16[4,32,128]{2,1,0:T(8,128)(2,1)S(1)} %get-tuple-element.42.refs_0_), channel_id=1, source_target_pairs={{0,24},{8,0},{16,8},{24,16},{1,25},{9,1},{17,9},{25,17},{2,26},{10... | collective-permute-start | bytes 98312 | tf_op jit(solution)/shard_map/ppermute | solution.py:505
  78.0 4.0 %collective-permute-start.13 = (bf16[4,32,128]{2,1,0:T(8,128)(2,1)S(1)}, bf16[4,32,128]{2,1,0:T(8,128)(2,1)S(1)}, u32[]{:S(2)}, u32[]{:S(2)}) collective-permute-start(bf16[4,32,128]{2,1,0:T(8,128)(2,1)S(1)} %get-tuple-element.42.refs_0_), channel_id=1, source_target_pairs={{0,16},{8,24},{16,0},{24,8},{1,17},{9,25},{17,1},{25,9},{2,18},{10... | collective-permute-start | bytes 98312 | tf_op jit(solution)/shard_map/ppermute | solution.py:505
  78.3 3.7 %collective-permute-start.12 = (bf16[4,32,128]{2,1,0:T(8,128)(2,1)S(1)}, bf16[4,32,128]{2,1,0:T(8,128)(2,1)S(1)}, u32[]{:S(2)}, u32[]{:S(2)}) collective-permute-start(bf16[4,32,128]{2,1,0:T(8,128)(2,1)S(1)} %get-tuple-element.42.refs_0_), channel_id=1, source_target_pairs={{0,8},{8,16},{16,24},{24,0},{1,9},{9,17},{17,25},{25,1},{2,10},{10... | collective-permute-start | bytes 98312 | tf_op jit(solution)/shard_map/ppermute | solution.py:505
  91.4 14.1 %all-to-all-start.4 = ((bf16[8,5,32,128]{3,2,1,0:T(8,128)(2,1)}), bf16[8,5,32,128]{3,2,1,0:T(8,128)(2,1)S(1)}, u32[]{:S(2)}, u32[]{:S(2)}) async-start(bf16[8,5,32,128]{3,2,1,0:T(8,128)(2,1)} %get-tuple-element.43), calls=%async_computation.4 | async-start | bytes 655360 | tf_op jit(solution)/shard_map/all_to_all | solution.py:511
  97.7 9.9 %collective-permute-start.9 = (bf16[4,32,128]{2,1,0:T(8,128)(2,1)S(1)}, bf16[4,32,128]{2,1,0:T(8,128)(2,1)S(1)}, u32[]{:S(2)}, u32[]{:S(2)}) collective-permute-start(bf16[4,32,128]{2,1,0:T(8,128)(2,1)S(1)} %get-tuple-element.39), channel_id=1, source_target_pairs={{0,8},{8,16},{16,24},{24,0},{1,9},{9,17},{17,25},{25,1},{2,10},{10... | collective-permute-start | bytes 98312 | tf_op jit(solution)/shard_map/ppermute | solution.py:505
  98.3 9.5 %collective-permute-start.10 = (bf16[4,32,128]{2,1,0:T(8,128)(2,1)S(1)}, bf16[4,32,128]{2,1,0:T(8,128)(2,1)S(1)}, u32[]{:S(2)}, u32[]{:S(2)}) collective-permute-start(bf16[4,32,128]{2,1,0:T(8,128)(2,1)S(1)} %get-tuple-element.40), channel_id=1, source_target_pairs={{0,16},{8,24},{16,0},{24,8},{1,17},{9,25},{17,1},{25,9},{2,18},{10... | collective-permute-start | bytes 98312 | tf_op jit(solution)/shard_map/ppermute | solution.py:505
  100.3 7.5 %collective-permute-start.11 = (bf16[4,32,128]{2,1,0:T(8,128)(2,1)S(1)}, bf16[4,32,128]{2,1,0:T(8,128)(2,1)S(1)}, u32[]{:S(2)}, u32[]{:S(2)}) collective-permute-start(bf16[4,32,128]{2,1,0:T(8,128)(2,1)S(1)} %get-tuple-element.41), channel_id=1, source_target_pairs={{0,24},{8,0},{16,8},{24,16},{1,25},{9,1},{17,9},{25,17},{2,26},{10... | collective-permute-start | bytes 98312 | tf_op jit(solution)/shard_map/ppermute | solution.py:505
  105.7 2.1 %collective-permute-start.17 = (f32[32,128]{1,0:T(8,128)S(1)}, f32[32,128]{1,0:T(8,128)S(1)}, u32[]{:S(2)}, u32[]{:S(2)}) collective-permute-start(f32[32,128]{1,0:T(8,128)S(1)} %gram_sum.1.refs_4_), channel_id=1, source_target_pairs={{0,24},{8,0},{16,8},{24,16},{1,25},{9,1},{17,9},{25,17},{2,26},{10... | collective-permute-start | bytes 49160 | tf_op jit(solution)/shard_map/ppermute | solution.py:505
  105.7 3.8 %collective-permute-start.16 = (f32[32,128]{1,0:T(8,128)S(1)}, f32[32,128]{1,0:T(8,128)S(1)}, u32[]{:S(2)}, u32[]{:S(2)}) collective-permute-start(f32[32,128]{1,0:T(8,128)S(1)} %gram_sum.1.refs_4_), channel_id=1, source_target_pairs={{0,16},{8,24},{16,0},{24,8},{1,17},{9,25},{17,1},{25,9},{2,18},{10... | collective-permute-start | bytes 49160 | tf_op jit(solution)/shard_map/ppermute | solution.py:505
  107.6 3.2 %collective-permute-start.15 = (f32[32,128]{1,0:T(8,128)S(1)}, f32[32,128]{1,0:T(8,128)S(1)}, u32[]{:S(2)}, u32[]{:S(2)}) collective-permute-start(f32[32,128]{1,0:T(8,128)S(1)} %gram_sum.1.refs_4_), channel_id=1, source_target_pairs={{0,8},{8,16},{16,24},{24,0},{1,9},{9,17},{17,25},{25,1},{2,10},{10... | collective-permute-start | bytes 49160 | tf_op jit(solution)/shard_map/ppermute | solution.py:505

commit v6 on v5

--- a/solution.py
+++ b/solution.py
@@ -53,19 +53,22 @@
     return pltpu.make_async_copy(source.at[window], target.at[window], sems.at[index])
 
 
-def build_kernel(row_count, spots_ref, live_ref, index_hbm, value_hbm, block_hbm, *refs):
-    row_outs = refs[:row_count]
+def build_kernel(spots_ref, live_ref, index_hbm, value_hbm, block_hbm, flipped_hbm, *refs):
     (
+        *row_outs,
         col_out_ref,
         index_ref,
         value_ref,
         block_ref,
+        flipped_ref,
         row_ref,
         col_ref,
         index_sems,
         value_sems,
         block_sems,
-    ) = refs[row_count:]
+        flipped_sems,
+    ) = refs
+    row_count = len(row_outs) + 1
     per_seg = row_outs[0].shape[0]
     col_blocks = col_out_ref.shape[0]
     groups = group_count(live_ref, BATCH) * (BATCH // GROUP)
@@ -79,7 +82,10 @@
     row_ref[...] = jnp.zeros_like(row_ref)
     col_ref[...] = jnp.zeros_like(col_ref)
     rows_16 = lax.broadcasted_iota(jnp.int32, (16, 128), 0)
-    ones = jnp.ones((128, 128), jnp.bfloat16)
+    diagonal = lax.broadcasted_iota(jnp.int32, (128, 128), 0) == lax.broadcasted_iota(
+        jnp.int32, (128, 128), 1
+    )
+    identity = jnp.where(diagonal, 1.0, 0.0).astype(jnp.bfloat16)
     zero = jnp.zeros((16, 128), jnp.bfloat16)
 
     def build_group(index, _):
@@ -107,25 +113,29 @@
             block = jnp.concatenate(sums, axis=0)
             block_ref[slot] = block
             row_ref[row_block] += value_f32[:8] + value_f32[8:]
-            col_ref[col_block] += dot_plain(block, ones)
+            turned = dot_across(identity, block)
+            flipped_ref[slot] = turned.astype(jnp.bfloat16)
+            col_ref[col_block] += jnp.sum(turned.reshape(16, 8, 128), axis=0)
         group_copy(block_ref, block_hbm, block_sems, index, GROUP).start()
+        group_copy(flipped_ref, flipped_hbm, flipped_sems, index, GROUP).start()
         return 0
 
     lax.fori_loop(0, groups, build_group, 0)
-    for ahead, out in enumerate(row_outs):
+    for ahead, out in enumerate(row_outs, 1):
         first = lax.rem(lax.axis_index("row") + ahead, row_count) * per_seg
         for part in range(per_seg):
             out[part : part + 1] = jnp.sum(row_ref[first + part], axis=0, keepdims=True)
-    diagonal = lax.broadcasted_iota(jnp.int32, (128, 128), 0) == lax.broadcasted_iota(
-        jnp.int32, (128, 128), 1
-    )
+    for part in range(per_seg):
+        own = lax.axis_index("col") * per_seg + part
+        col_ref[own] += row_ref[lax.axis_index("row") * per_seg + part]
     for col_block in range(col_blocks):
         col_out_ref[col_block : col_block + 1] = jnp.sum(
-            jnp.where(diagonal, col_ref[col_block], 0.0), axis=0, keepdims=True
+            col_ref[col_block], axis=0, keepdims=True
         )
 
     def finish_copies(index, _):
         group_copy(block_ref, block_hbm, block_sems, index, GROUP).wait()
+        group_copy(flipped_ref, flipped_hbm, flipped_sems, index, GROUP).wait()
         return 0
 
     lax.fori_loop(0, groups, finish_copies, 0)
@@ -139,19 +149,21 @@
 def build_blocks(spots, live, index_table, value_table, row_count, col_count, per_seg):
     slots = index_table.shape[0]
     groups = slots // GROUP
-    sum_shapes = [(per_seg, 128)] * row_count + [(col_count * per_seg, 128)]
+    sum_shapes = [(per_seg, 128)] * (row_count - 1) + [(col_count * per_seg, 128)]
     return pl.pallas_call(
-        functools.partial(build_kernel, row_count),
+        build_kernel,
         in_specs=[SCALARS, SCALARS, ANYWHERE, ANYWHERE],
-        out_specs=[ANYWHERE] + [IN_VMEM] * len(sum_shapes),
-        out_shape=[jax.ShapeDtypeStruct((SPARE * slots, 128, 128), jnp.bfloat16)]
+        out_specs=[ANYWHERE] * 2 + [IN_VMEM] * len(sum_shapes),
+        out_shape=[jax.ShapeDtypeStruct((SPARE * slots, 128, 128), jnp.bfloat16)] * 2
         + [jax.ShapeDtypeStruct(shape, jnp.float32) for shape in sum_shapes],
         scratch_shapes=[
             pltpu.VMEM(index_table.shape, index_table.dtype),
             pltpu.VMEM(value_table.shape, value_table.dtype),
             pltpu.VMEM((slots, 128, 128), jnp.bfloat16),
+            pltpu.VMEM((slots, 128, 128), jnp.bfloat16),
             pltpu.VMEM((row_count * per_seg, 8, 128), jnp.float32),
-            pltpu.VMEM((col_count * per_seg, 128, 128), jnp.float32),
+            pltpu.VMEM((col_count * per_seg, 8, 128), jnp.float32),
+            pltpu.SemaphoreType.DMA((groups,)),
             pltpu.SemaphoreType.DMA((groups,)),
             pltpu.SemaphoreType.DMA((groups,)),
             pltpu.SemaphoreType.DMA((groups,)),
@@ -179,11 +191,11 @@
     lax.fori_loop(0, groups, one_group, 0)
 
 
-def add_products(dot, places, first_slot, block_ref, direction, total_refs):
+def add_products(places, first_slot, block_ref, direction, total_refs):
     sums = []
     for inside in range(BATCH):
         slot = first_slot + inside
-        sums.append(dot(direction(places(slot)[0]), block_ref[slot]))
+        sums.append(dot_plain(direction(places(slot)[0]), block_ref[slot]))
     for inside in range(BATCH):
         total_ref = total_refs[inside % len(total_refs)]
         total_ref[places(first_slot + inside)[1]] += sums[inside]
@@ -209,7 +221,6 @@
 
     def run_group(first_slot):
         add_products(
-            dot_across,
             lambda slot: place_of(spots_ref, slot, col_blocks),
             first_slot,
             block_ref,
@@ -271,7 +282,6 @@
 
     def run_group(first_slot):
         add_products(
-            dot_plain,
             lambda slot: place_of(spots_ref, slot, col_blocks)[::-1],
             first_slot,
             block_ref,
@@ -351,7 +361,7 @@
 
 
 def start_kernel(*refs):
-    *row_refs, col_ref, query_ref, scaling_ref, scaled_ref, copies_ref = refs
+    *row_refs, col_ref, query_ref, scaling_ref, scaled_ref = refs
     degree = 1.0 + 0.5 * total_of([ref[...] for ref in [*row_refs, *leading(col_ref)]])
     scaling = 1.0 / jnp.sqrt(degree)
     scaling_ref[...] = scaling
@@ -360,8 +370,6 @@
             scaling[part : part + 1] * query_ref[:, part * 128 : part * 128 + 128]
         ).astype(jnp.bfloat16)
         scaled_ref[part] = scaled
-        for copy in range(copies_ref.shape[0]):
-            copies_ref[copy, part] = scaled
 
 
 def scaled_sum(row_refs, col_ref, scaling_ref, part):
@@ -371,7 +379,7 @@
 
 
 def middle_kernel(*refs):
-    *row_refs, col_ref, scaling_ref, query_ref, first_ref, scaled_ref, copies_ref = refs
+    *row_refs, col_ref, scaling_ref, query_ref, first_ref, scaled_ref, sent_ref = refs
     size = query_ref.shape[0]
     pair_gram = jnp.zeros((2 * size, 128), jnp.float32)
     for part in range(scaling_ref.shape[0]):
@@ -379,16 +387,14 @@
         first_ref[part] = first
         scaled = (scaling_ref[part : part + 1] * first).astype(jnp.bfloat16)
         scaled_ref[part] = scaled
-        for copy in range(copies_ref.shape[0]):
-            copies_ref[copy, part] = scaled
+        sent_ref[part] = scaled
         pair = jnp.concatenate(
             [query_ref[:, part * 128 : part * 128 + 128], first], axis=0
         )
         pair_gram += exact_across(pair, tall(pair))
     grams = beside(pair_gram[:size], pltpu.roll(window(pair_gram[size:], 1), size, 1))
     for term, values in enumerate(in_terms(grams)):
-        for copy in range(copies_ref.shape[0]):
-            copies_ref[copy, scaling_ref.shape[0] + term] = values
+        sent_ref[scaling_ref.shape[0] + term] = values
 
 
 def tall(flat):
@@ -536,27 +542,26 @@
     piece = (per_seg, query_rows, 128)
     wide = jax.ShapeDtypeStruct(piece, jnp.float32)
     narrow = jax.ShapeDtypeStruct(piece, jnp.bfloat16)
-    copies = jax.ShapeDtypeStruct((col_count,) + piece, jnp.bfloat16)
     gram_shape = jax.ShapeDtypeStruct((query_rows, 128), jnp.float32)
 
-    blocks, *row_sums, col_sums = build_blocks(
+    blocks, flipped_blocks, *row_sums, col_sums = build_blocks(
         *places, neighbor_cols[0, 0], neighbor_sims[0, 0], row_count, col_count, per_seg
     )
     col_part = exchange(col_sums.reshape(col_count, per_seg, 128), "col")
-    row_parts = pass_around(row_sums, "row")
-    scaling, scaled, scaled_copies = simple_call(
+    row_parts = pass_around([None, *row_sums], "row")[1:]
+    scaling, scaled = simple_call(
         start_kernel,
-        [jax.ShapeDtypeStruct((per_seg, 128), jnp.float32), narrow, copies],
+        [jax.ShapeDtypeStruct((per_seg, 128), jnp.float32), narrow],
         "start",
         *row_parts,
         col_part,
         queries,
     )
 
-    def product(vectors, vector_copies, with_grams):
-        col_dirs = exchange(vector_copies, "col")
+    def product(vectors, sent, with_grams):
         row_pieces = pass_around([vectors] * row_count, "row")
-        total = backward_product(places, blocks, row_pieces, col_count)
+        col_dirs = exchange(jnp.broadcast_to(sent[None], (col_count,) + sent.shape), "col")
+        total = backward_product(places, flipped_blocks, row_pieces, col_count)
         gram = None
         if with_grams:
             message = jax.ShapeDtypeStruct((col_count, per_seg + 1) + piece[1:], jnp.bfloat16)
@@ -567,20 +572,18 @@
         totals = forward_product(places, blocks, col_dirs, row_count, piece)
         return pass_around(totals, "row"), col_part, gram
 
-    row_parts, col_part, _ = product(scaled, scaled_copies, False)
-    more_copies = jax.ShapeDtypeStruct(
-        (col_count, per_seg + GRAM_TERMS) + piece[1:], jnp.bfloat16
-    )
-    first, scaled, scaled_copies = simple_call(
+    row_parts, col_part, _ = product(scaled, scaled, False)
+    more = jax.ShapeDtypeStruct((per_seg + GRAM_TERMS,) + piece[1:], jnp.bfloat16)
+    first, scaled, sent = simple_call(
         middle_kernel,
-        [wide, narrow, more_copies],
+        [wide, narrow, more],
         "middle",
         *row_parts,
         col_part,
         scaling,
         queries,
     )
-    row_parts, col_part, gram = product(scaled, scaled_copies, True)
+    row_parts, col_part, gram = product(scaled, sent, True)
     (gram,) = simple_call(sum_kernel, [gram_shape], "gram_sum", col_part, gram)
     flat = jax.ShapeDtypeStruct(queries.shape, jnp.float32)
     return tuple(

time: 114 us -> 112 us (0.982); the launches traced: 115 us -> 111 us
  starting transfers between devices: 60.3 us -> 47.4 us
  Pallas kernels: 28.5 us -> 34.9 us
  waiting for transfers between devices: 23 us -> 24.3 us
    all_to_all x5, starting transfers between devices: 35.9 us -> 25.7 us  [exchange(): return lax.all_to_all(pieces, axis, 0, 0, tiled=True)]
    pallas_call x1, Pallas kernels: 7.84 us -> 13.7 us  [build_blocks(): pl.pallas_call(build_kernel, in_specs=[SCALARS, SCALARS, ANYWHERE, ANYWHE...]
    ppermute x18, starting transfers between devices: 24.4 us -> 21.6 us  [pass_around(): lax.ppermute(pieces[ahead], axis, [(at, (at + ahead) % count) for at in r...]
    pallas_call x4, Pallas kernels: 12.5 us -> 14.6 us  [over_blocks(): pl.pallas_call(kernel, in_specs=[SCALARS, SCALARS, ANYWHERE] + [IN_VMEM]...]
    all_to_all x5, waiting for transfers between devices: 10.6 us -> 12.4 us  [exchange(): return lax.all_to_all(pieces, axis, 0, 0, tiled=True)]
    broadcast_in_dim x0 -> x2, local copies, waits for them, and re-layouts: none -> 1.63 us  [product(): jnp.broadcast_to(sent[None], (col_count,) + sent.shape)]
    pallas_call x5, Pallas kernels: 8.12 us -> 6.58 us  [simple_call(): pl.pallas_call(kernel, out_shape=shapes, compiler_params=pltpu.CompilerPa...]
  transfers between devices with their start and end apart: 23 -> 23, of which waited for: 12 -> 12; matrix products, arithmetic and copies ran while one was open for 0% -> 0% of each run, Pallas kernels for 11% -> 13%
where the time goes in v6:
time: 112 us; the launch traced here: 111 us
  starting transfers between devices  47.4 us (42%)
  Pallas kernels  34.9 us (31%)
  waiting for transfers between devices  24.3 us (22%)
  local copies, waits for them, and re-layouts  3.16 us (3%)
  between operations  1.42 us (1%)
    all_to_all x5, starting transfers between devices, exchange(): return lax.all_to_all(pieces, axis, 0, 0, tiled=True)  25.7 us
    ppermute x18, starting transfers between devices, pass_around(): lax.ppermute(pieces[ahead], axis, [(at, (at + ahead) % count) for at in r...  21.6 us
    pallas_call x4, Pallas kernels, over_blocks(): pl.pallas_call(kernel, in_specs=[SCALARS, SCALARS, ANYWHERE] + [IN_VMEM]...  14.6 us
    pallas_call x1, Pallas kernels, build_blocks(): pl.pallas_call(build_kernel, in_specs=[SCALARS, SCALARS, ANYWHERE, ANYWHE...  13.7 us
    all_to_all x5, waiting for transfers between devices, exchange(): return lax.all_to_all(pieces, axis, 0, 0, tiled=True)  12.4 us
    ppermute x18, waiting for transfers between devices, pass_around(): lax.ppermute(pieces[ahead], axis, [(at, (at + ahead) % count) for at in r...  11.8 us
    pallas_call x5, Pallas kernels, simple_call(): pl.pallas_call(kernel, out_shape=shapes, compiler_params=pltpu.CompilerPa...  6.58 us
  transfers between devices with their start and end apart: 23, of which 12 were waited for; matrix products, arithmetic and copies ran while one was open for 0% of the time, Pallas kernels for 13%

profile of v6, /device:TPU:0, one launch (start us, length us, event | category | flops | bytes accessed | tf_op | source)
XLA Modules:
  0.0 111.1 jit_solution(4056661339410671751)
XLA Ops:
  1.3 13.7 %build_blocks.1 = (bf16[1024,128,128]{2,1,0:T(8,128)(2,1)}, bf16[1024,128,128]{2,1,0:T(8,128)(2,1)}, f32[4,128]{1,0:T(4,128)}, f32[4,128]{1,0:T(4,128)}, f32[4,128]{1,0:T(4,128)}, /*index=5*/f32[32,128]{1,0:T(8,128)}) custom-call(s32[1,1,256]{2,1,0:T(1,128)} %spots_ref.9, s32[1,1]{1,0:T(1,128)S(6)} %copy.7.live_ref, s32[256,16,128]{2,1,0:T(8,128)} %bitcast.3, ...), custom_call_target="tpu_custom_call" | custom-call | tf_op jit(solution)/shard_map/build_blocks/pallas_call | solution.py:153
  15.1 6.3 %all-to-all-start = ((f32[8,4,128]{2,1,0:T(4,128)}), f32[8,4,128]{2,1,0:T(4,128)S(1)}, u32[]{:S(2)}, u32[]{:S(2)}) async-start(f32[8,4,128]{2,1,0:T(4,128)} %bitcast.5), calls=%async_computation | async-start | bytes 32768 | tf_op jit(solution)/shard_map/all_to_all | solution.py:517
  21.3 11.2 %collective-permute-start.1 = (f32[4,128]{1,0:T(4,128)}, f32[4,128]{1,0:T(4,128)S(1)}, u32[]{:S(2)}, u32[]{:S(2)}) collective-permute-start(f32[4,128]{1,0:T(4,128)} %get-tuple-element.25), channel_id=1, source_target_pairs={{0,16},{8,24},{16,0},{24,8},{1,17},{9,25},{17,1},{25,9},{2,18},{10... | collective-permute-start | bytes 6152 | tf_op jit(solution)/shard_map/ppermute | solution.py:511
  32.5 1.1 collective-permute-done.refs_0_
  34.3 0.8 copy-done
  35.9 5.7 %all-to-all-start.1 = ((bf16[8,4,32,128]{3,2,1,0:T(8,128)(2,1)}), bf16[8,4,32,128]{3,2,1,0:T(8,128)(2,1)S(1)}, u32[]{:S(2)}, u32[]{:S(2)}) async-start(bf16[8,4,32,128]{3,2,1,0:T(8,128)(2,1)} %broadcast_in_dim.4), calls=%async_computation.1 | async-start | bytes 524288 | tf_op jit(solution)/shard_map/all_to_all | solution.py:517
  41.7 1.5 %collective-permute-start.8 = (bf16[4,32,128]{2,1,0:T(8,128)(2,1)S(1)}, bf16[4,32,128]{2,1,0:T(8,128)(2,1)S(1)}, u32[]{:S(2)}, u32[]{:S(2)}) collective-permute-start(bf16[4,32,128]{2,1,0:T(8,128)(2,1)S(1)} %get-tuple-element.28.refs_0_), channel_id=1, source_target_pairs={{0,24},{8,0},{16,8},{24,16},{1,25},{9,1},{17,9},{25,17},{2,26},{10... | collective-permute-start | bytes 98312 | tf_op jit(solution)/shard_map/ppermute | solution.py:511
  43.1 1.1 collective-permute-start.7
  44.8 2.2 %collective-permute-done.7.refs_2_ = bf16[4,32,128]{2,1,0:T(8,128)(2,1)S(1)} collective-permute-done((bf16[4,32,128]{2,1,0:T(8,128)(2,1)S(1)}, bf16[4,32,128]{2,1,0:T(8,128)(2,1)S(1)}, u32[]{:S(2)}, u32[]{:S(2)}) %collective-permute-start.7) | collective-permute-done | bytes 32800 | tf_op jit(solution)/shard_map/ppermute | solution.py:511
  48.2 4.2 %backward_product.2 = bf16[8,4,32,128]{3,2,1,0:T(8,128)(2,1)} custom-call(s32[1,1,256]{2,1,0:T(1,128)S(1)} %copy-done.2, s32[1,1]{1,0:T(1,128)S(6)} %copy.7.live_ref, bf16[1024,128,128]{2,1,0:T(8,128)(2,1)} %get-tuple-element.33.block_hbm, bf16[4,32,128]{2,1,0:T(8,128)(2,1)S(1)} %get-tuple-element.28.refs_0_, ...), custom_call_target="tpu_custom_call" | custom-call | flops 268435456 | bytes 8388608 | tf_op jit(solution)/shard_map/backward_product/pallas_call | solution.py:302
  52.4 4.9 %all-to-all-start.2 = ((bf16[8,4,32,128]{3,2,1,0:T(8,128)(2,1)}), bf16[8,4,32,128]{3,2,1,0:T(8,128)(2,1)S(1)}, u32[]{:S(2)}, u32[]{:S(2)}) async-start(bf16[8,4,32,128]{3,2,1,0:T(8,128)(2,1)} %backward_product.2), calls=%async_computation.2 | async-start | bytes 524288 | tf_op jit(solution)/shard_map/all_to_all | solution.py:517
  57.4 3.5 %forward_product.2 = (bf16[4,32,128]{2,1,0:T(8,128)(2,1)S(1)}, bf16[4,32,128]{2,1,0:T(8,128)(2,1)S(1)}, bf16[4,32,128]{2,1,0:T(8,128)(2,1)S(1)}, bf16[4,32,128]{2,1,0:T(8,128)(2,1)S(1)}) custom-call(s32[1,1,256]{2,1,0:T(1,128)S(1)} %copy-done.3, s32[1,1]{1,0:T(1,128)S(6)} %copy.7.live_ref, bf16[1024,128,128]{2,1,0:T(8,128)(2,1)} %get-tuple-element.23.block_hbm, ...), custom_call_target="tpu_custom_call" | custom-call | flops 268435456 | bytes 8388608 | tf_op jit(solution)/shard_map/forward_product/pallas_call | solution.py:302
  60.9 1.2 %collective-permute-start.4 = (bf16[4,32,128]{2,1,0:T(8,128)(2,1)S(1)}, bf16[4,32,128]{2,1,0:T(8,128)(2,1)S(1)}, u32[]{:S(2)}, u32[]{:S(2)}) collective-permute-start(bf16[4,32,128]{2,1,0:T(8,128)(2,1)S(1)} %get-tuple-element.31), channel_id=1, source_target_pairs={{0,16},{8,24},{16,0},{24,8},{1,17},{9,25},{17,1},{25,9},{2,18},{10... | collective-permute-start | bytes 98312 | tf_op jit(solution)/shard_map/ppermute | solution.py:511
  62.1 0.8 collective-permute-start.5
  62.9 2.8 %all-to-all-done.2.refs_4_ = bf16[8,4,32,128]{3,2,1,0:T(8,128)(2,1)S(1)} async-done(((bf16[8,4,32,128]{3,2,1,0:T(8,128)(2,1)}), bf16[8,4,32,128]{3,2,1,0:T(8,128)(2,1)S(1)}, u32[]{:S(2)}, u32[]{:S(2)}) %all-to-all-start.2) | async-done | bytes 262176 | tf_op jit(solution)/shard_map/all_to_all | solution.py:517
  66.3 0.9 broadcast_in_dim.5
  67.2 5.2 %all-to-all-start.3 = ((bf16[8,7,32,128]{3,2,1,0:T(8,128)(2,1)}), bf16[8,7,32,128]{3,2,1,0:T(8,128)(2,1)S(1)}, u32[]{:S(2)}, u32[]{:S(2)}) async-start(bf16[8,7,32,128]{3,2,1,0:T(8,128)(2,1)} %broadcast_in_dim.5), calls=%async_computation.3 | async-start | bytes 917504 | tf_op jit(solution)/shard_map/all_to_all | solution.py:517
  72.3 1.5 %collective-permute-start.14 = (bf16[4,32,128]{2,1,0:T(8,128)(2,1)S(1)}, bf16[4,32,128]{2,1,0:T(8,128)(2,1)S(1)}, u32[]{:S(2)}, u32[]{:S(2)}) collective-permute-start(bf16[4,32,128]{2,1,0:T(8,128)(2,1)S(1)} %get-tuple-element.40.refs_0_), channel_id=1, source_target_pairs={{0,24},{8,0},{16,8},{24,16},{1,25},{9,1},{17,9},{25,17},{2,26},{10... | collective-permute-start | bytes 98312 | tf_op jit(solution)/shard_map/ppermute | solution.py:511
  74.4 1.0 collective-permute-done.14.refs_3_
  75.4 2.7 %collective-permute-done.13.refs_2_ = bf16[4,32,128]{2,1,0:T(8,128)(2,1)S(1)} collective-permute-done((bf16[4,32,128]{2,1,0:T(8,128)(2,1)S(1)}, bf16[4,32,128]{2,1,0:T(8,128)(2,1)S(1)}, u32[]{:S(2)}, u32[]{:S(2)}) %collective-permute-start.13) | collective-permute-done | bytes 32800 | tf_op jit(solution)/shard_map/ppermute | solution.py:511
  78.1 3.5 %backward_product.3.total_ref = bf16[8,4,32,128]{3,2,1,0:T(8,128)(2,1)S(1)} custom-call(s32[1,1,256]{2,1,0:T(1,128)S(1)} %copy-done.3, s32[1,1]{1,0:T(1,128)S(6)} %copy.7.live_ref, bf16[1024,128,128]{2,1,0:T(8,128)(2,1)} %get-tuple-element.33.block_hbm, bf16[4,32,128]{2,1,0:T(8,128)(2,1)S(1)} %get-tuple-element.40.refs_0_, ...), custom_call_target="tpu_custom_call" | custom-call | flops 268435456 | bytes 8388608 | tf_op jit(solution)/shard_map/backward_product/pallas_call | solution.py:302
  81.6 4.7 %all-to-all-done.3.col_dir_ref = bf16[8,7,32,128]{3,2,1,0:T(8,128)(2,1)S(1)} async-done(((bf16[8,7,32,128]{3,2,1,0:T(8,128)(2,1)}), bf16[8,7,32,128]{3,2,1,0:T(8,128)(2,1)S(1)}, u32[]{:S(2)}, u32[]{:S(2)}) %all-to-all-start.3) | async-done | bytes 458784 | tf_op jit(solution)/shard_map/all_to_all | solution.py:517
  86.3 1.2 %attach.1 = (bf16[8,5,32,128]{3,2,1,0:T(8,128)(2,1)}, f32[32,128]{1,0:T(8,128)S(1)}) custom-call(bf16[8,7,32,128]{3,2,1,0:T(8,128)(2,1)S(1)} %all-to-all-done.3.col_dir_ref, bf16[8,4,32,128]{3,2,1,0:T(8,128)(2,1)S(1)} %backward_product.3.total_ref), custom_call_target="tpu_custom_call" | custom-call | tf_op jit(solution)/shard_map/attach/pallas_call | solution.py:521
  87.5 3.6 %all-to-all-start.4 = ((bf16[8,5,32,128]{3,2,1,0:T(8,128)(2,1)}), bf16[8,5,32,128]{3,2,1,0:T(8,128)(2,1)S(1)}, u32[]{:S(2)}, u32[]{:S(2)}) async-start(bf16[8,5,32,128]{3,2,1,0:T(8,128)(2,1)} %get-tuple-element.41), calls=%async_computation.4 | async-start | bytes 655360 | tf_op jit(solution)/shard_map/all_to_all | solution.py:517
  91.1 3.5 %forward_product.3 = (bf16[4,32,128]{2,1,0:T(8,128)(2,1)S(1)}, bf16[4,32,128]{2,1,0:T(8,128)(2,1)S(1)}, bf16[4,32,128]{2,1,0:T(8,128)(2,1)S(1)}, bf16[4,32,128]{2,1,0:T(8,128)(2,1)S(1)}) custom-call(s32[1,1,256]{2,1,0:T(1,128)S(1)} %copy-done.3, s32[1,1]{1,0:T(1,128)S(6)} %copy.7.live_ref, bf16[1024,128,128]{2,1,0:T(8,128)(2,1)} %get-tuple-element.23.block_hbm, ...), custom_call_target="tpu_custom_call" | custom-call | flops 268435456 | bytes 8388608 | tf_op jit(solution)/shard_map/forward_product/pallas_call | solution.py:302
  94.6 1.2 %collective-permute-start.10 = (bf16[4,32,128]{2,1,0:T(8,128)(2,1)S(1)}, bf16[4,32,128]{2,1,0:T(8,128)(2,1)S(1)}, u32[]{:S(2)}, u32[]{:S(2)}) collective-permute-start(bf16[4,32,128]{2,1,0:T(8,128)(2,1)S(1)} %get-tuple-element.38), channel_id=1, source_target_pairs={{0,16},{8,24},{16,0},{24,8},{1,17},{9,25},{17,1},{25,9},{2,18},{10... | collective-permute-start | bytes 98312 | tf_op jit(solution)/shard_map/ppermute | solution.py:511
  95.8 0.9 collective-permute-start.11
  96.7 4.9 %all-to-all-done.4.col_ref.refs_8_ = bf16[8,5,32,128]{3,2,1,0:T(8,128)(2,1)S(1)} async-done(((bf16[8,5,32,128]{3,2,1,0:T(8,128)(2,1)}), bf16[8,5,32,128]{3,2,1,0:T(8,128)(2,1)S(1)}, u32[]{:S(2)}, u32[]{:S(2)}) %all-to-all-start.4) | async-done | bytes 327712 | tf_op jit(solution)/shard_map/all_to_all | solution.py:517
  101.8 1.5 %collective-permute-start.16 = (f32[32,128]{1,0:T(8,128)S(1)}, f32[32,128]{1,0:T(8,128)S(1)}, u32[]{:S(2)}, u32[]{:S(2)}) collective-permute-start(f32[32,128]{1,0:T(8,128)S(1)} %gram_sum.1.refs_4_), channel_id=1, source_target_pairs={{0,16},{8,24},{16,0},{24,8},{1,17},{9,25},{17,1},{25,9},{2,18},{10... | collective-permute-start | bytes 49160 | tf_op jit(solution)/shard_map/ppermute | solution.py:511
  103.4 2.1 %collective-permute-done.16.refs_6_ = f32[32,128]{1,0:T(8,128)S(1)} collective-permute-done((f32[32,128]{1,0:T(8,128)S(1)}, f32[32,128]{1,0:T(8,128)S(1)}, u32[]{:S(2)}, u32[]{:S(2)}) %collective-permute-start.16) | collective-permute-done | bytes 16416 | tf_op jit(solution)/shard_map/ppermute | solution.py:511
  105.6 0.8 collective-permute-done.15.refs_5_
  106.4 4.7 %close.1 = (f32[32,512]{1,0:T(8,128)}, f32[32,512]{1,0:T(8,128)}) custom-call(bf16[4,32,128]{2,1,0:T(8,128)(2,1)S(1)} %get-tuple-element.36.refs_0_, bf16[4,32,128]{2,1,0:T(8,128)(2,1)S(1)} %collective-permute-done.9.refs_1_, bf16[4,32,128]{2,1,0:T(8,128)(2,1)S(1)} %collective-permute-done.10.refs_2_, ...), custom_call_target="tpu_custom_call" | custom-call | tf_op jit(solution)/shard_map/close/pallas_call | solution.py:521
  (34 shorter events, 4.9 us)
Async XLA Ops:
  0.6 56.7 %copy-start.3 = (s32[1,1,256]{2,1,0:T(1,128)S(1)}, s32[1,1,256]{2,1,0:T(1,128)}, u32[]{:S(2)}) copy-start(s32[1,1,256]{2,1,0:T(1,128)} %spots_ref.9) | copy-start | bytes 3076
  15.1 19.3 %all-to-all-start = ((f32[8,4,128]{2,1,0:T(4,128)}), f32[8,4,128]{2,1,0:T(4,128)S(1)}, u32[]{:S(2)}, u32[]{:S(2)}) async-start(f32[8,4,128]{2,1,0:T(4,128)} %bitcast.5), calls=%async_computation | async-start | bytes 32768 | tf_op jit(solution)/shard_map/all_to_all | solution.py:517
  21.3 12.3 %collective-permute-start = (f32[4,128]{1,0:T(4,128)}, f32[4,128]{1,0:T(4,128)S(1)}, u32[]{:S(2)}, u32[]{:S(2)}) collective-permute-start(f32[4,128]{1,0:T(4,128)} %get-tuple-element.24), channel_id=1, source_target_pairs={{0,8},{8,16},{16,24},{24,0},{1,9},{9,17},{17,25},{25,1},{2,10},{10... | collective-permute-start | bytes 6152 | tf_op jit(solution)/shard_map/ppermute | solution.py:511
  21.3 13.0 %collective-permute-start.1 = (f32[4,128]{1,0:T(4,128)}, f32[4,128]{1,0:T(4,128)S(1)}, u32[]{:S(2)}, u32[]{:S(2)}) collective-permute-start(f32[4,128]{1,0:T(4,128)} %get-tuple-element.25), channel_id=1, source_target_pairs={{0,16},{8,24},{16,0},{24,8},{1,17},{9,25},{17,1},{25,9},{2,18},{10... | collective-permute-start | bytes 6152 | tf_op jit(solution)/shard_map/ppermute | solution.py:511
  32.5 1.8 %collective-permute-start.2 = (f32[4,128]{1,0:T(4,128)}, f32[4,128]{1,0:T(4,128)S(1)}, u32[]{:S(2)}, u32[]{:S(2)}) collective-permute-start(f32[4,128]{1,0:T(4,128)} %get-tuple-element.26), channel_id=1, source_target_pairs={{0,24},{8,0},{16,8},{24,16},{1,25},{9,1},{17,9},{25,17},{2,26},{10... | collective-permute-start | bytes 6152 | tf_op jit(solution)/shard_map/ppermute | solution.py:511
  34.3 0.8 copy-start
  35.9 16.5 %all-to-all-start.1 = ((bf16[8,4,32,128]{3,2,1,0:T(8,128)(2,1)}), bf16[8,4,32,128]{3,2,1,0:T(8,128)(2,1)S(1)}, u32[]{:S(2)}, u32[]{:S(2)}) async-start(bf16[8,4,32,128]{3,2,1,0:T(8,128)(2,1)} %broadcast_in_dim.4), calls=%async_computation.1 | async-start | bytes 524288 | tf_op jit(solution)/shard_map/all_to_all | solution.py:517
  41.7 3.1 %collective-permute-start.8 = (bf16[4,32,128]{2,1,0:T(8,128)(2,1)S(1)}, bf16[4,32,128]{2,1,0:T(8,128)(2,1)S(1)}, u32[]{:S(2)}, u32[]{:S(2)}) collective-permute-start(bf16[4,32,128]{2,1,0:T(8,128)(2,1)S(1)} %get-tuple-element.28.refs_0_), channel_id=1, source_target_pairs={{0,24},{8,0},{16,8},{24,16},{1,25},{9,1},{17,9},{25,17},{2,26},{10... | collective-permute-start | bytes 98312 | tf_op jit(solution)/shard_map/ppermute | solution.py:511
  43.1 3.9 %collective-permute-start.7 = (bf16[4,32,128]{2,1,0:T(8,128)(2,1)S(1)}, bf16[4,32,128]{2,1,0:T(8,128)(2,1)S(1)}, u32[]{:S(2)}, u32[]{:S(2)}) collective-permute-start(bf16[4,32,128]{2,1,0:T(8,128)(2,1)S(1)} %get-tuple-element.28.refs_0_), channel_id=1, source_target_pairs={{0,16},{8,24},{16,0},{24,8},{1,17},{9,25},{17,1},{25,9},{2,18},{10... | collective-permute-start | bytes 98312 | tf_op jit(solution)/shard_map/ppermute | solution.py:511
  44.2 3.3 %collective-permute-start.6 = (bf16[4,32,128]{2,1,0:T(8,128)(2,1)S(1)}, bf16[4,32,128]{2,1,0:T(8,128)(2,1)S(1)}, u32[]{:S(2)}, u32[]{:S(2)}) collective-permute-start(bf16[4,32,128]{2,1,0:T(8,128)(2,1)S(1)} %get-tuple-element.28.refs_0_), channel_id=1, source_target_pairs={{0,8},{8,16},{16,24},{24,0},{1,9},{9,17},{17,25},{25,1},{2,10},{10... | collective-permute-start | bytes 98312 | tf_op jit(solution)/shard_map/ppermute | solution.py:511
  47.5 0.7 copy-start.2
  48.2 17.6 %copy-start.1 = (f32[32,512]{1,0:T(8,128)S(1)}, f32[32,512]{1,0:T(8,128)}, u32[]{:S(2)}) copy-start(f32[32,512]{1,0:T(8,128)} %refs_10_.1) | copy-start | bytes 196612
  52.4 13.3 %all-to-all-start.2 = ((bf16[8,4,32,128]{3,2,1,0:T(8,128)(2,1)}), bf16[8,4,32,128]{3,2,1,0:T(8,128)(2,1)S(1)}, u32[]{:S(2)}, u32[]{:S(2)}) async-start(bf16[8,4,32,128]{3,2,1,0:T(8,128)(2,1)} %backward_product.2), calls=%async_computation.2 | async-start | bytes 524288 | tf_op jit(solution)/shard_map/all_to_all | solution.py:517
  60.8 4.9 %collective-permute-start.3 = (bf16[4,32,128]{2,1,0:T(8,128)(2,1)S(1)}, bf16[4,32,128]{2,1,0:T(8,128)(2,1)S(1)}, u32[]{:S(2)}, u32[]{:S(2)}) collective-permute-start(bf16[4,32,128]{2,1,0:T(8,128)(2,1)S(1)} %get-tuple-element.30), channel_id=1, source_target_pairs={{0,8},{8,16},{16,24},{24,0},{1,9},{9,17},{17,25},{25,1},{2,10},{10... | collective-permute-start | bytes 98312 | tf_op jit(solution)/shard_map/ppermute | solution.py:511
  60.9 4.9 %collective-permute-start.4 = (bf16[4,32,128]{2,1,0:T(8,128)(2,1)S(1)}, bf16[4,32,128]{2,1,0:T(8,128)(2,1)S(1)}, u32[]{:S(2)}, u32[]{:S(2)}) collective-permute-start(bf16[4,32,128]{2,1,0:T(8,128)(2,1)S(1)} %get-tuple-element.31), channel_id=1, source_target_pairs={{0,16},{8,24},{16,0},{24,8},{1,17},{9,25},{17,1},{25,9},{2,18},{10... | collective-permute-start | bytes 98312 | tf_op jit(solution)/shard_map/ppermute | solution.py:511
  62.1 3.7 %collective-permute-start.5 = (bf16[4,32,128]{2,1,0:T(8,128)(2,1)S(1)}, bf16[4,32,128]{2,1,0:T(8,128)(2,1)S(1)}, u32[]{:S(2)}, u32[]{:S(2)}) collective-permute-start(bf16[4,32,128]{2,1,0:T(8,128)(2,1)S(1)} %get-tuple-element.32), channel_id=1, source_target_pairs={{0,24},{8,0},{16,8},{24,16},{1,25},{9,1},{17,9},{25,17},{2,26},{10... | collective-permute-start | bytes 98312 | tf_op jit(solution)/shard_map/ppermute | solution.py:511
  67.2 19.1 %all-to-all-start.3 = ((bf16[8,7,32,128]{3,2,1,0:T(8,128)(2,1)}), bf16[8,7,32,128]{3,2,1,0:T(8,128)(2,1)S(1)}, u32[]{:S(2)}, u32[]{:S(2)}) async-start(bf16[8,7,32,128]{3,2,1,0:T(8,128)(2,1)} %broadcast_in_dim.5), calls=%async_computation.3 | async-start | bytes 917504 | tf_op jit(solution)/shard_map/all_to_all | solution.py:517
  72.3 3.1 %collective-permute-start.14 = (bf16[4,32,128]{2,1,0:T(8,128)(2,1)S(1)}, bf16[4,32,128]{2,1,0:T(8,128)(2,1)S(1)}, u32[]{:S(2)}, u32[]{:S(2)}) collective-permute-start(bf16[4,32,128]{2,1,0:T(8,128)(2,1)S(1)} %get-tuple-element.40.refs_0_), channel_id=1, source_target_pairs={{0,24},{8,0},{16,8},{24,16},{1,25},{9,1},{17,9},{25,17},{2,26},{10... | collective-permute-start | bytes 98312 | tf_op jit(solution)/shard_map/ppermute | solution.py:511
  73.8 4.3 %collective-permute-start.13 = (bf16[4,32,128]{2,1,0:T(8,128)(2,1)S(1)}, bf16[4,32,128]{2,1,0:T(8,128)(2,1)S(1)}, u32[]{:S(2)}, u32[]{:S(2)}) collective-permute-start(bf16[4,32,128]{2,1,0:T(8,128)(2,1)S(1)} %get-tuple-element.40.refs_0_), channel_id=1, source_target_pairs={{0,16},{8,24},{16,0},{24,8},{1,17},{9,25},{17,1},{25,9},{2,18},{10... | collective-permute-start | bytes 98312 | tf_op jit(solution)/shard_map/ppermute | solution.py:511
  74.4 3.7 %collective-permute-start.12 = (bf16[4,32,128]{2,1,0:T(8,128)(2,1)S(1)}, bf16[4,32,128]{2,1,0:T(8,128)(2,1)S(1)}, u32[]{:S(2)}, u32[]{:S(2)}) collective-permute-start(bf16[4,32,128]{2,1,0:T(8,128)(2,1)S(1)} %get-tuple-element.40.refs_0_), channel_id=1, source_target_pairs={{0,8},{8,16},{16,24},{24,0},{1,9},{9,17},{17,25},{25,1},{2,10},{10... | collective-permute-start | bytes 98312 | tf_op jit(solution)/shard_map/ppermute | solution.py:511
  87.5 14.1 %all-to-all-start.4 = ((bf16[8,5,32,128]{3,2,1,0:T(8,128)(2,1)}), bf16[8,5,32,128]{3,2,1,0:T(8,128)(2,1)S(1)}, u32[]{:S(2)}, u32[]{:S(2)}) async-start(bf16[8,5,32,128]{3,2,1,0:T(8,128)(2,1)} %get-tuple-element.41), calls=%async_computation.4 | async-start | bytes 655360 | tf_op jit(solution)/shard_map/all_to_all | solution.py:517
  94.6 8.7 %collective-permute-start.9 = (bf16[4,32,128]{2,1,0:T(8,128)(2,1)S(1)}, bf16[4,32,128]{2,1,0:T(8,128)(2,1)S(1)}, u32[]{:S(2)}, u32[]{:S(2)}) collective-permute-start(bf16[4,32,128]{2,1,0:T(8,128)(2,1)S(1)} %get-tuple-element.37), channel_id=1, source_target_pairs={{0,8},{8,16},{16,24},{24,0},{1,9},{9,17},{17,25},{25,1},{2,10},{10... | collective-permute-start | bytes 98312 | tf_op jit(solution)/shard_map/ppermute | solution.py:511
  94.6 8.8 %collective-permute-start.10 = (bf16[4,32,128]{2,1,0:T(8,128)(2,1)S(1)}, bf16[4,32,128]{2,1,0:T(8,128)(2,1)S(1)}, u32[]{:S(2)}, u32[]{:S(2)}) collective-permute-start(bf16[4,32,128]{2,1,0:T(8,128)(2,1)S(1)} %get-tuple-element.38), channel_id=1, source_target_pairs={{0,16},{8,24},{16,0},{24,8},{1,17},{9,25},{17,1},{25,9},{2,18},{10... | collective-permute-start | bytes 98312 | tf_op jit(solution)/shard_map/ppermute | solution.py:511
  95.8 7.6 %collective-permute-start.11 = (bf16[4,32,128]{2,1,0:T(8,128)(2,1)S(1)}, bf16[4,32,128]{2,1,0:T(8,128)(2,1)S(1)}, u32[]{:S(2)}, u32[]{:S(2)}) collective-permute-start(bf16[4,32,128]{2,1,0:T(8,128)(2,1)S(1)} %get-tuple-element.39), channel_id=1, source_target_pairs={{0,24},{8,0},{16,8},{24,16},{1,25},{9,1},{17,9},{25,17},{2,26},{10... | collective-permute-start | bytes 98312 | tf_op jit(solution)/shard_map/ppermute | solution.py:511
  101.8 1.7 %collective-permute-start.17 = (f32[32,128]{1,0:T(8,128)S(1)}, f32[32,128]{1,0:T(8,128)S(1)}, u32[]{:S(2)}, u32[]{:S(2)}) collective-permute-start(f32[32,128]{1,0:T(8,128)S(1)} %gram_sum.1.refs_4_), channel_id=1, source_target_pairs={{0,24},{8,0},{16,8},{24,16},{1,25},{9,1},{17,9},{25,17},{2,26},{10... | collective-permute-start | bytes 49160 | tf_op jit(solution)/shard_map/ppermute | solution.py:511
  101.8 3.8 %collective-permute-start.16 = (f32[32,128]{1,0:T(8,128)S(1)}, f32[32,128]{1,0:T(8,128)S(1)}, u32[]{:S(2)}, u32[]{:S(2)}) collective-permute-start(f32[32,128]{1,0:T(8,128)S(1)} %gram_sum.1.refs_4_), channel_id=1, source_target_pairs={{0,16},{8,24},{16,0},{24,8},{1,17},{9,25},{17,1},{25,9},{2,18},{10... | collective-permute-start | bytes 49160 | tf_op jit(solution)/shard_map/ppermute | solution.py:511
  103.3 3.2 %collective-permute-start.15 = (f32[32,128]{1,0:T(8,128)S(1)}, f32[32,128]{1,0:T(8,128)S(1)}, u32[]{:S(2)}, u32[]{:S(2)}) collective-permute-start(f32[32,128]{1,0:T(8,128)S(1)} %gram_sum.1.refs_4_), channel_id=1, source_target_pairs={{0,8},{8,16},{16,24},{24,0},{1,9},{9,17},{17,25},{25,1},{2,10},{10... | collective-permute-start | bytes 49160 | tf_op jit(solution)/shard_map/ppermute | solution.py:511

commit v7 on v6

--- a/solution.py
+++ b/solution.py
@@ -11,7 +11,6 @@
 GROUP = 16
 BATCH = 32
 SPARE = 4
-GRAM_TERMS = 3
 PANEL = 8
 BUILD_GRANT = 60 * 1024 * 1024
 PRODUCT_GRANT = 40 * 1024 * 1024
@@ -53,10 +52,14 @@
     return pltpu.make_async_copy(source.at[window], target.at[window], sems.at[index])
 
 
-def build_kernel(spots_ref, live_ref, index_hbm, value_hbm, block_hbm, flipped_hbm, *refs):
+def build_kernel(
+    spots_ref, live_ref, index_hbm, value_hbm, query_hbm, block_hbm, flipped_hbm, *refs
+):
     (
         *row_outs,
         col_out_ref,
+        gram_ref,
+        query_ref,
         index_ref,
         value_ref,
         block_ref,
@@ -67,6 +70,7 @@
         value_sems,
         block_sems,
         flipped_sems,
+        query_sem,
     ) = refs
     row_count = len(row_outs) + 1
     per_seg = row_outs[0].shape[0]
@@ -78,6 +82,8 @@
         group_copy(value_hbm, value_ref, value_sems, index, GROUP).start()
         return 0
 
+    query_copy = pltpu.make_async_copy(query_hbm, query_ref, query_sem)
+    query_copy.start()
     lax.fori_loop(0, groups, start_copies, 0)
     row_ref[...] = jnp.zeros_like(row_ref)
     col_ref[...] = jnp.zeros_like(col_ref)
@@ -92,33 +98,45 @@
         group_copy(index_hbm, index_ref, index_sems, index, GROUP).wait()
         group_copy(value_hbm, value_ref, value_sems, index, GROUP).wait()
         targets = [(rows_16 + 16 * part).astype(jnp.int16) for part in range(8)]
-        for inside in range(GROUP):
-            slot = index * GROUP + inside
-            row_block, col_block = place_of(spots_ref, slot, col_blocks)
-            active = (slot < live_ref[0, 0]).astype(jnp.float32)
-            index_i32 = index_ref[slot]
-            value_f32 = value_ref[slot].astype(jnp.float32) * active
-            sums = [zero] * 8
-            for entry in range(16):
-                index_row = jnp.broadcast_to(index_i32[entry : entry + 1], (16, 128)).astype(
-                    jnp.int16
-                )
-                value_row = jnp.broadcast_to(value_f32[entry : entry + 1], (16, 128)).astype(
-                    jnp.bfloat16
-                )
-                for part in range(8):
-                    sums[part] = sums[part] + jnp.where(
-                        index_row == targets[part], value_row, zero
-                    )
-            block = jnp.concatenate(sums, axis=0)
-            block_ref[slot] = block
-            row_ref[row_block] += value_f32[:8] + value_f32[8:]
-            turned = dot_across(identity, block)
-            flipped_ref[slot] = turned.astype(jnp.bfloat16)
-            col_ref[col_block] += jnp.sum(turned.reshape(16, 8, 128), axis=0)
+        for inside in range(0, GROUP, 2):
+            slots = [index * GROUP + inside, index * GROUP + inside + 1]
+            tables = []
+            for slot in slots:
+                active = (slot < live_ref[0, 0]).astype(jnp.float32)
+                tables.append((index_ref[slot], value_ref[slot].astype(jnp.float32) * active))
+            sums = [[zero] * 8 for _ in slots]
+            for entry in range(0, 16, 2):
+                for which, (indices, values) in enumerate(tables):
+                    pair = []
+                    for at in (entry, entry + 1):
+                        index_row = jnp.broadcast_to(indices[at : at + 1], (16, 128))
+                        value_row = jnp.broadcast_to(values[at : at + 1], (16, 128))
+                        pair.append((index_row.astype(jnp.int16), value_row.astype(jnp.bfloat16)))
+                    for part in range(8):
+                        first, second = [
+                            jnp.where(index_row == targets[part], value_row, zero)
+                            for index_row, value_row in pair
+                        ]
+                        sums[which][part] = sums[which][part] + (first + second)
+            for slot, (_, values), parts in zip(slots, tables, sums):
+                row_block, col_block = place_of(spots_ref, slot, col_blocks)
+                block = jnp.concatenate(parts, axis=0)
+                block_ref[slot] = block
+                row_ref[row_block] += values[:8] + values[8:]
+                turned = dot_across(identity, block)
+                flipped_ref[slot] = turned.astype(jnp.bfloat16)
+                col_ref[col_block] += jnp.sum(turned.reshape(16, 8, 128), axis=0)
         group_copy(block_ref, block_hbm, block_sems, index, GROUP).start()
         group_copy(flipped_ref, flipped_hbm, flipped_sems, index, GROUP).start()
         return 0
+
+    query_copy.wait()
+    size = query_ref.shape[0]
+    gram = jnp.zeros((size, 128), jnp.float32)
+    for part in range(per_seg):
+        query = query_ref[:, part * 128 : part * 128 + 128]
+        gram += exact_across(query, tall(query))
+    gram_ref[...] = side_by_side(in_terms(gram, 3))
 
     lax.fori_loop(0, groups, build_group, 0)
     for ahead, out in enumerate(row_outs, 1):
@@ -146,17 +164,22 @@
 IN_VMEM = pl.BlockSpec(memory_space=pltpu.VMEM)
 
 
-def build_blocks(spots, live, index_table, value_table, row_count, col_count, per_seg):
+def build_blocks(
+    spots, live, index_table, value_table, queries, row_count, col_count, per_seg
+):
     slots = index_table.shape[0]
     groups = slots // GROUP
     sum_shapes = [(per_seg, 128)] * (row_count - 1) + [(col_count * per_seg, 128)]
+    gram_shape = (queries.shape[0], 128)
     return pl.pallas_call(
         build_kernel,
-        in_specs=[SCALARS, SCALARS, ANYWHERE, ANYWHERE],
-        out_specs=[ANYWHERE] * 2 + [IN_VMEM] * len(sum_shapes),
+        in_specs=[SCALARS, SCALARS, ANYWHERE, ANYWHERE, ANYWHERE],
+        out_specs=[ANYWHERE] * 2 + [IN_VMEM] * (len(sum_shapes) + 1),
         out_shape=[jax.ShapeDtypeStruct((SPARE * slots, 128, 128), jnp.bfloat16)] * 2
-        + [jax.ShapeDtypeStruct(shape, jnp.float32) for shape in sum_shapes],
+        + [jax.ShapeDtypeStruct(shape, jnp.float32) for shape in sum_shapes]
+        + [jax.ShapeDtypeStruct(gram_shape, jnp.bfloat16)],
         scratch_shapes=[
+            pltpu.VMEM(queries.shape, queries.dtype),
             pltpu.VMEM(index_table.shape, index_table.dtype),
             pltpu.VMEM(value_table.shape, value_table.dtype),
             pltpu.VMEM((slots, 128, 128), jnp.bfloat16),
@@ -167,10 +190,11 @@
             pltpu.SemaphoreType.DMA((groups,)),
             pltpu.SemaphoreType.DMA((groups,)),
             pltpu.SemaphoreType.DMA((groups,)),
+            pltpu.SemaphoreType.DMA(()),
         ],
         compiler_params=pltpu.CompilerParams(vmem_limit_bytes=BUILD_GRANT),
         name="build_blocks",
-    )(spots, live, index_table, value_table)
+    )(spots, live, index_table, value_table, queries)
 
 
 def each_group(live_ref, block_hbm, block_ref, sems, prepare, run_group):
@@ -229,46 +253,57 @@
         )
 
     each_group(live_ref, block_hbm, block_ref, sems, prepare, run_group)
+    size = even_ref.shape[1]
     for segment in range(col_out_ref.shape[0]):
         for part in range(per_seg):
             col_block = segment * per_seg + part
             values = even_ref[col_block] + odd_ref[col_block]
-            col_out_ref[segment, part] = values.astype(col_out_ref.dtype)
-
-
-def in_terms(values):
+            col_out_ref[segment, part * size : part * size + size] = values.astype(
+                col_out_ref.dtype
+            )
+
+
+def in_terms(values, count):
     terms = []
-    for _ in range(GRAM_TERMS):
+    for _ in range(count):
         terms.append(values.astype(jnp.bfloat16))
         values = values - terms[-1].astype(jnp.float32)
     return terms
 
 
-def attach_kernel(col_dir_ref, total_ref, message_ref, gram_ref):
-    col_count, per_seg, size, _ = total_ref.shape
+def side_by_side(terms, width=32):
+    total = terms[0].astype(jnp.float32)
+    for place, term in enumerate(terms[1:], 1):
+        total = total + pltpu.roll(term.astype(jnp.float32), place * width, 1)
+    return total.astype(jnp.bfloat16)
+
+
+def attach_kernel(first_dir_ref, col_dir_ref, total_ref, message_ref, gram_ref):
+    col_count, sent, size, _ = col_dir_ref.shape
+    per_seg = sent - 1
 
     def add_segment(segment, gram):
         for part in range(per_seg):
-            values = total_ref[segment, part]
-            message_ref[segment, part] = values
+            rows = slice(part * size, part * size + size)
+            values = total_ref[segment, rows]
+            message_ref[segment, rows] = values
             gram += dot_across(values, tall(col_dir_ref[segment, part]))
         return gram
 
     gram = lax.fori_loop(
         0, col_count, add_segment, jnp.zeros((size, 128), jnp.float32), unroll=4
     )
-    together = jnp.zeros((size, 128), jnp.float32)
-    for term, values in enumerate(in_terms(gram)):
-        together = together + pltpu.roll(values.astype(jnp.float32), term * size, 1)
+    half = size // 2
+    terms = side_by_side(in_terms(gram, 2)).astype(jnp.float32)
+    folded = terms[:half] + pltpu.roll(terms[half:], 64, 1)
     for segment in range(col_count):
-        message_ref[segment, per_seg] = together.astype(message_ref.dtype)
-    gram_ref[...] = total_of(
-        [
-            col_dir_ref[segment, per_seg + term]
-            for term in range(GRAM_TERMS)
-            for segment in range(col_count)
-        ]
-    )
+        message_ref[segment, per_seg * size :] = folded.astype(message_ref.dtype)
+    queries = total_of([first_dir_ref[segment, per_seg] for segment in range(col_count)])
+    queries = total_of([window(queries, term) for term in range(3)])
+    pairs = total_of([col_dir_ref[segment, per_seg] for segment in range(col_count)])
+    lanes = lax.broadcasted_iota(jnp.int32, pairs.shape, 1)
+    pairs = jnp.where(lanes < 2 * size, pairs + pltpu.roll(pairs, 128 - 2 * size, 1), 0.0)
+    gram_ref[...] = beside(queries, pairs)
 
 
 def forward_kernel(spots_ref, live_ref, block_hbm, col_dir_ref, *refs):
@@ -326,7 +361,7 @@
         places,
         blocks,
         row_pieces,
-        [jax.ShapeDtypeStruct((col_count, per_seg, rows, lanes), jnp.bfloat16)],
+        [jax.ShapeDtypeStruct((col_count, per_seg * rows, lanes), jnp.bfloat16)],
         [
             pltpu.VMEM((len(row_pieces) * per_seg, rows, lanes), jnp.bfloat16),
             pltpu.VMEM(col_shape, jnp.float32),
@@ -372,29 +407,37 @@
         scaled_ref[part] = scaled
 
 
+def spread_kernel(scaled_ref, gram_ref, after_ref, copies_ref):
+    for copy in range(copies_ref.shape[0]):
+        copies_ref[copy, : scaled_ref.shape[0]] = scaled_ref[...]
+        copies_ref[copy, scaled_ref.shape[0]] = gram_ref[...]
+
+
 def scaled_sum(row_refs, col_ref, scaling_ref, part):
     scaling = scaling_ref[part : part + 1]
-    total = total_of([ref[part] for ref in [*row_refs, *leading(col_ref)]])
+    size = row_refs[0].shape[1]
+    rows = slice(part * size, part * size + size)
+    total = total_of([ref[part] for ref in row_refs] + [ref[rows] for ref in leading(col_ref)])
     return scaling * (0.5 * total)
 
 
 def middle_kernel(*refs):
-    *row_refs, col_ref, scaling_ref, query_ref, first_ref, scaled_ref, sent_ref = refs
+    *row_refs, col_ref, scaling_ref, query_ref, first_ref, scaled_ref, copies_ref = refs
     size = query_ref.shape[0]
-    pair_gram = jnp.zeros((2 * size, 128), jnp.float32)
-    for part in range(scaling_ref.shape[0]):
+    per_seg = scaling_ref.shape[0]
+    grams = jnp.zeros((size, 128), jnp.float32)
+    for part in range(per_seg):
         first = scaled_sum(row_refs, col_ref, scaling_ref, part)
         first_ref[part] = first
         scaled = (scaling_ref[part : part + 1] * first).astype(jnp.bfloat16)
         scaled_ref[part] = scaled
-        sent_ref[part] = scaled
-        pair = jnp.concatenate(
-            [query_ref[:, part * 128 : part * 128 + 128], first], axis=0
-        )
-        pair_gram += exact_across(pair, tall(pair))
-    grams = beside(pair_gram[:size], pltpu.roll(window(pair_gram[size:], 1), size, 1))
-    for term, values in enumerate(in_terms(grams)):
-        sent_ref[scaling_ref.shape[0] + term] = values
+        for copy in range(copies_ref.shape[0]):
+            copies_ref[copy, part] = scaled
+        query = query_ref[:, part * 128 : part * 128 + 128]
+        grams += exact_across(first, stacked(query, first))
+    terms = side_by_side(in_terms(grams, 2), 2 * size)
+    for copy in range(copies_ref.shape[0]):
+        copies_ref[copy, per_seg] = terms
 
 
 def tall(flat):
@@ -427,8 +470,8 @@
     return 0.5 * (flat + flipped(flat))
 
 
-def window(flat, place):
-    size = flat.shape[0]
+def window(flat, place, size=None):
+    size = size or flat.shape[0]
     if place:
         flat = pltpu.roll(flat, flat.shape[1] - place * size, 1)
     lanes = lax.broadcasted_iota(jnp.int32, flat.shape, 1)
@@ -466,7 +509,7 @@
     weight = graph_weight
     total = total_of([ref[...] for ref in gram_refs])
     g00 = symmetric(window(total, 0))
-    g01 = window(total, 1)
+    g01 = flipped(window(total, 1))
     g11 = symmetric(window(total, 2))
     g12 = symmetric(window(total, 3))
     eye = (
@@ -527,9 +570,12 @@
 
 
 def sum_kernel(col_ref, gram_ref, total_ref):
-    col_count, sent, size, _ = col_ref.shape
-    together = total_of([col_ref[segment, sent - 1] for segment in range(col_count)])
-    last = total_of([window(together, term) for term in range(GRAM_TERMS)])
+    size = gram_ref.shape[0]
+    col_count, sent, _ = col_ref.shape
+    folded = total_of([col_ref[segment, sent - size // 2 :] for segment in range(col_count)])
+    upper = window(folded, 0, size) + window(folded, 1, size)
+    lower = window(folded, 2, size) + window(folded, 3, size)
+    last = jnp.concatenate([upper, lower], axis=0)
     total_ref[...] = gram_ref[...] + pltpu.roll(last, 3 * size, 1)
 
 
@@ -544,8 +590,16 @@
     narrow = jax.ShapeDtypeStruct(piece, jnp.bfloat16)
     gram_shape = jax.ShapeDtypeStruct((query_rows, 128), jnp.float32)
 
-    blocks, flipped_blocks, *row_sums, col_sums = build_blocks(
-        *places, neighbor_cols[0, 0], neighbor_sims[0, 0], row_count, col_count, per_seg
+    message = jax.ShapeDtypeStruct((col_count, per_seg + 1) + piece[1:], jnp.bfloat16)
+
+    blocks, flipped_blocks, *row_sums, col_sums, query_gram = build_blocks(
+        *places,
+        neighbor_cols[0, 0],
+        neighbor_sims[0, 0],
+        queries,
+        row_count,
+        col_count,
+        per_seg,
     )
     col_part = exchange(col_sums.reshape(col_count, per_seg, 128), "col")
     row_parts = pass_around([None, *row_sums], "row")[1:]
@@ -558,32 +612,36 @@
         queries,
     )
 
-    def product(vectors, sent, with_grams):
-        row_pieces = pass_around([vectors] * row_count, "row")
-        col_dirs = exchange(jnp.broadcast_to(sent[None], (col_count,) + sent.shape), "col")
-        total = backward_product(places, flipped_blocks, row_pieces, col_count)
-        gram = None
-        if with_grams:
-            message = jax.ShapeDtypeStruct((col_count, per_seg + 1) + piece[1:], jnp.bfloat16)
-            total, gram = simple_call(
-                attach_kernel, [message, gram_shape], "attach", col_dirs, total
-            )
-        col_part = exchange(total, "col")
-        totals = forward_product(places, blocks, col_dirs, row_count, piece)
-        return pass_around(totals, "row"), col_part, gram
-
-    row_parts, col_part, _ = product(scaled, scaled, False)
-    more = jax.ShapeDtypeStruct((per_seg + GRAM_TERMS,) + piece[1:], jnp.bfloat16)
-    first, scaled, sent = simple_call(
+    row_pieces = pass_around([scaled] * row_count, "row")
+    (copies,) = simple_call(
+        spread_kernel, [message], "spread", scaled, query_gram, row_pieces[-1]
+    )
+    first_dirs = exchange(copies, "col")
+    total = backward_product(places, flipped_blocks, row_pieces, col_count)
+    col_part = exchange(total, "col")
+    totals = forward_product(places, blocks, first_dirs, row_count, piece)
+    first, scaled, copies = simple_call(
         middle_kernel,
-        [wide, narrow, more],
+        [wide, narrow, message],
         "middle",
-        *row_parts,
+        *pass_around(totals, "row"),
         col_part,
         scaling,
         queries,
     )
-    row_parts, col_part, gram = product(scaled, sent, True)
+
+    col_dirs = exchange(copies, "col")
+    row_pieces = pass_around([scaled] * row_count, "row")
+    total = backward_product(places, flipped_blocks, row_pieces, col_count)
+    more = jax.ShapeDtypeStruct(
+        (col_count, total.shape[1] + query_rows // 2, 128), jnp.bfloat16
+    )
+    total, gram = simple_call(
+        attach_kernel, [more, gram_shape], "attach", first_dirs, col_dirs, total
+    )
+    col_part = exchange(total, "col")
+    totals = forward_product(places, blocks, col_dirs, row_count, piece)
+    row_parts = pass_around(totals, "row")
     (gram,) = simple_call(sum_kernel, [gram_shape], "gram_sum", col_part, gram)
     flat = jax.ShapeDtypeStruct(queries.shape, jnp.float32)
     return tuple(

time: 112 us -> 110 us (0.982)
  starting transfers between devices: 47.4 us -> 44.7 us
  Pallas kernels: 34.9 us -> 36.5 us
    all_to_all x5, starting transfers between devices: 25.7 us -> 21.8 us  [exchange(): return lax.all_to_all(pieces, axis, 0, 0, tiled=True)]
    broadcast_in_dim x2 -> x0, local copies, waits for them, and re-layouts: 1.63 us -> none  [product(): jnp.broadcast_to(sent[None], (col_count,) + sent.shape)]
    pallas_call x5 -> x6, Pallas kernels: 6.58 us -> 8.05 us  [simple_call(): pl.pallas_call(kernel, out_shape=shapes, compiler_params=pltpu.CompilerPa...]
    ppermute x18, starting transfers between devices: 21.6 us -> 22.9 us  [pass_around(): lax.ppermute(pieces[ahead], axis, [(at, (at + ahead) % count) for at in r...]
  transfers between devices with their start and end apart: 23 -> 23, of which waited for: 12 -> 13; matrix products, arithmetic and copies ran while one was open for 0% -> 0% of each run, Pallas kernels for 13% -> 13%
where the time goes in v7:
time: 110 us
  starting transfers between devices  44.7 us (41%)
  Pallas kernels  36.5 us (33%)
  waiting for transfers between devices  24.7 us (22%)
  local copies, waits for them, and re-layouts  2.23 us (2%)
  between operations  1.4 us (1%)
    ppermute x18, starting transfers between devices, pass_around(): lax.ppermute(pieces[ahead], axis, [(at, (at + ahead) % count) for at in r...  22.9 us
    all_to_all x5, starting transfers between devices, exchange(): return lax.all_to_all(pieces, axis, 0, 0, tiled=True)  21.8 us
    pallas_call x4, Pallas kernels, over_blocks(): pl.pallas_call(kernel, in_specs=[SCALARS, SCALARS, ANYWHERE] + [IN_VMEM]...  14.6 us
    pallas_call x1, Pallas kernels, build_blocks(): pl.pallas_call(build_kernel, in_specs=[SCALARS, SCALARS, ANYWHERE, ANYWHE...  13.9 us
    all_to_all x5, waiting for transfers between devices, exchange(): return lax.all_to_all(pieces, axis, 0, 0, tiled=True)  12.6 us
    ppermute x18, waiting for transfers between devices, pass_around(): lax.ppermute(pieces[ahead], axis, [(at, (at + ahead) % count) for at in r...  12.1 us
    pallas_call x6, Pallas kernels, simple_call(): pl.pallas_call(kernel, out_shape=shapes, compiler_params=pltpu.CompilerPa...  8.05 us
    unnamed x10, local copies, waits for them, and re-layouts  2.23 us
  transfers between devices with their start and end apart: 23, of which 13 were waited for; matrix products, arithmetic and copies ran while one was open for 0% of the time, Pallas kernels for 13%

profile of v7, /device:TPU:0, one launch (start us, length us, event | category | flops | bytes accessed | tf_op | source)
XLA Modules:
  0.0 109.5 jit_solution(13105264954148332167)
XLA Ops:
  1.3 13.9 %build_blocks.1 = (bf16[1024,128,128]{2,1,0:T(8,128)(2,1)}, bf16[1024,128,128]{2,1,0:T(8,128)(2,1)}, f32[4,128]{1,0:T(4,128)}, f32[4,128]{1,0:T(4,128)}, f32[4,1...) custom-call(s32[1,1,256]{2,1,0:T(1,128)} %spots_ref.9, s32[1,1]{1,0:T(1,128)S(6)} %copy.7.live_ref, ...), custom_call_target="tpu_custom_call" | custom-call | tf_op jit(solution)/shard_map/build_blocks/pallas_call | solution.py:174
  15.2 4.8 %all-to-all-start = ((f32[8,4,128]{2,1,0:T(4,128)}), f32[8,4,128]{2,1,0:T(4,128)S(1)}, u32[]{:S(2)}, u32[]{:S(2)}) async-start(f32[8,4,128]{2,1,0:T(4,128)} %bitcast.5), calls=%async_computation | async-start | bytes 32768 | tf_op jit(solution)/shard_map/all_to_all | solution.py:560
  20.0 2.1 %collective-permute-start = (f32[4,128]{1,0:T(4,128)}, f32[4,128]{1,0:T(4,128)S(1)}, u32[]{:S(2)}, u32[]{:S(2)}) collective-permute-start(f32[4,128]{1,0:T(4,128)} %get-tuple-element.25), channel_id=1, source_target_pairs={{0,8},{8,16},{16,24},{24,0},{1,9},{9,17},{17,25},{25,1},{2,10},{10... | collective-permute-start | bytes 6152 | tf_op jit(solution)/shard_map/ppermute | solution.py:554
  22.1 9.0 %collective-permute-start.1 = (f32[4,128]{1,0:T(4,128)}, f32[4,128]{1,0:T(4,128)S(1)}, u32[]{:S(2)}, u32[]{:S(2)}) collective-permute-start(f32[4,128]{1,0:T(4,128)} %get-tuple-element.26), channel_id=1, source_target_pairs={{0,16},{8,24},{16,0},{24,8},{1,17},{9,25},{17,1},{25,9},{2,18},{10... | collective-permute-start | bytes 6152 | tf_op jit(solution)/shard_map/ppermute | solution.py:554
  31.0 1.4 %collective-permute-start.2 = (f32[4,128]{1,0:T(4,128)}, f32[4,128]{1,0:T(4,128)S(1)}, u32[]{:S(2)}, u32[]{:S(2)}) collective-permute-start(f32[4,128]{1,0:T(4,128)} %get-tuple-element.27), channel_id=1, source_target_pairs={{0,24},{8,0},{16,8},{24,16},{1,25},{9,1},{17,9},{25,17},{2,26},{10... | collective-permute-start | bytes 6152 | tf_op jit(solution)/shard_map/ppermute | solution.py:554
  32.8 1.1 %collective-permute-done.2.refs_2_ = f32[4,128]{1,0:T(4,128)S(1)} collective-permute-done((f32[4,128]{1,0:T(4,128)}, f32[4,128]{1,0:T(4,128)S(1)}, u32[]{:S(2)}, u32[]{:S(2)}) %collective-permute-start.2) | collective-permute-done | bytes 2080 | tf_op jit(solution)/shard_map/ppermute | solution.py:554
  34.8 2.0 %collective-permute-start.3 = (bf16[4,32,128]{2,1,0:T(8,128)(2,1)S(1)}, bf16[4,32,128]{2,1,0:T(8,128)(2,1)S(1)}, u32[]{:S(2)}, u32[]{:S(2)}) collective-permute-start(bf16[4,32,128]{2,1,0:T(8,128)(2,1)S(1)} %get-tuple-element.29.scaled_ref.refs_0_), channel_id=1, source_target_pairs={{0,24},{8,0},{16,8},{24,16},{1,25},{9,1},{17,9},{25,17},{2,26},{10... | collective-permute-start | bytes 98312 | tf_op jit(solution)/shard_map/ppermute | solution.py:554
  36.9 1.6 %collective-permute-done.3.after_ref.refs_3_ = bf16[4,32,128]{2,1,0:T(8,128)(2,1)S(1)} collective-permute-done((bf16[4,32,128]{2,1,0:T(8,128)(2,1)S(1)}, bf16[4,32,128]{2,1,0:T(8,128)(2,1)S(1)}, u32[]{:S(2)}, u32[]{:S(2)}) %collective-permute-start.3) | collective-permute-done | bytes 32800 | tf_op jit(solution)/shard_map/ppermute | solution.py:554
  39.9 5.7 %all-to-all-start.1 = ((bf16[8,5,32,128]{3,2,1,0:T(8,128)(2,1)}), bf16[8,5,32,128]{3,2,1,0:T(8,128)(2,1)S(1)}, u32[]{:S(2)}, u32[]{:S(2)}) async-start(bf16[8,5,32,128]{3,2,1,0:T(8,128)(2,1)} %spread.1), calls=%async_computation.1 | async-start | bytes 655360 | tf_op jit(solution)/shard_map/all_to_all | solution.py:560
  46.0 1.3 %collective-permute-start.7 = (bf16[4,32,128]{2,1,0:T(8,128)(2,1)S(1)}, bf16[4,32,128]{2,1,0:T(8,128)(2,1)S(1)}, u32[]{:S(2)}, u32[]{:S(2)}) collective-permute-start(bf16[4,32,128]{2,1,0:T(8,128)(2,1)S(1)} %get-tuple-element.29.scaled_ref.refs_0_), channel_id=1, source_target_pairs={{0,8},{8,16},{16,24},{24,0},{1,9},{9,17},{17,25},{25,1},{2,10},{10... | collective-permute-start | bytes 98312 | tf_op jit(solution)/shard_map/ppermute | solution.py:554
  47.2 2.4 %collective-permute-done.8.refs_2_ = bf16[4,32,128]{2,1,0:T(8,128)(2,1)S(1)} collective-permute-done((bf16[4,32,128]{2,1,0:T(8,128)(2,1)S(1)}, bf16[4,32,128]{2,1,0:T(8,128)(2,1)S(1)}, u32[]{:S(2)}, u32[]{:S(2)}) %collective-permute-start.8) | collective-permute-done | bytes 32800 | tf_op jit(solution)/shard_map/ppermute | solution.py:554
  50.3 4.2 %backward_product.2 = bf16[8,128,128]{2,1,0:T(8,128)(2,1)} custom-call(s32[1,1,256]{2,1,0:T(1,128)S(1)} %copy-done.2, s32[1,1]{1,0:T(1,128)S(6)} %copy.7.live_ref, bf16[1024,128,128]{2,1,0:T(8,128)(2,1)} %get-tuple-element.35.block_hbm, bf16[4,32,128]{2,1,0:T(8,128)(2,1)S(1)} %get-tuple-element.29.scaled_ref.refs_0_, ...), custom_call_target="tpu_custom_call" | custom-call | flops 268435456 | bytes 8388608 | tf_op jit(solution)/shard_map/backward_product/pallas_call | solution.py:337
  54.5 2.0 %all-to-all-done.1.col_dir_ref.first_dir_ref = bf16[8,5,32,128]{3,2,1,0:T(8,128)(2,1)S(1)} async-done(((bf16[8,5,32,128]{3,2,1,0:T(8,128)(2,1)}), bf16[8,5,32,128]{3,2,1,0:T(8,128)(2,1)S(1)}, u32[]{:S(2)}, u32[]{:S(2)}) %all-to-all-start.1) | async-done | bytes 327712 | tf_op jit(solution)/shard_map/all_to_all | solution.py:560
  56.5 3.6 %all-to-all-start.2 = ((bf16[8,128,128]{2,1,0:T(8,128)(2,1)}), bf16[8,128,128]{2,1,0:T(8,128)(2,1)S(1)}, u32[]{:S(2)}, u32[]{:S(2)}) async-start(bf16[8,128,128]{2,1,0:T(8,128)(2,1)} %backward_product.2), calls=%async_computation.2 | async-start | bytes 524288 | tf_op jit(solution)/shard_map/all_to_all | solution.py:560
  60.2 3.5 %forward_product.2 = (bf16[4,32,128]{2,1,0:T(8,128)(2,1)S(1)}, bf16[4,32,128]{2,1,0:T(8,128)(2,1)S(1)}, bf16[4,32,128]{2,1,0:T(8,128)(2,1)S(1)}, bf16[4,32,128]{2,1,0:T(8,128)(2,1)S(1)}) custom-call(s32[1,1,256]{2,1,0:T(1,128)S(1)} %copy-done.3, s32[1,1]{1,0:T(1,128)S(6)} %copy.7.live_ref, bf16[1024,128,128]{2,1,0:T(8,128)(2,1)} %get-tuple-element.24.block_hbm, ...), custom_call_target="tpu_custom_call" | custom-call | flops 268435456 | bytes 8388608 | tf_op jit(solution)/shard_map/forward_product/pallas_call | solution.py:337
  63.7 0.9 collective-permute-start.5
  64.6 0.9 collective-permute-start.6
  65.5 3.8 %all-to-all-done.2.refs_4_ = bf16[8,128,128]{2,1,0:T(8,128)(2,1)S(1)} async-done(((bf16[8,128,128]{2,1,0:T(8,128)(2,1)}), bf16[8,128,128]{2,1,0:T(8,128)(2,1)S(1)}, u32[]{:S(2)}, u32[]{:S(2)}) %all-to-all-start.2) | async-done | bytes 262176 | tf_op jit(solution)/shard_map/all_to_all | solution.py:560
  69.3 1.2 %middle.1 = (f32[4,32,128]{2,1,0:T(8,128)S(1)}, bf16[4,32,128]{2,1,0:T(8,128)(2,1)S(1)}, bf16[8,5,32,128]{3,2,1,0:T(8,128)(2,1)}) custom-call(bf16[4,32,128]{2,1,0:T(8,128)(2,1)S(1)} %get-tuple-element.31.refs_0_, bf16[4,32,128]{2,1,0:T(8,128)(2,1)S(1)} %collective-permute-done.4.refs_1_, bf16[4,32,128]{2,1,0:T(8,128)(2,1)S(1)} %collective-permute-done.5.refs_2_, ...), custom_call_target="tpu_custom_call" | custom-call | tf_op jit(solution)/shard_map/middle/pallas_call | solution.py:564
  70.5 4.1 %all-to-all-start.3 = ((bf16[8,5,32,128]{3,2,1,0:T(8,128)(2,1)}), bf16[8,5,32,128]{3,2,1,0:T(8,128)(2,1)S(1)}, u32[]{:S(2)}, u32[]{:S(2)}) async-start(bf16[8,5,32,128]{3,2,1,0:T(8,128)(2,1)} %get-tuple-element.37), calls=%async_computation.3 | async-start | bytes 655360 | tf_op jit(solution)/shard_map/all_to_all | solution.py:560
  74.5 1.1 %collective-permute-start.14 = (bf16[4,32,128]{2,1,0:T(8,128)(2,1)S(1)}, bf16[4,32,128]{2,1,0:T(8,128)(2,1)S(1)}, u32[]{:S(2)}, u32[]{:S(2)}) collective-permute-start(bf16[4,32,128]{2,1,0:T(8,128)(2,1)S(1)} %get-tuple-element.42.refs_0_), channel_id=1, source_target_pairs={{0,24},{8,0},{16,8},{24,16},{1,25},{9,1},{17,9},{25,17},{2,26},{10... | collective-permute-start | bytes 98312 | tf_op jit(solution)/shard_map/ppermute | solution.py:554
  75.7 1.4 %collective-permute-start.13 = (bf16[4,32,128]{2,1,0:T(8,128)(2,1)S(1)}, bf16[4,32,128]{2,1,0:T(8,128)(2,1)S(1)}, u32[]{:S(2)}, u32[]{:S(2)}) collective-permute-start(bf16[4,32,128]{2,1,0:T(8,128)(2,1)S(1)} %get-tuple-element.42.refs_0_), channel_id=1, source_target_pairs={{0,16},{8,24},{16,0},{24,8},{1,17},{9,25},{17,1},{25,9},{2,18},{10... | collective-permute-start | bytes 98312 | tf_op jit(solution)/shard_map/ppermute | solution.py:554
  77.3 2.3 %collective-permute-done.13.refs_2_ = bf16[4,32,128]{2,1,0:T(8,128)(2,1)S(1)} collective-permute-done((bf16[4,32,128]{2,1,0:T(8,128)(2,1)S(1)}, bf16[4,32,128]{2,1,0:T(8,128)(2,1)S(1)}, u32[]{:S(2)}, u32[]{:S(2)}) %collective-permute-start.13) | collective-permute-done | bytes 32800 | tf_op jit(solution)/shard_map/ppermute | solution.py:554
  80.4 3.5 %backward_product.3.total_ref = bf16[8,128,128]{2,1,0:T(8,128)(2,1)S(1)} custom-call(s32[1,1,256]{2,1,0:T(1,128)S(1)} %copy-done.3, s32[1,1]{1,0:T(1,128)S(6)} %copy.7.live_ref, bf16[1024,128,128]{2,1,0:T(8,128)(2,1)} %get-tuple-element.35.block_hbm, bf16[4,32,128]{2,1,0:T(8,128)(2,1)S(1)} %get-tuple-element.42.refs_0_, ...), custom_call_target="tpu_custom_call" | custom-call | flops 268435456 | bytes 8388608 | tf_op jit(solution)/shard_map/backward_product/pallas_call | solution.py:337
  83.8 2.3 %all-to-all-done.3.col_dir_ref = bf16[8,5,32,128]{3,2,1,0:T(8,128)(2,1)S(1)} async-done(((bf16[8,5,32,128]{3,2,1,0:T(8,128)(2,1)}), bf16[8,5,32,128]{3,2,1,0:T(8,128)(2,1)S(1)}, u32[]{:S(2)}, u32[]{:S(2)}) %all-to-all-start.3) | async-done | bytes 327712 | tf_op jit(solution)/shard_map/all_to_all | solution.py:560
  86.1 1.2 %attach.1 = (bf16[8,144,128]{2,1,0:T(8,128)(2,1)}, f32[32,128]{1,0:T(8,128)S(1)}) custom-call(bf16[8,5,32,128]{3,2,1,0:T(8,128)(2,1)S(1)} %all-to-all-done.1.col_dir_ref.first_dir_ref, bf16[8,5,32,128]{3,2,1,0:T(8,128)(2,1)S(1)} %all-to-all-done.3.col_dir_ref, bf16[8,128,128]{2,1,0:T(8,128)(2,1)S(1)} %backward_product.3.total_ref), custom_call_target="tpu_custom_call" | custom-call | tf_op jit(solution)/shard_map/attach/pallas_call | solution.py:564
  87.3 3.6 %all-to-all-start.4 = ((bf16[8,144,128]{2,1,0:T(8,128)(2,1)}), bf16[8,144,128]{2,1,0:T(8,128)(2,1)S(1)}, u32[]{:S(2)}, u32[]{:S(2)}) async-start(bf16[8,144,128]{2,1,0:T(8,128)(2,1)} %get-tuple-element.43), calls=%async_computation.4 | async-start | bytes 589824 | tf_op jit(solution)/shard_map/all_to_all | solution.py:560
  91.0 3.5 %forward_product.3 = (bf16[4,32,128]{2,1,0:T(8,128)(2,1)S(1)}, bf16[4,32,128]{2,1,0:T(8,128)(2,1)S(1)}, bf16[4,32,128]{2,1,0:T(8,128)(2,1)S(1)}, bf16[4,32,128]{2,1,0:T(8,128)(2,1)S(1)}) custom-call(s32[1,1,256]{2,1,0:T(1,128)S(1)} %copy-done.3, s32[1,1]{1,0:T(1,128)S(6)} %copy.7.live_ref, bf16[1024,128,128]{2,1,0:T(8,128)(2,1)} %get-tuple-element.24.block_hbm, ...), custom_call_target="tpu_custom_call" | custom-call | flops 268435456 | bytes 8388608 | tf_op jit(solution)/shard_map/forward_product/pallas_call | solution.py:337
  94.7 1.6 %collective-permute-start.11 = (bf16[4,32,128]{2,1,0:T(8,128)(2,1)S(1)}, bf16[4,32,128]{2,1,0:T(8,128)(2,1)S(1)}, u32[]{:S(2)}, u32[]{:S(2)}) collective-permute-start(bf16[4,32,128]{2,1,0:T(8,128)(2,1)S(1)} %get-tuple-element.41), channel_id=1, source_target_pairs={{0,24},{8,0},{16,8},{24,16},{1,25},{9,1},{17,9},{25,17},{2,26},{10... | collective-permute-start | bytes 98312 | tf_op jit(solution)/shard_map/ppermute | solution.py:554
  96.3 4.5 %all-to-all-done.4.col_ref.refs_8_ = bf16[8,144,128]{2,1,0:T(8,128)(2,1)S(1)} async-done(((bf16[8,144,128]{2,1,0:T(8,128)(2,1)}), bf16[8,144,128]{2,1,0:T(8,128)(2,1)S(1)}, u32[]{:S(2)}, u32[]{:S(2)}) %all-to-all-start.4) | async-done | bytes 294944 | tf_op jit(solution)/shard_map/all_to_all | solution.py:560
  102.4 2.4 %collective-permute-done.16.refs_6_ = f32[32,128]{1,0:T(8,128)S(1)} collective-permute-done((f32[32,128]{1,0:T(8,128)S(1)}, f32[32,128]{1,0:T(8,128)S(1)}, u32[]{:S(2)}, u32[]{:S(2)}) %collective-permute-start.16) | collective-permute-done | bytes 16416 | tf_op jit(solution)/shard_map/ppermute | solution.py:554
  104.8 4.7 %close.1 = (f32[32,512]{1,0:T(8,128)}, f32[32,512]{1,0:T(8,128)}) custom-call(bf16[4,32,128]{2,1,0:T(8,128)(2,1)S(1)} %get-tuple-element.38.refs_0_, bf16[4,32,128]{2,1,0:T(8,128)(2,1)S(1)} %collective-permute-done.9.refs_1_, bf16[4,32,128]{2,1,0:T(8,128)(2,1)S(1)} %collective-permute-done.10.refs_2_, ...), custom_call_target="tpu_custom_call" | custom-call | tf_op jit(solution)/shard_map/close/pallas_call | solution.py:564
  (35 shorter events, 6.7 us)
Async XLA Ops:
  0.6 59.5 %copy-start.3 = (s32[1,1,256]{2,1,0:T(1,128)S(1)}, s32[1,1,256]{2,1,0:T(1,128)}, u32[]{:S(2)}) copy-start(s32[1,1,256]{2,1,0:T(1,128)} %spots_ref.9) | copy-start | bytes 3076
  15.2 18.7 %all-to-all-start = ((f32[8,4,128]{2,1,0:T(4,128)}), f32[8,4,128]{2,1,0:T(4,128)S(1)}, u32[]{:S(2)}, u32[]{:S(2)}) async-start(f32[8,4,128]{2,1,0:T(4,128)} %bitcast.5), calls=%async_computation | async-start | bytes 32768 | tf_op jit(solution)/shard_map/all_to_all | solution.py:560
  20.0 12.5 %collective-permute-start = (f32[4,128]{1,0:T(4,128)}, f32[4,128]{1,0:T(4,128)S(1)}, u32[]{:S(2)}, u32[]{:S(2)}) collective-permute-start(f32[4,128]{1,0:T(4,128)} %get-tuple-element.25), channel_id=1, source_target_pairs={{0,8},{8,16},{16,24},{24,0},{1,9},{9,17},{17,25},{25,1},{2,10},{10... | collective-permute-start | bytes 6152 | tf_op jit(solution)/shard_map/ppermute | solution.py:554
  22.1 10.7 %collective-permute-start.1 = (f32[4,128]{1,0:T(4,128)}, f32[4,128]{1,0:T(4,128)S(1)}, u32[]{:S(2)}, u32[]{:S(2)}) collective-permute-start(f32[4,128]{1,0:T(4,128)} %get-tuple-element.26), channel_id=1, source_target_pairs={{0,16},{8,24},{16,0},{24,8},{1,17},{9,25},{17,1},{25,9},{2,18},{10... | collective-permute-start | bytes 6152 | tf_op jit(solution)/shard_map/ppermute | solution.py:554
  31.0 2.9 %collective-permute-start.2 = (f32[4,128]{1,0:T(4,128)}, f32[4,128]{1,0:T(4,128)S(1)}, u32[]{:S(2)}, u32[]{:S(2)}) collective-permute-start(f32[4,128]{1,0:T(4,128)} %get-tuple-element.27), channel_id=1, source_target_pairs={{0,24},{8,0},{16,8},{24,16},{1,25},{9,1},{17,9},{25,17},{2,26},{10... | collective-permute-start | bytes 6152 | tf_op jit(solution)/shard_map/ppermute | solution.py:554
  34.0 0.8 copy-start
  34.8 3.6 %collective-permute-start.3 = (bf16[4,32,128]{2,1,0:T(8,128)(2,1)S(1)}, bf16[4,32,128]{2,1,0:T(8,128)(2,1)S(1)}, u32[]{:S(2)}, u32[]{:S(2)}) collective-permute-start(bf16[4,32,128]{2,1,0:T(8,128)(2,1)S(1)} %get-tuple-element.29.scaled_ref.refs_0_), channel_id=1, source_target_pairs={{0,24},{8,0},{16,8},{24,16},{1,25},{9,1},{17,9},{25,17},{2,26},{10... | collective-permute-start | bytes 98312 | tf_op jit(solution)/shard_map/ppermute | solution.py:554
  38.5 0.7 copy-start.4
  39.9 16.6 %all-to-all-start.1 = ((bf16[8,5,32,128]{3,2,1,0:T(8,128)(2,1)}), bf16[8,5,32,128]{3,2,1,0:T(8,128)(2,1)S(1)}, u32[]{:S(2)}, u32[]{:S(2)}) async-start(bf16[8,5,32,128]{3,2,1,0:T(8,128)(2,1)} %spread.1), calls=%async_computation.1 | async-start | bytes 655360 | tf_op jit(solution)/shard_map/all_to_all | solution.py:560
  45.6 4.0 %collective-permute-start.8 = (bf16[4,32,128]{2,1,0:T(8,128)(2,1)S(1)}, bf16[4,32,128]{2,1,0:T(8,128)(2,1)S(1)}, u32[]{:S(2)}, u32[]{:S(2)}) collective-permute-start(bf16[4,32,128]{2,1,0:T(8,128)(2,1)S(1)} %get-tuple-element.29.scaled_ref.refs_0_), channel_id=1, source_target_pairs={{0,16},{8,24},{16,0},{24,8},{1,17},{9,25},{17,1},{25,9},{2,18},{10... | collective-permute-start | bytes 98312 | tf_op jit(solution)/shard_map/ppermute | solution.py:554
  46.0 3.7 %collective-permute-start.7 = (bf16[4,32,128]{2,1,0:T(8,128)(2,1)S(1)}, bf16[4,32,128]{2,1,0:T(8,128)(2,1)S(1)}, u32[]{:S(2)}, u32[]{:S(2)}) collective-permute-start(bf16[4,32,128]{2,1,0:T(8,128)(2,1)S(1)} %get-tuple-element.29.scaled_ref.refs_0_), channel_id=1, source_target_pairs={{0,8},{8,16},{16,24},{24,0},{1,9},{9,17},{17,25},{25,1},{2,10},{10... | collective-permute-start | bytes 98312 | tf_op jit(solution)/shard_map/ppermute | solution.py:554
  49.7 0.7 copy-start.2
  50.3 19.0 %copy-start.1 = (f32[32,512]{1,0:T(8,128)S(1)}, f32[32,512]{1,0:T(8,128)}, u32[]{:S(2)}) copy-start(f32[32,512]{1,0:T(8,128)} %refs_10_.1) | copy-start | bytes 196612
  56.5 12.8 %all-to-all-start.2 = ((bf16[8,128,128]{2,1,0:T(8,128)(2,1)}), bf16[8,128,128]{2,1,0:T(8,128)(2,1)S(1)}, u32[]{:S(2)}, u32[]{:S(2)}) async-start(bf16[8,128,128]{2,1,0:T(8,128)(2,1)} %backward_product.2), calls=%async_computation.2 | async-start | bytes 524288 | tf_op jit(solution)/shard_map/all_to_all | solution.py:560
  63.6 5.6 %collective-permute-start.4 = (bf16[4,32,128]{2,1,0:T(8,128)(2,1)S(1)}, bf16[4,32,128]{2,1,0:T(8,128)(2,1)S(1)}, u32[]{:S(2)}, u32[]{:S(2)}) collective-permute-start(bf16[4,32,128]{2,1,0:T(8,128)(2,1)S(1)} %get-tuple-element.32), channel_id=1, source_target_pairs={{0,8},{8,16},{16,24},{24,0},{1,9},{9,17},{17,25},{25,1},{2,10},{10... | collective-permute-start | bytes 98312 | tf_op jit(solution)/shard_map/ppermute | solution.py:554
  63.7 5.6 %collective-permute-start.5 = (bf16[4,32,128]{2,1,0:T(8,128)(2,1)S(1)}, bf16[4,32,128]{2,1,0:T(8,128)(2,1)S(1)}, u32[]{:S(2)}, u32[]{:S(2)}) collective-permute-start(bf16[4,32,128]{2,1,0:T(8,128)(2,1)S(1)} %get-tuple-element.33), channel_id=1, source_target_pairs={{0,16},{8,24},{16,0},{24,8},{1,17},{9,25},{17,1},{25,9},{2,18},{10... | collective-permute-start | bytes 98312 | tf_op jit(solution)/shard_map/ppermute | solution.py:554
  64.6 4.7 %collective-permute-start.6 = (bf16[4,32,128]{2,1,0:T(8,128)(2,1)S(1)}, bf16[4,32,128]{2,1,0:T(8,128)(2,1)S(1)}, u32[]{:S(2)}, u32[]{:S(2)}) collective-permute-start(bf16[4,32,128]{2,1,0:T(8,128)(2,1)S(1)} %get-tuple-element.34), channel_id=1, source_target_pairs={{0,24},{8,0},{16,8},{24,16},{1,25},{9,1},{17,9},{25,17},{2,26},{10... | collective-permute-start | bytes 98312 | tf_op jit(solution)/shard_map/ppermute | solution.py:554
  70.5 15.6 %all-to-all-start.3 = ((bf16[8,5,32,128]{3,2,1,0:T(8,128)(2,1)}), bf16[8,5,32,128]{3,2,1,0:T(8,128)(2,1)S(1)}, u32[]{:S(2)}, u32[]{:S(2)}) async-start(bf16[8,5,32,128]{3,2,1,0:T(8,128)(2,1)} %get-tuple-element.37), calls=%async_computation.3 | async-start | bytes 655360 | tf_op jit(solution)/shard_map/all_to_all | solution.py:560
  74.5 2.7 %collective-permute-start.14 = (bf16[4,32,128]{2,1,0:T(8,128)(2,1)S(1)}, bf16[4,32,128]{2,1,0:T(8,128)(2,1)S(1)}, u32[]{:S(2)}, u32[]{:S(2)}) collective-permute-start(bf16[4,32,128]{2,1,0:T(8,128)(2,1)S(1)} %get-tuple-element.42.refs_0_), channel_id=1, source_target_pairs={{0,24},{8,0},{16,8},{24,16},{1,25},{9,1},{17,9},{25,17},{2,26},{10... | collective-permute-start | bytes 98312 | tf_op jit(solution)/shard_map/ppermute | solution.py:554
  75.7 3.9 %collective-permute-start.13 = (bf16[4,32,128]{2,1,0:T(8,128)(2,1)S(1)}, bf16[4,32,128]{2,1,0:T(8,128)(2,1)S(1)}, u32[]{:S(2)}, u32[]{:S(2)}) collective-permute-start(bf16[4,32,128]{2,1,0:T(8,128)(2,1)S(1)} %get-tuple-element.42.refs_0_), channel_id=1, source_target_pairs={{0,16},{8,24},{16,0},{24,8},{1,17},{9,25},{17,1},{25,9},{2,18},{10... | collective-permute-start | bytes 98312 | tf_op jit(solution)/shard_map/ppermute | solution.py:554
  77.0 3.3 %collective-permute-start.12 = (bf16[4,32,128]{2,1,0:T(8,128)(2,1)S(1)}, bf16[4,32,128]{2,1,0:T(8,128)(2,1)S(1)}, u32[]{:S(2)}, u32[]{:S(2)}) collective-permute-start(bf16[4,32,128]{2,1,0:T(8,128)(2,1)S(1)} %get-tuple-element.42.refs_0_), channel_id=1, source_target_pairs={{0,8},{8,16},{16,24},{24,0},{1,9},{9,17},{17,25},{25,1},{2,10},{10... | collective-permute-start | bytes 98312 | tf_op jit(solution)/shard_map/ppermute | solution.py:554
  87.3 13.5 %all-to-all-start.4 = ((bf16[8,144,128]{2,1,0:T(8,128)(2,1)}), bf16[8,144,128]{2,1,0:T(8,128)(2,1)S(1)}, u32[]{:S(2)}, u32[]{:S(2)}) async-start(bf16[8,144,128]{2,1,0:T(8,128)(2,1)} %get-tuple-element.43), calls=%async_computation.4 | async-start | bytes 589824 | tf_op jit(solution)/shard_map/all_to_all | solution.py:560
  94.5 7.0 %collective-permute-start.9 = (bf16[4,32,128]{2,1,0:T(8,128)(2,1)S(1)}, bf16[4,32,128]{2,1,0:T(8,128)(2,1)S(1)}, u32[]{:S(2)}, u32[]{:S(2)}) collective-permute-start(bf16[4,32,128]{2,1,0:T(8,128)(2,1)S(1)} %get-tuple-element.39), channel_id=1, source_target_pairs={{0,8},{8,16},{16,24},{24,0},{1,9},{9,17},{17,25},{25,1},{2,10},{10... | collective-permute-start | bytes 98312 | tf_op jit(solution)/shard_map/ppermute | solution.py:554
  94.5 7.1 %collective-permute-start.10 = (bf16[4,32,128]{2,1,0:T(8,128)(2,1)S(1)}, bf16[4,32,128]{2,1,0:T(8,128)(2,1)S(1)}, u32[]{:S(2)}, u32[]{:S(2)}) collective-permute-start(bf16[4,32,128]{2,1,0:T(8,128)(2,1)S(1)} %get-tuple-element.40), channel_id=1, source_target_pairs={{0,16},{8,24},{16,0},{24,8},{1,17},{9,25},{17,1},{25,9},{2,18},{10... | collective-permute-start | bytes 98312 | tf_op jit(solution)/shard_map/ppermute | solution.py:554
  94.7 6.9 %collective-permute-start.11 = (bf16[4,32,128]{2,1,0:T(8,128)(2,1)S(1)}, bf16[4,32,128]{2,1,0:T(8,128)(2,1)S(1)}, u32[]{:S(2)}, u32[]{:S(2)}) collective-permute-start(bf16[4,32,128]{2,1,0:T(8,128)(2,1)S(1)} %get-tuple-element.41), channel_id=1, source_target_pairs={{0,24},{8,0},{16,8},{24,16},{1,25},{9,1},{17,9},{25,17},{2,26},{10... | collective-permute-start | bytes 98312 | tf_op jit(solution)/shard_map/ppermute | solution.py:554
  101.0 1.4 %collective-permute-start.17 = (f32[32,128]{1,0:T(8,128)S(1)}, f32[32,128]{1,0:T(8,128)S(1)}, u32[]{:S(2)}, u32[]{:S(2)}) collective-permute-start(f32[32,128]{1,0:T(8,128)S(1)} %gram_sum.1.refs_4_), channel_id=1, source_target_pairs={{0,24},{8,0},{16,8},{24,16},{1,25},{9,1},{17,9},{25,17},{2,26},{10... | collective-permute-start | bytes 49160 | tf_op jit(solution)/shard_map/ppermute | solution.py:554
  101.0 3.8 %collective-permute-start.16 = (f32[32,128]{1,0:T(8,128)S(1)}, f32[32,128]{1,0:T(8,128)S(1)}, u32[]{:S(2)}, u32[]{:S(2)}) collective-permute-start(f32[32,128]{1,0:T(8,128)S(1)} %gram_sum.1.refs_4_), channel_id=1, source_target_pairs={{0,16},{8,24},{16,0},{24,8},{1,17},{9,25},{17,1},{25,9},{2,18},{10... | collective-permute-start | bytes 49160 | tf_op jit(solution)/shard_map/ppermute | solution.py:554
  101.5 3.3 %collective-permute-start.15 = (f32[32,128]{1,0:T(8,128)S(1)}, f32[32,128]{1,0:T(8,128)S(1)}, u32[]{:S(2)}, u32[]{:S(2)}) collective-permute-start(f32[32,128]{1,0:T(8,128)S(1)} %gram_sum.1.refs_4_), channel_id=1, source_target_pairs={{0,8},{8,16},{16,24},{24,0},{1,9},{9,17},{17,25},{25,1},{2,10},{10... | collective-permute-start | bytes 49160 | tf_op jit(solution)/shard_map/ppermute | solution.py:554

commit v8 on v7

--- a/solution.py
+++ b/solution.py
@@ -39,12 +39,16 @@
     return number >> (size.bit_length() - 1), number & (size - 1)
 
 
-def place_of(spots_ref, slot, col_blocks):
-    return divided(spots_ref[0, 0, slot], col_blocks)
-
-
-def group_count(live_ref, group):
-    return (live_ref[0, 0] + group - 1) // group
+def place_of(places, slot, col_blocks):
+    return divided(places[0][0, 0, slot], col_blocks)
+
+
+def live_count(places):
+    return places[1][0, 0]
+
+
+def group_count(places, group):
+    return (live_count(places) + group - 1) // group
 
 
 def group_copy(source, target, sems, index, group):
@@ -53,13 +57,11 @@
 
 
 def build_kernel(
-    spots_ref, live_ref, index_hbm, value_hbm, query_hbm, block_hbm, flipped_hbm, *refs
+    spots_ref, live_ref, index_hbm, value_hbm, block_hbm, flipped_hbm, *refs
 ):
     (
         *row_outs,
         col_out_ref,
-        gram_ref,
-        query_ref,
         index_ref,
         value_ref,
         block_ref,
@@ -70,20 +72,18 @@
         value_sems,
         block_sems,
         flipped_sems,
-        query_sem,
     ) = refs
+    places = (spots_ref, live_ref)
     row_count = len(row_outs) + 1
     per_seg = row_outs[0].shape[0]
     col_blocks = col_out_ref.shape[0]
-    groups = group_count(live_ref, BATCH) * (BATCH // GROUP)
+    groups = group_count(places, BATCH) * (BATCH // GROUP)
 
     def start_copies(index, _):
         group_copy(index_hbm, index_ref, index_sems, index, GROUP).start()
         group_copy(value_hbm, value_ref, value_sems, index, GROUP).start()
         return 0
 
-    query_copy = pltpu.make_async_copy(query_hbm, query_ref, query_sem)
-    query_copy.start()
     lax.fori_loop(0, groups, start_copies, 0)
     row_ref[...] = jnp.zeros_like(row_ref)
     col_ref[...] = jnp.zeros_like(col_ref)
@@ -92,6 +92,7 @@
         jnp.int32, (128, 128), 1
     )
     identity = jnp.where(diagonal, 1.0, 0.0).astype(jnp.bfloat16)
+    ones = (lax.broadcasted_iota(jnp.int32, (8, 128), 0) == 0).astype(jnp.bfloat16)
     zero = jnp.zeros((16, 128), jnp.bfloat16)
 
     def build_group(index, _):
@@ -102,7 +103,7 @@
             slots = [index * GROUP + inside, index * GROUP + inside + 1]
             tables = []
             for slot in slots:
-                active = (slot < live_ref[0, 0]).astype(jnp.float32)
+                active = (slot < live_count(places)).astype(jnp.float32)
                 tables.append((index_ref[slot], value_ref[slot].astype(jnp.float32) * active))
             sums = [[zero] * 8 for _ in slots]
             for entry in range(0, 16, 2):
@@ -119,24 +120,17 @@
                         ]
                         sums[which][part] = sums[which][part] + (first + second)
             for slot, (_, values), parts in zip(slots, tables, sums):
-                row_block, col_block = place_of(spots_ref, slot, col_blocks)
+                row_block, col_block = place_of(places, slot, col_blocks)
                 block = jnp.concatenate(parts, axis=0)
                 block_ref[slot] = block
                 row_ref[row_block] += values[:8] + values[8:]
                 turned = dot_across(identity, block)
-                flipped_ref[slot] = turned.astype(jnp.bfloat16)
-                col_ref[col_block] += jnp.sum(turned.reshape(16, 8, 128), axis=0)
+                turned = turned.astype(jnp.bfloat16)
+                flipped_ref[slot] = turned
+                col_ref[col_block] += dot_plain(ones, turned)
         group_copy(block_ref, block_hbm, block_sems, index, GROUP).start()
         group_copy(flipped_ref, flipped_hbm, flipped_sems, index, GROUP).start()
         return 0
-
-    query_copy.wait()
-    size = query_ref.shape[0]
-    gram = jnp.zeros((size, 128), jnp.float32)
-    for part in range(per_seg):
-        query = query_ref[:, part * 128 : part * 128 + 128]
-        gram += exact_across(query, tall(query))
-    gram_ref[...] = side_by_side(in_terms(gram, 3))
 
     lax.fori_loop(0, groups, build_group, 0)
     for ahead, out in enumerate(row_outs, 1):
@@ -165,21 +159,18 @@
 
 
 def build_blocks(
-    spots, live, index_table, value_table, queries, row_count, col_count, per_seg
+    places, index_table, value_table, row_count, col_count, per_seg
 ):
     slots = index_table.shape[0]
     groups = slots // GROUP
     sum_shapes = [(per_seg, 128)] * (row_count - 1) + [(col_count * per_seg, 128)]
-    gram_shape = (queries.shape[0], 128)
     return pl.pallas_call(
         build_kernel,
-        in_specs=[SCALARS, SCALARS, ANYWHERE, ANYWHERE, ANYWHERE],
-        out_specs=[ANYWHERE] * 2 + [IN_VMEM] * (len(sum_shapes) + 1),
+        in_specs=[SCALARS, SCALARS, ANYWHERE, ANYWHERE],
+        out_specs=[ANYWHERE] * 2 + [IN_VMEM] * len(sum_shapes),
         out_shape=[jax.ShapeDtypeStruct((SPARE * slots, 128, 128), jnp.bfloat16)] * 2
-        + [jax.ShapeDtypeStruct(shape, jnp.float32) for shape in sum_shapes]
-        + [jax.ShapeDtypeStruct(gram_shape, jnp.bfloat16)],
+        + [jax.ShapeDtypeStruct(shape, jnp.float32) for shape in sum_shapes],
         scratch_shapes=[
-            pltpu.VMEM(queries.shape, queries.dtype),
             pltpu.VMEM(index_table.shape, index_table.dtype),
             pltpu.VMEM(value_table.shape, value_table.dtype),
             pltpu.VMEM((slots, 128, 128), jnp.bfloat16),
@@ -190,15 +181,14 @@
             pltpu.SemaphoreType.DMA((groups,)),
             pltpu.SemaphoreType.DMA((groups,)),
             pltpu.SemaphoreType.DMA((groups,)),
-            pltpu.SemaphoreType.DMA(()),
         ],
         compiler_params=pltpu.CompilerParams(vmem_limit_bytes=BUILD_GRANT),
         name="build_blocks",
-    )(spots, live, index_table, value_table, queries)
-
-
-def each_group(live_ref, block_hbm, block_ref, sems, prepare, run_group):
-    groups = group_count(live_ref, BATCH)
+    )(*places, index_table, value_table)
+
+
+def each_group(places, block_hbm, block_ref, sems, prepare, run_group):
+    groups = group_count(places, BATCH)
 
     def start_copy(index, _):
         group_copy(block_hbm, block_ref, sems, index, BATCH).start()
@@ -233,6 +223,7 @@
 
 
 def backward_kernel(row_count, spots_ref, live_ref, block_hbm, *refs):
+    places = (spots_ref, live_ref)
     row_pieces = refs[:row_count]
     col_out_ref, block_ref, sems, row_dir_ref, even_ref, odd_ref = refs[row_count:]
     per_seg = row_pieces[0].shape[0]
@@ -245,14 +236,14 @@
 
     def run_group(first_slot):
         add_products(
-            lambda slot: place_of(spots_ref, slot, col_blocks),
+            lambda slot: place_of(places, slot, col_blocks),
             first_slot,
             block_ref,
             lambda row_block: row_dir_ref[row_block],
             [even_ref, odd_ref],
         )
 
-    each_group(live_ref, block_hbm, block_ref, sems, prepare, run_group)
+    each_group(places, block_hbm, block_ref, sems, prepare, run_group)
     size = even_ref.shape[1]
     for segment in range(col_out_ref.shape[0]):
         for part in range(per_seg):
@@ -307,6 +298,7 @@
 
 
 def forward_kernel(spots_ref, live_ref, block_hbm, col_dir_ref, *refs):
+    places = (spots_ref, live_ref)
     *row_outs, block_ref, sems, even_ref, odd_ref = refs
     per_seg = row_outs[0].shape[0]
     col_blocks = col_dir_ref.shape[0] * per_seg
@@ -317,14 +309,14 @@
 
     def run_group(first_slot):
         add_products(
-            lambda slot: place_of(spots_ref, slot, col_blocks)[::-1],
+            lambda slot: place_of(places, slot, col_blocks)[::-1],
             first_slot,
             block_ref,
             lambda col_block: col_dir_ref[divided(col_block, per_seg)],
             [even_ref, odd_ref],
         )
 
-    each_group(live_ref, block_hbm, block_ref, sems, prepare, run_group)
+    each_group(places, block_hbm, block_ref, sems, prepare, run_group)
     for ahead, out in enumerate(row_outs):
         first = lax.rem(lax.axis_index("row") + ahead, len(row_outs)) * per_seg
         for part in range(per_seg):
@@ -407,10 +399,16 @@
         scaled_ref[part] = scaled
 
 
-def spread_kernel(scaled_ref, gram_ref, after_ref, copies_ref):
+def spread_kernel(scaled_ref, query_ref, copies_ref):
+    per_seg, size, _ = scaled_ref.shape
+    gram = jnp.zeros((size, 128), jnp.float32)
+    for part in range(per_seg):
+        query = query_ref[:, part * 128 : part * 128 + 128]
+        gram += exact_across(query, tall(query))
+    terms = side_by_side(in_terms(gram, 3))
     for copy in range(copies_ref.shape[0]):
-        copies_ref[copy, : scaled_ref.shape[0]] = scaled_ref[...]
-        copies_ref[copy, scaled_ref.shape[0]] = gram_ref[...]
+        copies_ref[copy, :per_seg] = scaled_ref[...]
+        copies_ref[copy, per_seg] = terms
 
 
 def scaled_sum(row_refs, col_ref, scaling_ref, part):
@@ -560,11 +558,15 @@
     return lax.all_to_all(pieces, axis, 0, 0, tiled=True)
 
 
-def simple_call(kernel, shapes, name, *operands):
+def simple_call(kernel, shapes, name, *operands, bytes_accessed=None):
+    cost = None
+    if bytes_accessed:
+        cost = pl.CostEstimate(flops=0, bytes_accessed=bytes_accessed, transcendentals=0)
     return pl.pallas_call(
         kernel,
         out_shape=shapes,
         compiler_params=pltpu.CompilerParams(vmem_limit_bytes=SMALL_GRANT),
+        cost_estimate=cost,
         name=name,
     )(*operands)
 
@@ -592,11 +594,10 @@
 
     message = jax.ShapeDtypeStruct((col_count, per_seg + 1) + piece[1:], jnp.bfloat16)
 
-    blocks, flipped_blocks, *row_sums, col_sums, query_gram = build_blocks(
-        *places,
+    blocks, flipped_blocks, *row_sums, col_sums = build_blocks(
+        places,
         neighbor_cols[0, 0],
         neighbor_sims[0, 0],
-        queries,
         row_count,
         col_count,
         per_seg,
@@ -614,7 +615,7 @@
 
     row_pieces = pass_around([scaled] * row_count, "row")
     (copies,) = simple_call(
-        spread_kernel, [message], "spread", scaled, query_gram, row_pieces[-1]
+        spread_kernel, [message], "spread", scaled, queries, bytes_accessed=16 * 1024 * 1024
     )
     first_dirs = exchange(copies, "col")
     total = backward_product(places, flipped_blocks, row_pieces, col_count)

time: 110 us -> 134 us (1.22)
  starting transfers between devices: 44.7 us -> 59 us
  Pallas kernels: 36.5 us -> 49.2 us
  waiting for transfers between devices: 24.7 us -> 21.9 us
    pallas_call x1, Pallas kernels: 13.9 us -> 26.3 us  [build_blocks(): pl.pallas_call(build_kernel, in_specs=[SCALARS, SCALARS, ANYWHERE, ANYWHE...]
    ppermute x18, starting transfers between devices: 22.9 us -> 31.6 us  [pass_around(): lax.ppermute(pieces[ahead], axis, [(at, (at + ahead) % count) for at in r...]
    all_to_all x5, starting transfers between devices: 21.8 us -> 27.3 us  [exchange(): return lax.all_to_all(pieces, axis, 0, 0, tiled=True)]
    all_to_all x5, waiting for transfers between devices: 12.6 us -> 10.1 us  [exchange(): return lax.all_to_all(pieces, axis, 0, 0, tiled=True)]
  transfers between devices with their start and end apart: 23 -> 23, of which waited for: 13 -> 13; matrix products, arithmetic and copies ran while one was open for 0% -> 0% of each run, Pallas kernels for 13% -> 11%
where the time goes in v8:
time: 134 us
  starting transfers between devices  59 us (44%)
  Pallas kernels  49.2 us (37%)
  waiting for transfers between devices  21.9 us (16%)
  local copies, waits for them, and re-layouts  2.37 us (2%)
  between operations  1.41 us (1%)
    ppermute x18, starting transfers between devices, pass_around(): lax.ppermute(pieces[ahead], axis, [(at, (at + ahead) % count) for at in r...  31.6 us
    all_to_all x5, starting transfers between devices, exchange(): return lax.all_to_all(pieces, axis, 0, 0, tiled=True)  27.3 us
    pallas_call x1, Pallas kernels, build_blocks(): pl.pallas_call(build_kernel, in_specs=[SCALARS, SCALARS, ANYWHERE, ANYWHE...  26.3 us
    pallas_call x4, Pallas kernels, over_blocks(): pl.pallas_call(kernel, in_specs=[SCALARS, SCALARS, ANYWHERE] + [IN_VMEM]...  14.6 us
    ppermute x18, waiting for transfers between devices, pass_around(): lax.ppermute(pieces[ahead], axis, [(at, (at + ahead) % count) for at in r...  11.7 us
    all_to_all x5, waiting for transfers between devices, exchange(): return lax.all_to_all(pieces, axis, 0, 0, tiled=True)  10.1 us
    pallas_call x6, Pallas kernels, simple_call(): pl.pallas_call(kernel, out_shape=shapes, compiler_params=pltpu.CompilerPa...  8.31 us
  transfers between devices with their start and end apart: 23, of which 13 were waited for; matrix products, arithmetic and copies ran while one was open for 0% of the time, Pallas kernels for 11%

profile of v8, /device:TPU:0, one launch (start us, length us, event | category | flops | bytes accessed | tf_op | source)
XLA Modules:
  0.0 133.8 jit_solution(14065256749423189964)
XLA Ops:
  1.3 26.3 %build_blocks.1 = (bf16[1024,128,128]{2,1,0:T(8,128)(2,1)}, bf16[1024,128,128]{2,1,0:T(8,128)(2,1)}, f32[4,128]{1,0:T(4,128)}, f32[4,128]{1,0:T(4,128)}, f32[4,128]{1,0:T(4,128)}, /*index=5*/f32[32,128]{1,0:T(8,128)}) custom-call(s32[1,1,256]{2,1,0:T(1,128)} %spots_ref.9, s32[1,1]{1,0:T(1,128)S(6)} %copy.7.live_ref, s32[256,16,128]{2,1,0:T(8,128)} %bitcast.3, ...), custom_call_target="tpu_custom_call" | custom-call | tf_op jit(solution)/shard_map/build_blocks/pallas_call | solution.py:167
  27.6 7.3 %all-to-all-start = ((f32[8,4,128]{2,1,0:T(4,128)}), f32[8,4,128]{2,1,0:T(4,128)S(1)}, u32[]{:S(2)}, u32[]{:S(2)}) async-start(f32[8,4,128]{2,1,0:T(4,128)} %bitcast.5), calls=%async_computation | async-start | bytes 32768 | tf_op jit(solution)/shard_map/all_to_all | solution.py:558
  34.9 21.3 %collective-permute-start.1 = (f32[4,128]{1,0:T(4,128)}, f32[4,128]{1,0:T(4,128)S(1)}, u32[]{:S(2)}, u32[]{:S(2)}) collective-permute-start(f32[4,128]{1,0:T(4,128)} %get-tuple-element.25), channel_id=1, source_target_pairs={{0,16},{8,24},{16,0},{24,8},{1,17},{9,25},{17,1},{25,9},{2,18},{10... | collective-permute-start | bytes 6152 | tf_op jit(solution)/shard_map/ppermute | solution.py:552
  56.3 1.4 %collective-permute-start.2 = (f32[4,128]{1,0:T(4,128)}, f32[4,128]{1,0:T(4,128)S(1)}, u32[]{:S(2)}, u32[]{:S(2)}) collective-permute-start(f32[4,128]{1,0:T(4,128)} %get-tuple-element.26), channel_id=1, source_target_pairs={{0,24},{8,0},{16,8},{24,16},{1,25},{9,1},{17,9},{25,17},{2,26},{10... | collective-permute-start | bytes 6152 | tf_op jit(solution)/shard_map/ppermute | solution.py:552
  58.0 1.1 collective-permute-done.2.refs_2_
  59.2 0.8 copy-done
  60.1 0.8 copy-done.1
  60.9 1.0 spread.1
  61.9 6.0 %all-to-all-start.1 = ((bf16[8,5,32,128]{3,2,1,0:T(8,128)(2,1)}), bf16[8,5,32,128]{3,2,1,0:T(8,128)(2,1)S(1)}, u32[]{:S(2)}, u32[]{:S(2)}) async-start(bf16[8,5,32,128]{3,2,1,0:T(8,128)(2,1)} %spread.1), calls=%async_computation.1 | async-start | bytes 655360 | tf_op jit(solution)/shard_map/all_to_all | solution.py:558
  68.0 1.4 %collective-permute-start.8 = (bf16[4,32,128]{2,1,0:T(8,128)(2,1)S(1)}, bf16[4,32,128]{2,1,0:T(8,128)(2,1)S(1)}, u32[]{:S(2)}, u32[]{:S(2)}) collective-permute-start(bf16[4,32,128]{2,1,0:T(8,128)(2,1)S(1)} %get-tuple-element.28.scaled_ref.refs_0_), channel_id=1, source_target_pairs={{0,24},{8,0},{16,8},{24,16},{1,25},{9,1},{17,9},{25,17},{2,26},{10... | collective-permute-start | bytes 98312 | tf_op jit(solution)/shard_map/ppermute | solution.py:552
  69.7 1.3 collective-permute-done.8.refs_3_
  71.0 2.4 %collective-permute-done.7.refs_2_ = bf16[4,32,128]{2,1,0:T(8,128)(2,1)S(1)} collective-permute-done((bf16[4,32,128]{2,1,0:T(8,128)(2,1)S(1)}, bf16[4,32,128]{2,1,0:T(8,128)(2,1)S(1)}, u32[]{:S(2)}, u32[]{:S(2)}) %collective-permute-start.7) | collective-permute-done | bytes 32800 | tf_op jit(solution)/shard_map/ppermute | solution.py:552
  74.0 4.2 %backward_product.2 = bf16[8,128,128]{2,1,0:T(8,128)(2,1)} custom-call(s32[1,1,256]{2,1,0:T(1,128)S(1)} %copy-done.3, s32[1,1]{1,0:T(1,128)S(6)} %copy.7.live_ref, bf16[1024,128,128]{2,1,0:T(8,128)(2,1)} %get-tuple-element.33.block_hbm, bf16[4,32,128]{2,1,0:T(8,128)(2,1)S(1)} %get-tuple-element.28.scaled_ref.refs_0_, ...), custom_call_target="tpu_custom_call" | custom-call | flops 268435456 | bytes 8388608 | tf_op jit(solution)/shard_map/backward_product/pallas_call | solution.py:329
  78.8 5.2 %all-to-all-start.2 = ((bf16[8,128,128]{2,1,0:T(8,128)(2,1)}), bf16[8,128,128]{2,1,0:T(8,128)(2,1)S(1)}, u32[]{:S(2)}, u32[]{:S(2)}) async-start(bf16[8,128,128]{2,1,0:T(8,128)(2,1)} %backward_product.2), calls=%async_computation.2 | async-start | bytes 524288 | tf_op jit(solution)/shard_map/all_to_all | solution.py:558
  84.0 3.5 %forward_product.2 = (bf16[4,32,128]{2,1,0:T(8,128)(2,1)S(1)}, bf16[4,32,128]{2,1,0:T(8,128)(2,1)S(1)}, bf16[4,32,128]{2,1,0:T(8,128)(2,1)S(1)}, bf16[4,32,128]{2,1,0:T(8,128)(2,1)S(1)}) custom-call(s32[1,1,256]{2,1,0:T(1,128)S(1)} %copy-done.4, s32[1,1]{1,0:T(1,128)S(6)} %copy.7.live_ref, bf16[1024,128,128]{2,1,0:T(8,128)(2,1)} %get-tuple-element.23.block_hbm, ...), custom_call_target="tpu_custom_call" | custom-call | flops 268435456 | bytes 8388608 | tf_op jit(solution)/shard_map/forward_product/pallas_call | solution.py:329
  88.2 1.4 %collective-permute-start.5 = (bf16[4,32,128]{2,1,0:T(8,128)(2,1)S(1)}, bf16[4,32,128]{2,1,0:T(8,128)(2,1)S(1)}, u32[]{:S(2)}, u32[]{:S(2)}) collective-permute-start(bf16[4,32,128]{2,1,0:T(8,128)(2,1)S(1)} %get-tuple-element.32), channel_id=1, source_target_pairs={{0,24},{8,0},{16,8},{24,16},{1,25},{9,1},{17,9},{25,17},{2,26},{10... | collective-permute-start | bytes 98312 | tf_op jit(solution)/shard_map/ppermute | solution.py:552
  89.5 2.8 %all-to-all-done.2.refs_4_ = bf16[8,128,128]{2,1,0:T(8,128)(2,1)S(1)} async-done(((bf16[8,128,128]{2,1,0:T(8,128)(2,1)}), bf16[8,128,128]{2,1,0:T(8,128)(2,1)S(1)}, u32[]{:S(2)}, u32[]{:S(2)}) %all-to-all-start.2) | async-done | bytes 262176 | tf_op jit(solution)/shard_map/all_to_all | solution.py:558
  92.4 1.2 middle.1
  93.5 5.2 %all-to-all-start.3 = ((bf16[8,5,32,128]{3,2,1,0:T(8,128)(2,1)}), bf16[8,5,32,128]{3,2,1,0:T(8,128)(2,1)S(1)}, u32[]{:S(2)}, u32[]{:S(2)}) async-start(bf16[8,5,32,128]{3,2,1,0:T(8,128)(2,1)} %get-tuple-element.35), calls=%async_computation.3 | async-start | bytes 655360 | tf_op jit(solution)/shard_map/all_to_all | solution.py:558
  98.7 1.0 collective-permute-start.14
  99.8 1.5 %collective-permute-start.13 = (bf16[4,32,128]{2,1,0:T(8,128)(2,1)S(1)}, bf16[4,32,128]{2,1,0:T(8,128)(2,1)S(1)}, u32[]{:S(2)}, u32[]{:S(2)}) collective-permute-start(bf16[4,32,128]{2,1,0:T(8,128)(2,1)S(1)} %get-tuple-element.40.refs_0_), channel_id=1, source_target_pairs={{0,16},{8,24},{16,0},{24,8},{1,17},{9,25},{17,1},{25,9},{2,18},{10... | collective-permute-start | bytes 98312 | tf_op jit(solution)/shard_map/ppermute | solution.py:552
  101.4 2.3 %collective-permute-done.13.refs_2_ = bf16[4,32,128]{2,1,0:T(8,128)(2,1)S(1)} collective-permute-done((bf16[4,32,128]{2,1,0:T(8,128)(2,1)S(1)}, bf16[4,32,128]{2,1,0:T(8,128)(2,1)S(1)}, u32[]{:S(2)}, u32[]{:S(2)}) %collective-permute-start.13) | collective-permute-done | bytes 32800 | tf_op jit(solution)/shard_map/ppermute | solution.py:552
  103.7 0.9 collective-permute-done.12.refs_1_
  104.6 3.5 %backward_product.3.total_ref = bf16[8,128,128]{2,1,0:T(8,128)(2,1)S(1)} custom-call(s32[1,1,256]{2,1,0:T(1,128)S(1)} %copy-done.4, s32[1,1]{1,0:T(1,128)S(6)} %copy.7.live_ref, bf16[1024,128,128]{2,1,0:T(8,128)(2,1)} %get-tuple-element.33.block_hbm, bf16[4,32,128]{2,1,0:T(8,128)(2,1)S(1)} %get-tuple-element.40.refs_0_, ...), custom_call_target="tpu_custom_call" | custom-call | flops 268435456 | bytes 8388608 | tf_op jit(solution)/shard_map/backward_product/pallas_call | solution.py:329
  108.1 2.3 %all-to-all-done.3.col_dir_ref = bf16[8,5,32,128]{3,2,1,0:T(8,128)(2,1)S(1)} async-done(((bf16[8,5,32,128]{3,2,1,0:T(8,128)(2,1)}), bf16[8,5,32,128]{3,2,1,0:T(8,128)(2,1)S(1)}, u32[]{:S(2)}, u32[]{:S(2)}) %all-to-all-start.3) | async-done | bytes 327712 | tf_op jit(solution)/shard_map/all_to_all | solution.py:558
  110.3 1.2 attach.1
  111.6 3.6 %all-to-all-start.4 = ((bf16[8,144,128]{2,1,0:T(8,128)(2,1)}), bf16[8,144,128]{2,1,0:T(8,128)(2,1)S(1)}, u32[]{:S(2)}, u32[]{:S(2)}) async-start(bf16[8,144,128]{2,1,0:T(8,128)(2,1)} %get-tuple-element.41), calls=%async_computation.4 | async-start | bytes 589824 | tf_op jit(solution)/shard_map/all_to_all | solution.py:558
  115.2 3.5 %forward_product.3 = (bf16[4,32,128]{2,1,0:T(8,128)(2,1)S(1)}, bf16[4,32,128]{2,1,0:T(8,128)(2,1)S(1)}, bf16[4,32,128]{2,1,0:T(8,128)(2,1)S(1)}, bf16[4,32,128]{2,1,0:T(8,128)(2,1)S(1)}) custom-call(s32[1,1,256]{2,1,0:T(1,128)S(1)} %copy-done.4, s32[1,1]{1,0:T(1,128)S(6)} %copy.7.live_ref, bf16[1024,128,128]{2,1,0:T(8,128)(2,1)} %get-tuple-element.23.block_hbm, ...), custom_call_target="tpu_custom_call" | custom-call | flops 268435456 | bytes 8388608 | tf_op jit(solution)/shard_map/forward_product/pallas_call | solution.py:329
  119.1 1.4 %collective-permute-start.11 = (bf16[4,32,128]{2,1,0:T(8,128)(2,1)S(1)}, bf16[4,32,128]{2,1,0:T(8,128)(2,1)S(1)}, u32[]{:S(2)}, u32[]{:S(2)}) collective-permute-start(bf16[4,32,128]{2,1,0:T(8,128)(2,1)S(1)} %get-tuple-element.39), channel_id=1, source_target_pairs={{0,24},{8,0},{16,8},{24,16},{1,25},{9,1},{17,9},{25,17},{2,26},{10... | collective-permute-start | bytes 98312 | tf_op jit(solution)/shard_map/ppermute | solution.py:552
  120.5 4.5 %all-to-all-done.4.col_ref.refs_8_ = bf16[8,144,128]{2,1,0:T(8,128)(2,1)S(1)} async-done(((bf16[8,144,128]{2,1,0:T(8,128)(2,1)}), bf16[8,144,128]{2,1,0:T(8,128)(2,1)S(1)}, u32[]{:S(2)}, u32[]{:S(2)}) %all-to-all-start.4) | async-done | bytes 294944 | tf_op jit(solution)/shard_map/all_to_all | solution.py:558
  126.6 2.5 %collective-permute-done.16.refs_6_ = f32[32,128]{1,0:T(8,128)S(1)} collective-permute-done((f32[32,128]{1,0:T(8,128)S(1)}, f32[32,128]{1,0:T(8,128)S(1)}, u32[]{:S(2)}, u32[]{:S(2)}) %collective-permute-start.16) | collective-permute-done | bytes 16416 | tf_op jit(solution)/shard_map/ppermute | solution.py:552
  129.2 4.7 %close.1 = (f32[32,512]{1,0:T(8,128)}, f32[32,512]{1,0:T(8,128)}) custom-call(bf16[4,32,128]{2,1,0:T(8,128)(2,1)S(1)} %get-tuple-element.36.refs_0_, bf16[4,32,128]{2,1,0:T(8,128)(2,1)S(1)} %collective-permute-done.9.refs_1_, bf16[4,32,128]{2,1,0:T(8,128)(2,1)S(1)} %collective-permute-done.10.refs_2_, ...), custom_call_target="tpu_custom_call" | custom-call | tf_op jit(solution)/shard_map/close/pallas_call | solution.py:565
  (35 shorter events, 4.8 us)
Async XLA Ops:
  0.6 83.3 %copy-start.4 = (s32[1,1,256]{2,1,0:T(1,128)S(1)}, s32[1,1,256]{2,1,0:T(1,128)}, u32[]{:S(2)}) copy-start(s32[1,1,256]{2,1,0:T(1,128)} %spots_ref.9) | copy-start | bytes 3076
  27.6 31.6 %all-to-all-start = ((f32[8,4,128]{2,1,0:T(4,128)}), f32[8,4,128]{2,1,0:T(4,128)S(1)}, u32[]{:S(2)}, u32[]{:S(2)}) async-start(f32[8,4,128]{2,1,0:T(4,128)} %bitcast.5), calls=%async_computation | async-start | bytes 32768 | tf_op jit(solution)/shard_map/all_to_all | solution.py:558
  34.9 22.7 %collective-permute-start = (f32[4,128]{1,0:T(4,128)}, f32[4,128]{1,0:T(4,128)S(1)}, u32[]{:S(2)}, u32[]{:S(2)}) collective-permute-start(f32[4,128]{1,0:T(4,128)} %get-tuple-element.24), channel_id=1, source_target_pairs={{0,8},{8,16},{16,24},{24,0},{1,9},{9,17},{17,25},{25,1},{2,10},{10... | collective-permute-start | bytes 6152 | tf_op jit(solution)/shard_map/ppermute | solution.py:552
  34.9 23.1 %collective-permute-start.1 = (f32[4,128]{1,0:T(4,128)}, f32[4,128]{1,0:T(4,128)S(1)}, u32[]{:S(2)}, u32[]{:S(2)}) collective-permute-start(f32[4,128]{1,0:T(4,128)} %get-tuple-element.25), channel_id=1, source_target_pairs={{0,16},{8,24},{16,0},{24,8},{1,17},{9,25},{17,1},{25,9},{2,18},{10... | collective-permute-start | bytes 6152 | tf_op jit(solution)/shard_map/ppermute | solution.py:552
  56.3 2.9 %collective-permute-start.2 = (f32[4,128]{1,0:T(4,128)}, f32[4,128]{1,0:T(4,128)S(1)}, u32[]{:S(2)}, u32[]{:S(2)}) collective-permute-start(f32[4,128]{1,0:T(4,128)} %get-tuple-element.26), channel_id=1, source_target_pairs={{0,24},{8,0},{16,8},{24,16},{1,25},{9,1},{17,9},{25,17},{2,26},{10... | collective-permute-start | bytes 6152 | tf_op jit(solution)/shard_map/ppermute | solution.py:552
  59.2 0.8 copy-start
  60.0 0.8 copy-start.1
  61.9 16.8 %all-to-all-start.1 = ((bf16[8,5,32,128]{3,2,1,0:T(8,128)(2,1)}), bf16[8,5,32,128]{3,2,1,0:T(8,128)(2,1)S(1)}, u32[]{:S(2)}, u32[]{:S(2)}) async-start(bf16[8,5,32,128]{3,2,1,0:T(8,128)(2,1)} %spread.1), calls=%async_computation.1 | async-start | bytes 655360 | tf_op jit(solution)/shard_map/all_to_all | solution.py:558
  68.0 3.0 %collective-permute-start.8 = (bf16[4,32,128]{2,1,0:T(8,128)(2,1)S(1)}, bf16[4,32,128]{2,1,0:T(8,128)(2,1)S(1)}, u32[]{:S(2)}, u32[]{:S(2)}) collective-permute-start(bf16[4,32,128]{2,1,0:T(8,128)(2,1)S(1)} %get-tuple-element.28.scaled_ref.refs_0_), channel_id=1, source_target_pairs={{0,24},{8,0},{16,8},{24,16},{1,25},{9,1},{17,9},{25,17},{2,26},{10... | collective-permute-start | bytes 98312 | tf_op jit(solution)/shard_map/ppermute | solution.py:552
  69.4 4.0 %collective-permute-start.7 = (bf16[4,32,128]{2,1,0:T(8,128)(2,1)S(1)}, bf16[4,32,128]{2,1,0:T(8,128)(2,1)S(1)}, u32[]{:S(2)}, u32[]{:S(2)}) collective-permute-start(bf16[4,32,128]{2,1,0:T(8,128)(2,1)S(1)} %get-tuple-element.28.scaled_ref.refs_0_), channel_id=1, source_target_pairs={{0,16},{8,24},{16,0},{24,8},{1,17},{9,25},{17,1},{25,9},{2,18},{10... | collective-permute-start | bytes 98312 | tf_op jit(solution)/shard_map/ppermute | solution.py:552
  69.7 3.7 %collective-permute-start.6 = (bf16[4,32,128]{2,1,0:T(8,128)(2,1)S(1)}, bf16[4,32,128]{2,1,0:T(8,128)(2,1)S(1)}, u32[]{:S(2)}, u32[]{:S(2)}) collective-permute-start(bf16[4,32,128]{2,1,0:T(8,128)(2,1)S(1)} %get-tuple-element.28.scaled_ref.refs_0_), channel_id=1, source_target_pairs={{0,8},{8,16},{16,24},{24,0},{1,9},{9,17},{17,25},{25,1},{2,10},{10... | collective-permute-start | bytes 98312 | tf_op jit(solution)/shard_map/ppermute | solution.py:552
  73.4 0.7 copy-start.3
  74.0 18.3 %copy-start.2 = (f32[32,512]{1,0:T(8,128)S(1)}, f32[32,512]{1,0:T(8,128)}, u32[]{:S(2)}) copy-start(f32[32,512]{1,0:T(8,128)} %refs_10_.1) | copy-start | bytes 196612
  78.8 13.6 %all-to-all-start.2 = ((bf16[8,128,128]{2,1,0:T(8,128)(2,1)}), bf16[8,128,128]{2,1,0:T(8,128)(2,1)S(1)}, u32[]{:S(2)}, u32[]{:S(2)}) async-start(bf16[8,128,128]{2,1,0:T(8,128)(2,1)} %backward_product.2), calls=%async_computation.2 | async-start | bytes 524288 | tf_op jit(solution)/shard_map/all_to_all | solution.py:558
  87.5 4.9 %collective-permute-start.3 = (bf16[4,32,128]{2,1,0:T(8,128)(2,1)S(1)}, bf16[4,32,128]{2,1,0:T(8,128)(2,1)S(1)}, u32[]{:S(2)}, u32[]{:S(2)}) collective-permute-start(bf16[4,32,128]{2,1,0:T(8,128)(2,1)S(1)} %get-tuple-element.30), channel_id=1, source_target_pairs={{0,8},{8,16},{16,24},{24,0},{1,9},{9,17},{17,25},{25,1},{2,10},{10... | collective-permute-start | bytes 98312 | tf_op jit(solution)/shard_map/ppermute | solution.py:552
  87.5 4.8 %collective-permute-start.4 = (bf16[4,32,128]{2,1,0:T(8,128)(2,1)S(1)}, bf16[4,32,128]{2,1,0:T(8,128)(2,1)S(1)}, u32[]{:S(2)}, u32[]{:S(2)}) collective-permute-start(bf16[4,32,128]{2,1,0:T(8,128)(2,1)S(1)} %get-tuple-element.31), channel_id=1, source_target_pairs={{0,16},{8,24},{16,0},{24,8},{1,17},{9,25},{17,1},{25,9},{2,18},{10... | collective-permute-start | bytes 98312 | tf_op jit(solution)/shard_map/ppermute | solution.py:552
  88.2 4.2 %collective-permute-start.5 = (bf16[4,32,128]{2,1,0:T(8,128)(2,1)S(1)}, bf16[4,32,128]{2,1,0:T(8,128)(2,1)S(1)}, u32[]{:S(2)}, u32[]{:S(2)}) collective-permute-start(bf16[4,32,128]{2,1,0:T(8,128)(2,1)S(1)} %get-tuple-element.32), channel_id=1, source_target_pairs={{0,24},{8,0},{16,8},{24,16},{1,25},{9,1},{17,9},{25,17},{2,26},{10... | collective-permute-start | bytes 98312 | tf_op jit(solution)/shard_map/ppermute | solution.py:552
  93.5 16.8 %all-to-all-start.3 = ((bf16[8,5,32,128]{3,2,1,0:T(8,128)(2,1)}), bf16[8,5,32,128]{3,2,1,0:T(8,128)(2,1)S(1)}, u32[]{:S(2)}, u32[]{:S(2)}) async-start(bf16[8,5,32,128]{3,2,1,0:T(8,128)(2,1)} %get-tuple-element.35), calls=%async_computation.3 | async-start | bytes 655360 | tf_op jit(solution)/shard_map/all_to_all | solution.py:558
  98.7 2.6 %collective-permute-start.14 = (bf16[4,32,128]{2,1,0:T(8,128)(2,1)S(1)}, bf16[4,32,128]{2,1,0:T(8,128)(2,1)S(1)}, u32[]{:S(2)}, u32[]{:S(2)}) collective-permute-start(bf16[4,32,128]{2,1,0:T(8,128)(2,1)S(1)} %get-tuple-element.40.refs_0_), channel_id=1, source_target_pairs={{0,24},{8,0},{16,8},{24,16},{1,25},{9,1},{17,9},{25,17},{2,26},{10... | collective-permute-start | bytes 98312 | tf_op jit(solution)/shard_map/ppermute | solution.py:552
  99.8 3.9 %collective-permute-start.13 = (bf16[4,32,128]{2,1,0:T(8,128)(2,1)S(1)}, bf16[4,32,128]{2,1,0:T(8,128)(2,1)S(1)}, u32[]{:S(2)}, u32[]{:S(2)}) collective-permute-start(bf16[4,32,128]{2,1,0:T(8,128)(2,1)S(1)} %get-tuple-element.40.refs_0_), channel_id=1, source_target_pairs={{0,16},{8,24},{16,0},{24,8},{1,17},{9,25},{17,1},{25,9},{2,18},{10... | collective-permute-start | bytes 98312 | tf_op jit(solution)/shard_map/ppermute | solution.py:552
  101.2 3.3 %collective-permute-start.12 = (bf16[4,32,128]{2,1,0:T(8,128)(2,1)S(1)}, bf16[4,32,128]{2,1,0:T(8,128)(2,1)S(1)}, u32[]{:S(2)}, u32[]{:S(2)}) collective-permute-start(bf16[4,32,128]{2,1,0:T(8,128)(2,1)S(1)} %get-tuple-element.40.refs_0_), channel_id=1, source_target_pairs={{0,8},{8,16},{16,24},{24,0},{1,9},{9,17},{17,25},{25,1},{2,10},{10... | collective-permute-start | bytes 98312 | tf_op jit(solution)/shard_map/ppermute | solution.py:552
  111.6 13.5 %all-to-all-start.4 = ((bf16[8,144,128]{2,1,0:T(8,128)(2,1)}), bf16[8,144,128]{2,1,0:T(8,128)(2,1)S(1)}, u32[]{:S(2)}, u32[]{:S(2)}) async-start(bf16[8,144,128]{2,1,0:T(8,128)(2,1)} %get-tuple-element.41), calls=%async_computation.4 | async-start | bytes 589824 | tf_op jit(solution)/shard_map/all_to_all | solution.py:558
  118.7 7.2 %collective-permute-start.9 = (bf16[4,32,128]{2,1,0:T(8,128)(2,1)S(1)}, bf16[4,32,128]{2,1,0:T(8,128)(2,1)S(1)}, u32[]{:S(2)}, u32[]{:S(2)}) collective-permute-start(bf16[4,32,128]{2,1,0:T(8,128)(2,1)S(1)} %get-tuple-element.37), channel_id=1, source_target_pairs={{0,8},{8,16},{16,24},{24,0},{1,9},{9,17},{17,25},{25,1},{2,10},{10... | collective-permute-start | bytes 98312 | tf_op jit(solution)/shard_map/ppermute | solution.py:552
  118.7 7.3 %collective-permute-start.10 = (bf16[4,32,128]{2,1,0:T(8,128)(2,1)S(1)}, bf16[4,32,128]{2,1,0:T(8,128)(2,1)S(1)}, u32[]{:S(2)}, u32[]{:S(2)}) collective-permute-start(bf16[4,32,128]{2,1,0:T(8,128)(2,1)S(1)} %get-tuple-element.38), channel_id=1, source_target_pairs={{0,16},{8,24},{16,0},{24,8},{1,17},{9,25},{17,1},{25,9},{2,18},{10... | collective-permute-start | bytes 98312 | tf_op jit(solution)/shard_map/ppermute | solution.py:552
  119.1 6.9 %collective-permute-start.11 = (bf16[4,32,128]{2,1,0:T(8,128)(2,1)S(1)}, bf16[4,32,128]{2,1,0:T(8,128)(2,1)S(1)}, u32[]{:S(2)}, u32[]{:S(2)}) collective-permute-start(bf16[4,32,128]{2,1,0:T(8,128)(2,1)S(1)} %get-tuple-element.39), channel_id=1, source_target_pairs={{0,24},{8,0},{16,8},{24,16},{1,25},{9,1},{17,9},{25,17},{2,26},{10... | collective-permute-start | bytes 98312 | tf_op jit(solution)/shard_map/ppermute | solution.py:552
  125.2 1.4 %collective-permute-start.17 = (f32[32,128]{1,0:T(8,128)S(1)}, f32[32,128]{1,0:T(8,128)S(1)}, u32[]{:S(2)}, u32[]{:S(2)}) collective-permute-start(f32[32,128]{1,0:T(8,128)S(1)} %gram_sum.1.refs_4_), channel_id=1, source_target_pairs={{0,24},{8,0},{16,8},{24,16},{1,25},{9,1},{17,9},{25,17},{2,26},{10... | collective-permute-start | bytes 49160 | tf_op jit(solution)/shard_map/ppermute | solution.py:552
  125.2 4.0 %collective-permute-start.16 = (f32[32,128]{1,0:T(8,128)S(1)}, f32[32,128]{1,0:T(8,128)S(1)}, u32[]{:S(2)}, u32[]{:S(2)}) collective-permute-start(f32[32,128]{1,0:T(8,128)S(1)} %gram_sum.1.refs_4_), channel_id=1, source_target_pairs={{0,16},{8,24},{16,0},{24,8},{1,17},{9,25},{17,1},{25,9},{2,18},{10... | collective-permute-start | bytes 49160 | tf_op jit(solution)/shard_map/ppermute | solution.py:552
  125.8 3.3 %collective-permute-start.15 = (f32[32,128]{1,0:T(8,128)S(1)}, f32[32,128]{1,0:T(8,128)S(1)}, u32[]{:S(2)}, u32[]{:S(2)}) collective-permute-start(f32[32,128]{1,0:T(8,128)S(1)} %gram_sum.1.refs_4_), channel_id=1, source_target_pairs={{0,8},{8,16},{16,24},{24,0},{1,9},{9,17},{17,25},{25,1},{2,10},{10... | collective-permute-start | bytes 49160 | tf_op jit(solution)/shard_map/ppermute | solution.py:552

commit v9 on v8

--- a/solution.py
+++ b/solution.py
@@ -8,7 +8,7 @@
 from jax.sharding import PartitionSpec as P
 
 graph_weight = 0.95
-GROUP = 16
+GROUP = 32
 BATCH = 32
 SPARE = 4
 PANEL = 8
@@ -92,22 +92,25 @@
         jnp.int32, (128, 128), 1
     )
     identity = jnp.where(diagonal, 1.0, 0.0).astype(jnp.bfloat16)
-    ones = (lax.broadcasted_iota(jnp.int32, (8, 128), 0) == 0).astype(jnp.bfloat16)
     zero = jnp.zeros((16, 128), jnp.bfloat16)
 
     def build_group(index, _):
         group_copy(index_hbm, index_ref, index_sems, index, GROUP).wait()
         group_copy(value_hbm, value_ref, value_sems, index, GROUP).wait()
         targets = [(rows_16 + 16 * part).astype(jnp.int16) for part in range(8)]
-        for inside in range(0, GROUP, 2):
-            slots = [index * GROUP + inside, index * GROUP + inside + 1]
+
+        def load_pair(inside):
             tables = []
-            for slot in slots:
+            for slot in (index * GROUP + inside, index * GROUP + inside + 1):
                 active = (slot < live_count(places)).astype(jnp.float32)
-                tables.append((index_ref[slot], value_ref[slot].astype(jnp.float32) * active))
-            sums = [[zero] * 8 for _ in slots]
+                values = value_ref[slot].astype(jnp.float32) * active
+                tables.append((slot, index_ref[slot], values))
+            return tables
+
+        def build_pair(tables):
+            sums = [[zero] * 8 for _ in tables]
             for entry in range(0, 16, 2):
-                for which, (indices, values) in enumerate(tables):
+                for which, (_, indices, values) in enumerate(tables):
                     pair = []
                     for at in (entry, entry + 1):
                         index_row = jnp.broadcast_to(indices[at : at + 1], (16, 128))
@@ -119,15 +122,27 @@
                             for index_row, value_row in pair
                         ]
                         sums[which][part] = sums[which][part] + (first + second)
-            for slot, (_, values), parts in zip(slots, tables, sums):
+            return [jnp.concatenate(parts, axis=0) for parts in sums]
+
+        def store_turned(tables, turned):
+            for (slot, _, values), block in zip(tables, turned):
                 row_block, col_block = place_of(places, slot, col_blocks)
-                block = jnp.concatenate(parts, axis=0)
+                flipped_ref[slot] = block.astype(jnp.bfloat16)
+                col_ref[col_block] += jnp.sum(block.reshape(16, 8, 128), axis=0)
+                row_ref[row_block] += values[:8] + values[8:]
+
+        tables = load_pair(0)
+        waiting = None
+        for inside in range(0, GROUP, 2):
+            following = load_pair(inside + 2) if inside + 2 < GROUP else None
+            blocks = build_pair(tables)
+            if waiting:
+                store_turned(*waiting)
+            for (slot, _, _), block in zip(tables, blocks):
                 block_ref[slot] = block
-                row_ref[row_block] += values[:8] + values[8:]
-                turned = dot_across(identity, block)
-                turned = turned.astype(jnp.bfloat16)
-                flipped_ref[slot] = turned
-                col_ref[col_block] += dot_plain(ones, turned)
+            waiting = (tables, [dot_across(identity, block) for block in blocks])
+            tables = following
+        store_turned(*waiting)
         group_copy(block_ref, block_hbm, block_sems, index, GROUP).start()
         group_copy(flipped_ref, flipped_hbm, flipped_sems, index, GROUP).start()
         return 0
@@ -388,26 +403,21 @@
 
 
 def start_kernel(*refs):
-    *row_refs, col_ref, query_ref, scaling_ref, scaled_ref = refs
+    *row_refs, col_ref, query_ref, scaling_ref, scaled_ref, copies_ref = refs
     degree = 1.0 + 0.5 * total_of([ref[...] for ref in [*row_refs, *leading(col_ref)]])
     scaling = 1.0 / jnp.sqrt(degree)
     scaling_ref[...] = scaling
-    for part in range(scaling.shape[0]):
-        scaled = (
-            scaling[part : part + 1] * query_ref[:, part * 128 : part * 128 + 128]
-        ).astype(jnp.bfloat16)
-        scaled_ref[part] = scaled
-
-
-def spread_kernel(scaled_ref, query_ref, copies_ref):
     per_seg, size, _ = scaled_ref.shape
     gram = jnp.zeros((size, 128), jnp.float32)
     for part in range(per_seg):
         query = query_ref[:, part * 128 : part * 128 + 128]
+        scaled = (scaling[part : part + 1] * query).astype(jnp.bfloat16)
+        scaled_ref[part] = scaled
+        for copy in range(copies_ref.shape[0]):
+            copies_ref[copy, part] = scaled
         gram += exact_across(query, tall(query))
     terms = side_by_side(in_terms(gram, 3))
     for copy in range(copies_ref.shape[0]):
-        copies_ref[copy, :per_seg] = scaled_ref[...]
         copies_ref[copy, per_seg] = terms
 
 
@@ -558,15 +568,11 @@
     return lax.all_to_all(pieces, axis, 0, 0, tiled=True)
 
 
-def simple_call(kernel, shapes, name, *operands, bytes_accessed=None):
-    cost = None
-    if bytes_accessed:
-        cost = pl.CostEstimate(flops=0, bytes_accessed=bytes_accessed, transcendentals=0)
+def simple_call(kernel, shapes, name, *operands):
     return pl.pallas_call(
         kernel,
         out_shape=shapes,
         compiler_params=pltpu.CompilerParams(vmem_limit_bytes=SMALL_GRANT),
-        cost_estimate=cost,
         name=name,
     )(*operands)
 
@@ -604,20 +610,17 @@
     )
     col_part = exchange(col_sums.reshape(col_count, per_seg, 128), "col")
     row_parts = pass_around([None, *row_sums], "row")[1:]
-    scaling, scaled = simple_call(
+    scaling, scaled, copies = simple_call(
         start_kernel,
-        [jax.ShapeDtypeStruct((per_seg, 128), jnp.float32), narrow],
+        [jax.ShapeDtypeStruct((per_seg, 128), jnp.float32), narrow, message],
         "start",
         *row_parts,
         col_part,
         queries,
     )
 
+    first_dirs = exchange(copies, "col")
     row_pieces = pass_around([scaled] * row_count, "row")
-    (copies,) = simple_call(
-        spread_kernel, [message], "spread", scaled, queries, bytes_accessed=16 * 1024 * 1024
-    )
-    first_dirs = exchange(copies, "col")
     total = backward_product(places, flipped_blocks, row_pieces, col_count)
     col_part = exchange(total, "col")
     totals = forward_product(places, blocks, first_dirs, row_count, piece)

time: 134 us -> 110 us (0.82)
  Pallas kernels: 49.2 us -> 36.2 us
  starting transfers between devices: 59 us -> 53.3 us
  waiting for transfers between devices: 21.9 us -> 18.5 us
    pallas_call x1, Pallas kernels: 26.3 us -> 13.3 us  [build_blocks(): pl.pallas_call(build_kernel, in_specs=[SCALARS, SCALARS, ANYWHERE, ANYWHE...]
    ppermute x18, starting transfers between devices: 31.6 us -> 27.2 us  [pass_around(): lax.ppermute(pieces[ahead], axis, [(at, (at + ahead) % count) for at in r...]
    all_to_all x5, waiting for transfers between devices: 10.1 us -> 6.21 us  [exchange(): return lax.all_to_all(pieces, axis, 0, 0, tiled=True)]
    pallas_call x6 -> x5, Pallas kernels: 8.31 us -> 8.28 us  [simple_call(): pl.pallas_call(kernel, out_shape=shapes, compiler_params=pltpu.CompilerPa...]
  transfers between devices with their start and end apart: 23 -> 23, of which waited for: 13 -> 13; matrix products, arithmetic and copies ran while one was open for 0% -> 0% of each run, Pallas kernels for 11% -> 13%
where the time goes in v9:
time: 110 us; the launch traced here: 111 us
  starting transfers between devices  53.3 us (48%)
  Pallas kernels  36.2 us (33%)
  waiting for transfers between devices  18.5 us (17%)
  local copies, waits for them, and re-layouts  1.53 us (1%)
  between operations  1.39 us (1%)
    ppermute x18, starting transfers between devices, pass_around(): lax.ppermute(pieces[ahead], axis, [(at, (at + ahead) % count) for at in r...  27.2 us
    all_to_all x5, starting transfers between devices, exchange(): return lax.all_to_all(pieces, axis, 0, 0, tiled=True)  26 us
    pallas_call x4, Pallas kernels, over_blocks(): pl.pallas_call(kernel, in_specs=[SCALARS, SCALARS, ANYWHERE] + [IN_VMEM]...  14.6 us
    pallas_call x1, Pallas kernels, build_blocks(): pl.pallas_call(build_kernel, in_specs=[SCALARS, SCALARS, ANYWHERE, ANYWHE...  13.3 us
    ppermute x18, waiting for transfers between devices, pass_around(): lax.ppermute(pieces[ahead], axis, [(at, (at + ahead) % count) for at in r...  12.3 us
    pallas_call x5, Pallas kernels, simple_call(): pl.pallas_call(kernel, out_shape=shapes, compiler_params=pltpu.CompilerPa...  8.28 us
    all_to_all x5, waiting for transfers between devices, exchange(): return lax.all_to_all(pieces, axis, 0, 0, tiled=True)  6.21 us
  transfers between devices with their start and end apart: 23, of which 13 were waited for; matrix products, arithmetic and copies ran while one was open for 0% of the time, Pallas kernels for 13%

profile of v9, /device:TPU:0, one launch (start us, length us, event | category | flops | bytes accessed | tf_op | source)
XLA Modules:
  0.0 110.9 jit_solution(8927859887219486817)
XLA Ops:
  1.3 13.3 %build_blocks.1 = (bf16[1024,128,128]{2,1,0:T(8,128)(2,1)}, bf16[1024,128,128]{2,1,0:T(8,128)(2,1)}, f32[4,128]{1,0:T(4,128)}, f32[4,128]{1,0:T(4,128)}, f32[4,128]{1,0:T(4,128)}, /*index=5*/f32[32,128]{1,0:T(8,128)}) custom-call(s32[1,1,256]{2,1,0:T(1,128)} %spots_ref.9, s32[1,1]{1,0:T(1,128)S(6)} %copy.7.live_ref, s32[256,16,128]{2,1,0:T(8,128)} %bitcast.3, ...), custom_call_target="tpu_custom_call" | custom-call | tf_op jit(solution)/shard_map/build_blocks/pallas_call | solution.py:182
  14.7 4.9 %all-to-all-start = ((f32[8,4,128]{2,1,0:T(4,128)}), f32[8,4,128]{2,1,0:T(4,128)S(1)}, u32[]{:S(2)}, u32[]{:S(2)}) async-start(f32[8,4,128]{2,1,0:T(4,128)} %bitcast.5), calls=%async_computation | async-start | bytes 32768 | tf_op jit(solution)/shard_map/all_to_all | solution.py:568
  19.5 2.0 %collective-permute-start = (f32[4,128]{1,0:T(4,128)}, f32[4,128]{1,0:T(4,128)S(1)}, u32[]{:S(2)}, u32[]{:S(2)}) collective-permute-start(f32[4,128]{1,0:T(4,128)} %get-tuple-element.25), channel_id=1, source_target_pairs={{0,8},{8,16},{16,24},{24,0},{1,9},{9,17},{17,25},{25,1},{2,10},{10... | collective-permute-start | bytes 6152 | tf_op jit(solution)/shard_map/ppermute | solution.py:562
  21.5 10.6 %collective-permute-start.1 = (f32[4,128]{1,0:T(4,128)}, f32[4,128]{1,0:T(4,128)S(1)}, u32[]{:S(2)}, u32[]{:S(2)}) collective-permute-start(f32[4,128]{1,0:T(4,128)} %get-tuple-element.26), channel_id=1, source_target_pairs={{0,16},{8,24},{16,0},{24,8},{1,17},{9,25},{17,1},{25,9},{2,18},{10... | collective-permute-start | bytes 6152 | tf_op jit(solution)/shard_map/ppermute | solution.py:562
  32.1 1.4 %collective-permute-start.2 = (f32[4,128]{1,0:T(4,128)}, f32[4,128]{1,0:T(4,128)S(1)}, u32[]{:S(2)}, u32[]{:S(2)}) collective-permute-start(f32[4,128]{1,0:T(4,128)} %get-tuple-element.27), channel_id=1, source_target_pairs={{0,24},{8,0},{16,8},{24,16},{1,25},{9,1},{17,9},{25,17},{2,26},{10... | collective-permute-start | bytes 6152 | tf_op jit(solution)/shard_map/ppermute | solution.py:562
  36.9 6.0 %all-to-all-start.1 = ((bf16[8,5,32,128]{3,2,1,0:T(8,128)(2,1)}), bf16[8,5,32,128]{3,2,1,0:T(8,128)(2,1)S(1)}, u32[]{:S(2)}, u32[]{:S(2)}) async-start(bf16[8,5,32,128]{3,2,1,0:T(8,128)(2,1)} %get-tuple-element.29), calls=%async_computation.1 | async-start | bytes 655360 | tf_op jit(solution)/shard_map/all_to_all | solution.py:568
  43.0 1.4 %collective-permute-start.8 = (bf16[4,32,128]{2,1,0:T(8,128)(2,1)S(1)}, bf16[4,32,128]{2,1,0:T(8,128)(2,1)S(1)}, u32[]{:S(2)}, u32[]{:S(2)}) collective-permute-start(bf16[4,32,128]{2,1,0:T(8,128)(2,1)S(1)} %get-tuple-element.35.refs_0_), channel_id=1, source_target_pairs={{0,24},{8,0},{16,8},{24,16},{1,25},{9,1},{17,9},{25,17},{2,26},{10... | collective-permute-start | bytes 98312 | tf_op jit(solution)/shard_map/ppermute | solution.py:562
  44.7 1.3 %collective-permute-done.8.refs_3_ = bf16[4,32,128]{2,1,0:T(8,128)(2,1)S(1)} collective-permute-done((bf16[4,32,128]{2,1,0:T(8,128)(2,1)S(1)}, bf16[4,32,128]{2,1,0:T(8,128)(2,1)S(1)}, u32[]{:S(2)}, u32[]{:S(2)}) %collective-permute-start.8) | collective-permute-done | bytes 32800 | tf_op jit(solution)/shard_map/ppermute | solution.py:562
  46.0 2.4 %collective-permute-done.7.refs_2_ = bf16[4,32,128]{2,1,0:T(8,128)(2,1)S(1)} collective-permute-done((bf16[4,32,128]{2,1,0:T(8,128)(2,1)S(1)}, bf16[4,32,128]{2,1,0:T(8,128)(2,1)S(1)}, u32[]{:S(2)}, u32[]{:S(2)}) %collective-permute-start.7) | collective-permute-done | bytes 32800 | tf_op jit(solution)/shard_map/ppermute | solution.py:562
  49.0 4.2 %backward_product.2 = bf16[8,128,128]{2,1,0:T(8,128)(2,1)} custom-call(s32[1,1,256]{2,1,0:T(1,128)S(1)} %copy-done.2, s32[1,1]{1,0:T(1,128)S(6)} %copy.7.live_ref, bf16[1024,128,128]{2,1,0:T(8,128)(2,1)} %get-tuple-element.34.block_hbm, bf16[4,32,128]{2,1,0:T(8,128)(2,1)S(1)} %get-tuple-element.35.refs_0_, ...), custom_call_target="tpu_custom_call" | custom-call | flops 268435456 | bytes 8388608 | tf_op jit(solution)/shard_map/backward_product/pallas_call | solution.py:344
  53.8 4.8 %all-to-all-start.2 = ((bf16[8,128,128]{2,1,0:T(8,128)(2,1)}), bf16[8,128,128]{2,1,0:T(8,128)(2,1)S(1)}, u32[]{:S(2)}, u32[]{:S(2)}) async-start(bf16[8,128,128]{2,1,0:T(8,128)(2,1)} %backward_product.2), calls=%async_computation.2 | async-start | bytes 524288 | tf_op jit(solution)/shard_map/all_to_all | solution.py:568
  58.6 3.5 %forward_product.2 = (bf16[4,32,128]{2,1,0:T(8,128)(2,1)S(1)}, bf16[4,32,128]{2,1,0:T(8,128)(2,1)S(1)}, bf16[4,32,128]{2,1,0:T(8,128)(2,1)S(1)}, bf16[4,32,128]{2,1,0:T(8,128)(2,1)S(1)}) custom-call(s32[1,1,256]{2,1,0:T(1,128)S(1)} %copy-done.3, s32[1,1]{1,0:T(1,128)S(6)} %copy.7.live_ref, bf16[1024,128,128]{2,1,0:T(8,128)(2,1)} %get-tuple-element.24.block_hbm, ...), custom_call_target="tpu_custom_call" | custom-call | flops 268435456 | bytes 8388608 | tf_op jit(solution)/shard_map/forward_product/pallas_call | solution.py:344
  62.1 2.5 %collective-permute-start.4 = (bf16[4,32,128]{2,1,0:T(8,128)(2,1)S(1)}, bf16[4,32,128]{2,1,0:T(8,128)(2,1)S(1)}, u32[]{:S(2)}, u32[]{:S(2)}) collective-permute-start(bf16[4,32,128]{2,1,0:T(8,128)(2,1)S(1)} %get-tuple-element.32), channel_id=1, source_target_pairs={{0,16},{8,24},{16,0},{24,8},{1,17},{9,25},{17,1},{25,9},{2,18},{10... | collective-permute-start | bytes 98312 | tf_op jit(solution)/shard_map/ppermute | solution.py:562
  64.6 1.4 %collective-permute-start.5 = (bf16[4,32,128]{2,1,0:T(8,128)(2,1)S(1)}, bf16[4,32,128]{2,1,0:T(8,128)(2,1)S(1)}, u32[]{:S(2)}, u32[]{:S(2)}) collective-permute-start(bf16[4,32,128]{2,1,0:T(8,128)(2,1)S(1)} %get-tuple-element.33), channel_id=1, source_target_pairs={{0,24},{8,0},{16,8},{24,16},{1,25},{9,1},{17,9},{25,17},{2,26},{10... | collective-permute-start | bytes 98312 | tf_op jit(solution)/shard_map/ppermute | solution.py:562
  66.0 1.2 %all-to-all-done.2.refs_4_ = bf16[8,128,128]{2,1,0:T(8,128)(2,1)S(1)} async-done(((bf16[8,128,128]{2,1,0:T(8,128)(2,1)}), bf16[8,128,128]{2,1,0:T(8,128)(2,1)S(1)}, u32[]{:S(2)}, u32[]{:S(2)}) %all-to-all-start.2) | async-done | bytes 262176 | tf_op jit(solution)/shard_map/all_to_all | solution.py:568
  67.6 1.2 %middle.1 = (f32[4,32,128]{2,1,0:T(8,128)S(1)}, bf16[4,32,128]{2,1,0:T(8,128)(2,1)S(1)}, bf16[8,5,32,128]{3,2,1,0:T(8,128)(2,1)}) custom-call(bf16[4,32,128]{2,1,0:T(8,128)(2,1)S(1)} %get-tuple-element.30.refs_0_, bf16[4,32,128]{2,1,0:T(8,128)(2,1)S(1)} %collective-permute-done.3.refs_1_, bf16[4,32,128]{2,1,0:T(8,128)(2,1)S(1)} %collective-permute-done.4.refs_2_, ...), custom_call_target="tpu_custom_call" | custom-call | tf_op jit(solution)/shard_map/middle/pallas_call | solution.py:572
  68.8 6.7 %all-to-all-start.3 = ((bf16[8,5,32,128]{3,2,1,0:T(8,128)(2,1)}), bf16[8,5,32,128]{3,2,1,0:T(8,128)(2,1)S(1)}, u32[]{:S(2)}, u32[]{:S(2)}) async-start(bf16[8,5,32,128]{3,2,1,0:T(8,128)(2,1)} %get-tuple-element.37), calls=%async_computation.3 | async-start | bytes 655360 | tf_op jit(solution)/shard_map/all_to_all | solution.py:568
  75.4 1.5 %collective-permute-start.14 = (bf16[4,32,128]{2,1,0:T(8,128)(2,1)S(1)}, bf16[4,32,128]{2,1,0:T(8,128)(2,1)S(1)}, u32[]{:S(2)}, u32[]{:S(2)}) collective-permute-start(bf16[4,32,128]{2,1,0:T(8,128)(2,1)S(1)} %get-tuple-element.42.refs_0_), channel_id=1, source_target_pairs={{0,24},{8,0},{16,8},{24,16},{1,25},{9,1},{17,9},{25,17},{2,26},{10... | collective-permute-start | bytes 98312 | tf_op jit(solution)/shard_map/ppermute | solution.py:562
  77.2 1.3 %collective-permute-done.14.refs_3_ = bf16[4,32,128]{2,1,0:T(8,128)(2,1)S(1)} collective-permute-done((bf16[4,32,128]{2,1,0:T(8,128)(2,1)S(1)}, bf16[4,32,128]{2,1,0:T(8,128)(2,1)S(1)}, u32[]{:S(2)}, u32[]{:S(2)}) %collective-permute-start.14) | collective-permute-done | bytes 32800 | tf_op jit(solution)/shard_map/ppermute | solution.py:562
  78.5 2.4 %collective-permute-done.13.refs_2_ = bf16[4,32,128]{2,1,0:T(8,128)(2,1)S(1)} collective-permute-done((bf16[4,32,128]{2,1,0:T(8,128)(2,1)S(1)}, bf16[4,32,128]{2,1,0:T(8,128)(2,1)S(1)}, u32[]{:S(2)}, u32[]{:S(2)}) %collective-permute-start.13) | collective-permute-done | bytes 32800 | tf_op jit(solution)/shard_map/ppermute | solution.py:562
  80.9 3.5 %backward_product.3.total_ref = bf16[8,128,128]{2,1,0:T(8,128)(2,1)S(1)} custom-call(s32[1,1,256]{2,1,0:T(1,128)S(1)} %copy-done.3, s32[1,1]{1,0:T(1,128)S(6)} %copy.7.live_ref, bf16[1024,128,128]{2,1,0:T(8,128)(2,1)} %get-tuple-element.34.block_hbm, bf16[4,32,128]{2,1,0:T(8,128)(2,1)S(1)} %get-tuple-element.42.refs_0_, ...), custom_call_target="tpu_custom_call" | custom-call | flops 268435456 | bytes 8388608 | tf_op jit(solution)/shard_map/backward_product/pallas_call | solution.py:344
  84.4 1.9 %all-to-all-done.3.col_dir_ref = bf16[8,5,32,128]{3,2,1,0:T(8,128)(2,1)S(1)} async-done(((bf16[8,5,32,128]{3,2,1,0:T(8,128)(2,1)}), bf16[8,5,32,128]{3,2,1,0:T(8,128)(2,1)S(1)}, u32[]{:S(2)}, u32[]{:S(2)}) %all-to-all-start.3) | async-done | bytes 327712 | tf_op jit(solution)/shard_map/all_to_all | solution.py:568
  86.3 1.3 %attach.1 = (bf16[8,144,128]{2,1,0:T(8,128)(2,1)}, f32[32,128]{1,0:T(8,128)S(1)}) custom-call(bf16[8,5,32,128]{3,2,1,0:T(8,128)(2,1)S(1)} %all-to-all-done.1.col_dir_ref.first_dir_ref, bf16[8,5,32,128]{3,2,1,0:T(8,128)(2,1)S(1)} %all-to-all-done.3.col_dir_ref, bf16[8,128,128]{2,1,0:T(8,128)(2,1)S(1)} %backward_product.3.total_ref), custom_call_target="tpu_custom_call" | custom-call | tf_op jit(solution)/shard_map/attach/pallas_call | solution.py:572
  87.6 3.6 %all-to-all-start.4 = ((bf16[8,144,128]{2,1,0:T(8,128)(2,1)}), bf16[8,144,128]{2,1,0:T(8,128)(2,1)S(1)}, u32[]{:S(2)}, u32[]{:S(2)}) async-start(bf16[8,144,128]{2,1,0:T(8,128)(2,1)} %get-tuple-element.43), calls=%async_computation.4 | async-start | bytes 589824 | tf_op jit(solution)/shard_map/all_to_all | solution.py:568
  91.2 3.5 %forward_product.3 = (bf16[4,32,128]{2,1,0:T(8,128)(2,1)S(1)}, bf16[4,32,128]{2,1,0:T(8,128)(2,1)S(1)}, bf16[4,32,128]{2,1,0:T(8,128)(2,1)S(1)}, bf16[4,32,128]{2,1,0:T(8,128)(2,1)S(1)}) custom-call(s32[1,1,256]{2,1,0:T(1,128)S(1)} %copy-done.3, s32[1,1]{1,0:T(1,128)S(6)} %copy.7.live_ref, bf16[1024,128,128]{2,1,0:T(8,128)(2,1)} %get-tuple-element.24.block_hbm, ...), custom_call_target="tpu_custom_call" | custom-call | flops 268435456 | bytes 8388608 | tf_op jit(solution)/shard_map/forward_product/pallas_call | solution.py:344
  94.7 2.3 %collective-permute-start.10 = (bf16[4,32,128]{2,1,0:T(8,128)(2,1)S(1)}, bf16[4,32,128]{2,1,0:T(8,128)(2,1)S(1)}, u32[]{:S(2)}, u32[]{:S(2)}) collective-permute-start(bf16[4,32,128]{2,1,0:T(8,128)(2,1)S(1)} %get-tuple-element.40), channel_id=1, source_target_pairs={{0,16},{8,24},{16,0},{24,8},{1,17},{9,25},{17,1},{25,9},{2,18},{10... | collective-permute-start | bytes 98312 | tf_op jit(solution)/shard_map/ppermute | solution.py:562
  97.0 1.4 %collective-permute-start.11 = (bf16[4,32,128]{2,1,0:T(8,128)(2,1)S(1)}, bf16[4,32,128]{2,1,0:T(8,128)(2,1)S(1)}, u32[]{:S(2)}, u32[]{:S(2)}) collective-permute-start(bf16[4,32,128]{2,1,0:T(8,128)(2,1)S(1)} %get-tuple-element.41), channel_id=1, source_target_pairs={{0,24},{8,0},{16,8},{24,16},{1,25},{9,1},{17,9},{25,17},{2,26},{10... | collective-permute-start | bytes 98312 | tf_op jit(solution)/shard_map/ppermute | solution.py:562
  98.4 2.6 %all-to-all-done.4.col_ref.refs_8_ = bf16[8,144,128]{2,1,0:T(8,128)(2,1)S(1)} async-done(((bf16[8,144,128]{2,1,0:T(8,128)(2,1)}), bf16[8,144,128]{2,1,0:T(8,128)(2,1)S(1)}, u32[]{:S(2)}, u32[]{:S(2)}) %all-to-all-start.4) | async-done | bytes 294944 | tf_op jit(solution)/shard_map/all_to_all | solution.py:568
  101.1 1.9 %collective-permute-start.16 = (f32[32,128]{1,0:T(8,128)S(1)}, f32[32,128]{1,0:T(8,128)S(1)}, u32[]{:S(2)}, u32[]{:S(2)}) collective-permute-start(f32[32,128]{1,0:T(8,128)S(1)} %gram_sum.1.refs_4_), channel_id=1, source_target_pairs={{0,16},{8,24},{16,0},{24,8},{1,17},{9,25},{17,1},{25,9},{2,18},{10... | collective-permute-start | bytes 49160 | tf_op jit(solution)/shard_map/ppermute | solution.py:562
  103.2 1.7 %collective-permute-done.16.refs_6_ = f32[32,128]{1,0:T(8,128)S(1)} collective-permute-done((f32[32,128]{1,0:T(8,128)S(1)}, f32[32,128]{1,0:T(8,128)S(1)}, u32[]{:S(2)}, u32[]{:S(2)}) %collective-permute-start.16) | collective-permute-done | bytes 16416 | tf_op jit(solution)/shard_map/ppermute | solution.py:562
  104.9 1.2 %collective-permute-done.15.refs_5_ = f32[32,128]{1,0:T(8,128)S(1)} collective-permute-done((f32[32,128]{1,0:T(8,128)S(1)}, f32[32,128]{1,0:T(8,128)S(1)}, u32[]{:S(2)}, u32[]{:S(2)}) %collective-permute-start.15) | collective-permute-done | bytes 16416 | tf_op jit(solution)/shard_map/ppermute | solution.py:562
  106.2 4.7 %close.1 = (f32[32,512]{1,0:T(8,128)}, f32[32,512]{1,0:T(8,128)}) custom-call(bf16[4,32,128]{2,1,0:T(8,128)(2,1)S(1)} %get-tuple-element.38.refs_0_, bf16[4,32,128]{2,1,0:T(8,128)(2,1)S(1)} %collective-permute-done.9.refs_1_, bf16[4,32,128]{2,1,0:T(8,128)(2,1)S(1)} %collective-permute-done.10.refs_2_, ...), custom_call_target="tpu_custom_call" | custom-call | tf_op jit(solution)/shard_map/close/pallas_call | solution.py:572
  (32 shorter events, 6.1 us)
Async XLA Ops:
  0.6 57.9 %copy-start.3 = (s32[1,1,256]{2,1,0:T(1,128)S(1)}, s32[1,1,256]{2,1,0:T(1,128)}, u32[]{:S(2)}) copy-start(s32[1,1,256]{2,1,0:T(1,128)} %spots_ref.9) | copy-start | bytes 3076
  14.7 20.4 %all-to-all-start = ((f32[8,4,128]{2,1,0:T(4,128)}), f32[8,4,128]{2,1,0:T(4,128)S(1)}, u32[]{:S(2)}, u32[]{:S(2)}) async-start(f32[8,4,128]{2,1,0:T(4,128)} %bitcast.5), calls=%async_computation | async-start | bytes 32768 | tf_op jit(solution)/shard_map/all_to_all | solution.py:568
  19.5 14.0 %collective-permute-start = (f32[4,128]{1,0:T(4,128)}, f32[4,128]{1,0:T(4,128)S(1)}, u32[]{:S(2)}, u32[]{:S(2)}) collective-permute-start(f32[4,128]{1,0:T(4,128)} %get-tuple-element.25), channel_id=1, source_target_pairs={{0,8},{8,16},{16,24},{24,0},{1,9},{9,17},{17,25},{25,1},{2,10},{10... | collective-permute-start | bytes 6152 | tf_op jit(solution)/shard_map/ppermute | solution.py:562
  21.5 12.4 %collective-permute-start.1 = (f32[4,128]{1,0:T(4,128)}, f32[4,128]{1,0:T(4,128)S(1)}, u32[]{:S(2)}, u32[]{:S(2)}) collective-permute-start(f32[4,128]{1,0:T(4,128)} %get-tuple-element.26), channel_id=1, source_target_pairs={{0,16},{8,24},{16,0},{24,8},{1,17},{9,25},{17,1},{25,9},{2,18},{10... | collective-permute-start | bytes 6152 | tf_op jit(solution)/shard_map/ppermute | solution.py:562
  32.1 2.9 %collective-permute-start.2 = (f32[4,128]{1,0:T(4,128)}, f32[4,128]{1,0:T(4,128)S(1)}, u32[]{:S(2)}, u32[]{:S(2)}) collective-permute-start(f32[4,128]{1,0:T(4,128)} %get-tuple-element.27), channel_id=1, source_target_pairs={{0,24},{8,0},{16,8},{24,16},{1,25},{9,1},{17,9},{25,17},{2,26},{10... | collective-permute-start | bytes 6152 | tf_op jit(solution)/shard_map/ppermute | solution.py:562
  35.1 0.8 copy-start
  36.9 16.8 %all-to-all-start.1 = ((bf16[8,5,32,128]{3,2,1,0:T(8,128)(2,1)}), bf16[8,5,32,128]{3,2,1,0:T(8,128)(2,1)S(1)}, u32[]{:S(2)}, u32[]{:S(2)}) async-start(bf16[8,5,32,128]{3,2,1,0:T(8,128)(2,1)} %get-tuple-element.29), calls=%async_computation.1 | async-start | bytes 655360 | tf_op jit(solution)/shard_map/all_to_all | solution.py:568
  43.0 3.0 %collective-permute-start.8 = (bf16[4,32,128]{2,1,0:T(8,128)(2,1)S(1)}, bf16[4,32,128]{2,1,0:T(8,128)(2,1)S(1)}, u32[]{:S(2)}, u32[]{:S(2)}) collective-permute-start(bf16[4,32,128]{2,1,0:T(8,128)(2,1)S(1)} %get-tuple-element.35.refs_0_), channel_id=1, source_target_pairs={{0,24},{8,0},{16,8},{24,16},{1,25},{9,1},{17,9},{25,17},{2,26},{10... | collective-permute-start | bytes 98312 | tf_op jit(solution)/shard_map/ppermute | solution.py:562
  44.4 4.0 %collective-permute-start.7 = (bf16[4,32,128]{2,1,0:T(8,128)(2,1)S(1)}, bf16[4,32,128]{2,1,0:T(8,128)(2,1)S(1)}, u32[]{:S(2)}, u32[]{:S(2)}) collective-permute-start(bf16[4,32,128]{2,1,0:T(8,128)(2,1)S(1)} %get-tuple-element.35.refs_0_), channel_id=1, source_target_pairs={{0,16},{8,24},{16,0},{24,8},{1,17},{9,25},{17,1},{25,9},{2,18},{10... | collective-permute-start | bytes 98312 | tf_op jit(solution)/shard_map/ppermute | solution.py:562
  44.7 3.7 %collective-permute-start.6 = (bf16[4,32,128]{2,1,0:T(8,128)(2,1)S(1)}, bf16[4,32,128]{2,1,0:T(8,128)(2,1)S(1)}, u32[]{:S(2)}, u32[]{:S(2)}) collective-permute-start(bf16[4,32,128]{2,1,0:T(8,128)(2,1)S(1)} %get-tuple-element.35.refs_0_), channel_id=1, source_target_pairs={{0,8},{8,16},{16,24},{24,0},{1,9},{9,17},{17,25},{25,1},{2,10},{10... | collective-permute-start | bytes 98312 | tf_op jit(solution)/shard_map/ppermute | solution.py:562
  48.4 0.7 copy-start.2
  49.0 18.6 %copy-start.1 = (f32[32,512]{1,0:T(8,128)S(1)}, f32[32,512]{1,0:T(8,128)}, u32[]{:S(2)}) copy-start(f32[32,512]{1,0:T(8,128)} %refs_10_.1) | copy-start | bytes 196612
  53.8 13.4 %all-to-all-start.2 = ((bf16[8,128,128]{2,1,0:T(8,128)(2,1)}), bf16[8,128,128]{2,1,0:T(8,128)(2,1)S(1)}, u32[]{:S(2)}, u32[]{:S(2)}) async-start(bf16[8,128,128]{2,1,0:T(8,128)(2,1)} %backward_product.2), calls=%async_computation.2 | async-start | bytes 524288 | tf_op jit(solution)/shard_map/all_to_all | solution.py:568
  62.0 5.2 %collective-permute-start.3 = (bf16[4,32,128]{2,1,0:T(8,128)(2,1)S(1)}, bf16[4,32,128]{2,1,0:T(8,128)(2,1)S(1)}, u32[]{:S(2)}, u32[]{:S(2)}) collective-permute-start(bf16[4,32,128]{2,1,0:T(8,128)(2,1)S(1)} %get-tuple-element.31), channel_id=1, source_target_pairs={{0,8},{8,16},{16,24},{24,0},{1,9},{9,17},{17,25},{25,1},{2,10},{10... | collective-permute-start | bytes 98312 | tf_op jit(solution)/shard_map/ppermute | solution.py:562
  62.1 5.1 %collective-permute-start.4 = (bf16[4,32,128]{2,1,0:T(8,128)(2,1)S(1)}, bf16[4,32,128]{2,1,0:T(8,128)(2,1)S(1)}, u32[]{:S(2)}, u32[]{:S(2)}) collective-permute-start(bf16[4,32,128]{2,1,0:T(8,128)(2,1)S(1)} %get-tuple-element.32), channel_id=1, source_target_pairs={{0,16},{8,24},{16,0},{24,8},{1,17},{9,25},{17,1},{25,9},{2,18},{10... | collective-permute-start | bytes 98312 | tf_op jit(solution)/shard_map/ppermute | solution.py:562
  64.6 3.0 %collective-permute-start.5 = (bf16[4,32,128]{2,1,0:T(8,128)(2,1)S(1)}, bf16[4,32,128]{2,1,0:T(8,128)(2,1)S(1)}, u32[]{:S(2)}, u32[]{:S(2)}) collective-permute-start(bf16[4,32,128]{2,1,0:T(8,128)(2,1)S(1)} %get-tuple-element.33), channel_id=1, source_target_pairs={{0,24},{8,0},{16,8},{24,16},{1,25},{9,1},{17,9},{25,17},{2,26},{10... | collective-permute-start | bytes 98312 | tf_op jit(solution)/shard_map/ppermute | solution.py:562
  68.8 17.6 %all-to-all-start.3 = ((bf16[8,5,32,128]{3,2,1,0:T(8,128)(2,1)}), bf16[8,5,32,128]{3,2,1,0:T(8,128)(2,1)S(1)}, u32[]{:S(2)}, u32[]{:S(2)}) async-start(bf16[8,5,32,128]{3,2,1,0:T(8,128)(2,1)} %get-tuple-element.37), calls=%async_computation.3 | async-start | bytes 655360 | tf_op jit(solution)/shard_map/all_to_all | solution.py:568
  75.4 3.1 %collective-permute-start.14 = (bf16[4,32,128]{2,1,0:T(8,128)(2,1)S(1)}, bf16[4,32,128]{2,1,0:T(8,128)(2,1)S(1)}, u32[]{:S(2)}, u32[]{:S(2)}) collective-permute-start(bf16[4,32,128]{2,1,0:T(8,128)(2,1)S(1)} %get-tuple-element.42.refs_0_), channel_id=1, source_target_pairs={{0,24},{8,0},{16,8},{24,16},{1,25},{9,1},{17,9},{25,17},{2,26},{10... | collective-permute-start | bytes 98312 | tf_op jit(solution)/shard_map/ppermute | solution.py:562
  76.9 4.0 %collective-permute-start.13 = (bf16[4,32,128]{2,1,0:T(8,128)(2,1)S(1)}, bf16[4,32,128]{2,1,0:T(8,128)(2,1)S(1)}, u32[]{:S(2)}, u32[]{:S(2)}) collective-permute-start(bf16[4,32,128]{2,1,0:T(8,128)(2,1)S(1)} %get-tuple-element.42.refs_0_), channel_id=1, source_target_pairs={{0,16},{8,24},{16,0},{24,8},{1,17},{9,25},{17,1},{25,9},{2,18},{10... | collective-permute-start | bytes 98312 | tf_op jit(solution)/shard_map/ppermute | solution.py:562
  77.2 3.7 %collective-permute-start.12 = (bf16[4,32,128]{2,1,0:T(8,128)(2,1)S(1)}, bf16[4,32,128]{2,1,0:T(8,128)(2,1)S(1)}, u32[]{:S(2)}, u32[]{:S(2)}) collective-permute-start(bf16[4,32,128]{2,1,0:T(8,128)(2,1)S(1)} %get-tuple-element.42.refs_0_), channel_id=1, source_target_pairs={{0,8},{8,16},{16,24},{24,0},{1,9},{9,17},{17,25},{25,1},{2,10},{10... | collective-permute-start | bytes 98312 | tf_op jit(solution)/shard_map/ppermute | solution.py:562
  87.6 13.4 %all-to-all-start.4 = ((bf16[8,144,128]{2,1,0:T(8,128)(2,1)}), bf16[8,144,128]{2,1,0:T(8,128)(2,1)S(1)}, u32[]{:S(2)}, u32[]{:S(2)}) async-start(bf16[8,144,128]{2,1,0:T(8,128)(2,1)} %get-tuple-element.43), calls=%async_computation.4 | async-start | bytes 589824 | tf_op jit(solution)/shard_map/all_to_all | solution.py:568
  94.7 8.3 %collective-permute-start.9 = (bf16[4,32,128]{2,1,0:T(8,128)(2,1)S(1)}, bf16[4,32,128]{2,1,0:T(8,128)(2,1)S(1)}, u32[]{:S(2)}, u32[]{:S(2)}) collective-permute-start(bf16[4,32,128]{2,1,0:T(8,128)(2,1)S(1)} %get-tuple-element.39), channel_id=1, source_target_pairs={{0,8},{8,16},{16,24},{24,0},{1,9},{9,17},{17,25},{25,1},{2,10},{10... | collective-permute-start | bytes 98312 | tf_op jit(solution)/shard_map/ppermute | solution.py:562
  94.7 8.5 %collective-permute-start.10 = (bf16[4,32,128]{2,1,0:T(8,128)(2,1)S(1)}, bf16[4,32,128]{2,1,0:T(8,128)(2,1)S(1)}, u32[]{:S(2)}, u32[]{:S(2)}) collective-permute-start(bf16[4,32,128]{2,1,0:T(8,128)(2,1)S(1)} %get-tuple-element.40), channel_id=1, source_target_pairs={{0,16},{8,24},{16,0},{24,8},{1,17},{9,25},{17,1},{25,9},{2,18},{10... | collective-permute-start | bytes 98312 | tf_op jit(solution)/shard_map/ppermute | solution.py:562
  97.0 6.2 %collective-permute-start.11 = (bf16[4,32,128]{2,1,0:T(8,128)(2,1)S(1)}, bf16[4,32,128]{2,1,0:T(8,128)(2,1)S(1)}, u32[]{:S(2)}, u32[]{:S(2)}) collective-permute-start(bf16[4,32,128]{2,1,0:T(8,128)(2,1)S(1)} %get-tuple-element.41), channel_id=1, source_target_pairs={{0,24},{8,0},{16,8},{24,16},{1,25},{9,1},{17,9},{25,17},{2,26},{10... | collective-permute-start | bytes 98312 | tf_op jit(solution)/shard_map/ppermute | solution.py:562
  101.1 2.1 %collective-permute-start.17 = (f32[32,128]{1,0:T(8,128)S(1)}, f32[32,128]{1,0:T(8,128)S(1)}, u32[]{:S(2)}, u32[]{:S(2)}) collective-permute-start(f32[32,128]{1,0:T(8,128)S(1)} %gram_sum.1.refs_4_), channel_id=1, source_target_pairs={{0,24},{8,0},{16,8},{24,16},{1,25},{9,1},{17,9},{25,17},{2,26},{10... | collective-permute-start | bytes 49160 | tf_op jit(solution)/shard_map/ppermute | solution.py:562
  101.1 3.8 %collective-permute-start.16 = (f32[32,128]{1,0:T(8,128)S(1)}, f32[32,128]{1,0:T(8,128)S(1)}, u32[]{:S(2)}, u32[]{:S(2)}) collective-permute-start(f32[32,128]{1,0:T(8,128)S(1)} %gram_sum.1.refs_4_), channel_id=1, source_target_pairs={{0,16},{8,24},{16,0},{24,8},{1,17},{9,25},{17,1},{25,9},{2,18},{10... | collective-permute-start | bytes 49160 | tf_op jit(solution)/shard_map/ppermute | solution.py:562
  103.0 3.2 %collective-permute-start.15 = (f32[32,128]{1,0:T(8,128)S(1)}, f32[32,128]{1,0:T(8,128)S(1)}, u32[]{:S(2)}, u32[]{:S(2)}) collective-permute-start(f32[32,128]{1,0:T(8,128)S(1)} %gram_sum.1.refs_4_), channel_id=1, source_target_pairs={{0,8},{8,16},{16,24},{24,0},{1,9},{9,17},{17,25},{25,1},{2,10},{10... | collective-permute-start | bytes 49160 | tf_op jit(solution)/shard_map/ppermute | solution.py:562

commit v10 on v9

--- a/solution.py
+++ b/solution.py
@@ -8,7 +8,7 @@
 from jax.sharding import PartitionSpec as P
 
 graph_weight = 0.95
-GROUP = 32
+GROUP = 16
 BATCH = 32
 SPARE = 4
 PANEL = 8
@@ -104,18 +104,19 @@
             for slot in (index * GROUP + inside, index * GROUP + inside + 1):
                 active = (slot < live_count(places)).astype(jnp.float32)
                 values = value_ref[slot].astype(jnp.float32) * active
-                tables.append((slot, index_ref[slot], values))
+                indices = index_ref[slot].astype(jnp.int16)
+                tables.append((slot, indices, values, values.astype(jnp.bfloat16)))
             return tables
 
         def build_pair(tables):
             sums = [[zero] * 8 for _ in tables]
             for entry in range(0, 16, 2):
-                for which, (_, indices, values) in enumerate(tables):
+                for which, (_, indices, _, narrow) in enumerate(tables):
                     pair = []
                     for at in (entry, entry + 1):
                         index_row = jnp.broadcast_to(indices[at : at + 1], (16, 128))
-                        value_row = jnp.broadcast_to(values[at : at + 1], (16, 128))
-                        pair.append((index_row.astype(jnp.int16), value_row.astype(jnp.bfloat16)))
+                        value_row = jnp.broadcast_to(narrow[at : at + 1], (16, 128))
+                        pair.append((index_row, value_row))
                     for part in range(8):
                         first, second = [
                             jnp.where(index_row == targets[part], value_row, zero)
@@ -125,7 +126,7 @@
             return [jnp.concatenate(parts, axis=0) for parts in sums]
 
         def store_turned(tables, turned):
-            for (slot, _, values), block in zip(tables, turned):
+            for (slot, _, values, _), block in zip(tables, turned):
                 row_block, col_block = place_of(places, slot, col_blocks)
                 flipped_ref[slot] = block.astype(jnp.bfloat16)
                 col_ref[col_block] += jnp.sum(block.reshape(16, 8, 128), axis=0)
@@ -138,7 +139,7 @@
             blocks = build_pair(tables)
             if waiting:
                 store_turned(*waiting)
-            for (slot, _, _), block in zip(tables, blocks):
+            for (slot, *_), block in zip(tables, blocks):
                 block_ref[slot] = block
             waiting = (tables, [dot_across(identity, block) for block in blocks])
             tables = following

time: 110 us -> 109 us (level)
  starting transfers between devices: 53.3 us -> 46.2 us
  waiting for transfers between devices: 18.5 us -> 24.9 us
    ppermute x18, starting transfers between devices: 27.2 us -> 10.8 us  [pass_around(): lax.ppermute(pieces[ahead], axis, [(at, (at + ahead) % count) for at in r...]
    all_to_all x5, starting transfers between devices: 26 us -> 35.4 us  [exchange(): return lax.all_to_all(pieces, axis, 0, 0, tiled=True)]
    all_to_all x5, waiting for transfers between devices: 6.21 us -> 12.9 us  [exchange(): return lax.all_to_all(pieces, axis, 0, 0, tiled=True)]
where the time goes in v10:
time: 109 us; the launch traced here: 111 us
  starting transfers between devices  46.2 us (42%)
  Pallas kernels  36.4 us (33%)
  waiting for transfers between devices  24.9 us (23%)
  local copies, waits for them, and re-layouts  1.53 us (1%)
  between operations  1.43 us (1%)
    all_to_all x5, starting transfers between devices, exchange(): return lax.all_to_all(pieces, axis, 0, 0, tiled=True)  35.4 us
    pallas_call x4, Pallas kernels, over_blocks(): pl.pallas_call(kernel, in_specs=[SCALARS, SCALARS, ANYWHERE] + [IN_VMEM]...  14.6 us
    pallas_call x1, Pallas kernels, build_blocks(): pl.pallas_call(build_kernel, in_specs=[SCALARS, SCALARS, ANYWHERE, ANYWHE...  13.6 us
    all_to_all x5, waiting for transfers between devices, exchange(): return lax.all_to_all(pieces, axis, 0, 0, tiled=True)  12.9 us
    ppermute x18, waiting for transfers between devices, pass_around(): lax.ppermute(pieces[ahead], axis, [(at, (at + ahead) % count) for at in r...  12.1 us
    ppermute x18, starting transfers between devices, pass_around(): lax.ppermute(pieces[ahead], axis, [(at, (at + ahead) % count) for at in r...  10.8 us
    pallas_call x5, Pallas kernels, simple_call(): pl.pallas_call(kernel, out_shape=shapes, compiler_params=pltpu.CompilerPa...  8.29 us
  transfers between devices with their start and end apart: 23, of which 13 were waited for; matrix products, arithmetic and copies ran while one was open for 0% of the time, Pallas kernels for 13%

profile of v10, /device:TPU:0, one launch (start us, length us, event | category | flops | bytes accessed | tf_op | source)
XLA Modules:
  0.0 110.5 jit_solution(895923237387081153)
XLA Ops:
  1.3 13.6 %build_blocks.1 = (bf16[1024,128,128]{2,1,0:T(8,128)(2,1)}, bf16[1024,128,128]{2,1,0:T(8,128)(2,1)}, f32[4,128]{1,0:T(4,128)}, f32[4,128]{1,0:T(4,128)}, f32[4,128]{1,0:T(4,128)}, /*index=5*/f32[32,128]{1,0:T(8,128)}) custom-call(s32[1,1,256]{2,1,0:T(1,128)} %spots_ref.9, s32[1,1]{1,0:T(1,128)S(6)} %copy.7.live_ref, s32[256,16,128]{2,1,0:T(8,128)} %bitcast.3, ...), custom_call_target="tpu_custom_call" | custom-call | tf_op jit(solution)/shard_map/build_blocks/pallas_call | solution.py:183
  14.9 16.3 %all-to-all-start = ((f32[8,4,128]{2,1,0:T(4,128)}), f32[8,4,128]{2,1,0:T(4,128)S(1)}, u32[]{:S(2)}, u32[]{:S(2)}) async-start(f32[8,4,128]{2,1,0:T(4,128)} %bitcast.5), calls=%async_computation | async-start | bytes 32768 | tf_op jit(solution)/shard_map/all_to_all | solution.py:569
  31.2 1.7 %collective-permute-start.2 = (f32[4,128]{1,0:T(4,128)}, f32[4,128]{1,0:T(4,128)S(1)}, u32[]{:S(2)}, u32[]{:S(2)}) collective-permute-start(f32[4,128]{1,0:T(4,128)} %get-tuple-element.27), channel_id=1, source_target_pairs={{0,24},{8,0},{16,8},{24,16},{1,25},{9,1},{17,9},{25,17},{2,26},{10... | collective-permute-start | bytes 6152 | tf_op jit(solution)/shard_map/ppermute | solution.py:563
  32.9 1.4 %collective-permute-done.refs_0_ = f32[4,128]{1,0:T(4,128)S(1)} collective-permute-done((f32[4,128]{1,0:T(4,128)}, f32[4,128]{1,0:T(4,128)S(1)}, u32[]{:S(2)}, u32[]{:S(2)}) %collective-permute-start) | collective-permute-done | bytes 2080 | tf_op jit(solution)/shard_map/ppermute | solution.py:563
  35.0 2.7 %all-to-all-done.refs_3_ = f32[8,4,128]{2,1,0:T(4,128)S(1)} async-done(((f32[8,4,128]{2,1,0:T(4,128)}), f32[8,4,128]{2,1,0:T(4,128)S(1)}, u32[]{:S(2)}, u32[]{:S(2)}) %all-to-all-start) | async-done | bytes 16416 | tf_op jit(solution)/shard_map/all_to_all | solution.py:569
  37.7 0.8 copy-done
  38.6 1.0 start.1
  39.6 3.4 %all-to-all-start.1 = ((bf16[8,5,32,128]{3,2,1,0:T(8,128)(2,1)}), bf16[8,5,32,128]{3,2,1,0:T(8,128)(2,1)S(1)}, u32[]{:S(2)}, u32[]{:S(2)}) async-start(bf16[8,5,32,128]{3,2,1,0:T(8,128)(2,1)} %get-tuple-element.29), calls=%async_computation.1 | async-start | bytes 655360 | tf_op jit(solution)/shard_map/all_to_all | solution.py:569
  43.7 1.7 %collective-permute-start.7 = (bf16[4,32,128]{2,1,0:T(8,128)(2,1)S(1)}, bf16[4,32,128]{2,1,0:T(8,128)(2,1)S(1)}, u32[]{:S(2)}, u32[]{:S(2)}) collective-permute-start(bf16[4,32,128]{2,1,0:T(8,128)(2,1)S(1)} %get-tuple-element.35.refs_0_), channel_id=1, source_target_pairs={{0,16},{8,24},{16,0},{24,8},{1,17},{9,25},{17,1},{25,9},{2,18},{10... | collective-permute-start | bytes 98312 | tf_op jit(solution)/shard_map/ppermute | solution.py:563
  45.5 2.2 %collective-permute-done.7.refs_2_ = bf16[4,32,128]{2,1,0:T(8,128)(2,1)S(1)} collective-permute-done((bf16[4,32,128]{2,1,0:T(8,128)(2,1)S(1)}, bf16[4,32,128]{2,1,0:T(8,128)(2,1)S(1)}, u32[]{:S(2)}, u32[]{:S(2)}) %collective-permute-start.7) | collective-permute-done | bytes 32800 | tf_op jit(solution)/shard_map/ppermute | solution.py:563
  47.7 1.1 collective-permute-done.6.refs_1_
  49.5 4.2 %backward_product.2 = bf16[8,128,128]{2,1,0:T(8,128)(2,1)} custom-call(s32[1,1,256]{2,1,0:T(1,128)S(1)} %copy-done.2, s32[1,1]{1,0:T(1,128)S(6)} %copy.7.live_ref, bf16[1024,128,128]{2,1,0:T(8,128)(2,1)} %get-tuple-element.34.block_hbm, bf16[4,32,128]{2,1,0:T(8,128)(2,1)S(1)} %get-tuple-element.35.refs_0_, ...), custom_call_target="tpu_custom_call" | custom-call | flops 268435456 | bytes 8388608 | tf_op jit(solution)/shard_map/backward_product/pallas_call | solution.py:345
  53.7 0.9 all-to-all-done.1.col_dir_ref.first_dir_ref
  54.5 5.5 %all-to-all-start.2 = ((bf16[8,128,128]{2,1,0:T(8,128)(2,1)}), bf16[8,128,128]{2,1,0:T(8,128)(2,1)S(1)}, u32[]{:S(2)}, u32[]{:S(2)}) async-start(bf16[8,128,128]{2,1,0:T(8,128)(2,1)} %backward_product.2), calls=%async_computation.2 | async-start | bytes 524288 | tf_op jit(solution)/shard_map/all_to_all | solution.py:569
  60.1 3.5 %forward_product.2 = (bf16[4,32,128]{2,1,0:T(8,128)(2,1)S(1)}, bf16[4,32,128]{2,1,0:T(8,128)(2,1)S(1)}, bf16[4,32,128]{2,1,0:T(8,128)(2,1)S(1)}, bf16[4,32,128]{2,1,0:T(8,128)(2,1)S(1)}) custom-call(s32[1,1,256]{2,1,0:T(1,128)S(1)} %copy-done.3, s32[1,1]{1,0:T(1,128)S(6)} %copy.7.live_ref, bf16[1024,128,128]{2,1,0:T(8,128)(2,1)} %get-tuple-element.24.block_hbm, ...), custom_call_target="tpu_custom_call" | custom-call | flops 268435456 | bytes 8388608 | tf_op jit(solution)/shard_map/forward_product/pallas_call | solution.py:345
  63.7 1.7 %collective-permute-start.5 = (bf16[4,32,128]{2,1,0:T(8,128)(2,1)S(1)}, bf16[4,32,128]{2,1,0:T(8,128)(2,1)S(1)}, u32[]{:S(2)}, u32[]{:S(2)}) collective-permute-start(bf16[4,32,128]{2,1,0:T(8,128)(2,1)S(1)} %get-tuple-element.33), channel_id=1, source_target_pairs={{0,24},{8,0},{16,8},{24,16},{1,25},{9,1},{17,9},{25,17},{2,26},{10... | collective-permute-start | bytes 98312 | tf_op jit(solution)/shard_map/ppermute | solution.py:563
  65.4 2.9 %all-to-all-done.2.refs_4_ = bf16[8,128,128]{2,1,0:T(8,128)(2,1)S(1)} async-done(((bf16[8,128,128]{2,1,0:T(8,128)(2,1)}), bf16[8,128,128]{2,1,0:T(8,128)(2,1)S(1)}, u32[]{:S(2)}, u32[]{:S(2)}) %all-to-all-start.2) | async-done | bytes 262176 | tf_op jit(solution)/shard_map/all_to_all | solution.py:569
  68.3 1.2 %middle.1 = (f32[4,32,128]{2,1,0:T(8,128)S(1)}, bf16[4,32,128]{2,1,0:T(8,128)(2,1)S(1)}, bf16[8,5,32,128]{3,2,1,0:T(8,128)(2,1)}) custom-call(bf16[4,32,128]{2,1,0:T(8,128)(2,1)S(1)} %get-tuple-element.30.refs_0_, bf16[4,32,128]{2,1,0:T(8,128)(2,1)S(1)} %collective-permute-done.3.refs_1_, bf16[4,32,128]{2,1,0:T(8,128)(2,1)S(1)} %collective-permute-done.4.refs_2_, ...), custom_call_target="tpu_custom_call" | custom-call | tf_op jit(solution)/shard_map/middle/pallas_call | solution.py:573
  69.5 6.0 %all-to-all-start.3 = ((bf16[8,5,32,128]{3,2,1,0:T(8,128)(2,1)}), bf16[8,5,32,128]{3,2,1,0:T(8,128)(2,1)S(1)}, u32[]{:S(2)}, u32[]{:S(2)}) async-start(bf16[8,5,32,128]{3,2,1,0:T(8,128)(2,1)} %get-tuple-element.37), calls=%async_computation.3 | async-start | bytes 655360 | tf_op jit(solution)/shard_map/all_to_all | solution.py:569
  76.3 1.7 %collective-permute-start.13 = (bf16[4,32,128]{2,1,0:T(8,128)(2,1)S(1)}, bf16[4,32,128]{2,1,0:T(8,128)(2,1)S(1)}, u32[]{:S(2)}, u32[]{:S(2)}) collective-permute-start(bf16[4,32,128]{2,1,0:T(8,128)(2,1)S(1)} %get-tuple-element.42.refs_0_), channel_id=1, source_target_pairs={{0,16},{8,24},{16,0},{24,8},{1,17},{9,25},{17,1},{25,9},{2,18},{10... | collective-permute-start | bytes 98312 | tf_op jit(solution)/shard_map/ppermute | solution.py:563
  78.0 2.2 %collective-permute-done.13.refs_2_ = bf16[4,32,128]{2,1,0:T(8,128)(2,1)S(1)} collective-permute-done((bf16[4,32,128]{2,1,0:T(8,128)(2,1)S(1)}, bf16[4,32,128]{2,1,0:T(8,128)(2,1)S(1)}, u32[]{:S(2)}, u32[]{:S(2)}) %collective-permute-start.13) | collective-permute-done | bytes 32800 | tf_op jit(solution)/shard_map/ppermute | solution.py:563
  80.2 1.1 collective-permute-done.12.refs_1_
  81.3 3.5 %backward_product.3.total_ref = bf16[8,128,128]{2,1,0:T(8,128)(2,1)S(1)} custom-call(s32[1,1,256]{2,1,0:T(1,128)S(1)} %copy-done.3, s32[1,1]{1,0:T(1,128)S(6)} %copy.7.live_ref, bf16[1024,128,128]{2,1,0:T(8,128)(2,1)} %get-tuple-element.34.block_hbm, bf16[4,32,128]{2,1,0:T(8,128)(2,1)S(1)} %get-tuple-element.42.refs_0_, ...), custom_call_target="tpu_custom_call" | custom-call | flops 268435456 | bytes 8388608 | tf_op jit(solution)/shard_map/backward_product/pallas_call | solution.py:345
  84.8 2.3 %all-to-all-done.3.col_dir_ref = bf16[8,5,32,128]{3,2,1,0:T(8,128)(2,1)S(1)} async-done(((bf16[8,5,32,128]{3,2,1,0:T(8,128)(2,1)}), bf16[8,5,32,128]{3,2,1,0:T(8,128)(2,1)S(1)}, u32[]{:S(2)}, u32[]{:S(2)}) %all-to-all-start.3) | async-done | bytes 327712 | tf_op jit(solution)/shard_map/all_to_all | solution.py:569
  87.1 1.3 %attach.1 = (bf16[8,144,128]{2,1,0:T(8,128)(2,1)}, f32[32,128]{1,0:T(8,128)S(1)}) custom-call(bf16[8,5,32,128]{3,2,1,0:T(8,128)(2,1)S(1)} %all-to-all-done.1.col_dir_ref.first_dir_ref, bf16[8,5,32,128]{3,2,1,0:T(8,128)(2,1)S(1)} %all-to-all-done.3.col_dir_ref, bf16[8,128,128]{2,1,0:T(8,128)(2,1)S(1)} %backward_product.3.total_ref), custom_call_target="tpu_custom_call" | custom-call | tf_op jit(solution)/shard_map/attach/pallas_call | solution.py:573
  88.3 4.1 %all-to-all-start.4 = ((bf16[8,144,128]{2,1,0:T(8,128)(2,1)}), bf16[8,144,128]{2,1,0:T(8,128)(2,1)S(1)}, u32[]{:S(2)}, u32[]{:S(2)}) async-start(bf16[8,144,128]{2,1,0:T(8,128)(2,1)} %get-tuple-element.43), calls=%async_computation.4 | async-start | bytes 589824 | tf_op jit(solution)/shard_map/all_to_all | solution.py:569
  92.5 3.5 %forward_product.3 = (bf16[4,32,128]{2,1,0:T(8,128)(2,1)S(1)}, bf16[4,32,128]{2,1,0:T(8,128)(2,1)S(1)}, bf16[4,32,128]{2,1,0:T(8,128)(2,1)S(1)}, bf16[4,32,128]{2,1,0:T(8,128)(2,1)S(1)}) custom-call(s32[1,1,256]{2,1,0:T(1,128)S(1)} %copy-done.3, s32[1,1]{1,0:T(1,128)S(6)} %copy.7.live_ref, bf16[1024,128,128]{2,1,0:T(8,128)(2,1)} %get-tuple-element.24.block_hbm, ...), custom_call_target="tpu_custom_call" | custom-call | flops 268435456 | bytes 8388608 | tf_op jit(solution)/shard_map/forward_product/pallas_call | solution.py:345
  96.1 1.7 %collective-permute-start.11 = (bf16[4,32,128]{2,1,0:T(8,128)(2,1)S(1)}, bf16[4,32,128]{2,1,0:T(8,128)(2,1)S(1)}, u32[]{:S(2)}, u32[]{:S(2)}) collective-permute-start(bf16[4,32,128]{2,1,0:T(8,128)(2,1)S(1)} %get-tuple-element.41), channel_id=1, source_target_pairs={{0,24},{8,0},{16,8},{24,16},{1,25},{9,1},{17,9},{25,17},{2,26},{10... | collective-permute-start | bytes 98312 | tf_op jit(solution)/shard_map/ppermute | solution.py:563
  97.8 4.1 %all-to-all-done.4.col_ref.refs_8_ = bf16[8,144,128]{2,1,0:T(8,128)(2,1)S(1)} async-done(((bf16[8,144,128]{2,1,0:T(8,128)(2,1)}), bf16[8,144,128]{2,1,0:T(8,128)(2,1)S(1)}, u32[]{:S(2)}, u32[]{:S(2)}) %all-to-all-start.4) | async-done | bytes 294944 | tf_op jit(solution)/shard_map/all_to_all | solution.py:569
  102.5 0.9 collective-permute-done.17.refs_7_
  103.5 2.4 %collective-permute-done.16.refs_6_ = f32[32,128]{1,0:T(8,128)S(1)} collective-permute-done((f32[32,128]{1,0:T(8,128)S(1)}, f32[32,128]{1,0:T(8,128)S(1)}, u32[]{:S(2)}, u32[]{:S(2)}) %collective-permute-start.16) | collective-permute-done | bytes 16416 | tf_op jit(solution)/shard_map/ppermute | solution.py:563
  105.8 4.7 %close.1 = (f32[32,512]{1,0:T(8,128)}, f32[32,512]{1,0:T(8,128)}) custom-call(bf16[4,32,128]{2,1,0:T(8,128)(2,1)S(1)} %get-tuple-element.38.refs_0_, bf16[4,32,128]{2,1,0:T(8,128)(2,1)S(1)} %collective-permute-done.9.refs_1_, bf16[4,32,128]{2,1,0:T(8,128)(2,1)S(1)} %collective-permute-done.10.refs_2_, ...), custom_call_target="tpu_custom_call" | custom-call | tf_op jit(solution)/shard_map/close/pallas_call | solution.py:573
  (32 shorter events, 3.9 us)
Async XLA Ops:
  0.6 59.4 %copy-start.3 = (s32[1,1,256]{2,1,0:T(1,128)S(1)}, s32[1,1,256]{2,1,0:T(1,128)}, u32[]{:S(2)}) copy-start(s32[1,1,256]{2,1,0:T(1,128)} %spots_ref.9) | copy-start | bytes 3076
  14.9 22.8 %all-to-all-start = ((f32[8,4,128]{2,1,0:T(4,128)}), f32[8,4,128]{2,1,0:T(4,128)S(1)}, u32[]{:S(2)}, u32[]{:S(2)}) async-start(f32[8,4,128]{2,1,0:T(4,128)} %bitcast.5), calls=%async_computation | async-start | bytes 32768 | tf_op jit(solution)/shard_map/all_to_all | solution.py:569
  31.1 3.2 %collective-permute-start = (f32[4,128]{1,0:T(4,128)}, f32[4,128]{1,0:T(4,128)S(1)}, u32[]{:S(2)}, u32[]{:S(2)}) collective-permute-start(f32[4,128]{1,0:T(4,128)} %get-tuple-element.25), channel_id=1, source_target_pairs={{0,8},{8,16},{16,24},{24,0},{1,9},{9,17},{17,25},{25,1},{2,10},{10... | collective-permute-start | bytes 6152 | tf_op jit(solution)/shard_map/ppermute | solution.py:563
  31.1 3.9 %collective-permute-start.1 = (f32[4,128]{1,0:T(4,128)}, f32[4,128]{1,0:T(4,128)S(1)}, u32[]{:S(2)}, u32[]{:S(2)}) collective-permute-start(f32[4,128]{1,0:T(4,128)} %get-tuple-element.26), channel_id=1, source_target_pairs={{0,16},{8,24},{16,0},{24,8},{1,17},{9,25},{17,1},{25,9},{2,18},{10... | collective-permute-start | bytes 6152 | tf_op jit(solution)/shard_map/ppermute | solution.py:563
  31.2 3.8 %collective-permute-start.2 = (f32[4,128]{1,0:T(4,128)}, f32[4,128]{1,0:T(4,128)S(1)}, u32[]{:S(2)}, u32[]{:S(2)}) collective-permute-start(f32[4,128]{1,0:T(4,128)} %get-tuple-element.27), channel_id=1, source_target_pairs={{0,24},{8,0},{16,8},{24,16},{1,25},{9,1},{17,9},{25,17},{2,26},{10... | collective-permute-start | bytes 6152 | tf_op jit(solution)/shard_map/ppermute | solution.py:563
  37.7 0.8 copy-start
  39.6 14.9 %all-to-all-start.1 = ((bf16[8,5,32,128]{3,2,1,0:T(8,128)(2,1)}), bf16[8,5,32,128]{3,2,1,0:T(8,128)(2,1)S(1)}, u32[]{:S(2)}, u32[]{:S(2)}) async-start(bf16[8,5,32,128]{3,2,1,0:T(8,128)(2,1)} %get-tuple-element.29), calls=%async_computation.1 | async-start | bytes 655360 | tf_op jit(solution)/shard_map/all_to_all | solution.py:569
  43.0 2.4 %collective-permute-start.8 = (bf16[4,32,128]{2,1,0:T(8,128)(2,1)S(1)}, bf16[4,32,128]{2,1,0:T(8,128)(2,1)S(1)}, u32[]{:S(2)}, u32[]{:S(2)}) collective-permute-start(bf16[4,32,128]{2,1,0:T(8,128)(2,1)S(1)} %get-tuple-element.35.refs_0_), channel_id=1, source_target_pairs={{0,24},{8,0},{16,8},{24,16},{1,25},{9,1},{17,9},{25,17},{2,26},{10... | collective-permute-start | bytes 98312 | tf_op jit(solution)/shard_map/ppermute | solution.py:563
  43.7 4.0 %collective-permute-start.7 = (bf16[4,32,128]{2,1,0:T(8,128)(2,1)S(1)}, bf16[4,32,128]{2,1,0:T(8,128)(2,1)S(1)}, u32[]{:S(2)}, u32[]{:S(2)}) collective-permute-start(bf16[4,32,128]{2,1,0:T(8,128)(2,1)S(1)} %get-tuple-element.35.refs_0_), channel_id=1, source_target_pairs={{0,16},{8,24},{16,0},{24,8},{1,17},{9,25},{17,1},{25,9},{2,18},{10... | collective-permute-start | bytes 98312 | tf_op jit(solution)/shard_map/ppermute | solution.py:563
  45.5 3.3 %collective-permute-start.6 = (bf16[4,32,128]{2,1,0:T(8,128)(2,1)S(1)}, bf16[4,32,128]{2,1,0:T(8,128)(2,1)S(1)}, u32[]{:S(2)}, u32[]{:S(2)}) collective-permute-start(bf16[4,32,128]{2,1,0:T(8,128)(2,1)S(1)} %get-tuple-element.35.refs_0_), channel_id=1, source_target_pairs={{0,8},{8,16},{16,24},{24,0},{1,9},{9,17},{17,25},{25,1},{2,10},{10... | collective-permute-start | bytes 98312 | tf_op jit(solution)/shard_map/ppermute | solution.py:563
  48.8 0.7 copy-start.2
  49.5 18.8 %copy-start.1 = (f32[32,512]{1,0:T(8,128)S(1)}, f32[32,512]{1,0:T(8,128)}, u32[]{:S(2)}) copy-start(f32[32,512]{1,0:T(8,128)} %refs_10_.1) | copy-start | bytes 196612
  54.5 13.7 %all-to-all-start.2 = ((bf16[8,128,128]{2,1,0:T(8,128)(2,1)}), bf16[8,128,128]{2,1,0:T(8,128)(2,1)S(1)}, u32[]{:S(2)}, u32[]{:S(2)}) async-start(bf16[8,128,128]{2,1,0:T(8,128)(2,1)} %backward_product.2), calls=%async_computation.2 | async-start | bytes 524288 | tf_op jit(solution)/shard_map/all_to_all | solution.py:569
  63.5 4.7 %collective-permute-start.3 = (bf16[4,32,128]{2,1,0:T(8,128)(2,1)S(1)}, bf16[4,32,128]{2,1,0:T(8,128)(2,1)S(1)}, u32[]{:S(2)}, u32[]{:S(2)}) collective-permute-start(bf16[4,32,128]{2,1,0:T(8,128)(2,1)S(1)} %get-tuple-element.31), channel_id=1, source_target_pairs={{0,8},{8,16},{16,24},{24,0},{1,9},{9,17},{17,25},{25,1},{2,10},{10... | collective-permute-start | bytes 98312 | tf_op jit(solution)/shard_map/ppermute | solution.py:563
  63.6 4.7 %collective-permute-start.4 = (bf16[4,32,128]{2,1,0:T(8,128)(2,1)S(1)}, bf16[4,32,128]{2,1,0:T(8,128)(2,1)S(1)}, u32[]{:S(2)}, u32[]{:S(2)}) collective-permute-start(bf16[4,32,128]{2,1,0:T(8,128)(2,1)S(1)} %get-tuple-element.32), channel_id=1, source_target_pairs={{0,16},{8,24},{16,0},{24,8},{1,17},{9,25},{17,1},{25,9},{2,18},{10... | collective-permute-start | bytes 98312 | tf_op jit(solution)/shard_map/ppermute | solution.py:563
  63.7 4.6 %collective-permute-start.5 = (bf16[4,32,128]{2,1,0:T(8,128)(2,1)S(1)}, bf16[4,32,128]{2,1,0:T(8,128)(2,1)S(1)}, u32[]{:S(2)}, u32[]{:S(2)}) collective-permute-start(bf16[4,32,128]{2,1,0:T(8,128)(2,1)S(1)} %get-tuple-element.33), channel_id=1, source_target_pairs={{0,24},{8,0},{16,8},{24,16},{1,25},{9,1},{17,9},{25,17},{2,26},{10... | collective-permute-start | bytes 98312 | tf_op jit(solution)/shard_map/ppermute | solution.py:563
  69.5 17.6 %all-to-all-start.3 = ((bf16[8,5,32,128]{3,2,1,0:T(8,128)(2,1)}), bf16[8,5,32,128]{3,2,1,0:T(8,128)(2,1)S(1)}, u32[]{:S(2)}, u32[]{:S(2)}) async-start(bf16[8,5,32,128]{3,2,1,0:T(8,128)(2,1)} %get-tuple-element.37), calls=%async_computation.3 | async-start | bytes 655360 | tf_op jit(solution)/shard_map/all_to_all | solution.py:569
  75.5 2.5 %collective-permute-start.14 = (bf16[4,32,128]{2,1,0:T(8,128)(2,1)S(1)}, bf16[4,32,128]{2,1,0:T(8,128)(2,1)S(1)}, u32[]{:S(2)}, u32[]{:S(2)}) collective-permute-start(bf16[4,32,128]{2,1,0:T(8,128)(2,1)S(1)} %get-tuple-element.42.refs_0_), channel_id=1, source_target_pairs={{0,24},{8,0},{16,8},{24,16},{1,25},{9,1},{17,9},{25,17},{2,26},{10... | collective-permute-start | bytes 98312 | tf_op jit(solution)/shard_map/ppermute | solution.py:563
  76.3 3.9 %collective-permute-start.13 = (bf16[4,32,128]{2,1,0:T(8,128)(2,1)S(1)}, bf16[4,32,128]{2,1,0:T(8,128)(2,1)S(1)}, u32[]{:S(2)}, u32[]{:S(2)}) collective-permute-start(bf16[4,32,128]{2,1,0:T(8,128)(2,1)S(1)} %get-tuple-element.42.refs_0_), channel_id=1, source_target_pairs={{0,16},{8,24},{16,0},{24,8},{1,17},{9,25},{17,1},{25,9},{2,18},{10... | collective-permute-start | bytes 98312 | tf_op jit(solution)/shard_map/ppermute | solution.py:563
  78.0 3.3 %collective-permute-start.12 = (bf16[4,32,128]{2,1,0:T(8,128)(2,1)S(1)}, bf16[4,32,128]{2,1,0:T(8,128)(2,1)S(1)}, u32[]{:S(2)}, u32[]{:S(2)}) collective-permute-start(bf16[4,32,128]{2,1,0:T(8,128)(2,1)S(1)} %get-tuple-element.42.refs_0_), channel_id=1, source_target_pairs={{0,8},{8,16},{16,24},{24,0},{1,9},{9,17},{17,25},{25,1},{2,10},{10... | collective-permute-start | bytes 98312 | tf_op jit(solution)/shard_map/ppermute | solution.py:563
  88.3 13.5 %all-to-all-start.4 = ((bf16[8,144,128]{2,1,0:T(8,128)(2,1)}), bf16[8,144,128]{2,1,0:T(8,128)(2,1)S(1)}, u32[]{:S(2)}, u32[]{:S(2)}) async-start(bf16[8,144,128]{2,1,0:T(8,128)(2,1)} %get-tuple-element.43), calls=%async_computation.4 | async-start | bytes 589824 | tf_op jit(solution)/shard_map/all_to_all | solution.py:569
  95.9 6.3 %collective-permute-start.9 = (bf16[4,32,128]{2,1,0:T(8,128)(2,1)S(1)}, bf16[4,32,128]{2,1,0:T(8,128)(2,1)S(1)}, u32[]{:S(2)}, u32[]{:S(2)}) collective-permute-start(bf16[4,32,128]{2,1,0:T(8,128)(2,1)S(1)} %get-tuple-element.39), channel_id=1, source_target_pairs={{0,8},{8,16},{16,24},{24,0},{1,9},{9,17},{17,25},{25,1},{2,10},{10... | collective-permute-start | bytes 98312 | tf_op jit(solution)/shard_map/ppermute | solution.py:563
  96.0 6.5 %collective-permute-start.10 = (bf16[4,32,128]{2,1,0:T(8,128)(2,1)S(1)}, bf16[4,32,128]{2,1,0:T(8,128)(2,1)S(1)}, u32[]{:S(2)}, u32[]{:S(2)}) collective-permute-start(bf16[4,32,128]{2,1,0:T(8,128)(2,1)S(1)} %get-tuple-element.40), channel_id=1, source_target_pairs={{0,16},{8,24},{16,0},{24,8},{1,17},{9,25},{17,1},{25,9},{2,18},{10... | collective-permute-start | bytes 98312 | tf_op jit(solution)/shard_map/ppermute | solution.py:563
  96.1 6.4 %collective-permute-start.11 = (bf16[4,32,128]{2,1,0:T(8,128)(2,1)S(1)}, bf16[4,32,128]{2,1,0:T(8,128)(2,1)S(1)}, u32[]{:S(2)}, u32[]{:S(2)}) collective-permute-start(bf16[4,32,128]{2,1,0:T(8,128)(2,1)S(1)} %get-tuple-element.41), channel_id=1, source_target_pairs={{0,24},{8,0},{16,8},{24,16},{1,25},{9,1},{17,9},{25,17},{2,26},{10... | collective-permute-start | bytes 98312 | tf_op jit(solution)/shard_map/ppermute | solution.py:563
  102.0 1.4 %collective-permute-start.17 = (f32[32,128]{1,0:T(8,128)S(1)}, f32[32,128]{1,0:T(8,128)S(1)}, u32[]{:S(2)}, u32[]{:S(2)}) collective-permute-start(f32[32,128]{1,0:T(8,128)S(1)} %gram_sum.1.refs_4_), channel_id=1, source_target_pairs={{0,24},{8,0},{16,8},{24,16},{1,25},{9,1},{17,9},{25,17},{2,26},{10... | collective-permute-start | bytes 49160 | tf_op jit(solution)/shard_map/ppermute | solution.py:563
  102.0 3.8 %collective-permute-start.16 = (f32[32,128]{1,0:T(8,128)S(1)}, f32[32,128]{1,0:T(8,128)S(1)}, u32[]{:S(2)}, u32[]{:S(2)}) collective-permute-start(f32[32,128]{1,0:T(8,128)S(1)} %gram_sum.1.refs_4_), channel_id=1, source_target_pairs={{0,16},{8,24},{16,0},{24,8},{1,17},{9,25},{17,1},{25,9},{2,18},{10... | collective-permute-start | bytes 49160 | tf_op jit(solution)/shard_map/ppermute | solution.py:563
  102.3 3.5 %collective-permute-start.15 = (f32[32,128]{1,0:T(8,128)S(1)}, f32[32,128]{1,0:T(8,128)S(1)}, u32[]{:S(2)}, u32[]{:S(2)}) collective-permute-start(f32[32,128]{1,0:T(8,128)S(1)} %gram_sum.1.refs_4_), channel_id=1, source_target_pairs={{0,8},{8,16},{16,24},{24,0},{1,9},{9,17},{17,25},{25,1},{2,10},{10... | collective-permute-start | bytes 49160 | tf_op jit(solution)/shard_map/ppermute | solution.py:563

commit v11 on v10

--- a/solution.py
+++ b/solution.py
@@ -94,61 +94,65 @@
     identity = jnp.where(diagonal, 1.0, 0.0).astype(jnp.bfloat16)
     zero = jnp.zeros((16, 128), jnp.bfloat16)
 
+    targets = [(rows_16 + 16 * part).astype(jnp.int16) for part in range(8)]
+
+    def turn_pair(first_slot):
+        return [dot_across(identity, block_ref[first_slot + which]) for which in range(2)]
+
+    def store_turned(first_slot, turned, started):
+        for which, block in enumerate(turned):
+            slot = first_slot + which
+            flipped_ref[slot] = block.astype(jnp.bfloat16)
+            sums = jnp.sum(block.reshape(16, 8, 128), axis=0)
+            _, col_block = place_of(places, slot, col_blocks)
+            col_ref[col_block] += jnp.where(started, sums, 0.0)
+
+    def build_pair(pair, _):
+        first_slot = 2 * pair
+        before = 2 * jnp.maximum(pair - 1, 0)
+        turned = turn_pair(before)
+        tables = []
+        for slot in (first_slot, first_slot + 1):
+            active = (slot < live_count(places)).astype(jnp.float32)
+            values = value_ref[slot].astype(jnp.float32) * active
+            tables.append((index_ref[slot].astype(jnp.int16), values.astype(jnp.bfloat16)))
+            row_block, _ = place_of(places, slot, col_blocks)
+            row_ref[row_block] += values[:8] + values[8:]
+        sums = [[zero] * 8 for _ in tables]
+        for entry in range(0, 16, 2):
+            for which, (indices, values) in enumerate(tables):
+                rows = [
+                    [jnp.broadcast_to(table[at : at + 1], (16, 128)) for table in (indices, values)]
+                    for at in (entry, entry + 1)
+                ]
+                for part in range(8):
+                    first, second = [
+                        jnp.where(index_row == targets[part], value_row, zero)
+                        for index_row, value_row in rows
+                    ]
+                    sums[which][part] = sums[which][part] + (first + second)
+        for which, parts in enumerate(sums):
+            block_ref[first_slot + which] = jnp.concatenate(parts, axis=0)
+        store_turned(before, turned, pair > 0)
+        return 0
+
     def build_group(index, _):
         group_copy(index_hbm, index_ref, index_sems, index, GROUP).wait()
         group_copy(value_hbm, value_ref, value_sems, index, GROUP).wait()
-        targets = [(rows_16 + 16 * part).astype(jnp.int16) for part in range(8)]
-
-        def load_pair(inside):
-            tables = []
-            for slot in (index * GROUP + inside, index * GROUP + inside + 1):
-                active = (slot < live_count(places)).astype(jnp.float32)
-                values = value_ref[slot].astype(jnp.float32) * active
-                indices = index_ref[slot].astype(jnp.int16)
-                tables.append((slot, indices, values, values.astype(jnp.bfloat16)))
-            return tables
-
-        def build_pair(tables):
-            sums = [[zero] * 8 for _ in tables]
-            for entry in range(0, 16, 2):
-                for which, (_, indices, _, narrow) in enumerate(tables):
-                    pair = []
-                    for at in (entry, entry + 1):
-                        index_row = jnp.broadcast_to(indices[at : at + 1], (16, 128))
-                        value_row = jnp.broadcast_to(narrow[at : at + 1], (16, 128))
-                        pair.append((index_row, value_row))
-                    for part in range(8):
-                        first, second = [
-                            jnp.where(index_row == targets[part], value_row, zero)
-                            for index_row, value_row in pair
-                        ]
-                        sums[which][part] = sums[which][part] + (first + second)
-            return [jnp.concatenate(parts, axis=0) for parts in sums]
-
-        def store_turned(tables, turned):
-            for (slot, _, values, _), block in zip(tables, turned):
-                row_block, col_block = place_of(places, slot, col_blocks)
-                flipped_ref[slot] = block.astype(jnp.bfloat16)
-                col_ref[col_block] += jnp.sum(block.reshape(16, 8, 128), axis=0)
-                row_ref[row_block] += values[:8] + values[8:]
-
-        tables = load_pair(0)
-        waiting = None
-        for inside in range(0, GROUP, 2):
-            following = load_pair(inside + 2) if inside + 2 < GROUP else None
-            blocks = build_pair(tables)
-            if waiting:
-                store_turned(*waiting)
-            for (slot, *_), block in zip(tables, blocks):
-                block_ref[slot] = block
-            waiting = (tables, [dot_across(identity, block) for block in blocks])
-            tables = following
-        store_turned(*waiting)
+        half = GROUP // 2
+        lax.fori_loop(index * half, index * half + half, build_pair, 0)
         group_copy(block_ref, block_hbm, block_sems, index, GROUP).start()
-        group_copy(flipped_ref, flipped_hbm, flipped_sems, index, GROUP).start()
+
+        @pl.when(index > 0)
+        def _():
+            group_copy(flipped_ref, flipped_hbm, flipped_sems, index - 1, GROUP).start()
+
         return 0
 
     lax.fori_loop(0, groups, build_group, 0)
+    last = groups * GROUP - 2
+    store_turned(last, turn_pair(last), True)
+    group_copy(flipped_ref, flipped_hbm, flipped_sems, groups - 1, GROUP).start()
     for ahead, out in enumerate(row_outs, 1):
         first = lax.rem(lax.axis_index("row") + ahead, row_count) * per_seg
         for part in range(per_seg):

time: 109 us -> 112 us (1.028); the launches traced: 111 us -> 110 us
  starting transfers between devices: 46.2 us -> 53.1 us
  Pallas kernels: 36.4 us -> 29.6 us
    ppermute x18, starting transfers between devices: 10.8 us -> 22.1 us  [pass_around(): lax.ppermute(pieces[ahead], axis, [(at, (at + ahead) % count) for at in r...]
    all_to_all x5, starting transfers between devices: 35.4 us -> 31 us  [exchange(): return lax.all_to_all(pieces, axis, 0, 0, tiled=True)]
    pallas_call x1, Pallas kernels: 13.6 us -> 9.94 us  [build_blocks(): pl.pallas_call(build_kernel, in_specs=[SCALARS, SCALARS, ANYWHERE, ANYWHE...]
    pallas_call x4, Pallas kernels: 14.6 us -> 11.4 us  [over_blocks(): pl.pallas_call(kernel, in_specs=[SCALARS, SCALARS, ANYWHERE] + [IN_VMEM]...]
  transfers between devices with their start and end apart: 23 -> 23, of which waited for: 13 -> 15; matrix products, arithmetic and copies ran while one was open for 0% -> 0% of each run, Pallas kernels for 13% -> 11%
where the time goes in v11:
time: 112 us; the launch traced here: 110 us
  starting transfers between devices  53.1 us (47%)
  Pallas kernels  29.6 us (26%)
  waiting for transfers between devices  24.2 us (22%)
  local copies, waits for them, and re-layouts  1.53 us (1%)
  between operations  1.4 us (1%)
    all_to_all x5, starting transfers between devices, exchange(): return lax.all_to_all(pieces, axis, 0, 0, tiled=True)  31 us
    ppermute x18, starting transfers between devices, pass_around(): lax.ppermute(pieces[ahead], axis, [(at, (at + ahead) % count) for at in r...  22.1 us
    all_to_all x5, waiting for transfers between devices, exchange(): return lax.all_to_all(pieces, axis, 0, 0, tiled=True)  12.7 us
    ppermute x18, waiting for transfers between devices, pass_around(): lax.ppermute(pieces[ahead], axis, [(at, (at + ahead) % count) for at in r...  11.5 us
    pallas_call x4, Pallas kernels, over_blocks(): pl.pallas_call(kernel, in_specs=[SCALARS, SCALARS, ANYWHERE] + [IN_VMEM]...  11.4 us
    pallas_call x1, Pallas kernels, build_blocks(): pl.pallas_call(build_kernel, in_specs=[SCALARS, SCALARS, ANYWHERE, ANYWHE...  9.94 us
    pallas_call x5, Pallas kernels, simple_call(): pl.pallas_call(kernel, out_shape=shapes, compiler_params=pltpu.CompilerPa...  8.29 us
  transfers between devices with their start and end apart: 23, of which 15 were waited for; matrix products, arithmetic and copies ran while one was open for 0% of the time, Pallas kernels for 11%

profile of v11, /device:TPU:0, one launch (start us, length us, event | category | flops | bytes accessed | tf_op | source)
XLA Modules:
  0.0 109.8 jit_solution(7848558335866087195)
XLA Ops:
  1.3 9.9 %build_blocks.1 = (bf16[1024,128,128]{2,1,0:T(8,128)(2,1)}, bf16[1024,128,128]{2,1,0:T(8,128)(2,1)}, f32[4,128]{1,0:T(4,128)}, f32[4,128]{1,0:T(4,128)}, f32[4,128]{1,0:T(4,128)}, /*index=5*/f32[32,128]{1,0:T(8,128)}) custom-call(s32[1,1,256]{2,1,0:T(1,128)} %spots_ref.9, s32[1,1]{1,0:T(1,128)S(6)} %copy.7.live_ref, s32[256,16,128]{2,1,0:T(8,128)} %bitcast.3, ...), custom_call_target="tpu_custom_call" | custom-call | tf_op jit(solution)/shard_map/build_blocks/pallas_call | solution.py:187
  11.2 12.3 %all-to-all-start = ((f32[8,4,128]{2,1,0:T(4,128)}), f32[8,4,128]{2,1,0:T(4,128)S(1)}, u32[]{:S(2)}, u32[]{:S(2)}) async-start(f32[8,4,128]{2,1,0:T(4,128)} %bitcast.5), calls=%async_computation | async-start | bytes 32768 | tf_op jit(solution)/shard_map/all_to_all | solution.py:573
  23.6 11.1 %collective-permute-start.1 = (f32[4,128]{1,0:T(4,128)}, f32[4,128]{1,0:T(4,128)S(1)}, u32[]{:S(2)}, u32[]{:S(2)}) collective-permute-start(f32[4,128]{1,0:T(4,128)} %get-tuple-element.26), channel_id=1, source_target_pairs={{0,16},{8,24},{16,0},{24,8},{1,17},{9,25},{17,1},{25,9},{2,18},{10... | collective-permute-start | bytes 6152 | tf_op jit(solution)/shard_map/ppermute | solution.py:567
  34.7 1.1 collective-permute-done.refs_0_
  37.3 1.0 start.1
  38.4 5.7 %all-to-all-start.1 = ((bf16[8,5,32,128]{3,2,1,0:T(8,128)(2,1)}), bf16[8,5,32,128]{3,2,1,0:T(8,128)(2,1)S(1)}, u32[]{:S(2)}, u32[]{:S(2)}) async-start(bf16[8,5,32,128]{3,2,1,0:T(8,128)(2,1)} %get-tuple-element.29), calls=%async_computation.1 | async-start | bytes 655360 | tf_op jit(solution)/shard_map/all_to_all | solution.py:573
  44.1 1.5 %collective-permute-start.8 = (bf16[4,32,128]{2,1,0:T(8,128)(2,1)S(1)}, bf16[4,32,128]{2,1,0:T(8,128)(2,1)S(1)}, u32[]{:S(2)}, u32[]{:S(2)}) collective-permute-start(bf16[4,32,128]{2,1,0:T(8,128)(2,1)S(1)} %get-tuple-element.35.refs_0_), channel_id=1, source_target_pairs={{0,24},{8,0},{16,8},{24,16},{1,25},{9,1},{17,9},{25,17},{2,26},{10... | collective-permute-start | bytes 98312 | tf_op jit(solution)/shard_map/ppermute | solution.py:567
  45.5 1.1 collective-permute-start.7
  47.2 2.2 %collective-permute-done.7.refs_2_ = bf16[4,32,128]{2,1,0:T(8,128)(2,1)S(1)} collective-permute-done((bf16[4,32,128]{2,1,0:T(8,128)(2,1)S(1)}, bf16[4,32,128]{2,1,0:T(8,128)(2,1)S(1)}, u32[]{:S(2)}, u32[]{:S(2)}) %collective-permute-start.7) | collective-permute-done | bytes 32800 | tf_op jit(solution)/shard_map/ppermute | solution.py:567
  50.6 3.4 %backward_product.2 = bf16[8,128,128]{2,1,0:T(8,128)(2,1)} custom-call(s32[1,1,256]{2,1,0:T(1,128)S(1)} %copy-done.2, s32[1,1]{1,0:T(1,128)S(6)} %copy.7.live_ref, bf16[1024,128,128]{2,1,0:T(8,128)(2,1)} %get-tuple-element.34.block_hbm, bf16[4,32,128]{2,1,0:T(8,128)(2,1)S(1)} %get-tuple-element.35.refs_0_, ...), custom_call_target="tpu_custom_call" | custom-call | flops 268435456 | bytes 8388608 | tf_op jit(solution)/shard_map/backward_product/pallas_call | solution.py:349
  54.0 1.7 %all-to-all-done.1.col_dir_ref.first_dir_ref = bf16[8,5,32,128]{3,2,1,0:T(8,128)(2,1)S(1)} async-done(((bf16[8,5,32,128]{3,2,1,0:T(8,128)(2,1)}), bf16[8,5,32,128]{3,2,1,0:T(8,128)(2,1)S(1)}, u32[]{:S(2)}, u32[]{:S(2)}) %all-to-all-start.1) | async-done | bytes 327712 | tf_op jit(solution)/shard_map/all_to_all | solution.py:573
  55.7 4.5 %all-to-all-start.2 = ((bf16[8,128,128]{2,1,0:T(8,128)(2,1)}), bf16[8,128,128]{2,1,0:T(8,128)(2,1)S(1)}, u32[]{:S(2)}, u32[]{:S(2)}) async-start(bf16[8,128,128]{2,1,0:T(8,128)(2,1)} %backward_product.2), calls=%async_computation.2 | async-start | bytes 524288 | tf_op jit(solution)/shard_map/all_to_all | solution.py:573
  60.2 2.7 %forward_product.2 = (bf16[4,32,128]{2,1,0:T(8,128)(2,1)S(1)}, bf16[4,32,128]{2,1,0:T(8,128)(2,1)S(1)}, bf16[4,32,128]{2,1,0:T(8,128)(2,1)S(1)}, bf16[4,32,128]{2,1,0:T(8,128)(2,1)S(1)}) custom-call(s32[1,1,256]{2,1,0:T(1,128)S(1)} %copy-done.3, s32[1,1]{1,0:T(1,128)S(6)} %copy.7.live_ref, bf16[1024,128,128]{2,1,0:T(8,128)(2,1)} %get-tuple-element.24.block_hbm, ...), custom_call_target="tpu_custom_call" | custom-call | flops 268435456 | bytes 8388608 | tf_op jit(solution)/shard_map/forward_product/pallas_call | solution.py:349
  62.9 1.0 collective-permute-start.4
  63.9 1.4 %collective-permute-start.5 = (bf16[4,32,128]{2,1,0:T(8,128)(2,1)S(1)}, bf16[4,32,128]{2,1,0:T(8,128)(2,1)S(1)}, u32[]{:S(2)}, u32[]{:S(2)}) collective-permute-start(bf16[4,32,128]{2,1,0:T(8,128)(2,1)S(1)} %get-tuple-element.33), channel_id=1, source_target_pairs={{0,24},{8,0},{16,8},{24,16},{1,25},{9,1},{17,9},{25,17},{2,26},{10... | collective-permute-start | bytes 98312 | tf_op jit(solution)/shard_map/ppermute | solution.py:567
  65.3 3.3 %all-to-all-done.2.refs_4_ = bf16[8,128,128]{2,1,0:T(8,128)(2,1)S(1)} async-done(((bf16[8,128,128]{2,1,0:T(8,128)(2,1)}), bf16[8,128,128]{2,1,0:T(8,128)(2,1)S(1)}, u32[]{:S(2)}, u32[]{:S(2)}) %all-to-all-start.2) | async-done | bytes 262176 | tf_op jit(solution)/shard_map/all_to_all | solution.py:573
  68.7 1.2 %middle.1 = (f32[4,32,128]{2,1,0:T(8,128)S(1)}, bf16[4,32,128]{2,1,0:T(8,128)(2,1)S(1)}, bf16[8,5,32,128]{3,2,1,0:T(8,128)(2,1)}) custom-call(bf16[4,32,128]{2,1,0:T(8,128)(2,1)S(1)} %get-tuple-element.30.refs_0_, bf16[4,32,128]{2,1,0:T(8,128)(2,1)S(1)} %collective-permute-done.3.refs_1_, bf16[4,32,128]{2,1,0:T(8,128)(2,1)S(1)} %collective-permute-done.4.refs_2_, ...), custom_call_target="tpu_custom_call" | custom-call | tf_op jit(solution)/shard_map/middle/pallas_call | solution.py:577
  69.9 4.9 %all-to-all-start.3 = ((bf16[8,5,32,128]{3,2,1,0:T(8,128)(2,1)}), bf16[8,5,32,128]{3,2,1,0:T(8,128)(2,1)S(1)}, u32[]{:S(2)}, u32[]{:S(2)}) async-start(bf16[8,5,32,128]{3,2,1,0:T(8,128)(2,1)} %get-tuple-element.37), calls=%async_computation.3 | async-start | bytes 655360 | tf_op jit(solution)/shard_map/all_to_all | solution.py:573
  74.7 1.2 %collective-permute-start.14 = (bf16[4,32,128]{2,1,0:T(8,128)(2,1)S(1)}, bf16[4,32,128]{2,1,0:T(8,128)(2,1)S(1)}, u32[]{:S(2)}, u32[]{:S(2)}) collective-permute-start(bf16[4,32,128]{2,1,0:T(8,128)(2,1)S(1)} %get-tuple-element.42.refs_0_), channel_id=1, source_target_pairs={{0,24},{8,0},{16,8},{24,16},{1,25},{9,1},{17,9},{25,17},{2,26},{10... | collective-permute-start | bytes 98312 | tf_op jit(solution)/shard_map/ppermute | solution.py:567
  75.9 1.1 collective-permute-start.13
  77.5 2.3 %collective-permute-done.13.refs_2_ = bf16[4,32,128]{2,1,0:T(8,128)(2,1)S(1)} collective-permute-done((bf16[4,32,128]{2,1,0:T(8,128)(2,1)S(1)}, bf16[4,32,128]{2,1,0:T(8,128)(2,1)S(1)}, u32[]{:S(2)}, u32[]{:S(2)}) %collective-permute-start.13) | collective-permute-done | bytes 32800 | tf_op jit(solution)/shard_map/ppermute | solution.py:567
  80.3 2.7 %backward_product.3.total_ref = bf16[8,128,128]{2,1,0:T(8,128)(2,1)S(1)} custom-call(s32[1,1,256]{2,1,0:T(1,128)S(1)} %copy-done.3, s32[1,1]{1,0:T(1,128)S(6)} %copy.7.live_ref, bf16[1024,128,128]{2,1,0:T(8,128)(2,1)} %get-tuple-element.34.block_hbm, bf16[4,32,128]{2,1,0:T(8,128)(2,1)S(1)} %get-tuple-element.42.refs_0_, ...), custom_call_target="tpu_custom_call" | custom-call | flops 268435456 | bytes 8388608 | tf_op jit(solution)/shard_map/backward_product/pallas_call | solution.py:349
  83.0 3.0 %all-to-all-done.3.col_dir_ref = bf16[8,5,32,128]{3,2,1,0:T(8,128)(2,1)S(1)} async-done(((bf16[8,5,32,128]{3,2,1,0:T(8,128)(2,1)}), bf16[8,5,32,128]{3,2,1,0:T(8,128)(2,1)S(1)}, u32[]{:S(2)}, u32[]{:S(2)}) %all-to-all-start.3) | async-done | bytes 327712 | tf_op jit(solution)/shard_map/all_to_all | solution.py:573
  86.1 1.3 %attach.1 = (bf16[8,144,128]{2,1,0:T(8,128)(2,1)}, f32[32,128]{1,0:T(8,128)S(1)}) custom-call(bf16[8,5,32,128]{3,2,1,0:T(8,128)(2,1)S(1)} %all-to-all-done.1.col_dir_ref.first_dir_ref, bf16[8,5,32,128]{3,2,1,0:T(8,128)(2,1)S(1)} %all-to-all-done.3.col_dir_ref, bf16[8,128,128]{2,1,0:T(8,128)(2,1)S(1)} %backward_product.3.total_ref), custom_call_target="tpu_custom_call" | custom-call | tf_op jit(solution)/shard_map/attach/pallas_call | solution.py:577
  87.3 3.6 %all-to-all-start.4 = ((bf16[8,144,128]{2,1,0:T(8,128)(2,1)}), bf16[8,144,128]{2,1,0:T(8,128)(2,1)S(1)}, u32[]{:S(2)}, u32[]{:S(2)}) async-start(bf16[8,144,128]{2,1,0:T(8,128)(2,1)} %get-tuple-element.43), calls=%async_computation.4 | async-start | bytes 589824 | tf_op jit(solution)/shard_map/all_to_all | solution.py:573
  91.0 2.7 %forward_product.3 = (bf16[4,32,128]{2,1,0:T(8,128)(2,1)S(1)}, bf16[4,32,128]{2,1,0:T(8,128)(2,1)S(1)}, bf16[4,32,128]{2,1,0:T(8,128)(2,1)S(1)}, bf16[4,32,128]{2,1,0:T(8,128)(2,1)S(1)}) custom-call(s32[1,1,256]{2,1,0:T(1,128)S(1)} %copy-done.3, s32[1,1]{1,0:T(1,128)S(6)} %copy.7.live_ref, bf16[1024,128,128]{2,1,0:T(8,128)(2,1)} %get-tuple-element.24.block_hbm, ...), custom_call_target="tpu_custom_call" | custom-call | flops 268435456 | bytes 8388608 | tf_op jit(solution)/shard_map/forward_product/pallas_call | solution.py:349
  94.3 1.0 collective-permute-start.10
  95.3 0.9 collective-permute-start.11
  96.1 4.7 %all-to-all-done.4.col_ref.refs_8_ = bf16[8,144,128]{2,1,0:T(8,128)(2,1)S(1)} async-done(((bf16[8,144,128]{2,1,0:T(8,128)(2,1)}), bf16[8,144,128]{2,1,0:T(8,128)(2,1)S(1)}, u32[]{:S(2)}, u32[]{:S(2)}) %all-to-all-start.4) | async-done | bytes 294944 | tf_op jit(solution)/shard_map/all_to_all | solution.py:573
  100.9 1.0 collective-permute-start.16
  102.4 2.4 %collective-permute-done.16.refs_6_ = f32[32,128]{1,0:T(8,128)S(1)} collective-permute-done((f32[32,128]{1,0:T(8,128)S(1)}, f32[32,128]{1,0:T(8,128)S(1)}, u32[]{:S(2)}, u32[]{:S(2)}) %collective-permute-start.16) | collective-permute-done | bytes 16416 | tf_op jit(solution)/shard_map/ppermute | solution.py:567
  105.1 4.7 %close.1 = (f32[32,512]{1,0:T(8,128)}, f32[32,512]{1,0:T(8,128)}) custom-call(bf16[4,32,128]{2,1,0:T(8,128)(2,1)S(1)} %get-tuple-element.38.refs_0_, bf16[4,32,128]{2,1,0:T(8,128)(2,1)S(1)} %collective-permute-done.9.refs_1_, bf16[4,32,128]{2,1,0:T(8,128)(2,1)S(1)} %collective-permute-done.10.refs_2_, ...), custom_call_target="tpu_custom_call" | custom-call | tf_op jit(solution)/shard_map/close/pallas_call | solution.py:577
  (32 shorter events, 6.0 us)
Async XLA Ops:
  0.6 59.5 %copy-start.3 = (s32[1,1,256]{2,1,0:T(1,128)S(1)}, s32[1,1,256]{2,1,0:T(1,128)}, u32[]{:S(2)}) copy-start(s32[1,1,256]{2,1,0:T(1,128)} %spots_ref.9) | copy-start | bytes 3076
  11.2 25.2 %all-to-all-start = ((f32[8,4,128]{2,1,0:T(4,128)}), f32[8,4,128]{2,1,0:T(4,128)S(1)}, u32[]{:S(2)}, u32[]{:S(2)}) async-start(f32[8,4,128]{2,1,0:T(4,128)} %bitcast.5), calls=%async_computation | async-start | bytes 32768 | tf_op jit(solution)/shard_map/all_to_all | solution.py:573
  23.5 12.2 %collective-permute-start = (f32[4,128]{1,0:T(4,128)}, f32[4,128]{1,0:T(4,128)S(1)}, u32[]{:S(2)}, u32[]{:S(2)}) collective-permute-start(f32[4,128]{1,0:T(4,128)} %get-tuple-element.25), channel_id=1, source_target_pairs={{0,8},{8,16},{16,24},{24,0},{1,9},{9,17},{17,25},{25,1},{2,10},{10... | collective-permute-start | bytes 6152 | tf_op jit(solution)/shard_map/ppermute | solution.py:567
  23.6 12.9 %collective-permute-start.1 = (f32[4,128]{1,0:T(4,128)}, f32[4,128]{1,0:T(4,128)S(1)}, u32[]{:S(2)}, u32[]{:S(2)}) collective-permute-start(f32[4,128]{1,0:T(4,128)} %get-tuple-element.26), channel_id=1, source_target_pairs={{0,16},{8,24},{16,0},{24,8},{1,17},{9,25},{17,1},{25,9},{2,18},{10... | collective-permute-start | bytes 6152 | tf_op jit(solution)/shard_map/ppermute | solution.py:567
  34.7 1.8 %collective-permute-start.2 = (f32[4,128]{1,0:T(4,128)}, f32[4,128]{1,0:T(4,128)S(1)}, u32[]{:S(2)}, u32[]{:S(2)}) collective-permute-start(f32[4,128]{1,0:T(4,128)} %get-tuple-element.27), channel_id=1, source_target_pairs={{0,24},{8,0},{16,8},{24,16},{1,25},{9,1},{17,9},{25,17},{2,26},{10... | collective-permute-start | bytes 6152 | tf_op jit(solution)/shard_map/ppermute | solution.py:567
  36.5 0.8 copy-start
  38.4 17.3 %all-to-all-start.1 = ((bf16[8,5,32,128]{3,2,1,0:T(8,128)(2,1)}), bf16[8,5,32,128]{3,2,1,0:T(8,128)(2,1)S(1)}, u32[]{:S(2)}, u32[]{:S(2)}) async-start(bf16[8,5,32,128]{3,2,1,0:T(8,128)(2,1)} %get-tuple-element.29), calls=%async_computation.1 | async-start | bytes 655360 | tf_op jit(solution)/shard_map/all_to_all | solution.py:573
  44.1 3.1 %collective-permute-start.8 = (bf16[4,32,128]{2,1,0:T(8,128)(2,1)S(1)}, bf16[4,32,128]{2,1,0:T(8,128)(2,1)S(1)}, u32[]{:S(2)}, u32[]{:S(2)}) collective-permute-start(bf16[4,32,128]{2,1,0:T(8,128)(2,1)S(1)} %get-tuple-element.35.refs_0_), channel_id=1, source_target_pairs={{0,24},{8,0},{16,8},{24,16},{1,25},{9,1},{17,9},{25,17},{2,26},{10... | collective-permute-start | bytes 98312 | tf_op jit(solution)/shard_map/ppermute | solution.py:567
  45.5 3.9 %collective-permute-start.7 = (bf16[4,32,128]{2,1,0:T(8,128)(2,1)S(1)}, bf16[4,32,128]{2,1,0:T(8,128)(2,1)S(1)}, u32[]{:S(2)}, u32[]{:S(2)}) collective-permute-start(bf16[4,32,128]{2,1,0:T(8,128)(2,1)S(1)} %get-tuple-element.35.refs_0_), channel_id=1, source_target_pairs={{0,16},{8,24},{16,0},{24,8},{1,17},{9,25},{17,1},{25,9},{2,18},{10... | collective-permute-start | bytes 98312 | tf_op jit(solution)/shard_map/ppermute | solution.py:567
  46.6 3.3 %collective-permute-start.6 = (bf16[4,32,128]{2,1,0:T(8,128)(2,1)S(1)}, bf16[4,32,128]{2,1,0:T(8,128)(2,1)S(1)}, u32[]{:S(2)}, u32[]{:S(2)}) collective-permute-start(bf16[4,32,128]{2,1,0:T(8,128)(2,1)S(1)} %get-tuple-element.35.refs_0_), channel_id=1, source_target_pairs={{0,8},{8,16},{16,24},{24,0},{1,9},{9,17},{17,25},{25,1},{2,10},{10... | collective-permute-start | bytes 98312 | tf_op jit(solution)/shard_map/ppermute | solution.py:567
  49.9 0.7 copy-start.2
  50.6 18.1 %copy-start.1 = (f32[32,512]{1,0:T(8,128)S(1)}, f32[32,512]{1,0:T(8,128)}, u32[]{:S(2)}) copy-start(f32[32,512]{1,0:T(8,128)} %refs_10_.1) | copy-start | bytes 196612
  55.7 13.0 %all-to-all-start.2 = ((bf16[8,128,128]{2,1,0:T(8,128)(2,1)}), bf16[8,128,128]{2,1,0:T(8,128)(2,1)S(1)}, u32[]{:S(2)}, u32[]{:S(2)}) async-start(bf16[8,128,128]{2,1,0:T(8,128)(2,1)} %backward_product.2), calls=%async_computation.2 | async-start | bytes 524288 | tf_op jit(solution)/shard_map/all_to_all | solution.py:573
  62.8 5.8 %collective-permute-start.3 = (bf16[4,32,128]{2,1,0:T(8,128)(2,1)S(1)}, bf16[4,32,128]{2,1,0:T(8,128)(2,1)S(1)}, u32[]{:S(2)}, u32[]{:S(2)}) collective-permute-start(bf16[4,32,128]{2,1,0:T(8,128)(2,1)S(1)} %get-tuple-element.31), channel_id=1, source_target_pairs={{0,8},{8,16},{16,24},{24,0},{1,9},{9,17},{17,25},{25,1},{2,10},{10... | collective-permute-start | bytes 98312 | tf_op jit(solution)/shard_map/ppermute | solution.py:567
  62.9 5.8 %collective-permute-start.4 = (bf16[4,32,128]{2,1,0:T(8,128)(2,1)S(1)}, bf16[4,32,128]{2,1,0:T(8,128)(2,1)S(1)}, u32[]{:S(2)}, u32[]{:S(2)}) collective-permute-start(bf16[4,32,128]{2,1,0:T(8,128)(2,1)S(1)} %get-tuple-element.32), channel_id=1, source_target_pairs={{0,16},{8,24},{16,0},{24,8},{1,17},{9,25},{17,1},{25,9},{2,18},{10... | collective-permute-start | bytes 98312 | tf_op jit(solution)/shard_map/ppermute | solution.py:567
  63.9 4.7 %collective-permute-start.5 = (bf16[4,32,128]{2,1,0:T(8,128)(2,1)S(1)}, bf16[4,32,128]{2,1,0:T(8,128)(2,1)S(1)}, u32[]{:S(2)}, u32[]{:S(2)}) collective-permute-start(bf16[4,32,128]{2,1,0:T(8,128)(2,1)S(1)} %get-tuple-element.33), channel_id=1, source_target_pairs={{0,24},{8,0},{16,8},{24,16},{1,25},{9,1},{17,9},{25,17},{2,26},{10... | collective-permute-start | bytes 98312 | tf_op jit(solution)/shard_map/ppermute | solution.py:567
  69.9 16.2 %all-to-all-start.3 = ((bf16[8,5,32,128]{3,2,1,0:T(8,128)(2,1)}), bf16[8,5,32,128]{3,2,1,0:T(8,128)(2,1)S(1)}, u32[]{:S(2)}, u32[]{:S(2)}) async-start(bf16[8,5,32,128]{3,2,1,0:T(8,128)(2,1)} %get-tuple-element.37), calls=%async_computation.3 | async-start | bytes 655360 | tf_op jit(solution)/shard_map/all_to_all | solution.py:573
  74.7 2.8 %collective-permute-start.14 = (bf16[4,32,128]{2,1,0:T(8,128)(2,1)S(1)}, bf16[4,32,128]{2,1,0:T(8,128)(2,1)S(1)}, u32[]{:S(2)}, u32[]{:S(2)}) collective-permute-start(bf16[4,32,128]{2,1,0:T(8,128)(2,1)S(1)} %get-tuple-element.42.refs_0_), channel_id=1, source_target_pairs={{0,24},{8,0},{16,8},{24,16},{1,25},{9,1},{17,9},{25,17},{2,26},{10... | collective-permute-start | bytes 98312 | tf_op jit(solution)/shard_map/ppermute | solution.py:567
  75.9 3.9 %collective-permute-start.13 = (bf16[4,32,128]{2,1,0:T(8,128)(2,1)S(1)}, bf16[4,32,128]{2,1,0:T(8,128)(2,1)S(1)}, u32[]{:S(2)}, u32[]{:S(2)}) collective-permute-start(bf16[4,32,128]{2,1,0:T(8,128)(2,1)S(1)} %get-tuple-element.42.refs_0_), channel_id=1, source_target_pairs={{0,16},{8,24},{16,0},{24,8},{1,17},{9,25},{17,1},{25,9},{2,18},{10... | collective-permute-start | bytes 98312 | tf_op jit(solution)/shard_map/ppermute | solution.py:567
  77.0 3.3 %collective-permute-start.12 = (bf16[4,32,128]{2,1,0:T(8,128)(2,1)S(1)}, bf16[4,32,128]{2,1,0:T(8,128)(2,1)S(1)}, u32[]{:S(2)}, u32[]{:S(2)}) collective-permute-start(bf16[4,32,128]{2,1,0:T(8,128)(2,1)S(1)} %get-tuple-element.42.refs_0_), channel_id=1, source_target_pairs={{0,8},{8,16},{16,24},{24,0},{1,9},{9,17},{17,25},{25,1},{2,10},{10... | collective-permute-start | bytes 98312 | tf_op jit(solution)/shard_map/ppermute | solution.py:567
  87.3 13.5 %all-to-all-start.4 = ((bf16[8,144,128]{2,1,0:T(8,128)(2,1)}), bf16[8,144,128]{2,1,0:T(8,128)(2,1)S(1)}, u32[]{:S(2)}, u32[]{:S(2)}) async-start(bf16[8,144,128]{2,1,0:T(8,128)(2,1)} %get-tuple-element.43), calls=%async_computation.4 | async-start | bytes 589824 | tf_op jit(solution)/shard_map/all_to_all | solution.py:573
  93.6 8.3 %collective-permute-start.9 = (bf16[4,32,128]{2,1,0:T(8,128)(2,1)S(1)}, bf16[4,32,128]{2,1,0:T(8,128)(2,1)S(1)}, u32[]{:S(2)}, u32[]{:S(2)}) collective-permute-start(bf16[4,32,128]{2,1,0:T(8,128)(2,1)S(1)} %get-tuple-element.39), channel_id=1, source_target_pairs={{0,8},{8,16},{16,24},{24,0},{1,9},{9,17},{17,25},{25,1},{2,10},{10... | collective-permute-start | bytes 98312 | tf_op jit(solution)/shard_map/ppermute | solution.py:567
  94.3 7.9 %collective-permute-start.10 = (bf16[4,32,128]{2,1,0:T(8,128)(2,1)S(1)}, bf16[4,32,128]{2,1,0:T(8,128)(2,1)S(1)}, u32[]{:S(2)}, u32[]{:S(2)}) collective-permute-start(bf16[4,32,128]{2,1,0:T(8,128)(2,1)S(1)} %get-tuple-element.40), channel_id=1, source_target_pairs={{0,16},{8,24},{16,0},{24,8},{1,17},{9,25},{17,1},{25,9},{2,18},{10... | collective-permute-start | bytes 98312 | tf_op jit(solution)/shard_map/ppermute | solution.py:567
  95.3 6.9 %collective-permute-start.11 = (bf16[4,32,128]{2,1,0:T(8,128)(2,1)S(1)}, bf16[4,32,128]{2,1,0:T(8,128)(2,1)S(1)}, u32[]{:S(2)}, u32[]{:S(2)}) collective-permute-start(bf16[4,32,128]{2,1,0:T(8,128)(2,1)S(1)} %get-tuple-element.41), channel_id=1, source_target_pairs={{0,24},{8,0},{16,8},{24,16},{1,25},{9,1},{17,9},{25,17},{2,26},{10... | collective-permute-start | bytes 98312 | tf_op jit(solution)/shard_map/ppermute | solution.py:567
  100.9 1.4 %collective-permute-start.17 = (f32[32,128]{1,0:T(8,128)S(1)}, f32[32,128]{1,0:T(8,128)S(1)}, u32[]{:S(2)}, u32[]{:S(2)}) collective-permute-start(f32[32,128]{1,0:T(8,128)S(1)} %gram_sum.1.refs_4_), channel_id=1, source_target_pairs={{0,24},{8,0},{16,8},{24,16},{1,25},{9,1},{17,9},{25,17},{2,26},{10... | collective-permute-start | bytes 49160 | tf_op jit(solution)/shard_map/ppermute | solution.py:567
  100.9 3.8 %collective-permute-start.16 = (f32[32,128]{1,0:T(8,128)S(1)}, f32[32,128]{1,0:T(8,128)S(1)}, u32[]{:S(2)}, u32[]{:S(2)}) collective-permute-start(f32[32,128]{1,0:T(8,128)S(1)} %gram_sum.1.refs_4_), channel_id=1, source_target_pairs={{0,16},{8,24},{16,0},{24,8},{1,17},{9,25},{17,1},{25,9},{2,18},{10... | collective-permute-start | bytes 49160 | tf_op jit(solution)/shard_map/ppermute | solution.py:567
  102.0 3.2 %collective-permute-start.15 = (f32[32,128]{1,0:T(8,128)S(1)}, f32[32,128]{1,0:T(8,128)S(1)}, u32[]{:S(2)}, u32[]{:S(2)}) collective-permute-start(f32[32,128]{1,0:T(8,128)S(1)} %gram_sum.1.refs_4_), channel_id=1, source_target_pairs={{0,8},{8,16},{16,24},{24,0},{1,9},{9,17},{17,25},{25,1},{2,10},{10... | collective-permute-start | bytes 49160 | tf_op jit(solution)/shard_map/ppermute | solution.py:567

commit v12 on v9

--- a/solution.py
+++ b/solution.py
@@ -240,7 +240,8 @@
 def backward_kernel(row_count, spots_ref, live_ref, block_hbm, *refs):
     places = (spots_ref, live_ref)
     row_pieces = refs[:row_count]
-    col_out_ref, block_ref, sems, row_dir_ref, even_ref, odd_ref = refs[row_count:]
+    terms_refs = refs[row_count:-6]
+    col_out_ref, block_ref, sems, row_dir_ref, even_ref, odd_ref = refs[-6:]
     per_seg = row_pieces[0].shape[0]
     col_blocks = even_ref.shape[0]
 
@@ -267,6 +268,8 @@
             col_out_ref[segment, part * size : part * size + size] = values.astype(
                 col_out_ref.dtype
             )
+        for terms_ref in terms_refs:
+            col_out_ref[segment, per_seg * size :] = terms_ref[...]
 
 
 def in_terms(values, count):
@@ -284,7 +287,7 @@
     return total.astype(jnp.bfloat16)
 
 
-def attach_kernel(first_dir_ref, col_dir_ref, total_ref, message_ref, gram_ref):
+def attach_kernel(first_col_ref, col_dir_ref, total_ref, message_ref, gram_ref):
     col_count, sent, size, _ = col_dir_ref.shape
     per_seg = sent - 1
 
@@ -297,14 +300,14 @@
         return gram
 
     gram = lax.fori_loop(
-        0, col_count, add_segment, jnp.zeros((size, 128), jnp.float32), unroll=4
+        0, col_count, add_segment, jnp.zeros((size, 128), jnp.float32), unroll=8
     )
     half = size // 2
     terms = side_by_side(in_terms(gram, 2)).astype(jnp.float32)
     folded = terms[:half] + pltpu.roll(terms[half:], 64, 1)
     for segment in range(col_count):
         message_ref[segment, per_seg * size :] = folded.astype(message_ref.dtype)
-    queries = total_of([first_dir_ref[segment, per_seg] for segment in range(col_count)])
+    queries = total_of([first_col_ref[segment, per_seg * size :] for segment in range(col_count)])
     queries = total_of([window(queries, term) for term in range(3)])
     pairs = total_of([col_dir_ref[segment, per_seg] for segment in range(col_count)])
     lanes = lax.broadcasted_iota(jnp.int32, pairs.shape, 1)
@@ -359,16 +362,17 @@
     )(*places, blocks, *inputs)
 
 
-def backward_product(places, blocks, row_pieces, col_count):
+def backward_product(places, blocks, row_pieces, col_count, *terms):
     per_seg, rows, lanes = row_pieces[0].shape
+    sent = per_seg + len(terms)
     col_shape = (col_count * per_seg, rows, lanes)
     (total,) = over_blocks(
         functools.partial(backward_kernel, len(row_pieces)),
         "backward_product",
         places,
         blocks,
-        row_pieces,
-        [jax.ShapeDtypeStruct((col_count, per_seg * rows, lanes), jnp.bfloat16)],
+        [*row_pieces, *terms],
+        [jax.ShapeDtypeStruct((col_count, sent * rows, lanes), jnp.bfloat16)],
         [
             pltpu.VMEM((len(row_pieces) * per_seg, rows, lanes), jnp.bfloat16),
             pltpu.VMEM(col_shape, jnp.float32),
@@ -407,18 +411,19 @@
     degree = 1.0 + 0.5 * total_of([ref[...] for ref in [*row_refs, *leading(col_ref)]])
     scaling = 1.0 / jnp.sqrt(degree)
     scaling_ref[...] = scaling
-    per_seg, size, _ = scaled_ref.shape
-    gram = jnp.zeros((size, 128), jnp.float32)
-    for part in range(per_seg):
+    for part in range(scaled_ref.shape[0]):
         query = query_ref[:, part * 128 : part * 128 + 128]
         scaled = (scaling[part : part + 1] * query).astype(jnp.bfloat16)
         scaled_ref[part] = scaled
         for copy in range(copies_ref.shape[0]):
             copies_ref[copy, part] = scaled
-        gram += exact_across(query, tall(query))
-    terms = side_by_side(in_terms(gram, 3))
-    for copy in range(copies_ref.shape[0]):
-        copies_ref[copy, per_seg] = terms
+
+
+def query_gram_kernel(query_ref, terms_ref):
+    queries = query_ref[...]
+    rest = jnp.zeros((128 - queries.shape[0], queries.shape[1]), queries.dtype)
+    gram = exact_across(queries, jnp.concatenate([queries, rest], axis=0))
+    terms_ref[...] = side_by_side(in_terms(gram, 3))
 
 
 def scaled_sum(row_refs, col_ref, scaling_ref, part):
@@ -433,7 +438,7 @@
     *row_refs, col_ref, scaling_ref, query_ref, first_ref, scaled_ref, copies_ref = refs
     size = query_ref.shape[0]
     per_seg = scaling_ref.shape[0]
-    grams = jnp.zeros((size, 128), jnp.float32)
+    firsts = []
     for part in range(per_seg):
         first = scaled_sum(row_refs, col_ref, scaling_ref, part)
         first_ref[part] = first
@@ -441,8 +446,10 @@
         scaled_ref[part] = scaled
         for copy in range(copies_ref.shape[0]):
             copies_ref[copy, part] = scaled
-        query = query_ref[:, part * 128 : part * 128 + 128]
-        grams += exact_across(first, stacked(query, first))
+        firsts.append(first)
+    first = jnp.concatenate(firsts, axis=1)
+    rest = jnp.zeros((128 - 2 * size, first.shape[1]), first.dtype)
+    grams = exact_across(first, jnp.concatenate([query_ref[...], first, rest], axis=0))
     terms = side_by_side(in_terms(grams, 2), 2 * size)
     for copy in range(copies_ref.shape[0]):
         copies_ref[copy, per_seg] = terms
@@ -612,7 +619,11 @@
     row_parts = pass_around([None, *row_sums], "row")[1:]
     scaling, scaled, copies = simple_call(
         start_kernel,
-        [jax.ShapeDtypeStruct((per_seg, 128), jnp.float32), narrow, message],
+        [
+            jax.ShapeDtypeStruct((per_seg, 128), jnp.float32),
+            narrow,
+            jax.ShapeDtypeStruct((col_count,) + piece, jnp.bfloat16),
+        ],
         "start",
         *row_parts,
         col_part,
@@ -621,15 +632,21 @@
 
     first_dirs = exchange(copies, "col")
     row_pieces = pass_around([scaled] * row_count, "row")
-    total = backward_product(places, flipped_blocks, row_pieces, col_count)
-    col_part = exchange(total, "col")
+    (terms,) = simple_call(
+        query_gram_kernel,
+        [jax.ShapeDtypeStruct((query_rows, 128), jnp.bfloat16)],
+        "query_gram",
+        queries,
+    )
+    total = backward_product(places, flipped_blocks, row_pieces, col_count, terms)
+    first_part = exchange(total, "col")
     totals = forward_product(places, blocks, first_dirs, row_count, piece)
     first, scaled, copies = simple_call(
         middle_kernel,
         [wide, narrow, message],
         "middle",
         *pass_around(totals, "row"),
-        col_part,
+        first_part,
         scaling,
         queries,
     )
@@ -641,7 +658,7 @@
         (col_count, total.shape[1] + query_rows // 2, 128), jnp.bfloat16
     )
     total, gram = simple_call(
-        attach_kernel, [more, gram_shape], "attach", first_dirs, col_dirs, total
+        attach_kernel, [more, gram_shape], "attach", first_part, col_dirs, total
     )
     col_part = exchange(total, "col")
     totals = forward_product(places, blocks, col_dirs, row_count, piece)

time: 110 us -> 107 us (0.973)
  Pallas kernels: 36.2 us -> 28.1 us
  waiting for transfers between devices: 18.5 us -> 21 us
  starting transfers between devices: 53.3 us -> 54.7 us
    all_to_all x5, starting transfers between devices: 26 us -> 33 us  [exchange(): return lax.all_to_all(pieces, axis, 0, 0, tiled=True)]
    ppermute x18, starting transfers between devices: 27.2 us -> 21.7 us  [pass_around(): lax.ppermute(pieces[ahead], axis, [(at, (at + ahead) % count) for at in r...]
    pallas_call x1, Pallas kernels: 13.3 us -> 8.55 us  [build_blocks(): pl.pallas_call(build_kernel, in_specs=[SCALARS, SCALARS, ANYWHERE, ANYWHE...]
    pallas_call x4, Pallas kernels: 14.6 us -> 11.5 us  [over_blocks(): pl.pallas_call(kernel, in_specs=[SCALARS, SCALARS, ANYWHERE] + [IN_VMEM]...]
    all_to_all x5, waiting for transfers between devices: 6.21 us -> 8.98 us  [exchange(): return lax.all_to_all(pieces, axis, 0, 0, tiled=True)]
    unnamed x8 -> x10, local copies, waits for them, and re-layouts: 1.53 us -> 2.37 us
    pallas_call x5 -> x6, Pallas kernels: 8.28 us -> 8.07 us  [simple_call(): pl.pallas_call(kernel, out_shape=shapes, compiler_params=pltpu.CompilerPa...]
  transfers between devices with their start and end apart: 23 -> 23, of which waited for: 13 -> 16; matrix products, arithmetic and copies ran while one was open for 0% -> 0% of each run, Pallas kernels for 13% -> 11%
where the time goes in v12:
time: 107 us; the launch traced here: 108 us
  starting transfers between devices  54.7 us (51%)
  Pallas kernels  28.1 us (26%)
  waiting for transfers between devices  21 us (20%)
  local copies, waits for them, and re-layouts  2.37 us (2%)
  between operations  1.39 us (1%)
    all_to_all x5, starting transfers between devices, exchange(): return lax.all_to_all(pieces, axis, 0, 0, tiled=True)  33 us
    ppermute x18, starting transfers between devices, pass_around(): lax.ppermute(pieces[ahead], axis, [(at, (at + ahead) % count) for at in r...  21.7 us
    ppermute x18, waiting for transfers between devices, pass_around(): lax.ppermute(pieces[ahead], axis, [(at, (at + ahead) % count) for at in r...  12 us
    pallas_call x4, Pallas kernels, over_blocks(): pl.pallas_call(kernel, in_specs=[SCALARS, SCALARS, ANYWHERE] + [IN_VMEM]...  11.5 us
    all_to_all x5, waiting for transfers between devices, exchange(): return lax.all_to_all(pieces, axis, 0, 0, tiled=True)  8.98 us
    pallas_call x1, Pallas kernels, build_blocks(): pl.pallas_call(build_kernel, in_specs=[SCALARS, SCALARS, ANYWHERE, ANYWHE...  8.55 us
    pallas_call x6, Pallas kernels, simple_call(): pl.pallas_call(kernel, out_shape=shapes, compiler_params=pltpu.CompilerPa...  8.07 us
    unnamed x10, local copies, waits for them, and re-layouts  2.37 us
  transfers between devices with their start and end apart: 23, of which 16 were waited for; matrix products, arithmetic and copies ran while one was open for 0% of the time, Pallas kernels for 11%

profile of v12, /device:TPU:0, one launch (start us, length us, event | category | flops | bytes accessed | tf_op | source)
XLA Modules:
  0.0 107.6 jit_solution(15967737377697551686)
XLA Ops:
  1.3 8.6 %build_blocks.1 = (bf16[1024,128,128]{2,1,0:T(8,128)(2,1)}, bf16[1024,128,128]{2,1,0:T(8,128)(2,1)}, f32[4,128]{1,0:T(4,128)}, f32[4,128]{1,0:T(4,128)}, f32[4,128]{1,0:T(4,128)}, /*index=5*/f32[32,128]{1,0:T(8,128)}) custom-call(s32[1,1,256]{2,1,0:T(1,128)} %spots_ref.9, s32[1,1]{1,0:T(1,128)S(6)} %copy.7.live_ref, s32[256,16,128]{2,1,0:T(8,128)} %bitcast.3, ...), custom_call_target="tpu_custom_call" | custom-call | tf_op jit(solution)/shard_map/build_blocks/pallas_call | solution.py:182
  9.9 12.1 %all-to-all-start = ((f32[8,4,128]{2,1,0:T(4,128)}), f32[8,4,128]{2,1,0:T(4,128)S(1)}, u32[]{:S(2)}, u32[]{:S(2)}) async-start(f32[8,4,128]{2,1,0:T(4,128)} %bitcast.5), calls=%async_computation | async-start | bytes 32768 | tf_op jit(solution)/shard_map/all_to_all | solution.py:575
  22.0 9.2 %collective-permute-start.1 = (f32[4,128]{1,0:T(4,128)}, f32[4,128]{1,0:T(4,128)S(1)}, u32[]{:S(2)}, u32[]{:S(2)}) collective-permute-start(f32[4,128]{1,0:T(4,128)} %get-tuple-element.26), channel_id=1, source_target_pairs={{0,16},{8,24},{16,0},{24,8},{1,17},{9,25},{17,1},{25,9},{2,18},{10... | collective-permute-start | bytes 6152 | tf_op jit(solution)/shard_map/ppermute | solution.py:569
  31.1 1.4 %collective-permute-start.2 = (f32[4,128]{1,0:T(4,128)}, f32[4,128]{1,0:T(4,128)S(1)}, u32[]{:S(2)}, u32[]{:S(2)}) collective-permute-start(f32[4,128]{1,0:T(4,128)} %get-tuple-element.27), channel_id=1, source_target_pairs={{0,24},{8,0},{16,8},{24,16},{1,25},{9,1},{17,9},{25,17},{2,26},{10... | collective-permute-start | bytes 6152 | tf_op jit(solution)/shard_map/ppermute | solution.py:569
  32.9 1.1 %collective-permute-done.2.refs_2_ = f32[4,128]{1,0:T(4,128)S(1)} collective-permute-done((f32[4,128]{1,0:T(4,128)}, f32[4,128]{1,0:T(4,128)S(1)}, u32[]{:S(2)}, u32[]{:S(2)}) %collective-permute-start.2) | collective-permute-done | bytes 2080 | tf_op jit(solution)/shard_map/ppermute | solution.py:569
  34.0 0.8 copy-done
  35.6 6.0 %all-to-all-start.1 = ((bf16[8,4,32,128]{3,2,1,0:T(8,128)(2,1)}), bf16[8,4,32,128]{3,2,1,0:T(8,128)(2,1)S(1)}, u32[]{:S(2)}, u32[]{:S(2)}) async-start(bf16[8,4,32,128]{3,2,1,0:T(8,128)(2,1)} %get-tuple-element.29), calls=%async_computation.1 | async-start | bytes 524288 | tf_op jit(solution)/shard_map/all_to_all | solution.py:575
  41.7 1.4 %collective-permute-start.8 = (bf16[4,32,128]{2,1,0:T(8,128)(2,1)S(1)}, bf16[4,32,128]{2,1,0:T(8,128)(2,1)S(1)}, u32[]{:S(2)}, u32[]{:S(2)}) collective-permute-start(bf16[4,32,128]{2,1,0:T(8,128)(2,1)S(1)} %get-tuple-element.35.refs_0_), channel_id=1, source_target_pairs={{0,24},{8,0},{16,8},{24,16},{1,25},{9,1},{17,9},{25,17},{2,26},{10... | collective-permute-start | bytes 98312 | tf_op jit(solution)/shard_map/ppermute | solution.py:569
  43.4 0.8 copy-done.1
  44.7 2.4 %collective-permute-done.7.refs_2_ = bf16[4,32,128]{2,1,0:T(8,128)(2,1)S(1)} collective-permute-done((bf16[4,32,128]{2,1,0:T(8,128)(2,1)S(1)}, bf16[4,32,128]{2,1,0:T(8,128)(2,1)S(1)}, u32[]{:S(2)}, u32[]{:S(2)}) %collective-permute-start.7) | collective-permute-done | bytes 32800 | tf_op jit(solution)/shard_map/ppermute | solution.py:569
  47.8 3.4 %backward_product.2 = bf16[8,160,128]{2,1,0:T(8,128)(2,1)} custom-call(s32[1,1,256]{2,1,0:T(1,128)S(1)} %copy-done.3, s32[1,1]{1,0:T(1,128)S(6)} %copy.7.live_ref, bf16[1024,128,128]{2,1,0:T(8,128)(2,1)} %get-tuple-element.34.block_hbm, bf16[4,32,128]{2,1,0:T(8,128)(2,1)S(1)} %get-tuple-element.35.refs_0_, ...), custom_call_target="tpu_custom_call" | custom-call | flops 268435456 | bytes 8388608 | tf_op jit(solution)/shard_map/backward_product/pallas_call | solution.py:347
  51.2 6.5 %all-to-all-start.2 = ((bf16[8,160,128]{2,1,0:T(8,128)(2,1)}), bf16[8,160,128]{2,1,0:T(8,128)(2,1)S(1)}, u32[]{:S(2)}, u32[]{:S(2)}) async-start(bf16[8,160,128]{2,1,0:T(8,128)(2,1)} %backward_product.2), calls=%async_computation.2 | async-start | bytes 655360 | tf_op jit(solution)/shard_map/all_to_all | solution.py:575
  57.7 2.7 %forward_product.2 = (bf16[4,32,128]{2,1,0:T(8,128)(2,1)S(1)}, bf16[4,32,128]{2,1,0:T(8,128)(2,1)S(1)}, bf16[4,32,128]{2,1,0:T(8,128)(2,1)S(1)}, bf16[4,32,128]{2,1,0:T(8,128)(2,1)S(1)}) custom-call(s32[1,1,256]{2,1,0:T(1,128)S(1)} %copy-done.4, s32[1,1]{1,0:T(1,128)S(6)} %copy.7.live_ref, bf16[1024,128,128]{2,1,0:T(8,128)(2,1)} %get-tuple-element.24.block_hbm, ...), custom_call_target="tpu_custom_call" | custom-call | flops 268435456 | bytes 8388608 | tf_op jit(solution)/shard_map/forward_product/pallas_call | solution.py:347
  60.5 1.6 %collective-permute-start.4 = (bf16[4,32,128]{2,1,0:T(8,128)(2,1)S(1)}, bf16[4,32,128]{2,1,0:T(8,128)(2,1)S(1)}, u32[]{:S(2)}, u32[]{:S(2)}) collective-permute-start(bf16[4,32,128]{2,1,0:T(8,128)(2,1)S(1)} %get-tuple-element.32), channel_id=1, source_target_pairs={{0,16},{8,24},{16,0},{24,8},{1,17},{9,25},{17,1},{25,9},{2,18},{10... | collective-permute-start | bytes 98312 | tf_op jit(solution)/shard_map/ppermute | solution.py:569
  62.1 1.4 %collective-permute-start.5 = (bf16[4,32,128]{2,1,0:T(8,128)(2,1)S(1)}, bf16[4,32,128]{2,1,0:T(8,128)(2,1)S(1)}, u32[]{:S(2)}, u32[]{:S(2)}) collective-permute-start(bf16[4,32,128]{2,1,0:T(8,128)(2,1)S(1)} %get-tuple-element.33), channel_id=1, source_target_pairs={{0,24},{8,0},{16,8},{24,16},{1,25},{9,1},{17,9},{25,17},{2,26},{10... | collective-permute-start | bytes 98312 | tf_op jit(solution)/shard_map/ppermute | solution.py:569
  65.1 1.6 %all-to-all-done.2.refs_4_.first_col_ref = bf16[8,160,128]{2,1,0:T(8,128)(2,1)S(1)} async-done(((bf16[8,160,128]{2,1,0:T(8,128)(2,1)}), bf16[8,160,128]{2,1,0:T(8,128)(2,1)S(1)}, u32[]{:S(2)}, u32[]{:S(2)}) %all-to-all-start.2) | async-done | bytes 327712 | tf_op jit(solution)/shard_map/all_to_all | solution.py:575
  66.7 1.1 %middle.1 = (f32[4,32,128]{2,1,0:T(8,128)S(1)}, bf16[4,32,128]{2,1,0:T(8,128)(2,1)S(1)}, bf16[8,5,32,128]{3,2,1,0:T(8,128)(2,1)}) custom-call(bf16[4,32,128]{2,1,0:T(8,128)(2,1)S(1)} %get-tuple-element.30.refs_0_, bf16[4,32,128]{2,1,0:T(8,128)(2,1)S(1)} %collective-permute-done.3.refs_1_, bf16[4,32,128]{2,1,0:T(8,128)(2,1)S(1)} %collective-permute-done.4.refs_2_, ...), custom_call_target="tpu_custom_call" | custom-call | tf_op jit(solution)/shard_map/middle/pallas_call | solution.py:579
  67.8 4.8 %all-to-all-start.3 = ((bf16[8,5,32,128]{3,2,1,0:T(8,128)(2,1)}), bf16[8,5,32,128]{3,2,1,0:T(8,128)(2,1)S(1)}, u32[]{:S(2)}, u32[]{:S(2)}) async-start(bf16[8,5,32,128]{3,2,1,0:T(8,128)(2,1)} %get-tuple-element.37), calls=%async_computation.3 | async-start | bytes 655360 | tf_op jit(solution)/shard_map/all_to_all | solution.py:575
  72.5 1.3 %collective-permute-start.14 = (bf16[4,32,128]{2,1,0:T(8,128)(2,1)S(1)}, bf16[4,32,128]{2,1,0:T(8,128)(2,1)S(1)}, u32[]{:S(2)}, u32[]{:S(2)}) collective-permute-start(bf16[4,32,128]{2,1,0:T(8,128)(2,1)S(1)} %get-tuple-element.42.refs_0_), channel_id=1, source_target_pairs={{0,24},{8,0},{16,8},{24,16},{1,25},{9,1},{17,9},{25,17},{2,26},{10... | collective-permute-start | bytes 98312 | tf_op jit(solution)/shard_map/ppermute | solution.py:569
  73.8 1.1 %collective-permute-start.13 = (bf16[4,32,128]{2,1,0:T(8,128)(2,1)S(1)}, bf16[4,32,128]{2,1,0:T(8,128)(2,1)S(1)}, u32[]{:S(2)}, u32[]{:S(2)}) collective-permute-start(bf16[4,32,128]{2,1,0:T(8,128)(2,1)S(1)} %get-tuple-element.42.refs_0_), channel_id=1, source_target_pairs={{0,16},{8,24},{16,0},{24,8},{1,17},{9,25},{17,1},{25,9},{2,18},{10... | collective-permute-start | bytes 98312 | tf_op jit(solution)/shard_map/ppermute | solution.py:569
  75.4 2.3 %collective-permute-done.13.refs_2_ = bf16[4,32,128]{2,1,0:T(8,128)(2,1)S(1)} collective-permute-done((bf16[4,32,128]{2,1,0:T(8,128)(2,1)S(1)}, bf16[4,32,128]{2,1,0:T(8,128)(2,1)S(1)}, u32[]{:S(2)}, u32[]{:S(2)}) %collective-permute-start.13) | collective-permute-done | bytes 32800 | tf_op jit(solution)/shard_map/ppermute | solution.py:569
  78.2 2.7 %backward_product.3.total_ref = bf16[8,128,128]{2,1,0:T(8,128)(2,1)S(1)} custom-call(s32[1,1,256]{2,1,0:T(1,128)S(1)} %copy-done.4, s32[1,1]{1,0:T(1,128)S(6)} %copy.7.live_ref, bf16[1024,128,128]{2,1,0:T(8,128)(2,1)} %get-tuple-element.34.block_hbm, bf16[4,32,128]{2,1,0:T(8,128)(2,1)S(1)} %get-tuple-element.42.refs_0_, ...), custom_call_target="tpu_custom_call" | custom-call | flops 268435456 | bytes 8388608 | tf_op jit(solution)/shard_map/backward_product/pallas_call | solution.py:347
  80.9 3.0 %all-to-all-done.3.col_dir_ref = bf16[8,5,32,128]{3,2,1,0:T(8,128)(2,1)S(1)} async-done(((bf16[8,5,32,128]{3,2,1,0:T(8,128)(2,1)}), bf16[8,5,32,128]{3,2,1,0:T(8,128)(2,1)S(1)}, u32[]{:S(2)}, u32[]{:S(2)}) %all-to-all-start.3) | async-done | bytes 327712 | tf_op jit(solution)/shard_map/all_to_all | solution.py:575
  84.0 1.1 %attach.1 = (bf16[8,144,128]{2,1,0:T(8,128)(2,1)}, f32[32,128]{1,0:T(8,128)S(1)}) custom-call(bf16[8,160,128]{2,1,0:T(8,128)(2,1)S(1)} %all-to-all-done.2.refs_4_.first_col_ref, bf16[8,5,32,128]{3,2,1,0:T(8,128)(2,1)S(1)} %all-to-all-done.3.col_dir_ref, bf16[8,128,128]{2,1,0:T(8,128)(2,1)S(1)} %backward_product.3.total_ref), custom_call_target="tpu_custom_call" | custom-call | tf_op jit(solution)/shard_map/attach/pallas_call | solution.py:579
  85.1 3.6 %all-to-all-start.4 = ((bf16[8,144,128]{2,1,0:T(8,128)(2,1)}), bf16[8,144,128]{2,1,0:T(8,128)(2,1)S(1)}, u32[]{:S(2)}, u32[]{:S(2)}) async-start(bf16[8,144,128]{2,1,0:T(8,128)(2,1)} %get-tuple-element.43), calls=%async_computation.4 | async-start | bytes 589824 | tf_op jit(solution)/shard_map/all_to_all | solution.py:575
  88.8 2.7 %forward_product.3 = (bf16[4,32,128]{2,1,0:T(8,128)(2,1)S(1)}, bf16[4,32,128]{2,1,0:T(8,128)(2,1)S(1)}, bf16[4,32,128]{2,1,0:T(8,128)(2,1)S(1)}, bf16[4,32,128]{2,1,0:T(8,128)(2,1)S(1)}) custom-call(s32[1,1,256]{2,1,0:T(1,128)S(1)} %copy-done.4, s32[1,1]{1,0:T(1,128)S(6)} %copy.7.live_ref, bf16[1024,128,128]{2,1,0:T(8,128)(2,1)} %get-tuple-element.24.block_hbm, ...), custom_call_target="tpu_custom_call" | custom-call | flops 268435456 | bytes 8388608 | tf_op jit(solution)/shard_map/forward_product/pallas_call | solution.py:347
  92.1 0.8 collective-permute-start.10
  92.9 1.4 %collective-permute-start.11 = (bf16[4,32,128]{2,1,0:T(8,128)(2,1)S(1)}, bf16[4,32,128]{2,1,0:T(8,128)(2,1)S(1)}, u32[]{:S(2)}, u32[]{:S(2)}) collective-permute-start(bf16[4,32,128]{2,1,0:T(8,128)(2,1)S(1)} %get-tuple-element.41), channel_id=1, source_target_pairs={{0,24},{8,0},{16,8},{24,16},{1,25},{9,1},{17,9},{25,17},{2,26},{10... | collective-permute-start | bytes 98312 | tf_op jit(solution)/shard_map/ppermute | solution.py:569
  94.3 4.3 %all-to-all-done.4.col_ref.refs_8_ = bf16[8,144,128]{2,1,0:T(8,128)(2,1)S(1)} async-done(((bf16[8,144,128]{2,1,0:T(8,128)(2,1)}), bf16[8,144,128]{2,1,0:T(8,128)(2,1)S(1)}, u32[]{:S(2)}, u32[]{:S(2)}) %all-to-all-start.4) | async-done | bytes 294944 | tf_op jit(solution)/shard_map/all_to_all | solution.py:575
  98.7 1.0 collective-permute-start.16
  100.2 2.4 %collective-permute-done.16.refs_6_ = f32[32,128]{1,0:T(8,128)S(1)} collective-permute-done((f32[32,128]{1,0:T(8,128)S(1)}, f32[32,128]{1,0:T(8,128)S(1)}, u32[]{:S(2)}, u32[]{:S(2)}) %collective-permute-start.16) | collective-permute-done | bytes 16416 | tf_op jit(solution)/shard_map/ppermute | solution.py:569
  102.9 4.7 %close.1 = (f32[32,512]{1,0:T(8,128)}, f32[32,512]{1,0:T(8,128)}) custom-call(bf16[4,32,128]{2,1,0:T(8,128)(2,1)S(1)} %get-tuple-element.38.refs_0_, bf16[4,32,128]{2,1,0:T(8,128)(2,1)S(1)} %collective-permute-done.9.refs_1_, bf16[4,32,128]{2,1,0:T(8,128)(2,1)S(1)} %collective-permute-done.10.refs_2_, ...), custom_call_target="tpu_custom_call" | custom-call | tf_op jit(solution)/shard_map/close/pallas_call | solution.py:579
  (35 shorter events, 6.9 us)
Async XLA Ops:
  0.6 57.1 %copy-start.4 = (s32[1,1,256]{2,1,0:T(1,128)S(1)}, s32[1,1,256]{2,1,0:T(1,128)}, u32[]{:S(2)}) copy-start(s32[1,1,256]{2,1,0:T(1,128)} %spots_ref.9) | copy-start | bytes 3076
  9.9 24.2 %all-to-all-start = ((f32[8,4,128]{2,1,0:T(4,128)}), f32[8,4,128]{2,1,0:T(4,128)S(1)}, u32[]{:S(2)}, u32[]{:S(2)}) async-start(f32[8,4,128]{2,1,0:T(4,128)} %bitcast.5), calls=%async_computation | async-start | bytes 32768 | tf_op jit(solution)/shard_map/all_to_all | solution.py:575
  21.9 10.6 %collective-permute-start = (f32[4,128]{1,0:T(4,128)}, f32[4,128]{1,0:T(4,128)S(1)}, u32[]{:S(2)}, u32[]{:S(2)}) collective-permute-start(f32[4,128]{1,0:T(4,128)} %get-tuple-element.25), channel_id=1, source_target_pairs={{0,8},{8,16},{16,24},{24,0},{1,9},{9,17},{17,25},{25,1},{2,10},{10... | collective-permute-start | bytes 6152 | tf_op jit(solution)/shard_map/ppermute | solution.py:569
  22.0 11.0 %collective-permute-start.1 = (f32[4,128]{1,0:T(4,128)}, f32[4,128]{1,0:T(4,128)S(1)}, u32[]{:S(2)}, u32[]{:S(2)}) collective-permute-start(f32[4,128]{1,0:T(4,128)} %get-tuple-element.26), channel_id=1, source_target_pairs={{0,16},{8,24},{16,0},{24,8},{1,17},{9,25},{17,1},{25,9},{2,18},{10... | collective-permute-start | bytes 6152 | tf_op jit(solution)/shard_map/ppermute | solution.py:569
  31.1 2.9 %collective-permute-start.2 = (f32[4,128]{1,0:T(4,128)}, f32[4,128]{1,0:T(4,128)S(1)}, u32[]{:S(2)}, u32[]{:S(2)}) collective-permute-start(f32[4,128]{1,0:T(4,128)} %get-tuple-element.27), channel_id=1, source_target_pairs={{0,24},{8,0},{16,8},{24,16},{1,25},{9,1},{17,9},{25,17},{2,26},{10... | collective-permute-start | bytes 6152 | tf_op jit(solution)/shard_map/ppermute | solution.py:569
  34.0 0.8 copy-start
  35.6 15.6 %all-to-all-start.1 = ((bf16[8,4,32,128]{3,2,1,0:T(8,128)(2,1)}), bf16[8,4,32,128]{3,2,1,0:T(8,128)(2,1)S(1)}, u32[]{:S(2)}, u32[]{:S(2)}) async-start(bf16[8,4,32,128]{3,2,1,0:T(8,128)(2,1)} %get-tuple-element.29), calls=%async_computation.1 | async-start | bytes 524288 | tf_op jit(solution)/shard_map/all_to_all | solution.py:575
  41.7 3.0 %collective-permute-start.8 = (bf16[4,32,128]{2,1,0:T(8,128)(2,1)S(1)}, bf16[4,32,128]{2,1,0:T(8,128)(2,1)S(1)}, u32[]{:S(2)}, u32[]{:S(2)}) collective-permute-start(bf16[4,32,128]{2,1,0:T(8,128)(2,1)S(1)} %get-tuple-element.35.refs_0_), channel_id=1, source_target_pairs={{0,24},{8,0},{16,8},{24,16},{1,25},{9,1},{17,9},{25,17},{2,26},{10... | collective-permute-start | bytes 98312 | tf_op jit(solution)/shard_map/ppermute | solution.py:569
  43.1 4.0 %collective-permute-start.7 = (bf16[4,32,128]{2,1,0:T(8,128)(2,1)S(1)}, bf16[4,32,128]{2,1,0:T(8,128)(2,1)S(1)}, u32[]{:S(2)}, u32[]{:S(2)}) collective-permute-start(bf16[4,32,128]{2,1,0:T(8,128)(2,1)S(1)} %get-tuple-element.35.refs_0_), channel_id=1, source_target_pairs={{0,16},{8,24},{16,0},{24,8},{1,17},{9,25},{17,1},{25,9},{2,18},{10... | collective-permute-start | bytes 98312 | tf_op jit(solution)/shard_map/ppermute | solution.py:569
  43.4 3.7 %collective-permute-start.6 = (bf16[4,32,128]{2,1,0:T(8,128)(2,1)S(1)}, bf16[4,32,128]{2,1,0:T(8,128)(2,1)S(1)}, u32[]{:S(2)}, u32[]{:S(2)}) collective-permute-start(bf16[4,32,128]{2,1,0:T(8,128)(2,1)S(1)} %get-tuple-element.35.refs_0_), channel_id=1, source_target_pairs={{0,8},{8,16},{16,24},{24,0},{1,9},{9,17},{17,25},{25,1},{2,10},{10... | collective-permute-start | bytes 98312 | tf_op jit(solution)/shard_map/ppermute | solution.py:569
  43.4 0.8 copy-start.1
  47.1 0.7 copy-start.3
  47.8 18.9 %copy-start.2 = (f32[32,512]{1,0:T(8,128)S(1)}, f32[32,512]{1,0:T(8,128)}, u32[]{:S(2)}) copy-start(f32[32,512]{1,0:T(8,128)} %refs_10_.1) | copy-start | bytes 196612
  51.2 15.5 %all-to-all-start.2 = ((bf16[8,160,128]{2,1,0:T(8,128)(2,1)}), bf16[8,160,128]{2,1,0:T(8,128)(2,1)S(1)}, u32[]{:S(2)}, u32[]{:S(2)}) async-start(bf16[8,160,128]{2,1,0:T(8,128)(2,1)} %backward_product.2), calls=%async_computation.2 | async-start | bytes 655360 | tf_op jit(solution)/shard_map/all_to_all | solution.py:575
  60.4 3.4 %collective-permute-start.3 = (bf16[4,32,128]{2,1,0:T(8,128)(2,1)S(1)}, bf16[4,32,128]{2,1,0:T(8,128)(2,1)S(1)}, u32[]{:S(2)}, u32[]{:S(2)}) collective-permute-start(bf16[4,32,128]{2,1,0:T(8,128)(2,1)S(1)} %get-tuple-element.31), channel_id=1, source_target_pairs={{0,8},{8,16},{16,24},{24,0},{1,9},{9,17},{17,25},{25,1},{2,10},{10... | collective-permute-start | bytes 98312 | tf_op jit(solution)/shard_map/ppermute | solution.py:569
  60.5 4.0 %collective-permute-start.4 = (bf16[4,32,128]{2,1,0:T(8,128)(2,1)S(1)}, bf16[4,32,128]{2,1,0:T(8,128)(2,1)S(1)}, u32[]{:S(2)}, u32[]{:S(2)}) collective-permute-start(bf16[4,32,128]{2,1,0:T(8,128)(2,1)S(1)} %get-tuple-element.32), channel_id=1, source_target_pairs={{0,16},{8,24},{16,0},{24,8},{1,17},{9,25},{17,1},{25,9},{2,18},{10... | collective-permute-start | bytes 98312 | tf_op jit(solution)/shard_map/ppermute | solution.py:569
  62.1 3.0 %collective-permute-start.5 = (bf16[4,32,128]{2,1,0:T(8,128)(2,1)S(1)}, bf16[4,32,128]{2,1,0:T(8,128)(2,1)S(1)}, u32[]{:S(2)}, u32[]{:S(2)}) collective-permute-start(bf16[4,32,128]{2,1,0:T(8,128)(2,1)S(1)} %get-tuple-element.33), channel_id=1, source_target_pairs={{0,24},{8,0},{16,8},{24,16},{1,25},{9,1},{17,9},{25,17},{2,26},{10... | collective-permute-start | bytes 98312 | tf_op jit(solution)/shard_map/ppermute | solution.py:569
  67.8 16.2 %all-to-all-start.3 = ((bf16[8,5,32,128]{3,2,1,0:T(8,128)(2,1)}), bf16[8,5,32,128]{3,2,1,0:T(8,128)(2,1)S(1)}, u32[]{:S(2)}, u32[]{:S(2)}) async-start(bf16[8,5,32,128]{3,2,1,0:T(8,128)(2,1)} %get-tuple-element.37), calls=%async_computation.3 | async-start | bytes 655360 | tf_op jit(solution)/shard_map/all_to_all | solution.py:575
  72.5 2.9 %collective-permute-start.14 = (bf16[4,32,128]{2,1,0:T(8,128)(2,1)S(1)}, bf16[4,32,128]{2,1,0:T(8,128)(2,1)S(1)}, u32[]{:S(2)}, u32[]{:S(2)}) collective-permute-start(bf16[4,32,128]{2,1,0:T(8,128)(2,1)S(1)} %get-tuple-element.42.refs_0_), channel_id=1, source_target_pairs={{0,24},{8,0},{16,8},{24,16},{1,25},{9,1},{17,9},{25,17},{2,26},{10... | collective-permute-start | bytes 98312 | tf_op jit(solution)/shard_map/ppermute | solution.py:569
  73.8 3.9 %collective-permute-start.13 = (bf16[4,32,128]{2,1,0:T(8,128)(2,1)S(1)}, bf16[4,32,128]{2,1,0:T(8,128)(2,1)S(1)}, u32[]{:S(2)}, u32[]{:S(2)}) collective-permute-start(bf16[4,32,128]{2,1,0:T(8,128)(2,1)S(1)} %get-tuple-element.42.refs_0_), channel_id=1, source_target_pairs={{0,16},{8,24},{16,0},{24,8},{1,17},{9,25},{17,1},{25,9},{2,18},{10... | collective-permute-start | bytes 98312 | tf_op jit(solution)/shard_map/ppermute | solution.py:569
  74.9 3.3 %collective-permute-start.12 = (bf16[4,32,128]{2,1,0:T(8,128)(2,1)S(1)}, bf16[4,32,128]{2,1,0:T(8,128)(2,1)S(1)}, u32[]{:S(2)}, u32[]{:S(2)}) collective-permute-start(bf16[4,32,128]{2,1,0:T(8,128)(2,1)S(1)} %get-tuple-element.42.refs_0_), channel_id=1, source_target_pairs={{0,8},{8,16},{16,24},{24,0},{1,9},{9,17},{17,25},{25,1},{2,10},{10... | collective-permute-start | bytes 98312 | tf_op jit(solution)/shard_map/ppermute | solution.py:569
  85.1 13.5 %all-to-all-start.4 = ((bf16[8,144,128]{2,1,0:T(8,128)(2,1)}), bf16[8,144,128]{2,1,0:T(8,128)(2,1)S(1)}, u32[]{:S(2)}, u32[]{:S(2)}) async-start(bf16[8,144,128]{2,1,0:T(8,128)(2,1)} %get-tuple-element.43), calls=%async_computation.4 | async-start | bytes 589824 | tf_op jit(solution)/shard_map/all_to_all | solution.py:575
  91.4 8.3 %collective-permute-start.9 = (bf16[4,32,128]{2,1,0:T(8,128)(2,1)S(1)}, bf16[4,32,128]{2,1,0:T(8,128)(2,1)S(1)}, u32[]{:S(2)}, u32[]{:S(2)}) collective-permute-start(bf16[4,32,128]{2,1,0:T(8,128)(2,1)S(1)} %get-tuple-element.39), channel_id=1, source_target_pairs={{0,8},{8,16},{16,24},{24,0},{1,9},{9,17},{17,25},{25,1},{2,10},{10... | collective-permute-start | bytes 98312 | tf_op jit(solution)/shard_map/ppermute | solution.py:569
  92.1 7.8 %collective-permute-start.10 = (bf16[4,32,128]{2,1,0:T(8,128)(2,1)S(1)}, bf16[4,32,128]{2,1,0:T(8,128)(2,1)S(1)}, u32[]{:S(2)}, u32[]{:S(2)}) collective-permute-start(bf16[4,32,128]{2,1,0:T(8,128)(2,1)S(1)} %get-tuple-element.40), channel_id=1, source_target_pairs={{0,16},{8,24},{16,0},{24,8},{1,17},{9,25},{17,1},{25,9},{2,18},{10... | collective-permute-start | bytes 98312 | tf_op jit(solution)/shard_map/ppermute | solution.py:569
  92.9 7.0 %collective-permute-start.11 = (bf16[4,32,128]{2,1,0:T(8,128)(2,1)S(1)}, bf16[4,32,128]{2,1,0:T(8,128)(2,1)S(1)}, u32[]{:S(2)}, u32[]{:S(2)}) collective-permute-start(bf16[4,32,128]{2,1,0:T(8,128)(2,1)S(1)} %get-tuple-element.41), channel_id=1, source_target_pairs={{0,24},{8,0},{16,8},{24,16},{1,25},{9,1},{17,9},{25,17},{2,26},{10... | collective-permute-start | bytes 98312 | tf_op jit(solution)/shard_map/ppermute | solution.py:569
  98.7 1.4 %collective-permute-start.17 = (f32[32,128]{1,0:T(8,128)S(1)}, f32[32,128]{1,0:T(8,128)S(1)}, u32[]{:S(2)}, u32[]{:S(2)}) collective-permute-start(f32[32,128]{1,0:T(8,128)S(1)} %gram_sum.1.refs_4_), channel_id=1, source_target_pairs={{0,24},{8,0},{16,8},{24,16},{1,25},{9,1},{17,9},{25,17},{2,26},{10... | collective-permute-start | bytes 49160 | tf_op jit(solution)/shard_map/ppermute | solution.py:569
  98.7 3.8 %collective-permute-start.16 = (f32[32,128]{1,0:T(8,128)S(1)}, f32[32,128]{1,0:T(8,128)S(1)}, u32[]{:S(2)}, u32[]{:S(2)}) collective-permute-start(f32[32,128]{1,0:T(8,128)S(1)} %gram_sum.1.refs_4_), channel_id=1, source_target_pairs={{0,16},{8,24},{16,0},{24,8},{1,17},{9,25},{17,1},{25,9},{2,18},{10... | collective-permute-start | bytes 49160 | tf_op jit(solution)/shard_map/ppermute | solution.py:569
  99.7 3.2 %collective-permute-start.15 = (f32[32,128]{1,0:T(8,128)S(1)}, f32[32,128]{1,0:T(8,128)S(1)}, u32[]{:S(2)}, u32[]{:S(2)}) collective-permute-start(f32[32,128]{1,0:T(8,128)S(1)} %gram_sum.1.refs_4_), channel_id=1, source_target_pairs={{0,8},{8,16},{16,24},{24,0},{1,9},{9,17},{17,25},{25,1},{2,10},{10... | collective-permute-start | bytes 49160 | tf_op jit(solution)/shard_map/ppermute | solution.py:569

commit v13 on v9

--- a/solution.py
+++ b/solution.py
@@ -9,6 +9,7 @@
 
 graph_weight = 0.95
 GROUP = 32
+HALF = GROUP // 2
 BATCH = 32
 SPARE = 4
 PANEL = 8
@@ -138,13 +139,16 @@
             blocks = build_pair(tables)
             if waiting:
                 store_turned(*waiting)
+            if inside == HALF:
+                group_copy(block_ref, block_hbm, block_sems, 2 * index, HALF).start()
+                group_copy(flipped_ref, flipped_hbm, flipped_sems, 2 * index, HALF).start()
             for (slot, _, _), block in zip(tables, blocks):
                 block_ref[slot] = block
             waiting = (tables, [dot_across(identity, block) for block in blocks])
             tables = following
         store_turned(*waiting)
-        group_copy(block_ref, block_hbm, block_sems, index, GROUP).start()
-        group_copy(flipped_ref, flipped_hbm, flipped_sems, index, GROUP).start()
+        group_copy(block_ref, block_hbm, block_sems, 2 * index + 1, HALF).start()
+        group_copy(flipped_ref, flipped_hbm, flipped_sems, 2 * index + 1, HALF).start()
         return 0
 
     lax.fori_loop(0, groups, build_group, 0)
@@ -161,11 +165,11 @@
         )
 
     def finish_copies(index, _):
-        group_copy(block_ref, block_hbm, block_sems, index, GROUP).wait()
-        group_copy(flipped_ref, flipped_hbm, flipped_sems, index, GROUP).wait()
+        group_copy(block_ref, block_hbm, block_sems, index, HALF).wait()
+        group_copy(flipped_ref, flipped_hbm, flipped_sems, index, HALF).wait()
         return 0
 
-    lax.fori_loop(0, groups, finish_copies, 0)
+    lax.fori_loop(0, 2 * groups, finish_copies, 0)
 
 
 SCALARS = pl.BlockSpec(memory_space=pltpu.SMEM)
@@ -194,8 +198,8 @@
             pltpu.VMEM((col_count * per_seg, 8, 128), jnp.float32),
             pltpu.SemaphoreType.DMA((groups,)),
             pltpu.SemaphoreType.DMA((groups,)),
-            pltpu.SemaphoreType.DMA((groups,)),
-            pltpu.SemaphoreType.DMA((groups,)),
+            pltpu.SemaphoreType.DMA((2 * groups,)),
+            pltpu.SemaphoreType.DMA((2 * groups,)),
         ],
         compiler_params=pltpu.CompilerParams(vmem_limit_bytes=BUILD_GRANT),
         name="build_blocks",

time: 110 us -> 105 us (0.955)
  Pallas kernels: 36.2 us -> 28.2 us
  waiting for transfers between devices: 18.5 us -> 21.7 us
  starting transfers between devices: 53.3 us -> 52 us
    pallas_call x1, Pallas kernels: 13.3 us -> 8.49 us  [build_blocks(): pl.pallas_call(build_kernel, in_specs=[SCALARS, SCALARS, ANYWHERE, ANYWHE...]
    ppermute x18, starting transfers between devices: 27.2 us -> 22.4 us  [pass_around(): lax.ppermute(pieces[ahead], axis, [(at, (at + ahead) % count) for at in r...]
    all_to_all x5, starting transfers between devices: 26 us -> 29.6 us  [exchange(): return lax.all_to_all(pieces, axis, 0, 0, tiled=True)]
    pallas_call x4, Pallas kernels: 14.6 us -> 11.4 us  [over_blocks(): pl.pallas_call(kernel, in_specs=[SCALARS, SCALARS, ANYWHERE] + [IN_VMEM]...]
    all_to_all x5, waiting for transfers between devices: 6.21 us -> 9.3 us  [exchange(): return lax.all_to_all(pieces, axis, 0, 0, tiled=True)]
  transfers between devices with their start and end apart: 23 -> 23, of which waited for: 13 -> 12; matrix products, arithmetic and copies ran while one was open for 0% -> 0% of each run, Pallas kernels for 13% -> 11%
where the time goes in v13:
time: 105 us
  starting transfers between devices  52 us (50%)
  Pallas kernels  28.2 us (27%)
  waiting for transfers between devices  21.7 us (21%)
  local copies, waits for them, and re-layouts  1.53 us (1%)
  between operations  1.39 us (1%)
    all_to_all x5, starting transfers between devices, exchange(): return lax.all_to_all(pieces, axis, 0, 0, tiled=True)  29.6 us
    ppermute x18, starting transfers between devices, pass_around(): lax.ppermute(pieces[ahead], axis, [(at, (at + ahead) % count) for at in r...  22.4 us
    ppermute x18, waiting for transfers between devices, pass_around(): lax.ppermute(pieces[ahead], axis, [(at, (at + ahead) % count) for at in r...  12.4 us
    pallas_call x4, Pallas kernels, over_blocks(): pl.pallas_call(kernel, in_specs=[SCALARS, SCALARS, ANYWHERE] + [IN_VMEM]...  11.4 us
    all_to_all x5, waiting for transfers between devices, exchange(): return lax.all_to_all(pieces, axis, 0, 0, tiled=True)  9.3 us
    pallas_call x1, Pallas kernels, build_blocks(): pl.pallas_call(build_kernel, in_specs=[SCALARS, SCALARS, ANYWHERE, ANYWHE...  8.49 us
    pallas_call x5, Pallas kernels, simple_call(): pl.pallas_call(kernel, out_shape=shapes, compiler_params=pltpu.CompilerPa...  8.29 us
  transfers between devices with their start and end apart: 23, of which 12 were waited for; matrix products, arithmetic and copies ran while one was open for 0% of the time, Pallas kernels for 11%

profile of v13, /device:TPU:0, one launch (start us, length us, event | category | flops | bytes accessed | tf_op | source)
XLA Modules:
  0.0 104.8 jit_solution(15523974014956850510)
XLA Ops:
  1.3 8.5 %build_blocks.1 = (bf16[1024,128,128]{2,1,0:T(8,128)(2,1)}, bf16[1024,128,128]{2,1,0:T(8,128)(2,1)}, f32[4,128]{1,0:T(4,128)}, f32[4,128]{1,0:T(4,128)}, f32[4,128]{1,0:T(4,128)}, /*index=5*/f32[32,128]{1,0:T(8,128)}) custom-call(s32[1,1,256]{2,1,0:T(1,128)} %spots_ref.9, s32[1,1]{1,0:T(1,128)S(6)} %copy.7.live_ref, s32[256,16,128]{2,1,0:T(8,128)} %bitcast.3, ...), custom_call_target="tpu_custom_call" | custom-call | tf_op jit(solution)/shard_map/build_blocks/pallas_call | solution.py:186
  9.8 10.0 %all-to-all-start = ((f32[8,4,128]{2,1,0:T(4,128)}), f32[8,4,128]{2,1,0:T(4,128)S(1)}, u32[]{:S(2)}, u32[]{:S(2)}) async-start(f32[8,4,128]{2,1,0:T(4,128)} %bitcast.5), calls=%async_computation | async-start | bytes 32768 | tf_op jit(solution)/shard_map/all_to_all | solution.py:572
  19.8 8.0 %collective-permute-start = (f32[4,128]{1,0:T(4,128)}, f32[4,128]{1,0:T(4,128)S(1)}, u32[]{:S(2)}, u32[]{:S(2)}) collective-permute-start(f32[4,128]{1,0:T(4,128)} %get-tuple-element.25), channel_id=1, source_target_pairs={{0,8},{8,16},{16,24},{24,0},{1,9},{9,17},{17,25},{25,1},{2,10},{10... | collective-permute-start | bytes 6152 | tf_op jit(solution)/shard_map/ppermute | solution.py:566
  27.8 1.4 %collective-permute-start.2 = (f32[4,128]{1,0:T(4,128)}, f32[4,128]{1,0:T(4,128)S(1)}, u32[]{:S(2)}, u32[]{:S(2)}) collective-permute-start(f32[4,128]{1,0:T(4,128)} %get-tuple-element.27), channel_id=1, source_target_pairs={{0,24},{8,0},{16,8},{24,16},{1,25},{9,1},{17,9},{25,17},{2,26},{10... | collective-permute-start | bytes 6152 | tf_op jit(solution)/shard_map/ppermute | solution.py:566
  29.2 2.4 %collective-permute-done.1.refs_1_ = f32[4,128]{1,0:T(4,128)S(1)} collective-permute-done((f32[4,128]{1,0:T(4,128)}, f32[4,128]{1,0:T(4,128)S(1)}, u32[]{:S(2)}, u32[]{:S(2)}) %collective-permute-start.1) | collective-permute-done | bytes 2080 | tf_op jit(solution)/shard_map/ppermute | solution.py:566
  32.4 1.0 start.1
  33.5 5.7 %all-to-all-start.1 = ((bf16[8,5,32,128]{3,2,1,0:T(8,128)(2,1)}), bf16[8,5,32,128]{3,2,1,0:T(8,128)(2,1)S(1)}, u32[]{:S(2)}, u32[]{:S(2)}) async-start(bf16[8,5,32,128]{3,2,1,0:T(8,128)(2,1)} %get-tuple-element.29), calls=%async_computation.1 | async-start | bytes 655360 | tf_op jit(solution)/shard_map/all_to_all | solution.py:572
  41.3 2.3 %collective-permute-done.7.refs_2_ = bf16[4,32,128]{2,1,0:T(8,128)(2,1)S(1)} collective-permute-done((bf16[4,32,128]{2,1,0:T(8,128)(2,1)S(1)}, bf16[4,32,128]{2,1,0:T(8,128)(2,1)S(1)}, u32[]{:S(2)}, u32[]{:S(2)}) %collective-permute-start.7) | collective-permute-done | bytes 32800 | tf_op jit(solution)/shard_map/ppermute | solution.py:566
  44.7 3.4 %backward_product.2 = bf16[8,128,128]{2,1,0:T(8,128)(2,1)} custom-call(s32[1,1,256]{2,1,0:T(1,128)S(1)} %copy-done.2, s32[1,1]{1,0:T(1,128)S(6)} %copy.7.live_ref, bf16[1024,128,128]{2,1,0:T(8,128)(2,1)} %get-tuple-element.34.block_hbm, bf16[4,32,128]{2,1,0:T(8,128)(2,1)S(1)} %get-tuple-element.35.refs_0_, ...), custom_call_target="tpu_custom_call" | custom-call | flops 268435456 | bytes 8388608 | tf_op jit(solution)/shard_map/backward_product/pallas_call | solution.py:348
  48.1 1.7 %all-to-all-done.1.col_dir_ref.first_dir_ref = bf16[8,5,32,128]{3,2,1,0:T(8,128)(2,1)S(1)} async-done(((bf16[8,5,32,128]{3,2,1,0:T(8,128)(2,1)}), bf16[8,5,32,128]{3,2,1,0:T(8,128)(2,1)S(1)}, u32[]{:S(2)}, u32[]{:S(2)}) %all-to-all-start.1) | async-done | bytes 327712 | tf_op jit(solution)/shard_map/all_to_all | solution.py:572
  49.7 4.5 %all-to-all-start.2 = ((bf16[8,128,128]{2,1,0:T(8,128)(2,1)}), bf16[8,128,128]{2,1,0:T(8,128)(2,1)S(1)}, u32[]{:S(2)}, u32[]{:S(2)}) async-start(bf16[8,128,128]{2,1,0:T(8,128)(2,1)} %backward_product.2), calls=%async_computation.2 | async-start | bytes 524288 | tf_op jit(solution)/shard_map/all_to_all | solution.py:572
  54.2 2.7 %forward_product.2 = (bf16[4,32,128]{2,1,0:T(8,128)(2,1)S(1)}, bf16[4,32,128]{2,1,0:T(8,128)(2,1)S(1)}, bf16[4,32,128]{2,1,0:T(8,128)(2,1)S(1)}, bf16[4,32,128]{2,1,0:T(8,128)(2,1)S(1)}) custom-call(s32[1,1,256]{2,1,0:T(1,128)S(1)} %copy-done.3, s32[1,1]{1,0:T(1,128)S(6)} %copy.7.live_ref, bf16[1024,128,128]{2,1,0:T(8,128)(2,1)} %get-tuple-element.24.block_hbm, ...), custom_call_target="tpu_custom_call" | custom-call | flops 268435456 | bytes 8388608 | tf_op jit(solution)/shard_map/forward_product/pallas_call | solution.py:348
  57.0 2.3 %collective-permute-start.4 = (bf16[4,32,128]{2,1,0:T(8,128)(2,1)S(1)}, bf16[4,32,128]{2,1,0:T(8,128)(2,1)S(1)}, u32[]{:S(2)}, u32[]{:S(2)}) collective-permute-start(bf16[4,32,128]{2,1,0:T(8,128)(2,1)S(1)} %get-tuple-element.32), channel_id=1, source_target_pairs={{0,16},{8,24},{16,0},{24,8},{1,17},{9,25},{17,1},{25,9},{2,18},{10... | collective-permute-start | bytes 98312 | tf_op jit(solution)/shard_map/ppermute | solution.py:566
  59.3 1.4 %collective-permute-start.5 = (bf16[4,32,128]{2,1,0:T(8,128)(2,1)S(1)}, bf16[4,32,128]{2,1,0:T(8,128)(2,1)S(1)}, u32[]{:S(2)}, u32[]{:S(2)}) collective-permute-start(bf16[4,32,128]{2,1,0:T(8,128)(2,1)S(1)} %get-tuple-element.33), channel_id=1, source_target_pairs={{0,24},{8,0},{16,8},{24,16},{1,25},{9,1},{17,9},{25,17},{2,26},{10... | collective-permute-start | bytes 98312 | tf_op jit(solution)/shard_map/ppermute | solution.py:566
  60.6 1.8 %all-to-all-done.2.refs_4_ = bf16[8,128,128]{2,1,0:T(8,128)(2,1)S(1)} async-done(((bf16[8,128,128]{2,1,0:T(8,128)(2,1)}), bf16[8,128,128]{2,1,0:T(8,128)(2,1)S(1)}, u32[]{:S(2)}, u32[]{:S(2)}) %all-to-all-start.2) | async-done | bytes 262176 | tf_op jit(solution)/shard_map/all_to_all | solution.py:572
  62.5 1.2 %middle.1 = (f32[4,32,128]{2,1,0:T(8,128)S(1)}, bf16[4,32,128]{2,1,0:T(8,128)(2,1)S(1)}, bf16[8,5,32,128]{3,2,1,0:T(8,128)(2,1)}) custom-call(bf16[4,32,128]{2,1,0:T(8,128)(2,1)S(1)} %get-tuple-element.30.refs_0_, bf16[4,32,128]{2,1,0:T(8,128)(2,1)S(1)} %collective-permute-done.3.refs_1_, bf16[4,32,128]{2,1,0:T(8,128)(2,1)S(1)} %collective-permute-done.4.refs_2_, ...), custom_call_target="tpu_custom_call" | custom-call | tf_op jit(solution)/shard_map/middle/pallas_call | solution.py:576
  63.7 5.7 %all-to-all-start.3 = ((bf16[8,5,32,128]{3,2,1,0:T(8,128)(2,1)}), bf16[8,5,32,128]{3,2,1,0:T(8,128)(2,1)S(1)}, u32[]{:S(2)}, u32[]{:S(2)}) async-start(bf16[8,5,32,128]{3,2,1,0:T(8,128)(2,1)} %get-tuple-element.37), calls=%async_computation.3 | async-start | bytes 655360 | tf_op jit(solution)/shard_map/all_to_all | solution.py:572
  69.4 1.5 %collective-permute-start.14 = (bf16[4,32,128]{2,1,0:T(8,128)(2,1)S(1)}, bf16[4,32,128]{2,1,0:T(8,128)(2,1)S(1)}, u32[]{:S(2)}, u32[]{:S(2)}) collective-permute-start(bf16[4,32,128]{2,1,0:T(8,128)(2,1)S(1)} %get-tuple-element.42.refs_0_), channel_id=1, source_target_pairs={{0,24},{8,0},{16,8},{24,16},{1,25},{9,1},{17,9},{25,17},{2,26},{10... | collective-permute-start | bytes 98312 | tf_op jit(solution)/shard_map/ppermute | solution.py:566
  71.2 1.3 %collective-permute-done.14.refs_3_ = bf16[4,32,128]{2,1,0:T(8,128)(2,1)S(1)} collective-permute-done((bf16[4,32,128]{2,1,0:T(8,128)(2,1)S(1)}, bf16[4,32,128]{2,1,0:T(8,128)(2,1)S(1)}, u32[]{:S(2)}, u32[]{:S(2)}) %collective-permute-start.14) | collective-permute-done | bytes 32800 | tf_op jit(solution)/shard_map/ppermute | solution.py:566
  72.5 2.4 %collective-permute-done.13.refs_2_ = bf16[4,32,128]{2,1,0:T(8,128)(2,1)S(1)} collective-permute-done((bf16[4,32,128]{2,1,0:T(8,128)(2,1)S(1)}, bf16[4,32,128]{2,1,0:T(8,128)(2,1)S(1)}, u32[]{:S(2)}, u32[]{:S(2)}) %collective-permute-start.13) | collective-permute-done | bytes 32800 | tf_op jit(solution)/shard_map/ppermute | solution.py:566
  74.9 2.7 %backward_product.3.total_ref = bf16[8,128,128]{2,1,0:T(8,128)(2,1)S(1)} custom-call(s32[1,1,256]{2,1,0:T(1,128)S(1)} %copy-done.3, s32[1,1]{1,0:T(1,128)S(6)} %copy.7.live_ref, bf16[1024,128,128]{2,1,0:T(8,128)(2,1)} %get-tuple-element.34.block_hbm, bf16[4,32,128]{2,1,0:T(8,128)(2,1)S(1)} %get-tuple-element.42.refs_0_, ...), custom_call_target="tpu_custom_call" | custom-call | flops 268435456 | bytes 8388608 | tf_op jit(solution)/shard_map/backward_product/pallas_call | solution.py:348
  77.6 2.7 %all-to-all-done.3.col_dir_ref = bf16[8,5,32,128]{3,2,1,0:T(8,128)(2,1)S(1)} async-done(((bf16[8,5,32,128]{3,2,1,0:T(8,128)(2,1)}), bf16[8,5,32,128]{3,2,1,0:T(8,128)(2,1)S(1)}, u32[]{:S(2)}, u32[]{:S(2)}) %all-to-all-start.3) | async-done | bytes 327712 | tf_op jit(solution)/shard_map/all_to_all | solution.py:572
  80.3 1.3 %attach.1 = (bf16[8,144,128]{2,1,0:T(8,128)(2,1)}, f32[32,128]{1,0:T(8,128)S(1)}) custom-call(bf16[8,5,32,128]{3,2,1,0:T(8,128)(2,1)S(1)} %all-to-all-done.1.col_dir_ref.first_dir_ref, bf16[8,5,32,128]{3,2,1,0:T(8,128)(2,1)S(1)} %all-to-all-done.3.col_dir_ref, bf16[8,128,128]{2,1,0:T(8,128)(2,1)S(1)} %backward_product.3.total_ref), custom_call_target="tpu_custom_call" | custom-call | tf_op jit(solution)/shard_map/attach/pallas_call | solution.py:576
  81.5 3.6 %all-to-all-start.4 = ((bf16[8,144,128]{2,1,0:T(8,128)(2,1)}), bf16[8,144,128]{2,1,0:T(8,128)(2,1)S(1)}, u32[]{:S(2)}, u32[]{:S(2)}) async-start(bf16[8,144,128]{2,1,0:T(8,128)(2,1)} %get-tuple-element.43), calls=%async_computation.4 | async-start | bytes 589824 | tf_op jit(solution)/shard_map/all_to_all | solution.py:572
  85.2 2.7 %forward_product.3 = (bf16[4,32,128]{2,1,0:T(8,128)(2,1)S(1)}, bf16[4,32,128]{2,1,0:T(8,128)(2,1)S(1)}, bf16[4,32,128]{2,1,0:T(8,128)(2,1)S(1)}, bf16[4,32,128]{2,1,0:T(8,128)(2,1)S(1)}) custom-call(s32[1,1,256]{2,1,0:T(1,128)S(1)} %copy-done.3, s32[1,1]{1,0:T(1,128)S(6)} %copy.7.live_ref, bf16[1024,128,128]{2,1,0:T(8,128)(2,1)} %get-tuple-element.24.block_hbm, ...), custom_call_target="tpu_custom_call" | custom-call | flops 268435456 | bytes 8388608 | tf_op jit(solution)/shard_map/forward_product/pallas_call | solution.py:348
  88.5 2.0 %collective-permute-start.10 = (bf16[4,32,128]{2,1,0:T(8,128)(2,1)S(1)}, bf16[4,32,128]{2,1,0:T(8,128)(2,1)S(1)}, u32[]{:S(2)}, u32[]{:S(2)}) collective-permute-start(bf16[4,32,128]{2,1,0:T(8,128)(2,1)S(1)} %get-tuple-element.40), channel_id=1, source_target_pairs={{0,16},{8,24},{16,0},{24,8},{1,17},{9,25},{17,1},{25,9},{2,18},{10... | collective-permute-start | bytes 98312 | tf_op jit(solution)/shard_map/ppermute | solution.py:566
  90.5 1.4 %collective-permute-start.11 = (bf16[4,32,128]{2,1,0:T(8,128)(2,1)S(1)}, bf16[4,32,128]{2,1,0:T(8,128)(2,1)S(1)}, u32[]{:S(2)}, u32[]{:S(2)}) collective-permute-start(bf16[4,32,128]{2,1,0:T(8,128)(2,1)S(1)} %get-tuple-element.41), channel_id=1, source_target_pairs={{0,24},{8,0},{16,8},{24,16},{1,25},{9,1},{17,9},{25,17},{2,26},{10... | collective-permute-start | bytes 98312 | tf_op jit(solution)/shard_map/ppermute | solution.py:566
  91.9 3.1 %all-to-all-done.4.col_ref.refs_8_ = bf16[8,144,128]{2,1,0:T(8,128)(2,1)S(1)} async-done(((bf16[8,144,128]{2,1,0:T(8,128)(2,1)}), bf16[8,144,128]{2,1,0:T(8,128)(2,1)S(1)}, u32[]{:S(2)}, u32[]{:S(2)}) %all-to-all-start.4) | async-done | bytes 294944 | tf_op jit(solution)/shard_map/all_to_all | solution.py:572
  95.1 1.8 %collective-permute-start.16 = (f32[32,128]{1,0:T(8,128)S(1)}, f32[32,128]{1,0:T(8,128)S(1)}, u32[]{:S(2)}, u32[]{:S(2)}) collective-permute-start(f32[32,128]{1,0:T(8,128)S(1)} %gram_sum.1.refs_4_), channel_id=1, source_target_pairs={{0,16},{8,24},{16,0},{24,8},{1,17},{9,25},{17,1},{25,9},{2,18},{10... | collective-permute-start | bytes 49160 | tf_op jit(solution)/shard_map/ppermute | solution.py:566
  97.1 1.8 %collective-permute-done.16.refs_6_ = f32[32,128]{1,0:T(8,128)S(1)} collective-permute-done((f32[32,128]{1,0:T(8,128)S(1)}, f32[32,128]{1,0:T(8,128)S(1)}, u32[]{:S(2)}, u32[]{:S(2)}) %collective-permute-start.16) | collective-permute-done | bytes 16416 | tf_op jit(solution)/shard_map/ppermute | solution.py:566
  98.9 1.2 %collective-permute-done.15.refs_5_ = f32[32,128]{1,0:T(8,128)S(1)} collective-permute-done((f32[32,128]{1,0:T(8,128)S(1)}, f32[32,128]{1,0:T(8,128)S(1)}, u32[]{:S(2)}, u32[]{:S(2)}) %collective-permute-start.15) | collective-permute-done | bytes 16416 | tf_op jit(solution)/shard_map/ppermute | solution.py:566
  100.1 4.7 %close.1 = (f32[32,512]{1,0:T(8,128)}, f32[32,512]{1,0:T(8,128)}) custom-call(bf16[4,32,128]{2,1,0:T(8,128)(2,1)S(1)} %get-tuple-element.38.refs_0_, bf16[4,32,128]{2,1,0:T(8,128)(2,1)S(1)} %collective-permute-done.9.refs_1_, bf16[4,32,128]{2,1,0:T(8,128)(2,1)S(1)} %collective-permute-done.10.refs_2_, ...), custom_call_target="tpu_custom_call" | custom-call | tf_op jit(solution)/shard_map/close/pallas_call | solution.py:576
  (32 shorter events, 5.3 us)
Async XLA Ops:
  0.6 53.6 %copy-start.3 = (s32[1,1,256]{2,1,0:T(1,128)S(1)}, s32[1,1,256]{2,1,0:T(1,128)}, u32[]{:S(2)}) copy-start(s32[1,1,256]{2,1,0:T(1,128)} %spots_ref.9) | copy-start | bytes 3076
  9.8 21.8 %all-to-all-start = ((f32[8,4,128]{2,1,0:T(4,128)}), f32[8,4,128]{2,1,0:T(4,128)S(1)}, u32[]{:S(2)}, u32[]{:S(2)}) async-start(f32[8,4,128]{2,1,0:T(4,128)} %bitcast.5), calls=%async_computation | async-start | bytes 32768 | tf_op jit(solution)/shard_map/all_to_all | solution.py:572
  19.8 9.4 %collective-permute-start = (f32[4,128]{1,0:T(4,128)}, f32[4,128]{1,0:T(4,128)S(1)}, u32[]{:S(2)}, u32[]{:S(2)}) collective-permute-start(f32[4,128]{1,0:T(4,128)} %get-tuple-element.25), channel_id=1, source_target_pairs={{0,8},{8,16},{16,24},{24,0},{1,9},{9,17},{17,25},{25,1},{2,10},{10... | collective-permute-start | bytes 6152 | tf_op jit(solution)/shard_map/ppermute | solution.py:566
  27.8 3.8 %collective-permute-start.1 = (f32[4,128]{1,0:T(4,128)}, f32[4,128]{1,0:T(4,128)S(1)}, u32[]{:S(2)}, u32[]{:S(2)}) collective-permute-start(f32[4,128]{1,0:T(4,128)} %get-tuple-element.26), channel_id=1, source_target_pairs={{0,16},{8,24},{16,0},{24,8},{1,17},{9,25},{17,1},{25,9},{2,18},{10... | collective-permute-start | bytes 6152 | tf_op jit(solution)/shard_map/ppermute | solution.py:566
  27.8 3.8 %collective-permute-start.2 = (f32[4,128]{1,0:T(4,128)}, f32[4,128]{1,0:T(4,128)S(1)}, u32[]{:S(2)}, u32[]{:S(2)}) collective-permute-start(f32[4,128]{1,0:T(4,128)} %get-tuple-element.27), channel_id=1, source_target_pairs={{0,24},{8,0},{16,8},{24,16},{1,25},{9,1},{17,9},{25,17},{2,26},{10... | collective-permute-start | bytes 6152 | tf_op jit(solution)/shard_map/ppermute | solution.py:566
  31.6 0.8 copy-start
  33.5 16.3 %all-to-all-start.1 = ((bf16[8,5,32,128]{3,2,1,0:T(8,128)(2,1)}), bf16[8,5,32,128]{3,2,1,0:T(8,128)(2,1)S(1)}, u32[]{:S(2)}, u32[]{:S(2)}) async-start(bf16[8,5,32,128]{3,2,1,0:T(8,128)(2,1)} %get-tuple-element.29), calls=%async_computation.1 | async-start | bytes 655360 | tf_op jit(solution)/shard_map/all_to_all | solution.py:572
  39.2 2.1 %collective-permute-start.8 = (bf16[4,32,128]{2,1,0:T(8,128)(2,1)S(1)}, bf16[4,32,128]{2,1,0:T(8,128)(2,1)S(1)}, u32[]{:S(2)}, u32[]{:S(2)}) collective-permute-start(bf16[4,32,128]{2,1,0:T(8,128)(2,1)S(1)} %get-tuple-element.35.refs_0_), channel_id=1, source_target_pairs={{0,24},{8,0},{16,8},{24,16},{1,25},{9,1},{17,9},{25,17},{2,26},{10... | collective-permute-start | bytes 98312 | tf_op jit(solution)/shard_map/ppermute | solution.py:566
  39.7 3.9 %collective-permute-start.7 = (bf16[4,32,128]{2,1,0:T(8,128)(2,1)S(1)}, bf16[4,32,128]{2,1,0:T(8,128)(2,1)S(1)}, u32[]{:S(2)}, u32[]{:S(2)}) collective-permute-start(bf16[4,32,128]{2,1,0:T(8,128)(2,1)S(1)} %get-tuple-element.35.refs_0_), channel_id=1, source_target_pairs={{0,16},{8,24},{16,0},{24,8},{1,17},{9,25},{17,1},{25,9},{2,18},{10... | collective-permute-start | bytes 98312 | tf_op jit(solution)/shard_map/ppermute | solution.py:566
  40.7 3.3 %collective-permute-start.6 = (bf16[4,32,128]{2,1,0:T(8,128)(2,1)S(1)}, bf16[4,32,128]{2,1,0:T(8,128)(2,1)S(1)}, u32[]{:S(2)}, u32[]{:S(2)}) collective-permute-start(bf16[4,32,128]{2,1,0:T(8,128)(2,1)S(1)} %get-tuple-element.35.refs_0_), channel_id=1, source_target_pairs={{0,8},{8,16},{16,24},{24,0},{1,9},{9,17},{17,25},{25,1},{2,10},{10... | collective-permute-start | bytes 98312 | tf_op jit(solution)/shard_map/ppermute | solution.py:566
  44.0 0.7 copy-start.2
  44.7 17.8 %copy-start.1 = (f32[32,512]{1,0:T(8,128)S(1)}, f32[32,512]{1,0:T(8,128)}, u32[]{:S(2)}) copy-start(f32[32,512]{1,0:T(8,128)} %refs_10_.1) | copy-start | bytes 196612
  49.7 12.7 %all-to-all-start.2 = ((bf16[8,128,128]{2,1,0:T(8,128)(2,1)}), bf16[8,128,128]{2,1,0:T(8,128)(2,1)S(1)}, u32[]{:S(2)}, u32[]{:S(2)}) async-start(bf16[8,128,128]{2,1,0:T(8,128)(2,1)} %backward_product.2), calls=%async_computation.2 | async-start | bytes 524288 | tf_op jit(solution)/shard_map/all_to_all | solution.py:572
  56.9 5.6 %collective-permute-start.3 = (bf16[4,32,128]{2,1,0:T(8,128)(2,1)S(1)}, bf16[4,32,128]{2,1,0:T(8,128)(2,1)S(1)}, u32[]{:S(2)}, u32[]{:S(2)}) collective-permute-start(bf16[4,32,128]{2,1,0:T(8,128)(2,1)S(1)} %get-tuple-element.31), channel_id=1, source_target_pairs={{0,8},{8,16},{16,24},{24,0},{1,9},{9,17},{17,25},{25,1},{2,10},{10... | collective-permute-start | bytes 98312 | tf_op jit(solution)/shard_map/ppermute | solution.py:566
  57.0 5.5 %collective-permute-start.4 = (bf16[4,32,128]{2,1,0:T(8,128)(2,1)S(1)}, bf16[4,32,128]{2,1,0:T(8,128)(2,1)S(1)}, u32[]{:S(2)}, u32[]{:S(2)}) collective-permute-start(bf16[4,32,128]{2,1,0:T(8,128)(2,1)S(1)} %get-tuple-element.32), channel_id=1, source_target_pairs={{0,16},{8,24},{16,0},{24,8},{1,17},{9,25},{17,1},{25,9},{2,18},{10... | collective-permute-start | bytes 98312 | tf_op jit(solution)/shard_map/ppermute | solution.py:566
  59.3 3.2 %collective-permute-start.5 = (bf16[4,32,128]{2,1,0:T(8,128)(2,1)S(1)}, bf16[4,32,128]{2,1,0:T(8,128)(2,1)S(1)}, u32[]{:S(2)}, u32[]{:S(2)}) collective-permute-start(bf16[4,32,128]{2,1,0:T(8,128)(2,1)S(1)} %get-tuple-element.33), channel_id=1, source_target_pairs={{0,24},{8,0},{16,8},{24,16},{1,25},{9,1},{17,9},{25,17},{2,26},{10... | collective-permute-start | bytes 98312 | tf_op jit(solution)/shard_map/ppermute | solution.py:566
  63.7 16.6 %all-to-all-start.3 = ((bf16[8,5,32,128]{3,2,1,0:T(8,128)(2,1)}), bf16[8,5,32,128]{3,2,1,0:T(8,128)(2,1)S(1)}, u32[]{:S(2)}, u32[]{:S(2)}) async-start(bf16[8,5,32,128]{3,2,1,0:T(8,128)(2,1)} %get-tuple-element.37), calls=%async_computation.3 | async-start | bytes 655360 | tf_op jit(solution)/shard_map/all_to_all | solution.py:572
  69.4 3.1 %collective-permute-start.14 = (bf16[4,32,128]{2,1,0:T(8,128)(2,1)S(1)}, bf16[4,32,128]{2,1,0:T(8,128)(2,1)S(1)}, u32[]{:S(2)}, u32[]{:S(2)}) collective-permute-start(bf16[4,32,128]{2,1,0:T(8,128)(2,1)S(1)} %get-tuple-element.42.refs_0_), channel_id=1, source_target_pairs={{0,24},{8,0},{16,8},{24,16},{1,25},{9,1},{17,9},{25,17},{2,26},{10... | collective-permute-start | bytes 98312 | tf_op jit(solution)/shard_map/ppermute | solution.py:566
  70.9 4.0 %collective-permute-start.13 = (bf16[4,32,128]{2,1,0:T(8,128)(2,1)S(1)}, bf16[4,32,128]{2,1,0:T(8,128)(2,1)S(1)}, u32[]{:S(2)}, u32[]{:S(2)}) collective-permute-start(bf16[4,32,128]{2,1,0:T(8,128)(2,1)S(1)} %get-tuple-element.42.refs_0_), channel_id=1, source_target_pairs={{0,16},{8,24},{16,0},{24,8},{1,17},{9,25},{17,1},{25,9},{2,18},{10... | collective-permute-start | bytes 98312 | tf_op jit(solution)/shard_map/ppermute | solution.py:566
  71.2 3.7 %collective-permute-start.12 = (bf16[4,32,128]{2,1,0:T(8,128)(2,1)S(1)}, bf16[4,32,128]{2,1,0:T(8,128)(2,1)S(1)}, u32[]{:S(2)}, u32[]{:S(2)}) collective-permute-start(bf16[4,32,128]{2,1,0:T(8,128)(2,1)S(1)} %get-tuple-element.42.refs_0_), channel_id=1, source_target_pairs={{0,8},{8,16},{16,24},{24,0},{1,9},{9,17},{17,25},{25,1},{2,10},{10... | collective-permute-start | bytes 98312 | tf_op jit(solution)/shard_map/ppermute | solution.py:566
  81.5 13.4 %all-to-all-start.4 = ((bf16[8,144,128]{2,1,0:T(8,128)(2,1)}), bf16[8,144,128]{2,1,0:T(8,128)(2,1)S(1)}, u32[]{:S(2)}, u32[]{:S(2)}) async-start(bf16[8,144,128]{2,1,0:T(8,128)(2,1)} %get-tuple-element.43), calls=%async_computation.4 | async-start | bytes 589824 | tf_op jit(solution)/shard_map/all_to_all | solution.py:572
  87.8 9.1 %collective-permute-start.9 = (bf16[4,32,128]{2,1,0:T(8,128)(2,1)S(1)}, bf16[4,32,128]{2,1,0:T(8,128)(2,1)S(1)}, u32[]{:S(2)}, u32[]{:S(2)}) collective-permute-start(bf16[4,32,128]{2,1,0:T(8,128)(2,1)S(1)} %get-tuple-element.39), channel_id=1, source_target_pairs={{0,8},{8,16},{16,24},{24,0},{1,9},{9,17},{17,25},{25,1},{2,10},{10... | collective-permute-start | bytes 98312 | tf_op jit(solution)/shard_map/ppermute | solution.py:566
  88.5 8.7 %collective-permute-start.10 = (bf16[4,32,128]{2,1,0:T(8,128)(2,1)S(1)}, bf16[4,32,128]{2,1,0:T(8,128)(2,1)S(1)}, u32[]{:S(2)}, u32[]{:S(2)}) collective-permute-start(bf16[4,32,128]{2,1,0:T(8,128)(2,1)S(1)} %get-tuple-element.40), channel_id=1, source_target_pairs={{0,16},{8,24},{16,0},{24,8},{1,17},{9,25},{17,1},{25,9},{2,18},{10... | collective-permute-start | bytes 98312 | tf_op jit(solution)/shard_map/ppermute | solution.py:566
  90.5 6.6 %collective-permute-start.11 = (bf16[4,32,128]{2,1,0:T(8,128)(2,1)S(1)}, bf16[4,32,128]{2,1,0:T(8,128)(2,1)S(1)}, u32[]{:S(2)}, u32[]{:S(2)}) collective-permute-start(bf16[4,32,128]{2,1,0:T(8,128)(2,1)S(1)} %get-tuple-element.41), channel_id=1, source_target_pairs={{0,24},{8,0},{16,8},{24,16},{1,25},{9,1},{17,9},{25,17},{2,26},{10... | collective-permute-start | bytes 98312 | tf_op jit(solution)/shard_map/ppermute | solution.py:566
  95.1 2.0 %collective-permute-start.17 = (f32[32,128]{1,0:T(8,128)S(1)}, f32[32,128]{1,0:T(8,128)S(1)}, u32[]{:S(2)}, u32[]{:S(2)}) collective-permute-start(f32[32,128]{1,0:T(8,128)S(1)} %gram_sum.1.refs_4_), channel_id=1, source_target_pairs={{0,24},{8,0},{16,8},{24,16},{1,25},{9,1},{17,9},{25,17},{2,26},{10... | collective-permute-start | bytes 49160 | tf_op jit(solution)/shard_map/ppermute | solution.py:566
  95.1 3.8 %collective-permute-start.16 = (f32[32,128]{1,0:T(8,128)S(1)}, f32[32,128]{1,0:T(8,128)S(1)}, u32[]{:S(2)}, u32[]{:S(2)}) collective-permute-start(f32[32,128]{1,0:T(8,128)S(1)} %gram_sum.1.refs_4_), channel_id=1, source_target_pairs={{0,16},{8,24},{16,0},{24,8},{1,17},{9,25},{17,1},{25,9},{2,18},{10... | collective-permute-start | bytes 49160 | tf_op jit(solution)/shard_map/ppermute | solution.py:566
  96.9 3.2 %collective-permute-start.15 = (f32[32,128]{1,0:T(8,128)S(1)}, f32[32,128]{1,0:T(8,128)S(1)}, u32[]{:S(2)}, u32[]{:S(2)}) collective-permute-start(f32[32,128]{1,0:T(8,128)S(1)} %gram_sum.1.refs_4_), channel_id=1, source_target_pairs={{0,8},{8,16},{16,24},{24,0},{1,9},{9,17},{17,25},{25,1},{2,10},{10... | collective-permute-start | bytes 49160 | tf_op jit(solution)/shard_map/ppermute | solution.py:566

commit v14 on v12

--- a/solution.py
+++ b/solution.py
@@ -9,6 +9,7 @@
 
 graph_weight = 0.95
 GROUP = 32
+HALF = GROUP // 2
 BATCH = 32
 SPARE = 4
 PANEL = 8
@@ -138,13 +139,16 @@
             blocks = build_pair(tables)
             if waiting:
                 store_turned(*waiting)
+            if inside == HALF:
+                group_copy(block_ref, block_hbm, block_sems, 2 * index, HALF).start()
+                group_copy(flipped_ref, flipped_hbm, flipped_sems, 2 * index, HALF).start()
             for (slot, _, _), block in zip(tables, blocks):
                 block_ref[slot] = block
             waiting = (tables, [dot_across(identity, block) for block in blocks])
             tables = following
         store_turned(*waiting)
-        group_copy(block_ref, block_hbm, block_sems, index, GROUP).start()
-        group_copy(flipped_ref, flipped_hbm, flipped_sems, index, GROUP).start()
+        group_copy(block_ref, block_hbm, block_sems, 2 * index + 1, HALF).start()
+        group_copy(flipped_ref, flipped_hbm, flipped_sems, 2 * index + 1, HALF).start()
         return 0
 
     lax.fori_loop(0, groups, build_group, 0)
@@ -161,11 +165,11 @@
         )
 
     def finish_copies(index, _):
-        group_copy(block_ref, block_hbm, block_sems, index, GROUP).wait()
-        group_copy(flipped_ref, flipped_hbm, flipped_sems, index, GROUP).wait()
+        group_copy(block_ref, block_hbm, block_sems, index, HALF).wait()
+        group_copy(flipped_ref, flipped_hbm, flipped_sems, index, HALF).wait()
         return 0
 
-    lax.fori_loop(0, groups, finish_copies, 0)
+    lax.fori_loop(0, 2 * groups, finish_copies, 0)
 
 
 SCALARS = pl.BlockSpec(memory_space=pltpu.SMEM)
@@ -194,8 +198,8 @@
             pltpu.VMEM((col_count * per_seg, 8, 128), jnp.float32),
             pltpu.SemaphoreType.DMA((groups,)),
             pltpu.SemaphoreType.DMA((groups,)),
-            pltpu.SemaphoreType.DMA((groups,)),
-            pltpu.SemaphoreType.DMA((groups,)),
+            pltpu.SemaphoreType.DMA((2 * groups,)),
+            pltpu.SemaphoreType.DMA((2 * groups,)),
         ],
         compiler_params=pltpu.CompilerParams(vmem_limit_bytes=BUILD_GRANT),
         name="build_blocks",

time: 107 us -> 106 us (level); the launches traced: 108 us -> 104 us
  starting transfers between devices: 54.7 us -> 46 us
  Pallas kernels: 28.1 us -> 31.9 us
  waiting for transfers between devices: 21 us -> 22.3 us
    ppermute x18, starting transfers between devices: 21.7 us -> 15.9 us  [pass_around(): lax.ppermute(pieces[ahead], axis, [(at, (at + ahead) % count) for at in r...]
    all_to_all x5, starting transfers between devices: 33 us -> 30 us  [exchange(): return lax.all_to_all(pieces, axis, 0, 0, tiled=True)]
    pallas_call x1, Pallas kernels: 8.55 us -> 10.8 us  [build_blocks(): pl.pallas_call(build_kernel, in_specs=[SCALARS, SCALARS, ANYWHERE, ANYWHE...]
    pallas_call x4, Pallas kernels: 11.5 us -> 13 us  [over_blocks(): pl.pallas_call(kernel, in_specs=[SCALARS, SCALARS, ANYWHERE] + [IN_VMEM]...]
    ppermute x18, waiting for transfers between devices: 12 us -> 13.2 us  [pass_around(): lax.ppermute(pieces[ahead], axis, [(at, (at + ahead) % count) for at in r...]
  transfers between devices with their start and end apart: 23 -> 23, of which waited for: 16 -> 12; matrix products, arithmetic and copies ran while one was open for 0% -> 0% of each run, Pallas kernels for 11% -> 13%
where the time goes in v14:
time: 106 us; the launch traced here: 104 us
  starting transfers between devices  46 us (43%)
  Pallas kernels  31.9 us (30%)
  waiting for transfers between devices  22.3 us (21%)
  local copies, waits for them, and re-layouts  2.37 us (2%)
  between operations  1.39 us (1%)
    all_to_all x5, starting transfers between devices, exchange(): return lax.all_to_all(pieces, axis, 0, 0, tiled=True)  30 us
    ppermute x18, starting transfers between devices, pass_around(): lax.ppermute(pieces[ahead], axis, [(at, (at + ahead) % count) for at in r...  15.9 us
    ppermute x18, waiting for transfers between devices, pass_around(): lax.ppermute(pieces[ahead], axis, [(at, (at + ahead) % count) for at in r...  13.2 us
    pallas_call x4, Pallas kernels, over_blocks(): pl.pallas_call(kernel, in_specs=[SCALARS, SCALARS, ANYWHERE] + [IN_VMEM]...  13 us
    pallas_call x1, Pallas kernels, build_blocks(): pl.pallas_call(build_kernel, in_specs=[SCALARS, SCALARS, ANYWHERE, ANYWHE...  10.8 us
    all_to_all x5, waiting for transfers between devices, exchange(): return lax.all_to_all(pieces, axis, 0, 0, tiled=True)  9.1 us
    pallas_call x6, Pallas kernels, simple_call(): pl.pallas_call(kernel, out_shape=shapes, compiler_params=pltpu.CompilerPa...  8.07 us
    unnamed x10, local copies, waits for them, and re-layouts  2.37 us
  transfers between devices with their start and end apart: 23, of which 12 were waited for; matrix products, arithmetic and copies ran while one was open for 0% of the time, Pallas kernels for 13%

profile of v14, /device:TPU:0, one launch (start us, length us, event | category | flops | bytes accessed | tf_op | source)
XLA Modules:
  0.0 103.9 jit_solution(384920391619676619)
XLA Ops:
  1.3 10.8 %build_blocks.1 = (bf16[1024,128,128]{2,1,0:T(8,128)(2,1)}, bf16[1024,128,128]{2,1,0:T(8,128)(2,1)}, f32[4,128]{1,0:T(4,128)}, f32[4,128]{1,0:T(4,128)}, f32[4,128]{1,0:T(4,128)}, /*index=5*/f32[32,128]{1,0:T(8,128)}) custom-call(s32[1,1,256]{2,1,0:T(1,128)} %spots_ref.9, s32[1,1]{1,0:T(1,128)S(6)} %copy.7.live_ref, s32[256,16,128]{2,1,0:T(8,128)} %bitcast.3, ...), custom_call_target="tpu_custom_call" | custom-call | tf_op jit(solution)/shard_map/build_blocks/pallas_call | solution.py:186
  12.1 9.7 %all-to-all-start = ((f32[8,4,128]{2,1,0:T(4,128)}), f32[8,4,128]{2,1,0:T(4,128)S(1)}, u32[]{:S(2)}, u32[]{:S(2)}) async-start(f32[8,4,128]{2,1,0:T(4,128)} %bitcast.5), calls=%async_computation | async-start | bytes 32768 | tf_op jit(solution)/shard_map/all_to_all | solution.py:579
  21.8 6.0 %collective-permute-start = (f32[4,128]{1,0:T(4,128)}, f32[4,128]{1,0:T(4,128)S(1)}, u32[]{:S(2)}, u32[]{:S(2)}) collective-permute-start(f32[4,128]{1,0:T(4,128)} %get-tuple-element.25), channel_id=1, source_target_pairs={{0,8},{8,16},{16,24},{24,0},{1,9},{9,17},{17,25},{25,1},{2,10},{10... | collective-permute-start | bytes 6152 | tf_op jit(solution)/shard_map/ppermute | solution.py:573
  27.8 1.4 %collective-permute-start.2 = (f32[4,128]{1,0:T(4,128)}, f32[4,128]{1,0:T(4,128)S(1)}, u32[]{:S(2)}, u32[]{:S(2)}) collective-permute-start(f32[4,128]{1,0:T(4,128)} %get-tuple-element.27), channel_id=1, source_target_pairs={{0,24},{8,0},{16,8},{24,16},{1,25},{9,1},{17,9},{25,17},{2,26},{10... | collective-permute-start | bytes 6152 | tf_op jit(solution)/shard_map/ppermute | solution.py:573
  29.2 2.4 %collective-permute-done.1.refs_1_ = f32[4,128]{1,0:T(4,128)S(1)} collective-permute-done((f32[4,128]{1,0:T(4,128)}, f32[4,128]{1,0:T(4,128)S(1)}, u32[]{:S(2)}, u32[]{:S(2)}) %collective-permute-start.1) | collective-permute-done | bytes 2080 | tf_op jit(solution)/shard_map/ppermute | solution.py:573
  31.6 0.8 copy-done
  33.2 5.7 %all-to-all-start.1 = ((bf16[8,4,32,128]{3,2,1,0:T(8,128)(2,1)}), bf16[8,4,32,128]{3,2,1,0:T(8,128)(2,1)S(1)}, u32[]{:S(2)}, u32[]{:S(2)}) async-start(bf16[8,4,32,128]{3,2,1,0:T(8,128)(2,1)} %get-tuple-element.29), calls=%async_computation.1 | async-start | bytes 524288 | tf_op jit(solution)/shard_map/all_to_all | solution.py:579
  39.4 1.0 collective-permute-start.7
  40.4 0.8 copy-done.1
  41.5 1.8 %collective-permute-done.7.refs_2_ = bf16[4,32,128]{2,1,0:T(8,128)(2,1)S(1)} collective-permute-done((bf16[4,32,128]{2,1,0:T(8,128)(2,1)S(1)}, bf16[4,32,128]{2,1,0:T(8,128)(2,1)S(1)}, u32[]{:S(2)}, u32[]{:S(2)}) %collective-permute-start.7) | collective-permute-done | bytes 32800 | tf_op jit(solution)/shard_map/ppermute | solution.py:573
  44.4 3.8 %backward_product.2 = bf16[8,160,128]{2,1,0:T(8,128)(2,1)} custom-call(s32[1,1,256]{2,1,0:T(1,128)S(1)} %copy-done.3, s32[1,1]{1,0:T(1,128)S(6)} %copy.7.live_ref, bf16[1024,128,128]{2,1,0:T(8,128)(2,1)} %get-tuple-element.34.block_hbm, bf16[4,32,128]{2,1,0:T(8,128)(2,1)S(1)} %get-tuple-element.35.refs_0_, ...), custom_call_target="tpu_custom_call" | custom-call | flops 268435456 | bytes 8388608 | tf_op jit(solution)/shard_map/backward_product/pallas_call | solution.py:351
  48.3 6.1 %all-to-all-start.2 = ((bf16[8,160,128]{2,1,0:T(8,128)(2,1)}), bf16[8,160,128]{2,1,0:T(8,128)(2,1)S(1)}, u32[]{:S(2)}, u32[]{:S(2)}) async-start(bf16[8,160,128]{2,1,0:T(8,128)(2,1)} %backward_product.2), calls=%async_computation.2 | async-start | bytes 655360 | tf_op jit(solution)/shard_map/all_to_all | solution.py:579
  54.4 3.1 %forward_product.2 = (bf16[4,32,128]{2,1,0:T(8,128)(2,1)S(1)}, bf16[4,32,128]{2,1,0:T(8,128)(2,1)S(1)}, bf16[4,32,128]{2,1,0:T(8,128)(2,1)S(1)}, bf16[4,32,128]{2,1,0:T(8,128)(2,1)S(1)}) custom-call(s32[1,1,256]{2,1,0:T(1,128)S(1)} %copy-done.4, s32[1,1]{1,0:T(1,128)S(6)} %copy.7.live_ref, bf16[1024,128,128]{2,1,0:T(8,128)(2,1)} %get-tuple-element.24.block_hbm, ...), custom_call_target="tpu_custom_call" | custom-call | flops 268435456 | bytes 8388608 | tf_op jit(solution)/shard_map/forward_product/pallas_call | solution.py:351
  58.3 1.4 %collective-permute-start.5 = (bf16[4,32,128]{2,1,0:T(8,128)(2,1)S(1)}, bf16[4,32,128]{2,1,0:T(8,128)(2,1)S(1)}, u32[]{:S(2)}, u32[]{:S(2)}) collective-permute-start(bf16[4,32,128]{2,1,0:T(8,128)(2,1)S(1)} %get-tuple-element.33), channel_id=1, source_target_pairs={{0,24},{8,0},{16,8},{24,16},{1,25},{9,1},{17,9},{25,17},{2,26},{10... | collective-permute-start | bytes 98312 | tf_op jit(solution)/shard_map/ppermute | solution.py:573
  59.7 1.2 %collective-permute-done.3.refs_1_ = bf16[4,32,128]{2,1,0:T(8,128)(2,1)S(1)} collective-permute-done((bf16[4,32,128]{2,1,0:T(8,128)(2,1)S(1)}, bf16[4,32,128]{2,1,0:T(8,128)(2,1)S(1)}, u32[]{:S(2)}, u32[]{:S(2)}) %collective-permute-start.3) | collective-permute-done | bytes 32800 | tf_op jit(solution)/shard_map/ppermute | solution.py:573
  61.6 1.5 %all-to-all-done.2.refs_4_.first_col_ref = bf16[8,160,128]{2,1,0:T(8,128)(2,1)S(1)} async-done(((bf16[8,160,128]{2,1,0:T(8,128)(2,1)}), bf16[8,160,128]{2,1,0:T(8,128)(2,1)S(1)}, u32[]{:S(2)}, u32[]{:S(2)}) %all-to-all-start.2) | async-done | bytes 327712 | tf_op jit(solution)/shard_map/all_to_all | solution.py:579
  63.1 1.1 %middle.1 = (f32[4,32,128]{2,1,0:T(8,128)S(1)}, bf16[4,32,128]{2,1,0:T(8,128)(2,1)S(1)}, bf16[8,5,32,128]{3,2,1,0:T(8,128)(2,1)}) custom-call(bf16[4,32,128]{2,1,0:T(8,128)(2,1)S(1)} %get-tuple-element.30.refs_0_, bf16[4,32,128]{2,1,0:T(8,128)(2,1)S(1)} %collective-permute-done.3.refs_1_, bf16[4,32,128]{2,1,0:T(8,128)(2,1)S(1)} %collective-permute-done.4.refs_2_, ...), custom_call_target="tpu_custom_call" | custom-call | tf_op jit(solution)/shard_map/middle/pallas_call | solution.py:583
  64.2 4.9 %all-to-all-start.3 = ((bf16[8,5,32,128]{3,2,1,0:T(8,128)(2,1)}), bf16[8,5,32,128]{3,2,1,0:T(8,128)(2,1)S(1)}, u32[]{:S(2)}, u32[]{:S(2)}) async-start(bf16[8,5,32,128]{3,2,1,0:T(8,128)(2,1)} %get-tuple-element.37), calls=%async_computation.3 | async-start | bytes 655360 | tf_op jit(solution)/shard_map/all_to_all | solution.py:579
  69.1 0.8 collective-permute-start.14
  69.9 1.7 %collective-permute-start.13 = (bf16[4,32,128]{2,1,0:T(8,128)(2,1)S(1)}, bf16[4,32,128]{2,1,0:T(8,128)(2,1)S(1)}, u32[]{:S(2)}, u32[]{:S(2)}) collective-permute-start(bf16[4,32,128]{2,1,0:T(8,128)(2,1)S(1)} %get-tuple-element.42.refs_0_), channel_id=1, source_target_pairs={{0,16},{8,24},{16,0},{24,8},{1,17},{9,25},{17,1},{25,9},{2,18},{10... | collective-permute-start | bytes 98312 | tf_op jit(solution)/shard_map/ppermute | solution.py:573
  71.6 2.2 %collective-permute-done.13.refs_2_ = bf16[4,32,128]{2,1,0:T(8,128)(2,1)S(1)} collective-permute-done((bf16[4,32,128]{2,1,0:T(8,128)(2,1)S(1)}, bf16[4,32,128]{2,1,0:T(8,128)(2,1)S(1)}, u32[]{:S(2)}, u32[]{:S(2)}) %collective-permute-start.13) | collective-permute-done | bytes 32800 | tf_op jit(solution)/shard_map/ppermute | solution.py:573
  73.8 1.1 %collective-permute-done.12.refs_1_ = bf16[4,32,128]{2,1,0:T(8,128)(2,1)S(1)} collective-permute-done((bf16[4,32,128]{2,1,0:T(8,128)(2,1)S(1)}, bf16[4,32,128]{2,1,0:T(8,128)(2,1)S(1)}, u32[]{:S(2)}, u32[]{:S(2)}) %collective-permute-start.12) | collective-permute-done | bytes 32800 | tf_op jit(solution)/shard_map/ppermute | solution.py:573
  74.9 3.1 %backward_product.3.total_ref = bf16[8,128,128]{2,1,0:T(8,128)(2,1)S(1)} custom-call(s32[1,1,256]{2,1,0:T(1,128)S(1)} %copy-done.4, s32[1,1]{1,0:T(1,128)S(6)} %copy.7.live_ref, bf16[1024,128,128]{2,1,0:T(8,128)(2,1)} %get-tuple-element.34.block_hbm, bf16[4,32,128]{2,1,0:T(8,128)(2,1)S(1)} %get-tuple-element.42.refs_0_, ...), custom_call_target="tpu_custom_call" | custom-call | flops 268435456 | bytes 8388608 | tf_op jit(solution)/shard_map/backward_product/pallas_call | solution.py:351
  78.0 2.7 %all-to-all-done.3.col_dir_ref = bf16[8,5,32,128]{3,2,1,0:T(8,128)(2,1)S(1)} async-done(((bf16[8,5,32,128]{3,2,1,0:T(8,128)(2,1)}), bf16[8,5,32,128]{3,2,1,0:T(8,128)(2,1)S(1)}, u32[]{:S(2)}, u32[]{:S(2)}) %all-to-all-start.3) | async-done | bytes 327712 | tf_op jit(solution)/shard_map/all_to_all | solution.py:579
  80.7 1.1 %attach.1 = (bf16[8,144,128]{2,1,0:T(8,128)(2,1)}, f32[32,128]{1,0:T(8,128)S(1)}) custom-call(bf16[8,160,128]{2,1,0:T(8,128)(2,1)S(1)} %all-to-all-done.2.refs_4_.first_col_ref, bf16[8,5,32,128]{3,2,1,0:T(8,128)(2,1)S(1)} %all-to-all-done.3.col_dir_ref, bf16[8,128,128]{2,1,0:T(8,128)(2,1)S(1)} %backward_product.3.total_ref), custom_call_target="tpu_custom_call" | custom-call | tf_op jit(solution)/shard_map/attach/pallas_call | solution.py:583
  81.8 3.6 %all-to-all-start.4 = ((bf16[8,144,128]{2,1,0:T(8,128)(2,1)}), bf16[8,144,128]{2,1,0:T(8,128)(2,1)S(1)}, u32[]{:S(2)}, u32[]{:S(2)}) async-start(bf16[8,144,128]{2,1,0:T(8,128)(2,1)} %get-tuple-element.43), calls=%async_computation.4 | async-start | bytes 589824 | tf_op jit(solution)/shard_map/all_to_all | solution.py:579
  85.4 3.1 %forward_product.3 = (bf16[4,32,128]{2,1,0:T(8,128)(2,1)S(1)}, bf16[4,32,128]{2,1,0:T(8,128)(2,1)S(1)}, bf16[4,32,128]{2,1,0:T(8,128)(2,1)S(1)}, bf16[4,32,128]{2,1,0:T(8,128)(2,1)S(1)}) custom-call(s32[1,1,256]{2,1,0:T(1,128)S(1)} %copy-done.4, s32[1,1]{1,0:T(1,128)S(6)} %copy.7.live_ref, bf16[1024,128,128]{2,1,0:T(8,128)(2,1)} %get-tuple-element.24.block_hbm, ...), custom_call_target="tpu_custom_call" | custom-call | flops 268435456 | bytes 8388608 | tf_op jit(solution)/shard_map/forward_product/pallas_call | solution.py:351
  89.0 1.4 %collective-permute-start.11 = (bf16[4,32,128]{2,1,0:T(8,128)(2,1)S(1)}, bf16[4,32,128]{2,1,0:T(8,128)(2,1)S(1)}, u32[]{:S(2)}, u32[]{:S(2)}) collective-permute-start(bf16[4,32,128]{2,1,0:T(8,128)(2,1)S(1)} %get-tuple-element.41), channel_id=1, source_target_pairs={{0,24},{8,0},{16,8},{24,16},{1,25},{9,1},{17,9},{25,17},{2,26},{10... | collective-permute-start | bytes 98312 | tf_op jit(solution)/shard_map/ppermute | solution.py:573
  90.4 4.9 %all-to-all-done.4.col_ref.refs_8_ = bf16[8,144,128]{2,1,0:T(8,128)(2,1)S(1)} async-done(((bf16[8,144,128]{2,1,0:T(8,128)(2,1)}), bf16[8,144,128]{2,1,0:T(8,128)(2,1)S(1)}, u32[]{:S(2)}, u32[]{:S(2)}) %all-to-all-start.4) | async-done | bytes 294944 | tf_op jit(solution)/shard_map/all_to_all | solution.py:579
  96.0 0.9 collective-permute-done.17.refs_7_
  96.9 2.4 %collective-permute-done.16.refs_6_ = f32[32,128]{1,0:T(8,128)S(1)} collective-permute-done((f32[32,128]{1,0:T(8,128)S(1)}, f32[32,128]{1,0:T(8,128)S(1)}, u32[]{:S(2)}, u32[]{:S(2)}) %collective-permute-start.16) | collective-permute-done | bytes 16416 | tf_op jit(solution)/shard_map/ppermute | solution.py:573
  99.3 4.7 %close.1 = (f32[32,512]{1,0:T(8,128)}, f32[32,512]{1,0:T(8,128)}) custom-call(bf16[4,32,128]{2,1,0:T(8,128)(2,1)S(1)} %get-tuple-element.38.refs_0_, bf16[4,32,128]{2,1,0:T(8,128)(2,1)S(1)} %collective-permute-done.9.refs_1_, bf16[4,32,128]{2,1,0:T(8,128)(2,1)S(1)} %collective-permute-done.10.refs_2_, ...), custom_call_target="tpu_custom_call" | custom-call | tf_op jit(solution)/shard_map/close/pallas_call | solution.py:583
  (35 shorter events, 5.3 us)
Async XLA Ops:
  0.6 53.8 %copy-start.4 = (s32[1,1,256]{2,1,0:T(1,128)S(1)}, s32[1,1,256]{2,1,0:T(1,128)}, u32[]{:S(2)}) copy-start(s32[1,1,256]{2,1,0:T(1,128)} %spots_ref.9) | copy-start | bytes 3076
  12.1 19.5 %all-to-all-start = ((f32[8,4,128]{2,1,0:T(4,128)}), f32[8,4,128]{2,1,0:T(4,128)S(1)}, u32[]{:S(2)}, u32[]{:S(2)}) async-start(f32[8,4,128]{2,1,0:T(4,128)} %bitcast.5), calls=%async_computation | async-start | bytes 32768 | tf_op jit(solution)/shard_map/all_to_all | solution.py:579
  21.8 7.4 %collective-permute-start = (f32[4,128]{1,0:T(4,128)}, f32[4,128]{1,0:T(4,128)S(1)}, u32[]{:S(2)}, u32[]{:S(2)}) collective-permute-start(f32[4,128]{1,0:T(4,128)} %get-tuple-element.25), channel_id=1, source_target_pairs={{0,8},{8,16},{16,24},{24,0},{1,9},{9,17},{17,25},{25,1},{2,10},{10... | collective-permute-start | bytes 6152 | tf_op jit(solution)/shard_map/ppermute | solution.py:573
  27.8 3.8 %collective-permute-start.1 = (f32[4,128]{1,0:T(4,128)}, f32[4,128]{1,0:T(4,128)S(1)}, u32[]{:S(2)}, u32[]{:S(2)}) collective-permute-start(f32[4,128]{1,0:T(4,128)} %get-tuple-element.26), channel_id=1, source_target_pairs={{0,16},{8,24},{16,0},{24,8},{1,17},{9,25},{17,1},{25,9},{2,18},{10... | collective-permute-start | bytes 6152 | tf_op jit(solution)/shard_map/ppermute | solution.py:573
  27.8 3.8 %collective-permute-start.2 = (f32[4,128]{1,0:T(4,128)}, f32[4,128]{1,0:T(4,128)S(1)}, u32[]{:S(2)}, u32[]{:S(2)}) collective-permute-start(f32[4,128]{1,0:T(4,128)} %get-tuple-element.27), channel_id=1, source_target_pairs={{0,24},{8,0},{16,8},{24,16},{1,25},{9,1},{17,9},{25,17},{2,26},{10... | collective-permute-start | bytes 6152 | tf_op jit(solution)/shard_map/ppermute | solution.py:573
  31.6 0.8 copy-start
  33.2 15.0 %all-to-all-start.1 = ((bf16[8,4,32,128]{3,2,1,0:T(8,128)(2,1)}), bf16[8,4,32,128]{3,2,1,0:T(8,128)(2,1)S(1)}, u32[]{:S(2)}, u32[]{:S(2)}) async-start(bf16[8,4,32,128]{3,2,1,0:T(8,128)(2,1)} %get-tuple-element.29), calls=%async_computation.1 | async-start | bytes 524288 | tf_op jit(solution)/shard_map/all_to_all | solution.py:579
  38.9 2.6 %collective-permute-start.8 = (bf16[4,32,128]{2,1,0:T(8,128)(2,1)S(1)}, bf16[4,32,128]{2,1,0:T(8,128)(2,1)S(1)}, u32[]{:S(2)}, u32[]{:S(2)}) collective-permute-start(bf16[4,32,128]{2,1,0:T(8,128)(2,1)S(1)} %get-tuple-element.35.refs_0_), channel_id=1, source_target_pairs={{0,24},{8,0},{16,8},{24,16},{1,25},{9,1},{17,9},{25,17},{2,26},{10... | collective-permute-start | bytes 98312 | tf_op jit(solution)/shard_map/ppermute | solution.py:573
  39.4 3.9 %collective-permute-start.7 = (bf16[4,32,128]{2,1,0:T(8,128)(2,1)S(1)}, bf16[4,32,128]{2,1,0:T(8,128)(2,1)S(1)}, u32[]{:S(2)}, u32[]{:S(2)}) collective-permute-start(bf16[4,32,128]{2,1,0:T(8,128)(2,1)S(1)} %get-tuple-element.35.refs_0_), channel_id=1, source_target_pairs={{0,16},{8,24},{16,0},{24,8},{1,17},{9,25},{17,1},{25,9},{2,18},{10... | collective-permute-start | bytes 98312 | tf_op jit(solution)/shard_map/ppermute | solution.py:573
  40.4 3.3 %collective-permute-start.6 = (bf16[4,32,128]{2,1,0:T(8,128)(2,1)S(1)}, bf16[4,32,128]{2,1,0:T(8,128)(2,1)S(1)}, u32[]{:S(2)}, u32[]{:S(2)}) collective-permute-start(bf16[4,32,128]{2,1,0:T(8,128)(2,1)S(1)} %get-tuple-element.35.refs_0_), channel_id=1, source_target_pairs={{0,8},{8,16},{16,24},{24,0},{1,9},{9,17},{17,25},{25,1},{2,10},{10... | collective-permute-start | bytes 98312 | tf_op jit(solution)/shard_map/ppermute | solution.py:573
  40.4 0.8 copy-start.1
  43.7 0.7 copy-start.3
  44.4 18.7 %copy-start.2 = (f32[32,512]{1,0:T(8,128)S(1)}, f32[32,512]{1,0:T(8,128)}, u32[]{:S(2)}) copy-start(f32[32,512]{1,0:T(8,128)} %refs_10_.1) | copy-start | bytes 196612
  48.3 14.8 %all-to-all-start.2 = ((bf16[8,160,128]{2,1,0:T(8,128)(2,1)}), bf16[8,160,128]{2,1,0:T(8,128)(2,1)S(1)}, u32[]{:S(2)}, u32[]{:S(2)}) async-start(bf16[8,160,128]{2,1,0:T(8,128)(2,1)} %backward_product.2), calls=%async_computation.2 | async-start | bytes 655360 | tf_op jit(solution)/shard_map/all_to_all | solution.py:579
  57.5 3.4 %collective-permute-start.3 = (bf16[4,32,128]{2,1,0:T(8,128)(2,1)S(1)}, bf16[4,32,128]{2,1,0:T(8,128)(2,1)S(1)}, u32[]{:S(2)}, u32[]{:S(2)}) collective-permute-start(bf16[4,32,128]{2,1,0:T(8,128)(2,1)S(1)} %get-tuple-element.31), channel_id=1, source_target_pairs={{0,8},{8,16},{16,24},{24,0},{1,9},{9,17},{17,25},{25,1},{2,10},{10... | collective-permute-start | bytes 98312 | tf_op jit(solution)/shard_map/ppermute | solution.py:573
  57.5 4.1 %collective-permute-start.4 = (bf16[4,32,128]{2,1,0:T(8,128)(2,1)S(1)}, bf16[4,32,128]{2,1,0:T(8,128)(2,1)S(1)}, u32[]{:S(2)}, u32[]{:S(2)}) collective-permute-start(bf16[4,32,128]{2,1,0:T(8,128)(2,1)S(1)} %get-tuple-element.32), channel_id=1, source_target_pairs={{0,16},{8,24},{16,0},{24,8},{1,17},{9,25},{17,1},{25,9},{2,18},{10... | collective-permute-start | bytes 98312 | tf_op jit(solution)/shard_map/ppermute | solution.py:573
  58.3 3.3 %collective-permute-start.5 = (bf16[4,32,128]{2,1,0:T(8,128)(2,1)S(1)}, bf16[4,32,128]{2,1,0:T(8,128)(2,1)S(1)}, u32[]{:S(2)}, u32[]{:S(2)}) collective-permute-start(bf16[4,32,128]{2,1,0:T(8,128)(2,1)S(1)} %get-tuple-element.33), channel_id=1, source_target_pairs={{0,24},{8,0},{16,8},{24,16},{1,25},{9,1},{17,9},{25,17},{2,26},{10... | collective-permute-start | bytes 98312 | tf_op jit(solution)/shard_map/ppermute | solution.py:573
  64.2 16.5 %all-to-all-start.3 = ((bf16[8,5,32,128]{3,2,1,0:T(8,128)(2,1)}), bf16[8,5,32,128]{3,2,1,0:T(8,128)(2,1)S(1)}, u32[]{:S(2)}, u32[]{:S(2)}) async-start(bf16[8,5,32,128]{3,2,1,0:T(8,128)(2,1)} %get-tuple-element.37), calls=%async_computation.3 | async-start | bytes 655360 | tf_op jit(solution)/shard_map/all_to_all | solution.py:579
  69.1 2.5 %collective-permute-start.14 = (bf16[4,32,128]{2,1,0:T(8,128)(2,1)S(1)}, bf16[4,32,128]{2,1,0:T(8,128)(2,1)S(1)}, u32[]{:S(2)}, u32[]{:S(2)}) collective-permute-start(bf16[4,32,128]{2,1,0:T(8,128)(2,1)S(1)} %get-tuple-element.42.refs_0_), channel_id=1, source_target_pairs={{0,24},{8,0},{16,8},{24,16},{1,25},{9,1},{17,9},{25,17},{2,26},{10... | collective-permute-start | bytes 98312 | tf_op jit(solution)/shard_map/ppermute | solution.py:573
  69.9 3.9 %collective-permute-start.13 = (bf16[4,32,128]{2,1,0:T(8,128)(2,1)S(1)}, bf16[4,32,128]{2,1,0:T(8,128)(2,1)S(1)}, u32[]{:S(2)}, u32[]{:S(2)}) collective-permute-start(bf16[4,32,128]{2,1,0:T(8,128)(2,1)S(1)} %get-tuple-element.42.refs_0_), channel_id=1, source_target_pairs={{0,16},{8,24},{16,0},{24,8},{1,17},{9,25},{17,1},{25,9},{2,18},{10... | collective-permute-start | bytes 98312 | tf_op jit(solution)/shard_map/ppermute | solution.py:573
  71.6 3.3 %collective-permute-start.12 = (bf16[4,32,128]{2,1,0:T(8,128)(2,1)S(1)}, bf16[4,32,128]{2,1,0:T(8,128)(2,1)S(1)}, u32[]{:S(2)}, u32[]{:S(2)}) collective-permute-start(bf16[4,32,128]{2,1,0:T(8,128)(2,1)S(1)} %get-tuple-element.42.refs_0_), channel_id=1, source_target_pairs={{0,8},{8,16},{16,24},{24,0},{1,9},{9,17},{17,25},{25,1},{2,10},{10... | collective-permute-start | bytes 98312 | tf_op jit(solution)/shard_map/ppermute | solution.py:573
  81.8 13.5 %all-to-all-start.4 = ((bf16[8,144,128]{2,1,0:T(8,128)(2,1)}), bf16[8,144,128]{2,1,0:T(8,128)(2,1)S(1)}, u32[]{:S(2)}, u32[]{:S(2)}) async-start(bf16[8,144,128]{2,1,0:T(8,128)(2,1)} %get-tuple-element.43), calls=%async_computation.4 | async-start | bytes 589824 | tf_op jit(solution)/shard_map/all_to_all | solution.py:579
  88.5 7.3 %collective-permute-start.9 = (bf16[4,32,128]{2,1,0:T(8,128)(2,1)S(1)}, bf16[4,32,128]{2,1,0:T(8,128)(2,1)S(1)}, u32[]{:S(2)}, u32[]{:S(2)}) collective-permute-start(bf16[4,32,128]{2,1,0:T(8,128)(2,1)S(1)} %get-tuple-element.39), channel_id=1, source_target_pairs={{0,8},{8,16},{16,24},{24,0},{1,9},{9,17},{17,25},{25,1},{2,10},{10... | collective-permute-start | bytes 98312 | tf_op jit(solution)/shard_map/ppermute | solution.py:573
  88.8 7.2 %collective-permute-start.10 = (bf16[4,32,128]{2,1,0:T(8,128)(2,1)S(1)}, bf16[4,32,128]{2,1,0:T(8,128)(2,1)S(1)}, u32[]{:S(2)}, u32[]{:S(2)}) collective-permute-start(bf16[4,32,128]{2,1,0:T(8,128)(2,1)S(1)} %get-tuple-element.40), channel_id=1, source_target_pairs={{0,16},{8,24},{16,0},{24,8},{1,17},{9,25},{17,1},{25,9},{2,18},{10... | collective-permute-start | bytes 98312 | tf_op jit(solution)/shard_map/ppermute | solution.py:573
  89.0 7.0 %collective-permute-start.11 = (bf16[4,32,128]{2,1,0:T(8,128)(2,1)S(1)}, bf16[4,32,128]{2,1,0:T(8,128)(2,1)S(1)}, u32[]{:S(2)}, u32[]{:S(2)}) collective-permute-start(bf16[4,32,128]{2,1,0:T(8,128)(2,1)S(1)} %get-tuple-element.41), channel_id=1, source_target_pairs={{0,24},{8,0},{16,8},{24,16},{1,25},{9,1},{17,9},{25,17},{2,26},{10... | collective-permute-start | bytes 98312 | tf_op jit(solution)/shard_map/ppermute | solution.py:573
  95.4 1.4 %collective-permute-start.17 = (f32[32,128]{1,0:T(8,128)S(1)}, f32[32,128]{1,0:T(8,128)S(1)}, u32[]{:S(2)}, u32[]{:S(2)}) collective-permute-start(f32[32,128]{1,0:T(8,128)S(1)} %gram_sum.1.refs_4_), channel_id=1, source_target_pairs={{0,24},{8,0},{16,8},{24,16},{1,25},{9,1},{17,9},{25,17},{2,26},{10... | collective-permute-start | bytes 49160 | tf_op jit(solution)/shard_map/ppermute | solution.py:573
  95.4 3.8 %collective-permute-start.16 = (f32[32,128]{1,0:T(8,128)S(1)}, f32[32,128]{1,0:T(8,128)S(1)}, u32[]{:S(2)}, u32[]{:S(2)}) collective-permute-start(f32[32,128]{1,0:T(8,128)S(1)} %gram_sum.1.refs_4_), channel_id=1, source_target_pairs={{0,16},{8,24},{16,0},{24,8},{1,17},{9,25},{17,1},{25,9},{2,18},{10... | collective-permute-start | bytes 49160 | tf_op jit(solution)/shard_map/ppermute | solution.py:573
  95.8 3.5 %collective-permute-start.15 = (f32[32,128]{1,0:T(8,128)S(1)}, f32[32,128]{1,0:T(8,128)S(1)}, u32[]{:S(2)}, u32[]{:S(2)}) collective-permute-start(f32[32,128]{1,0:T(8,128)S(1)} %gram_sum.1.refs_4_), channel_id=1, source_target_pairs={{0,8},{8,16},{16,24},{24,0},{1,9},{9,17},{17,25},{25,1},{2,10},{10... | collective-permute-start | bytes 49160 | tf_op jit(solution)/shard_map/ppermute | solution.py:573
